TPU v7x, 32 devices: a whole 2x2x4 slice. The times are simulated.
32 devices in a mesh: clip: 2 (over x), seq: 16 (over z, y, core).
Axes of the slice: x: 2, y: 2, z: 4, core: 2. Of those that a mesh axis runs over, the one named last changes fastest.
Arguments:
- video_query: bfloat16 [512, 4096], P(('clip', 'seq')), parts along dimension 0, may hold values from -6 to 6
- video_keys: bfloat16 [512, 4096], P(('clip', 'seq')), parts along dimension 0, may hold values from -6 to 6
- video_values: bfloat16 [512, 4096], P(('clip', 'seq')), parts along dimension 0, may hold values from -6 to 6
- audio_query: bfloat16 [256, 2048], P(('clip', 'seq')), parts along dimension 0, may hold values from -6 to 6
- audio_keys: bfloat16 [256, 2048], P(('clip', 'seq')), parts along dimension 0, may hold values from -6 to 6
- audio_values: bfloat16 [256, 2048], P(('clip', 'seq')), parts along dimension 0, may hold values from -6 to 6
- cross_video_query: bfloat16 [512, 2048], P(('clip', 'seq')), parts along dimension 0, may hold values from -6 to 6
- cross_video_keys: bfloat16 [512, 2048], P(('clip', 'seq')), parts along dimension 0, may hold values from -6 to 6
- cross_video_values: bfloat16 [512, 2048], P(('clip', 'seq')), parts along dimension 0, may hold values from -6 to 6
- cross_audio_query: bfloat16 [256, 2048], P(('clip', 'seq')), parts along dimension 0, may hold values from -6 to 6
- cross_audio_keys: bfloat16 [256, 2048], P(('clip', 'seq')), parts along dimension 0, may hold values from -6 to 6
- cross_audio_values: bfloat16 [256, 2048], P(('clip', 'seq')), parts along dimension 0, may hold values from -6 to 6
- video_length: int32 [2], P('clip'), parts along dimension 0, may hold values from 128 to 256
- audio_length: int32 [2], P('clip'), parts along dimension 0, may hold values from 64 to 128
- align_offset: int32 [2], P('clip'), parts along dimension 0, may hold values from -8 to 8
Outputs:
- video_mixed: bfloat16 [512, 4096], P(('clip', 'seq')), parts along dimension 0
- audio_mixed: bfloat16 [256, 2048], P(('clip', 'seq')), parts along dimension 0
- video_cross: bfloat16 [512, 2048], P(('clip', 'seq')), parts along dimension 0
- audio_cross: bfloat16 [256, 2048], P(('clip', 'seq')), parts along dimension 0
There are 2 independent parts, one for each index of `clip`. A program takes and returns all parts, laid end to end along the dimension named above; each array names one. Nothing has to cross between parts.
All inputs are finite; a program needn't handle non-finite values.
Results may differ from a plain program's by a relative error of at most 0.006.
Values may be sent and summed in bfloat16 or wider, within the bound.
No kernel may reach another device: no remote copies, remote signals or barrier semaphores. Data moves between devices by JAX's collectives and lax.ppermute only.
A program may use at most 128 MiB of HBM per device.

v0:
```python
import math

import jax
import jax.numpy as jnp
from jax import lax
from jax.sharding import PartitionSpec as P

HV = 32
HDV = 128
HA = 32
HDA = 64


def block_size(total, limit):
    chosen = min(total, limit)
    while total % chosen:
        chosen -= 1
    return chosen


def split_heads(tokens, heads, depth, copies):
    rows = tokens.shape[0]
    shaped = tokens.reshape(copies, rows // copies, heads, depth).transpose(2, 0, 1, 3)
    return shaped.reshape(heads * copies, rows // copies, depth)


def spread_heads(tokens, heads, depth, copies):
    rows = tokens.shape[0]
    shaped = tokens.reshape(rows, heads, depth).transpose(1, 0, 2)
    shaped = jnp.broadcast_to(shaped[:, None], (heads, copies, rows, depth))
    return shaped.reshape(heads * copies, rows, depth)


def join_heads(owned, heads, depth, copies):
    part_rows = owned.shape[1]
    shaped = owned.reshape(heads, copies, part_rows, depth).transpose(1, 2, 0, 3)
    return shaped.reshape(copies * part_rows, heads * depth)


def owned_positions(rows, copies, devices, index):
    part_rows = rows // copies
    flat = jnp.arange(devices * part_rows, dtype=jnp.int32)
    return flat // part_rows * rows + index % copies * part_rows + flat % part_rows


def online_update(carry, scores, permit, value_tile, value_form):
    running, total, accum = carry
    scores = jnp.where(permit, scores, -1e30)
    newmax = jnp.maximum(running, jnp.max(scores, axis=2))
    weights = jnp.where(permit, jnp.exp(scores - newmax[:, :, None]), 0.0)
    factor = jnp.exp(running - newmax)
    total = total * factor + jnp.sum(weights, axis=2)
    mixed = jnp.einsum(
        value_form, weights.astype(jnp.bfloat16), value_tile, preferred_element_type=jnp.float32
    )
    accum = accum * factor[:, :, None] + mixed
    return (newmax, total, accum)


def fold_initial(rows, heads, depth):
    return (
        jnp.full((heads, rows), -1e30, jnp.float32),
        jnp.zeros((heads, rows), jnp.float32),
        jnp.zeros((heads, rows, depth), jnp.float32),
    )


def fold_piece(carry, local_query, key_rows, value_rows, permit, heads, depth):
    keyed = key_rows.reshape(key_rows.shape[0], heads, depth)
    valued = value_rows.reshape(value_rows.shape[0], heads, depth)
    scores = jnp.einsum("qhd,khd->hqk", local_query, keyed, preferred_element_type=jnp.float32) * (
        1.0 / math.sqrt(depth)
    )
    return online_update(carry, scores, permit[None], valued, "hqk,khd->hqd")


def fold_finish(carry, heads, depth):
    running, total, accum = carry
    result = (accum / total[:, :, None]).astype(jnp.bfloat16)
    return result.transpose(1, 0, 2).reshape(result.shape[1], heads * depth)


def attend_local(queries, keys, values, query_pos, key_pos, allowed):
    heads, q_count, depth = queries.shape
    k_count = keys.shape[1]
    q_block = block_size(q_count, 512)
    k_block = block_size(k_count, 2048)
    scale = 1.0 / math.sqrt(depth)
    q_tiles = queries.reshape(heads, q_count // q_block, q_block, depth).transpose(1, 0, 2, 3)
    k_tiles = keys.reshape(heads, k_count // k_block, k_block, depth).transpose(1, 0, 2, 3)
    v_tiles = values.reshape(heads, k_count // k_block, k_block, depth).transpose(1, 0, 2, 3)
    q_places = query_pos.reshape(q_count // q_block, q_block)
    k_places = key_pos.reshape(k_count // k_block, k_block)

    def one_tile(packed):
        q_tile, q_where = packed

        def absorb(carry, piece):
            k_tile, v_tile, k_where = piece
            scores = (
                jnp.einsum("hqd,hkd->hqk", q_tile, k_tile, preferred_element_type=jnp.float32)
                * scale
            )
            permit = allowed(q_where[:, None], k_where[None, :])[None]
            return (online_update(carry, scores, permit, v_tile, "hqk,hkd->hqd"), None)

        initial = fold_initial(q_block, heads, depth)
        final_state, unused = lax.scan(absorb, initial, (k_tiles, v_tiles, k_places))
        running, total, accum = final_state
        return (accum / total[:, :, None]).astype(jnp.bfloat16)

    tiles = lax.map(one_tile, (q_tiles, q_places))
    return tiles.transpose(1, 0, 2, 3).reshape(heads, q_count, depth)


def shards(
    video_query,
    video_keys,
    video_values,
    audio_query,
    audio_keys,
    audio_values,
    cross_video_query,
    cross_video_keys,
    cross_video_values,
    cross_audio_query,
    cross_audio_keys,
    cross_audio_values,
    video_length,
    audio_length,
    align_offset,
):
    devices = lax.axis_size("seq")
    index = lax.axis_index("seq")
    video_rows = video_query.shape[0]
    audio_rows = audio_query.shape[0]
    video_total = video_rows * devices
    audio_total = audio_rows * devices
    video_reach = video_total // 8
    audio_reach = 5 * audio_total // 8
    video_valid = video_length[0]
    audio_valid = audio_length[0]
    align_shift = align_offset[0]
    copies = max(devices // HV, 1)
    video_places = jnp.arange(video_total, dtype=jnp.int32)
    audio_places = jnp.arange(audio_total, dtype=jnp.int32)

    def video_open(q_where, k_where):
        return k_where < video_valid

    def toward_video(q_where, k_where):
        center = jnp.clip(q_where * audio_total // video_total + align_shift, 0, audio_valid - 1)
        return (k_where < audio_valid) & (jnp.abs(k_where - center) <= audio_reach)

    def toward_audio(q_where, k_where):
        center = jnp.clip((q_where - align_shift) * video_total // audio_total, 0, video_valid - 1)
        return (k_where < video_valid) & (jnp.abs(k_where - center) <= video_reach)

    video_owned = (
        lax.all_to_all(
            split_heads(video_query, HV, HDV, copies),
            "seq",
            split_axis=0,
            concat_axis=1,
            tiled=True,
        ),
        lax.all_to_all(
            spread_heads(video_keys, HV, HDV, copies),
            "seq",
            split_axis=0,
            concat_axis=1,
            tiled=True,
        ),
        lax.all_to_all(
            spread_heads(video_values, HV, HDV, copies),
            "seq",
            split_axis=0,
            concat_axis=1,
            tiled=True,
        ),
    )
    video_done = attend_local(
        video_owned[0],
        video_owned[1],
        video_owned[2],
        owned_positions(video_rows, copies, devices, index),
        video_places,
        video_open,
    )
    video_mixed = join_heads(
        lax.all_to_all(video_done, "seq", split_axis=1, concat_axis=0, tiled=True), HV, HDV, copies
    )
    audio_local = audio_query.reshape(audio_rows, HA, HDA)
    piece = (
        lax.all_gather(audio_keys, "seq", axis=0, tiled=True),
        lax.all_gather(audio_values, "seq", axis=0, tiled=True),
    )
    k_where = jnp.arange(piece[0].shape[0], dtype=jnp.int32)
    audio_k_where = k_where[None, :]
    permit = audio_k_where < audio_valid
    audio_state = fold_piece(
        fold_initial(audio_rows, HA, HDA), audio_local, piece[0], piece[1], permit, HA, HDA
    )
    audio_mixed = fold_finish(audio_state, HA, HDA)
    cross_owned = (
        lax.all_to_all(
            split_heads(cross_video_query, HA, HDA, copies),
            "seq",
            split_axis=0,
            concat_axis=1,
            tiled=True,
        ),
        lax.all_to_all(
            spread_heads(cross_audio_keys, HA, HDA, copies),
            "seq",
            split_axis=0,
            concat_axis=1,
            tiled=True,
        ),
        lax.all_to_all(
            spread_heads(cross_audio_values, HA, HDA, copies),
            "seq",
            split_axis=0,
            concat_axis=1,
            tiled=True,
        ),
    )
    cross_done = attend_local(
        cross_owned[0],
        cross_owned[1],
        cross_owned[2],
        owned_positions(video_rows, copies, devices, index),
        audio_places,
        toward_video,
    )
    video_cross = join_heads(
        lax.all_to_all(cross_done, "seq", split_axis=1, concat_axis=0, tiled=True), HA, HDA, copies
    )
    listen_owned = (
        lax.all_to_all(
            split_heads(cross_audio_query, HA, HDA, copies),
            "seq",
            split_axis=0,
            concat_axis=1,
            tiled=True,
        ),
        lax.all_to_all(
            spread_heads(cross_video_keys, HA, HDA, copies),
            "seq",
            split_axis=0,
            concat_axis=1,
            tiled=True,
        ),
        lax.all_to_all(
            spread_heads(cross_video_values, HA, HDA, copies),
            "seq",
            split_axis=0,
            concat_axis=1,
            tiled=True,
        ),
    )
    listen_done = attend_local(
        listen_owned[0],
        listen_owned[1],
        listen_owned[2],
        owned_positions(audio_rows, copies, devices, index),
        video_places,
        toward_audio,
    )
    audio_cross = join_heads(
        lax.all_to_all(listen_done, "seq", split_axis=1, concat_axis=0, tiled=True), HA, HDA, copies
    )
    return (video_mixed, audio_mixed, video_cross, audio_cross)


def solution(mesh):
    placed = (
        P(("clip", "seq"), None),
        P(("clip", "seq"), None),
        P(("clip", "seq"), None),
        P(("clip", "seq"), None),
        P(("clip", "seq"), None),
        P(("clip", "seq"), None),
        P(("clip", "seq"), None),
        P(("clip", "seq"), None),
        P(("clip", "seq"), None),
        P(("clip", "seq"), None),
        P(("clip", "seq"), None),
        P(("clip", "seq"), None),
        P("clip"),
        P("clip"),
        P("clip"),
    )
    return jax.shard_map(
        shards,
        mesh=mesh,
        in_specs=placed,
        out_specs=(
            P(("clip", "seq"), None),
            P(("clip", "seq"), None),
            P(("clip", "seq"), None),
            P(("clip", "seq"), None),
        ),
        check_vma=False,
    )
```

profile of v0, /device:TPU:0, one launch (start us, length us, event | category | flops | bytes accessed | tf_op | source)
XLA Modules:
  0.0 177.1 jit_solution(16282840157543856620)
XLA Ops:
  0.6 0.9 reshape.311
  1.6 0.7 reshape.329
  2.3 7.5 %all-to-all-start.8 = ((bf16[16,2,512]{2,1,0:T(2,128)(2,1)}), bf16[16,2,512]{2,1,0:T(2,128)(2,1)S(1)}, u32[]{:S(2)}, u32[]{:S(2)}) async-start(bf16[16,2,512]{2,1,0:T(2,128)(2,1)} %reshape.329), calls=%async_computation.8 | async-start | bytes 65536 | tf_op jit(solution)/shard_map/all_to_all | solution.py:240
  11.9 0.6 copy-done.7
  12.7 0.7 reshape.319
  13.6 0.7 reshape.321
  14.6 0.7 copy-done.9
  15.3 23.2 %all_gather.6 = bf16[128,2048]{1,0:T(8,128)(2,1)S(1)} all-gather(bf16[8,2048]{1,0:T(8,128)(2,1)S(1)} %copy-done.9), channel_id=1, replica_groups=mesh['clip'=2,'seq'=16] {'seq'}, dimensions={0}, use_global_device_ids=true | all-gather | bytes 557056 | tf_op jit(solution)/shard_map/all_gather | solution.py:195
  38.5 0.3 copy.139
  38.9 0.3 fusion.63
  39.3 0.7 copy-done.10
  40.0 18.9 %all_gather.7 = bf16[128,2048]{1,0:T(8,128)(2,1)S(1)} all-gather(bf16[8,2048]{1,0:T(8,128)(2,1)S(1)} %copy-done.10), channel_id=1, replica_groups=mesh['clip'=2,'seq'=16] {'seq'}, dimensions={0}, use_global_device_ids=true | all-gather | bytes 557056 | tf_op jit(solution)/shard_map/all_gather | solution.py:196
  58.9 3.5 %all-to-all-start.5 = ((bf16[16,2,512]{2,1,0:T(2,128)(2,1)}), bf16[16,2,512]{2,1,0:T(2,128)(2,1)S(1)}, u32[]{:S(2)}, u32[]{:S(2)}) async-start(bf16[16,2,512]{2,1,0:T(2,128)(2,1)} %reshape.319), calls=%async_computation.5 | async-start | bytes 65536 | tf_op jit(solution)/shard_map/all_to_all | solution.py:213
  62.4 6.6 %all-to-all-done.5 = bf16[16,2,512]{2,1,0:T(2,128)(2,1)S(1)} async-done(((bf16[16,2,512]{2,1,0:T(2,128)(2,1)}), bf16[16,2,512]{2,1,0:T(2,128)(2,1)S(1)}, u32[]{:S(2)}, u32[]{:S(2)}) %all-to-all-start.5) | async-done | bytes 32800 | tf_op jit(solution)/shard_map/all_to_all | solution.py:213
  69.0 3.5 %all-to-all-start.6 = ((bf16[16,2,512]{2,1,0:T(2,128)(2,1)}), bf16[16,2,512]{2,1,0:T(2,128)(2,1)S(1)}, u32[]{:S(2)}, u32[]{:S(2)}) async-start(bf16[16,2,512]{2,1,0:T(2,128)(2,1)} %reshape.321), calls=%async_computation.6 | async-start | bytes 65536 | tf_op jit(solution)/shard_map/all_to_all | solution.py:220
  72.6 0.7 copy.128
  73.3 0.2 copy-done.1
  73.5 0.7 copy.130
  74.2 0.2 copy-done.2
  74.5 0.8 copy-done.3
  75.3 0.2 reshape.305
  75.5 0.8 reshape.317
  76.3 2.8 %all-to-all-done.6 = bf16[16,2,512]{2,1,0:T(2,128)(2,1)S(1)} async-done(((bf16[16,2,512]{2,1,0:T(2,128)(2,1)}), bf16[16,2,512]{2,1,0:T(2,128)(2,1)S(1)}, u32[]{:S(2)}, u32[]{:S(2)}) %all-to-all-start.6) | async-done | bytes 32800 | tf_op jit(solution)/shard_map/all_to_all | solution.py:220
  79.1 3.5 %all-to-all-start.4 = ((bf16[16,2,1024]{2,1,0:T(2,128)(2,1)}), bf16[16,2,1024]{2,1,0:T(2,128)(2,1)S(1)}, u32[]{:S(2)}, u32[]{:S(2)}) async-start(bf16[16,2,1024]{2,1,0:T(2,128)(2,1)} %reshape.317), calls=%async_computation.4 | async-start | bytes 131072 | tf_op jit(solution)/shard_map/all_to_all | solution.py:206
  82.6 0.7 copy.132
  83.4 0.2 reshape.313
  83.7 0.8 reshape.327
  84.5 0.2 reshape.314
  84.8 0.8 reshape.325
  85.5 0.2 fusion.33
  86.0 3.4 %all-to-all-done.4 = bf16[16,2,1024]{2,1,0:T(2,128)(2,1)S(1)} async-done(((bf16[16,2,1024]{2,1,0:T(2,128)(2,1)}), bf16[16,2,1024]{2,1,0:T(2,128)(2,1)S(1)}, u32[]{:S(2)}, u32[]{:S(2)}) %all-to-all-start.4) | async-done | bytes 65568 | tf_op jit(solution)/shard_map/all_to_all | solution.py:206
  89.5 3.5 %all-to-all-start.9 = ((bf16[16,2,1024]{2,1,0:T(2,128)(2,1)}), bf16[16,2,1024]{2,1,0:T(2,128)(2,1)S(1)}, u32[]{:S(2)}, u32[]{:S(2)}) async-start(bf16[16,2,1024]{2,1,0:T(2,128)(2,1)} %reshape.327), calls=%async_computation.9 | async-start | bytes 131072 | tf_op jit(solution)/shard_map/all_to_all | solution.py:247
  92.9 0.1 reshape.318
  93.1 0.2 fusion.64
  93.4 6.4 %all-to-all-done.9 = bf16[16,2,1024]{2,1,0:T(2,128)(2,1)S(1)} async-done(((bf16[16,2,1024]{2,1,0:T(2,128)(2,1)}), bf16[16,2,1024]{2,1,0:T(2,128)(2,1)S(1)}, u32[]{:S(2)}, u32[]{:S(2)}) %all-to-all-start.9) | async-done | bytes 65568 | tf_op jit(solution)/shard_map/all_to_all | solution.py:247
  99.8 3.5 %all-to-all-start.10 = ((bf16[16,2,1024]{2,1,0:T(2,128)(2,1)}), bf16[16,2,1024]{2,1,0:T(2,128)(2,1)S(1)}, u32[]{:S(2)}, u32[]{:S(2)}) async-start(bf16[16,2,1024]{2,1,0:T(2,128)(2,1)} %reshape.325), calls=%async_computation.10 | async-start | bytes 131072 | tf_op jit(solution)/shard_map/all_to_all | solution.py:254
  103.5 0.3 fusion.65
  103.8 6.4 %all-to-all-done.10 = bf16[16,2,1024]{2,1,0:T(2,128)(2,1)S(1)} async-done(((bf16[16,2,1024]{2,1,0:T(2,128)(2,1)}), bf16[16,2,1024]{2,1,0:T(2,128)(2,1)S(1)}, u32[]{:S(2)}, u32[]{:S(2)}) %all-to-all-start.10) | async-done | bytes 65568 | tf_op jit(solution)/shard_map/all_to_all | solution.py:254
  110.2 3.5 %all-to-all-start = ((bf16[32,16,128]{2,1,0:T(8,128)(2,1)}), bf16[32,16,128]{2,1,0:T(8,128)(2,1)S(1)}, u32[]{:S(2)}, u32[]{:S(2)}) async-start(bf16[32,16,128]{2,1,0:T(8,128)(2,1)} %copy.128), calls=%async_computation | async-start | bytes 262144 | tf_op jit(solution)/shard_map/all_to_all | solution.py:160
  113.7 0.2 fusion.21
  113.9 0.2 fusion.9
  114.1 7.5 %all-to-all-done = bf16[32,16,128]{2,1,0:T(8,128)(2,1)S(1)} async-done(((bf16[32,16,128]{2,1,0:T(8,128)(2,1)}), bf16[32,16,128]{2,1,0:T(8,128)(2,1)S(1)}, u32[]{:S(2)}, u32[]{:S(2)}) %all-to-all-start) | async-done | bytes 131104 | tf_op jit(solution)/shard_map/all_to_all | solution.py:160
  121.6 3.5 %all-to-all-start.1 = ((bf16[32,16,128]{2,1,0:T(8,128)(2,1)}), bf16[32,16,128]{2,1,0:T(8,128)(2,1)S(1)}, u32[]{:S(2)}, u32[]{:S(2)}) async-start(bf16[32,16,128]{2,1,0:T(8,128)(2,1)} %copy.130), calls=%async_computation.1 | async-start | bytes 262144 | tf_op jit(solution)/shard_map/all_to_all | solution.py:167
  125.2 0.8 reshape.323
  126.2 0.3 fusion.12
  126.6 0.7 reshape.331
  127.3 5.7 %all-to-all-done.1 = bf16[32,16,128]{2,1,0:T(8,128)(2,1)S(1)} async-done(((bf16[32,16,128]{2,1,0:T(8,128)(2,1)}), bf16[32,16,128]{2,1,0:T(8,128)(2,1)S(1)}, u32[]{:S(2)}, u32[]{:S(2)}) %all-to-all-start.1) | async-done | bytes 131104 | tf_op jit(solution)/shard_map/all_to_all | solution.py:167
  133.0 3.5 %all-to-all-start.2 = ((bf16[32,16,128]{2,1,0:T(8,128)(2,1)}), bf16[32,16,128]{2,1,0:T(8,128)(2,1)S(1)}, u32[]{:S(2)}, u32[]{:S(2)}) async-start(bf16[32,16,128]{2,1,0:T(8,128)(2,1)} %copy.132), calls=%async_computation.2 | async-start | bytes 262144 | tf_op jit(solution)/shard_map/all_to_all | solution.py:174
  136.5 0.2 fusion.62
  136.9 7.5 %all-to-all-done.2 = bf16[32,16,128]{2,1,0:T(8,128)(2,1)S(1)} async-done(((bf16[32,16,128]{2,1,0:T(8,128)(2,1)}), bf16[32,16,128]{2,1,0:T(8,128)(2,1)S(1)}, u32[]{:S(2)}, u32[]{:S(2)}) %all-to-all-start.2) | async-done | bytes 131104 | tf_op jit(solution)/shard_map/all_to_all | solution.py:174
  144.4 3.5 %all-to-all-start.11 = ((bf16[16,2,512]{2,1,0:T(2,128)(2,1)}), bf16[16,2,512]{2,1,0:T(2,128)(2,1)S(1)}, u32[]{:S(2)}, u32[]{:S(2)}) async-start(bf16[16,2,512]{2,1,0:T(2,128)(2,1)} %reshape.331), calls=%async_computation.11 | async-start | bytes 65536 | tf_op jit(solution)/shard_map/all_to_all | solution.py:271
  148.0 6.6 %all-to-all-done.11 = bf16[16,2,512]{2,1,0:T(2,128)(2,1)S(1)} async-done(((bf16[16,2,512]{2,1,0:T(2,128)(2,1)}), bf16[16,2,512]{2,1,0:T(2,128)(2,1)S(1)}, u32[]{:S(2)}, u32[]{:S(2)}) %all-to-all-start.11) | async-done | bytes 32800 | tf_op jit(solution)/shard_map/all_to_all | solution.py:271
  154.5 3.5 %all-to-all-start.7 = ((bf16[16,2,1024]{2,1,0:T(2,128)(2,1)}), bf16[16,2,1024]{2,1,0:T(2,128)(2,1)S(1)}, u32[]{:S(2)}, u32[]{:S(2)}) async-start(bf16[16,2,1024]{2,1,0:T(2,128)(2,1)} %reshape.323), calls=%async_computation.7 | async-start | bytes 131072 | tf_op jit(solution)/shard_map/all_to_all | solution.py:237
  158.0 0.4 fusion.4
  158.4 0.8 copy.135
  159.2 5.7 %all-to-all-done.7 = bf16[16,2,1024]{2,1,0:T(2,128)(2,1)S(1)} async-done(((bf16[16,2,1024]{2,1,0:T(2,128)(2,1)}), bf16[16,2,1024]{2,1,0:T(2,128)(2,1)S(1)}, u32[]{:S(2)}, u32[]{:S(2)}) %all-to-all-start.7) | async-done | bytes 65568 | tf_op jit(solution)/shard_map/all_to_all | solution.py:237
  164.9 3.5 %all-to-all-start.3 = ((bf16[2,256,128]{2,0,1:T(2,128)(2,1)}), bf16[2,256,128]{2,0,1:T(2,128)(2,1)S(1)}, u32[]{:S(2)}, u32[]{:S(2)}) async-start(bf16[2,256,128]{2,0,1:T(2,128)(2,1)} %copy.135), calls=%async_computation.3 | async-start | bytes 262144 | tf_op jit(solution)/shard_map/all_to_all | solution.py:191
  168.4 0.3 copy.141
  168.7 0.4 fusion.10
  169.2 0.7 reshape.304
  170.1 0.7 reshape.316
  171.1 0.8 reshape.310
  171.9 4.4 %all-to-all-done.3 = bf16[2,256,128]{2,0,1:T(2,128)(2,1)S(1)} async-done(((bf16[2,256,128]{2,0,1:T(2,128)(2,1)}), bf16[2,256,128]{2,0,1:T(2,128)(2,1)S(1)}, u32[]{:S(2)}, u32[]{:S(2)}) %all-to-all-start.3) | async-done | bytes 131104 | tf_op jit(solution)/shard_map/all_to_all | solution.py:191
  176.4 0.7 copy.204
  (71 shorter events, 3.0 us)
Async XLA Ops:
  2.3 9.5 %copy-start.6 = (bf16[8,2048]{1,0:T(8,128)(2,1)S(1)}, bf16[8,2048]{1,0:T(8,128)(2,1)}, u32[]{:S(2)}) copy-start(bf16[8,2048]{1,0:T(8,128)(2,1)} %param.18) | copy-start | bytes 98308
  2.3 56.6 %all-to-all-start.8 = ((bf16[16,2,512]{2,1,0:T(2,128)(2,1)}), bf16[16,2,512]{2,1,0:T(2,128)(2,1)S(1)}, u32[]{:S(2)}, u32[]{:S(2)}) async-start(bf16[16,2,512]{2,1,0:T(2,128)(2,1)} %reshape.329), calls=%async_computation.8 | async-start | bytes 65536 | tf_op jit(solution)/shard_map/all_to_all | solution.py:240
  11.8 0.8 copy-start.7
  12.7 0.8 copy-start.8
  13.6 0.9 copy-start
  14.5 0.8 copy-start.9
  39.2 0.8 copy-start.10
  58.9 10.1 %all-to-all-start.5 = ((bf16[16,2,512]{2,1,0:T(2,128)(2,1)}), bf16[16,2,512]{2,1,0:T(2,128)(2,1)S(1)}, u32[]{:S(2)}, u32[]{:S(2)}) async-start(bf16[16,2,512]{2,1,0:T(2,128)(2,1)} %reshape.319), calls=%async_computation.5 | async-start | bytes 65536 | tf_op jit(solution)/shard_map/all_to_all | solution.py:213
  69.0 10.1 %all-to-all-start.6 = ((bf16[16,2,512]{2,1,0:T(2,128)(2,1)}), bf16[16,2,512]{2,1,0:T(2,128)(2,1)S(1)}, u32[]{:S(2)}, u32[]{:S(2)}) async-start(bf16[16,2,512]{2,1,0:T(2,128)(2,1)} %reshape.321), calls=%async_computation.6 | async-start | bytes 65536 | tf_op jit(solution)/shard_map/all_to_all | solution.py:220
  72.6 0.9 copy-start.1
  73.5 0.9 copy-start.2
  74.4 0.8 copy-start.3
  79.1 10.4 %all-to-all-start.4 = ((bf16[16,2,1024]{2,1,0:T(2,128)(2,1)}), bf16[16,2,1024]{2,1,0:T(2,128)(2,1)S(1)}, u32[]{:S(2)}, u32[]{:S(2)}) async-start(bf16[16,2,1024]{2,1,0:T(2,128)(2,1)} %reshape.317), calls=%async_computation.4 | async-start | bytes 131072 | tf_op jit(solution)/shard_map/all_to_all | solution.py:206
  82.6 0.8 copy-start.4
  83.7 0.8 copy-start.5
  89.5 10.3 %all-to-all-start.9 = ((bf16[16,2,1024]{2,1,0:T(2,128)(2,1)}), bf16[16,2,1024]{2,1,0:T(2,128)(2,1)S(1)}, u32[]{:S(2)}, u32[]{:S(2)}) async-start(bf16[16,2,1024]{2,1,0:T(2,128)(2,1)} %reshape.327), calls=%async_computation.9 | async-start | bytes 131072 | tf_op jit(solution)/shard_map/all_to_all | solution.py:247
  99.8 10.4 %all-to-all-start.10 = ((bf16[16,2,1024]{2,1,0:T(2,128)(2,1)}), bf16[16,2,1024]{2,1,0:T(2,128)(2,1)S(1)}, u32[]{:S(2)}, u32[]{:S(2)}) async-start(bf16[16,2,1024]{2,1,0:T(2,128)(2,1)} %reshape.325), calls=%async_computation.10 | async-start | bytes 131072 | tf_op jit(solution)/shard_map/all_to_all | solution.py:254
  110.2 11.4 %all-to-all-start = ((bf16[32,16,128]{2,1,0:T(8,128)(2,1)}), bf16[32,16,128]{2,1,0:T(8,128)(2,1)S(1)}, u32[]{:S(2)}, u32[]{:S(2)}) async-start(bf16[32,16,128]{2,1,0:T(8,128)(2,1)} %copy.128), calls=%async_computation | async-start | bytes 262144 | tf_op jit(solution)/shard_map/all_to_all | solution.py:160
  121.6 11.4 %all-to-all-start.1 = ((bf16[32,16,128]{2,1,0:T(8,128)(2,1)}), bf16[32,16,128]{2,1,0:T(8,128)(2,1)S(1)}, u32[]{:S(2)}, u32[]{:S(2)}) async-start(bf16[32,16,128]{2,1,0:T(8,128)(2,1)} %copy.130), calls=%async_computation.1 | async-start | bytes 262144 | tf_op jit(solution)/shard_map/all_to_all | solution.py:167
  133.0 11.4 %all-to-all-start.2 = ((bf16[32,16,128]{2,1,0:T(8,128)(2,1)}), bf16[32,16,128]{2,1,0:T(8,128)(2,1)S(1)}, u32[]{:S(2)}, u32[]{:S(2)}) async-start(bf16[32,16,128]{2,1,0:T(8,128)(2,1)} %copy.132), calls=%async_computation.2 | async-start | bytes 262144 | tf_op jit(solution)/shard_map/all_to_all | solution.py:174
  144.4 10.1 %all-to-all-start.11 = ((bf16[16,2,512]{2,1,0:T(2,128)(2,1)}), bf16[16,2,512]{2,1,0:T(2,128)(2,1)S(1)}, u32[]{:S(2)}, u32[]{:S(2)}) async-start(bf16[16,2,512]{2,1,0:T(2,128)(2,1)} %reshape.331), calls=%async_computation.11 | async-start | bytes 65536 | tf_op jit(solution)/shard_map/all_to_all | solution.py:271
  154.5 10.4 %all-to-all-start.7 = ((bf16[16,2,1024]{2,1,0:T(2,128)(2,1)}), bf16[16,2,1024]{2,1,0:T(2,128)(2,1)S(1)}, u32[]{:S(2)}, u32[]{:S(2)}) async-start(bf16[16,2,1024]{2,1,0:T(2,128)(2,1)} %reshape.323), calls=%async_computation.7 | async-start | bytes 131072 | tf_op jit(solution)/shard_map/all_to_all | solution.py:237
  164.9 11.4 %all-to-all-start.3 = ((bf16[2,256,128]{2,0,1:T(2,128)(2,1)}), bf16[2,256,128]{2,0,1:T(2,128)(2,1)S(1)}, u32[]{:S(2)}, u32[]{:S(2)}) async-start(bf16[2,256,128]{2,0,1:T(2,128)(2,1)} %copy.135), calls=%async_computation.3 | async-start | bytes 262144 | tf_op jit(solution)/shard_map/all_to_all | solution.py:191
where the time goes:
time: 179 us; the launch traced here: 177 us
  waiting for transfers between devices  62.9 us (35%)
  starting transfers between devices  46 us (26%)
  blocking collectives  42.1 us (24%)
  local copies, waits for them, and re-layouts  19.7 us (11%)
  between operations  3.15 us (2%)
  matrix products  2.36 us (1%)
    all_gather x1, blocking collectives, shards(): lax.all_gather(audio_keys, 'seq', axis=0, tiled=True)  23.2 us
    all_gather x1, blocking collectives, shards(): lax.all_gather(audio_values, 'seq', axis=0, tiled=True)  18.9 us
    unnamed x42, local copies, waits for them, and re-layouts  11.4 us
    all_to_all x1, starting transfers between devices, shards(): lax.all_to_all(split_heads(cross_audio_query, HA, HDA, copies), 'seq', sp...  7.52 us
    all_to_all x1, waiting for transfers between devices, shards(): lax.all_to_all(spread_heads(video_values, HV, HDV, copies), 'seq', split_...  7.49 us
    all_to_all x1, waiting for transfers between devices, shards(): lax.all_to_all(split_heads(video_query, HV, HDV, copies), 'seq', split_ax...  7.49 us
    all_to_all x1, waiting for transfers between devices, shards(): lax.all_to_all(spread_heads(cross_audio_keys, HA, HDA, copies), 'seq', sp...  6.57 us
    all_to_all x1, waiting for transfers between devices, shards(): lax.all_to_all(listen_done, 'seq', split_axis=1, concat_axis=0, tiled=True)  6.56 us
  transfers between devices with their start and end apart: 12, of which 11 were waited for; matrix products, arithmetic and copies ran while one was open for 9% of the time, Pallas kernels for 0%

commit v1 on v0

--- a/solution.py
+++ b/solution.py
@@ -1,8 +1,11 @@
+import functools
 import math
 
 import jax
 import jax.numpy as jnp
 from jax import lax
+from jax.experimental import pallas as pl
+from jax.experimental.pallas import tpu as pltpu
 from jax.sharding import PartitionSpec as P
 
 HV = 32
@@ -113,7 +116,7 @@
     return tiles.transpose(1, 0, 2, 3).reshape(heads, q_count, depth)
 
 
-def shards(
+def shards_general(
     video_query,
     video_keys,
     video_values,
@@ -273,6 +276,194 @@
     return (video_mixed, audio_mixed, video_cross, audio_cross)
 
 
+LANES = 128
+
+
+def pack_kernel(n, *refs):
+    video, cross, audio, packed = refs[0:3], refs[3:6], refs[6:12], refs[12]
+    parts = video[0].shape[1] // n // LANES
+    rows = cross[0].shape[0]
+    for d in range(n):
+        at = 0
+        for ref in video:
+            for part in range(parts):
+                packed[d, at : at + rows, :] = ref[:, (d * parts + part) * LANES : (d * parts + part + 1) * LANES]
+                at += rows
+        for ref in cross:
+            packed[d, at : at + rows, :] = ref[:, d * LANES : (d + 1) * LANES]
+            at += rows
+        for first, second in zip(audio[0::2], audio[1::2]):
+            pair = jnp.concatenate(
+                [first[:, d * LANES : (d + 1) * LANES], second[:, d * LANES : (d + 1) * LANES]], axis=0
+            )
+            packed[d, at : at + pair.shape[0], :] = pair
+            at += pair.shape[0]
+
+
+def softmax_mix(query, key, value, scale, permit):
+    scores = lax.dot_general(
+        query, key, (((1,), (1,)), ((), ())), preferred_element_type=jnp.float32
+    )
+    scores = jnp.where(permit, scores * scale, -1e30)
+    peak = jnp.max(scores, axis=1, keepdims=True)
+    weights = jnp.exp(scores - peak)
+    total = jnp.sum(weights, axis=1, keepdims=True)
+    mixed = jnp.dot(weights.astype(jnp.bfloat16), value, preferred_element_type=jnp.float32)
+    return mixed / total
+
+
+def paired_mix(query, key, value, depth, permit):
+    scale = 1.0 / math.sqrt(depth)
+    lane = lax.broadcasted_iota(jnp.int32, query.shape, 1) // depth
+    zero = jnp.zeros_like(query)
+    result = None
+    for h in range(LANES // depth):
+        one = softmax_mix(jnp.where(lane == h, query, zero), key, value, scale, permit)
+        result = one if h == 0 else jnp.where(lane == h, one, result)
+    return result
+
+
+def attend_kernel(n, rows, parts, video_len, audio_len, shift, got, done):
+    half = rows // 2
+    tv, ta = n * rows, n * half
+    ratio = tv // ta
+    bits = ratio.bit_length() - 1
+    video_valid, audio_valid, offset = video_len[0], audio_len[0], shift[0]
+
+    def slab(at):
+        return got[:, at : at + rows, :].reshape(tv, LANES)
+
+    def halves(at):
+        both = got[:, at : at + rows, :].astype(jnp.float32)
+        first = both[:, :half, :].reshape(ta, LANES).astype(jnp.bfloat16)
+        second = both[:, half:, :].reshape(ta, LANES).astype(jnp.bfloat16)
+        return first, second
+
+    def places(q_count, k_count):
+        return (
+            lax.broadcasted_iota(jnp.int32, (q_count, k_count), 0),
+            lax.broadcasted_iota(jnp.int32, (q_count, k_count), 1),
+        )
+
+    q_at, k_at = places(tv, tv)
+    permit = k_at < video_valid
+    for h in range(parts):
+        mixed = softmax_mix(
+            slab(h * rows),
+            slab((parts + h) * rows),
+            slab((2 * parts + h) * rows),
+            1.0 / math.sqrt(HDV),
+            permit,
+        )
+        done[:, h * rows : (h + 1) * rows, :] = mixed.astype(jnp.bfloat16).reshape(n, rows, LANES)
+    at = 3 * parts * rows
+    cross_query, cross_keys, cross_values = slab(at), slab(at + rows), slab(at + 2 * rows)
+    at += 3 * rows
+    audio_query, audio_keys = halves(at)
+    audio_values, listen_query = halves(at + rows)
+    sound_keys, sound_values = halves(at + 2 * rows)
+
+    q_at, k_at = places(tv, ta)
+    center = jnp.clip((q_at >> bits) + offset, 0, audio_valid - 1)
+    permit = (k_at < audio_valid) & (jnp.abs(k_at - center) <= 5 * ta // 8)
+    mixed = paired_mix(cross_query, sound_keys, sound_values, HDA, permit)
+    out = parts * rows
+    done[:, out : out + rows, :] = mixed.astype(jnp.bfloat16).reshape(n, rows, LANES)
+
+    q_at, k_at = places(ta, ta)
+    heard = paired_mix(audio_query, audio_keys, audio_values, HDA, k_at < audio_valid)
+    q_at, k_at = places(ta, tv)
+    center = jnp.clip((q_at - offset) * ratio, 0, video_valid - 1)
+    permit = (k_at < video_valid) & (jnp.abs(k_at - center) <= tv // 8)
+    listened = paired_mix(listen_query, cross_keys, cross_values, HDA, permit)
+    both = jnp.concatenate(
+        [heard.reshape(n, half, LANES), listened.reshape(n, half, LANES)], axis=1
+    )
+    out += rows
+    done[:, out : out + rows, :] = both.astype(jnp.bfloat16)
+
+
+def unpack_kernel(n, back, video_mixed, audio_mixed, video_cross, audio_cross):
+    rows = video_mixed.shape[0]
+    half = audio_mixed.shape[0]
+    parts = video_mixed.shape[1] // n // LANES
+    for s in range(n):
+        for h in range(parts):
+            at = (s * parts + h) * LANES
+            video_mixed[:, at : at + LANES] = back[s, h * rows : (h + 1) * rows, :]
+        at = s * LANES
+        out = parts * rows
+        video_cross[:, at : at + LANES] = back[s, out : out + rows, :]
+        both = back[s, out + rows : out + 2 * rows, :]
+        audio_mixed[:, at : at + LANES] = both[:half, :]
+        audio_cross[:, at : at + LANES] = both[half:, :]
+
+
+def shards_packed(*arrays):
+    (
+        video_query, video_keys, video_values,
+        audio_query, audio_keys, audio_values,
+        cross_video_query, cross_video_keys, cross_video_values,
+        cross_audio_query, cross_audio_keys, cross_audio_values,
+        video_length, audio_length, align_offset,
+    ) = arrays
+    n = lax.axis_size("seq")
+    rows, half = video_query.shape[0], audio_query.shape[0]
+    parts = video_query.shape[1] // n // LANES
+    vmem = pl.BlockSpec(memory_space=pltpu.VMEM)
+    smem = pl.BlockSpec(memory_space=pltpu.SMEM)
+    params = pltpu.CompilerParams(vmem_limit_bytes=32 * 1024 * 1024)
+    in_rows = (3 * parts + 6) * rows
+    out_rows = (parts + 2) * rows
+    packed = pl.pallas_call(
+        functools.partial(pack_kernel, n),
+        out_shape=jax.ShapeDtypeStruct((n, in_rows, LANES), jnp.bfloat16),
+        in_specs=[vmem] * 12,
+        out_specs=vmem,
+        compiler_params=params,
+    )(
+        video_query, video_keys, video_values,
+        cross_video_query, cross_video_keys, cross_video_values,
+        audio_query, audio_keys, audio_values,
+        cross_audio_query, cross_audio_keys, cross_audio_values,
+    )
+    got = lax.all_to_all(packed, "seq", split_axis=0, concat_axis=0, tiled=True)
+    done = pl.pallas_call(
+        functools.partial(attend_kernel, n, rows, parts),
+        out_shape=jax.ShapeDtypeStruct((n, out_rows, LANES), jnp.bfloat16),
+        in_specs=[smem] * 3 + [vmem],
+        out_specs=vmem,
+        compiler_params=params,
+    )(video_length, audio_length, align_offset, got)
+    back = lax.all_to_all(done, "seq", split_axis=0, concat_axis=0, tiled=True)
+    return pl.pallas_call(
+        functools.partial(unpack_kernel, n),
+        out_shape=(
+            jax.ShapeDtypeStruct(video_query.shape, jnp.bfloat16),
+            jax.ShapeDtypeStruct(audio_query.shape, jnp.bfloat16),
+            jax.ShapeDtypeStruct(cross_video_query.shape, jnp.bfloat16),
+            jax.ShapeDtypeStruct(cross_audio_query.shape, jnp.bfloat16),
+        ),
+        in_specs=[vmem],
+        out_specs=(vmem,) * 4,
+        compiler_params=params,
+    )(back)
+
+
+def shards(*arrays):
+    n = lax.axis_size("seq")
+    rows, half = arrays[0].shape[0], arrays[3].shape[0]
+    fits = (
+        arrays[0].shape[1] % (n * LANES) == 0
+        and arrays[3].shape[1] == n * LANES
+        and HDV == LANES
+        and LANES % HDA == 0
+        and rows == 2 * half
+        and half % 8 == 0
+    )
+    return shards_packed(*arrays) if fits else shards_general(*arrays)
+
+
 def solution(mesh):
     placed = (
         P(("clip", "seq"), None),

time: 179 us -> 55.8 us (0.31)
  waiting for transfers between devices: 62.9 us -> 16.8 us
  starting transfers between devices: 46 us -> 7.39 us
  blocking collectives: 42.1 us -> 15.3 us
  local copies, waits for them, and re-layouts: 19.7 us -> 9.77 us
  Pallas kernels: 0 us -> 3.09 us
  matrix products: 2.36 us -> 0 us
    all_to_all x12 -> x1, waiting for transfers between devices: 62.9 us -> 16.8 us  [shards_packed(): got = lax.all_to_all(packed, 'seq', split_axis=0, concat_axis=0, tiled=True)]
    all_gather x2 -> x0, blocking collectives: 42.1 us -> none  [the longest x1 23.2 us: shards(): lax.all_gather(audio_keys, 'seq', axis=0, tiled=True)]
    all_to_all x12 -> x1, starting transfers between devices: 46 us -> 7.39 us  [shards_packed(): got = lax.all_to_all(packed, 'seq', split_axis=0, concat_axis=0, tiled=True)]
    all_to_all x0 -> x1, blocking collectives: none -> 15.3 us  [shards_packed(): back = lax.all_to_all(done, 'seq', split_axis=0, concat_axis=0, tiled=True)]
    reshape x14 -> x0, local copies, waits for them, and re-layouts: 4.87 us -> none  [the longest x2 1.55 us: join_heads(): return shaped.reshape(copies * part_rows, heads * depth)]
    pallas_call x0 -> x3, Pallas kernels: none -> 3.09 us  [the longest x1 1.32 us: shards_packed(): pl.pallas_call(functools.partial(attend_kernel, n, rows, parts), out_shap...]
    dot_general x8 -> x0, matrix products: 2.36 us -> none  [the longest x4 1.31 us: online_update(): jnp.einsum(value_form, weights.astype(jnp.bfloat16), value_tile, preferre...]
    unnamed x42 -> x24, local copies, waits for them, and re-layouts: 11.4 us -> 9.77 us
  transfers between devices with their start and end apart: 12 -> 1, of which waited for: 11 -> 1; matrix products, arithmetic and copies ran while one was open for 9% -> 0% of each run, Pallas kernels for 0% -> 0%
where the time goes in v1:
time: 55.8 us; the launch traced here: 54.9 us
  waiting for transfers between devices  16.8 us (30%)
  blocking collectives  15.3 us (27%)
  local copies, waits for them, and re-layouts  9.77 us (18%)
  starting transfers between devices  7.39 us (13%)
  Pallas kernels  3.09 us (6%)
  between operations  2.61 us (5%)
    all_to_all x1, waiting for transfers between devices, shards_packed(): got = lax.all_to_all(packed, 'seq', split_axis=0, concat_axis=0, tiled=True)  16.8 us
    all_to_all x1, blocking collectives, shards_packed(): back = lax.all_to_all(done, 'seq', split_axis=0, concat_axis=0, tiled=True)  15.3 us
    unnamed x24, local copies, waits for them, and re-layouts  9.77 us
    all_to_all x1, starting transfers between devices, shards_packed(): got = lax.all_to_all(packed, 'seq', split_axis=0, concat_axis=0, tiled=True)  7.39 us
    pallas_call x1, Pallas kernels, shards_packed(): pl.pallas_call(functools.partial(attend_kernel, n, rows, parts), out_shap...  1.32 us
  transfers between devices with their start and end apart: 1, of which 1 were waited for; matrix products, arithmetic and copies ran while one was open for 0% of the time, Pallas kernels for 0%

profile of v1, /device:TPU:0, one launch (start us, length us, event | category | flops | bytes accessed | tf_op | source)
XLA Modules:
  0.0 54.9 jit_solution(13267075467893198389)
XLA Ops:
  0.6 0.0 copy-start
  0.6 0.9 %copy-done = bf16[16,4096]{1,0:T(8,128)(2,1)S(1)} copy-done((bf16[16,4096]{1,0:T(8,128)(2,1)S(1)}, bf16[16,4096]{1,0:T(8,128)(2,1)}, u32[]{:S(2)}) %copy-start) | copy-done | bytes 131096
  1.5 0.0 copy-start.1
  1.5 0.9 %copy-done.1 = bf16[16,4096]{1,0:T(8,128)(2,1)S(1)} copy-done((bf16[16,4096]{1,0:T(8,128)(2,1)S(1)}, bf16[16,4096]{1,0:T(8,128)(2,1)}, u32[]{:S(2)}) %copy-start.1) | copy-done | bytes 131096
  2.4 0.0 copy-start.2
  2.4 0.9 %copy-done.2 = bf16[16,4096]{1,0:T(8,128)(2,1)S(1)} copy-done((bf16[16,4096]{1,0:T(8,128)(2,1)S(1)}, bf16[16,4096]{1,0:T(8,128)(2,1)}, u32[]{:S(2)}) %copy-start.2) | copy-done | bytes 131096
  3.4 0.0 copy-start.3
  3.4 0.8 %copy-done.3 = bf16[16,2048]{1,0:T(8,128)(2,1)S(1)} copy-done((bf16[16,2048]{1,0:T(8,128)(2,1)S(1)}, bf16[16,2048]{1,0:T(8,128)(2,1)}, u32[]{:S(2)}) %copy-start.3) | copy-done | bytes 65560
  4.2 0.0 copy-start.4
  4.2 0.8 %copy-done.4 = bf16[16,2048]{1,0:T(8,128)(2,1)S(1)} copy-done((bf16[16,2048]{1,0:T(8,128)(2,1)S(1)}, bf16[16,2048]{1,0:T(8,128)(2,1)}, u32[]{:S(2)}) %copy-start.4) | copy-done | bytes 65560
  5.0 0.0 copy-start.5
  5.0 0.8 %copy-done.5 = bf16[16,2048]{1,0:T(8,128)(2,1)S(1)} copy-done((bf16[16,2048]{1,0:T(8,128)(2,1)S(1)}, bf16[16,2048]{1,0:T(8,128)(2,1)}, u32[]{:S(2)}) %copy-start.5) | copy-done | bytes 65560
  5.9 0.0 copy-start.6
  5.9 0.8 %copy-done.6 = bf16[8,2048]{1,0:T(8,128)(2,1)S(1)} copy-done((bf16[8,2048]{1,0:T(8,128)(2,1)S(1)}, bf16[8,2048]{1,0:T(8,128)(2,1)}, u32[]{:S(2)}) %copy-start.6) | copy-done | bytes 32792
  6.6 0.0 copy-start.7
  6.6 0.8 %copy-done.7 = bf16[8,2048]{1,0:T(8,128)(2,1)S(1)} copy-done((bf16[8,2048]{1,0:T(8,128)(2,1)S(1)}, bf16[8,2048]{1,0:T(8,128)(2,1)}, u32[]{:S(2)}) %copy-start.7) | copy-done | bytes 32792
  7.4 0.0 copy-start.8
  7.4 0.8 %copy-done.8 = bf16[8,2048]{1,0:T(8,128)(2,1)S(1)} copy-done((bf16[8,2048]{1,0:T(8,128)(2,1)S(1)}, bf16[8,2048]{1,0:T(8,128)(2,1)}, u32[]{:S(2)}) %copy-start.8) | copy-done | bytes 32792
  8.1 0.0 copy-start.9
  8.1 0.8 %copy-done.9 = bf16[8,2048]{1,0:T(8,128)(2,1)S(1)} copy-done((bf16[8,2048]{1,0:T(8,128)(2,1)S(1)}, bf16[8,2048]{1,0:T(8,128)(2,1)}, u32[]{:S(2)}) %copy-start.9) | copy-done | bytes 32792
  8.9 0.0 copy-start.10
  8.9 0.8 %copy-done.10 = bf16[8,2048]{1,0:T(8,128)(2,1)S(1)} copy-done((bf16[8,2048]{1,0:T(8,128)(2,1)S(1)}, bf16[8,2048]{1,0:T(8,128)(2,1)}, u32[]{:S(2)}) %copy-start.10) | copy-done | bytes 32792
  9.7 0.0 copy-start.11
  9.7 0.8 %copy-done.11 = bf16[8,2048]{1,0:T(8,128)(2,1)S(1)} copy-done((bf16[8,2048]{1,0:T(8,128)(2,1)S(1)}, bf16[8,2048]{1,0:T(8,128)(2,1)}, u32[]{:S(2)}) %copy-start.11) | copy-done | bytes 32792
  10.4 1.0 %shard_map.174 = bf16[16,192,128]{2,1,0:T(8,128)(2,1)} custom-call(bf16[16,4096]{1,0:T(8,128)(2,1)S(1)} %copy-done, bf16[16,4096]{1,0:T(8,128)(2,1)S(1)} %copy-done.1, bf16[16,4096]{1,0:T(8,128)(2,1)S(1)} %copy-done.2, bf16[16,2048]{1,0:T(8,128)(2,1)S(1)} %copy-done.3, bf16[16,2048]{1,0:T(8,128)(2,1)S(1)} %copy-done.4, bf16[16,2048]{1,0:T(8,128)(2,1)S(1)} %copy-done.5, ...), custom_call_target="tpu_custom_call" | custom-call | tf_op jit(solution)/shard_map/pallas_call | solution.py:418
  11.5 7.4 %all-to-all-start = ((bf16[16,192,128]{2,1,0:T(8,128)(2,1)}), bf16[16,192,128]{2,1,0:T(8,128)(2,1)S(1)}, u32[]{:S(2)}, u32[]{:S(2)}) async-start(bf16[16,192,128]{2,1,0:T(8,128)(2,1)} %shard_map.174), calls=%async_computation | async-start | bytes 1572864 | tf_op jit(solution)/shard_map/all_to_all | solution.py:430
  20.8 16.8 %all-to-all-done.got = bf16[16,192,128]{2,1,0:T(8,128)(2,1)S(1)} async-done(((bf16[16,192,128]{2,1,0:T(8,128)(2,1)}), bf16[16,192,128]{2,1,0:T(8,128)(2,1)S(1)}, u32[]{:S(2)}, u32[]{:S(2)}) %all-to-all-start) | async-done | bytes 786464 | tf_op jit(solution)/shard_map/all_to_all | solution.py:430
  37.6 1.3 %shard_map.175 = bf16[16,64,128]{2,1,0:T(8,128)(2,1)S(1)} custom-call(s32[1]{0:T(128)S(6)} %copy.19.video_len, s32[1]{0:T(128)S(6)} %copy.20.audio_len, s32[1]{0:T(128)S(6)} %copy.21.shift, bf16[16,192,128]{2,1,0:T(8,128)(2,1)S(1)} %all-to-all-done.got), custom_call_target="tpu_custom_call" | custom-call | tf_op jit(solution)/shard_map/pallas_call | solution.py:431
  38.9 15.3 %all_to_all.10.back = bf16[16,64,128]{2,1,0:T(8,128)(2,1)S(1)} all-to-all(bf16[16,64,128]{2,1,0:T(8,128)(2,1)S(1)} %shard_map.175), channel_id=1, replica_groups=mesh['clip'=2,'seq'=16] {'seq'}, dimensions={0} | all-to-all | bytes 524288 | tf_op jit(solution)/shard_map/all_to_all | solution.py:438
  54.2 0.7 %shard_map.176 = (bf16[16,4096]{1,0:T(8,128)(2,1)}, bf16[8,2048]{1,0:T(8,128)(2,1)}, bf16[16,2048]{1,0:T(8,128)(2,1)}, bf16[8,2048]{1,0:T(8,128)(2,1)}) custom-call(bf16[16,64,128]{2,1,0:T(8,128)(2,1)S(1)} %all_to_all.10.back), custom_call_target="tpu_custom_call" | custom-call | tf_op jit(solution)/shard_map/pallas_call | solution.py:439
Async XLA Ops:
  0.6 0.9 %copy-start = (bf16[16,4096]{1,0:T(8,128)(2,1)S(1)}, bf16[16,4096]{1,0:T(8,128)(2,1)}, u32[]{:S(2)}) copy-start(bf16[16,4096]{1,0:T(8,128)(2,1)} %refs_0_.1) | copy-start | bytes 393220
  1.5 0.9 %copy-start.1 = (bf16[16,4096]{1,0:T(8,128)(2,1)S(1)}, bf16[16,4096]{1,0:T(8,128)(2,1)}, u32[]{:S(2)}) copy-start(bf16[16,4096]{1,0:T(8,128)(2,1)} %refs_1_.1) | copy-start | bytes 393220
  2.4 0.9 %copy-start.2 = (bf16[16,4096]{1,0:T(8,128)(2,1)S(1)}, bf16[16,4096]{1,0:T(8,128)(2,1)}, u32[]{:S(2)}) copy-start(bf16[16,4096]{1,0:T(8,128)(2,1)} %refs_2_.1) | copy-start | bytes 393220
  3.4 0.8 %copy-start.3 = (bf16[16,2048]{1,0:T(8,128)(2,1)S(1)}, bf16[16,2048]{1,0:T(8,128)(2,1)}, u32[]{:S(2)}) copy-start(bf16[16,2048]{1,0:T(8,128)(2,1)} %refs_3_.1) | copy-start | bytes 196612
  4.2 0.8 %copy-start.4 = (bf16[16,2048]{1,0:T(8,128)(2,1)S(1)}, bf16[16,2048]{1,0:T(8,128)(2,1)}, u32[]{:S(2)}) copy-start(bf16[16,2048]{1,0:T(8,128)(2,1)} %refs_4_.1) | copy-start | bytes 196612
  5.0 0.8 %copy-start.5 = (bf16[16,2048]{1,0:T(8,128)(2,1)S(1)}, bf16[16,2048]{1,0:T(8,128)(2,1)}, u32[]{:S(2)}) copy-start(bf16[16,2048]{1,0:T(8,128)(2,1)} %refs_5_.1) | copy-start | bytes 196612
  5.9 0.8 %copy-start.6 = (bf16[8,2048]{1,0:T(8,128)(2,1)S(1)}, bf16[8,2048]{1,0:T(8,128)(2,1)}, u32[]{:S(2)}) copy-start(bf16[8,2048]{1,0:T(8,128)(2,1)} %refs_6_.1) | copy-start | bytes 98308
  6.6 0.8 %copy-start.7 = (bf16[8,2048]{1,0:T(8,128)(2,1)S(1)}, bf16[8,2048]{1,0:T(8,128)(2,1)}, u32[]{:S(2)}) copy-start(bf16[8,2048]{1,0:T(8,128)(2,1)} %refs_7_.1) | copy-start | bytes 98308
  7.4 0.8 %copy-start.8 = (bf16[8,2048]{1,0:T(8,128)(2,1)S(1)}, bf16[8,2048]{1,0:T(8,128)(2,1)}, u32[]{:S(2)}) copy-start(bf16[8,2048]{1,0:T(8,128)(2,1)} %refs_8_.1) | copy-start | bytes 98308
  8.1 0.8 %copy-start.9 = (bf16[8,2048]{1,0:T(8,128)(2,1)S(1)}, bf16[8,2048]{1,0:T(8,128)(2,1)}, u32[]{:S(2)}) copy-start(bf16[8,2048]{1,0:T(8,128)(2,1)} %refs_9_.1) | copy-start | bytes 98308
  8.9 0.8 %copy-start.10 = (bf16[8,2048]{1,0:T(8,128)(2,1)S(1)}, bf16[8,2048]{1,0:T(8,128)(2,1)}, u32[]{:S(2)}) copy-start(bf16[8,2048]{1,0:T(8,128)(2,1)} %refs_10_.1) | copy-start | bytes 98308
  9.7 0.8 %copy-start.11 = (bf16[8,2048]{1,0:T(8,128)(2,1)S(1)}, bf16[8,2048]{1,0:T(8,128)(2,1)}, u32[]{:S(2)}) copy-start(bf16[8,2048]{1,0:T(8,128)(2,1)} %refs_11_.1) | copy-start | bytes 98308
  11.5 26.1 %all-to-all-start = ((bf16[16,192,128]{2,1,0:T(8,128)(2,1)}), bf16[16,192,128]{2,1,0:T(8,128)(2,1)S(1)}, u32[]{:S(2)}, u32[]{:S(2)}) async-start(bf16[16,192,128]{2,1,0:T(8,128)(2,1)} %shard_map.174), calls=%async_computation | async-start | bytes 1572864 | tf_op jit(solution)/shard_map/all_to_all | solution.py:430

commit v2 on v1

--- a/solution.py
+++ b/solution.py
@@ -280,24 +280,41 @@
 
 
 def pack_kernel(n, *refs):
-    video, cross, audio, packed = refs[0:3], refs[3:6], refs[6:12], refs[12]
+    sources, packed, held, arrived = refs[0:12], refs[12], refs[13:25], refs[25]
+    copies = [
+        pltpu.make_async_copy(source, slot, arrived.at[i])
+        for i, (source, slot) in enumerate(zip(sources, held))
+    ]
+    for copy in copies:
+        copy.start()
+    video, cross, audio = held[0:3], held[3:6], held[6:12]
     parts = video[0].shape[1] // n // LANES
     rows = cross[0].shape[0]
-    for d in range(n):
-        at = 0
-        for ref in video:
-            for part in range(parts):
+    at = 0
+    for i, ref in enumerate(video):
+        copies[i].wait()
+        for part in range(parts):
+            for d in range(n):
                 packed[d, at : at + rows, :] = ref[:, (d * parts + part) * LANES : (d * parts + part + 1) * LANES]
-                at += rows
-        for ref in cross:
+            at += rows
+    for i, ref in enumerate(cross):
+        copies[3 + i].wait()
+        for d in range(n):
             packed[d, at : at + rows, :] = ref[:, d * LANES : (d + 1) * LANES]
-            at += rows
-        for first, second in zip(audio[0::2], audio[1::2]):
+        at += rows
+    for i in range(0, 6, 2):
+        copies[6 + i].wait()
+        copies[7 + i].wait()
+        for d in range(n):
             pair = jnp.concatenate(
-                [first[:, d * LANES : (d + 1) * LANES], second[:, d * LANES : (d + 1) * LANES]], axis=0
+                [
+                    audio[i][:, d * LANES : (d + 1) * LANES],
+                    audio[i + 1][:, d * LANES : (d + 1) * LANES],
+                ],
+                axis=0,
             )
             packed[d, at : at + pair.shape[0], :] = pair
-            at += pair.shape[0]
+        at += rows
 
 
 def softmax_mix(query, key, value, scale, permit):
@@ -415,18 +432,21 @@
     params = pltpu.CompilerParams(vmem_limit_bytes=32 * 1024 * 1024)
     in_rows = (3 * parts + 6) * rows
     out_rows = (parts + 2) * rows
-    packed = pl.pallas_call(
-        functools.partial(pack_kernel, n),
-        out_shape=jax.ShapeDtypeStruct((n, in_rows, LANES), jnp.bfloat16),
-        in_specs=[vmem] * 12,
-        out_specs=vmem,
-        compiler_params=params,
-    )(
+    sources = (
         video_query, video_keys, video_values,
         cross_video_query, cross_video_keys, cross_video_values,
         audio_query, audio_keys, audio_values,
         cross_audio_query, cross_audio_keys, cross_audio_values,
     )
+    packed = pl.pallas_call(
+        functools.partial(pack_kernel, n),
+        out_shape=jax.ShapeDtypeStruct((n, in_rows, LANES), jnp.bfloat16),
+        in_specs=[pl.BlockSpec(memory_space=pltpu.HBM)] * 12,
+        out_specs=vmem,
+        scratch_shapes=[pltpu.VMEM(source.shape, source.dtype) for source in sources]
+        + [pltpu.SemaphoreType.DMA((12,))],
+        compiler_params=pltpu.CompilerParams(vmem_limit_bytes=60 * 1024 * 1024),
+    )(*sources)
     got = lax.all_to_all(packed, "seq", split_axis=0, concat_axis=0, tiled=True)
     done = pl.pallas_call(
         functools.partial(attend_kernel, n, rows, parts),

time: 55.8 us -> 46.6 us (0.84)
  local copies, waits for them, and re-layouts: 9.77 us -> 0 us
  Pallas kernels: 3.09 us -> 4.19 us
    unnamed x24 -> x0, local copies, waits for them, and re-layouts: 9.77 us -> none
    pallas_call x1, Pallas kernels: 1.04 us -> 2.13 us  [shards_packed(): pl.pallas_call(functools.partial(pack_kernel, n), out_shape=jax.ShapeDtyp...]
where the time goes in v2:
time: 46.6 us; the launch traced here: 46.3 us
  waiting for transfers between devices  16.8 us (36%)
  blocking collectives  15.3 us (33%)
  starting transfers between devices  7.4 us (16%)
  Pallas kernels  4.19 us (9%)
  between operations  2.6 us (6%)
    all_to_all x1, waiting for transfers between devices, shards_packed(): got = lax.all_to_all(packed, 'seq', split_axis=0, concat_axis=0, tiled=True)  16.8 us
    all_to_all x1, blocking collectives, shards_packed(): back = lax.all_to_all(done, 'seq', split_axis=0, concat_axis=0, tiled=True)  15.3 us
    all_to_all x1, starting transfers between devices, shards_packed(): got = lax.all_to_all(packed, 'seq', split_axis=0, concat_axis=0, tiled=True)  7.4 us
    pallas_call x1, Pallas kernels, shards_packed(): pl.pallas_call(functools.partial(pack_kernel, n), out_shape=jax.ShapeDtyp...  2.13 us
    pallas_call x1, Pallas kernels, shards_packed(): pl.pallas_call(functools.partial(attend_kernel, n, rows, parts), out_shap...  1.32 us
  transfers between devices with their start and end apart: 1, of which 1 were waited for; matrix products, arithmetic and copies ran while one was open for 0% of the time, Pallas kernels for 0%

profile of v2, /device:TPU:0, one launch (start us, length us, event | category | flops | bytes accessed | tf_op | source)
XLA Modules:
  0.0 46.3 jit_solution(7162199353117112009)
XLA Ops:
  0.6 2.1 %shard_map.174 = bf16[16,192,128]{2,1,0:T(8,128)(2,1)} custom-call(bf16[16,4096]{1,0:T(8,128)(2,1)} %refs_0_.1, bf16[16,4096]{1,0:T(8,128)(2,1)} %refs_1_.1, bf16[16,4096]{1,0:T(8,128)(2,1)} %refs_2_.1, bf16[16,2048]{1,0:T(8,128)(2,1)} %refs_3_.1, bf16[16,2048]{1,0:T(8,128)(2,1)} %refs_4_.1, bf16[16,2048]{1,0:T(8,128)(2,1)} %refs_5_.1, ...), custom_call_target="tpu_custom_call" | custom-call | tf_op jit(solution)/shard_map/pallas_call | solution.py:441
  2.8 7.4 %all-to-all-start = ((bf16[16,192,128]{2,1,0:T(8,128)(2,1)}), bf16[16,192,128]{2,1,0:T(8,128)(2,1)S(1)}, u32[]{:S(2)}, u32[]{:S(2)}) async-start(bf16[16,192,128]{2,1,0:T(8,128)(2,1)} %shard_map.174), calls=%async_computation | async-start | bytes 1572864 | tf_op jit(solution)/shard_map/all_to_all | solution.py:450
  12.1 16.8 %all-to-all-done.got = bf16[16,192,128]{2,1,0:T(8,128)(2,1)S(1)} async-done(((bf16[16,192,128]{2,1,0:T(8,128)(2,1)}), bf16[16,192,128]{2,1,0:T(8,128)(2,1)S(1)}, u32[]{:S(2)}, u32[]{:S(2)}) %all-to-all-start) | async-done | bytes 786464 | tf_op jit(solution)/shard_map/all_to_all | solution.py:450
  28.9 1.3 %shard_map.175 = bf16[16,64,128]{2,1,0:T(8,128)(2,1)S(1)} custom-call(s32[1]{0:T(128)S(6)} %copy.19.video_len, s32[1]{0:T(128)S(6)} %copy.20.audio_len, s32[1]{0:T(128)S(6)} %copy.21.shift, bf16[16,192,128]{2,1,0:T(8,128)(2,1)S(1)} %all-to-all-done.got), custom_call_target="tpu_custom_call" | custom-call | tf_op jit(solution)/shard_map/pallas_call | solution.py:451
  30.2 15.3 %all_to_all.10.back = bf16[16,64,128]{2,1,0:T(8,128)(2,1)S(1)} all-to-all(bf16[16,64,128]{2,1,0:T(8,128)(2,1)S(1)} %shard_map.175), channel_id=1, replica_groups=mesh['clip'=2,'seq'=16] {'seq'}, dimensions={0} | all-to-all | bytes 524288 | tf_op jit(solution)/shard_map/all_to_all | solution.py:458
  45.5 0.7 %shard_map.176 = (bf16[16,4096]{1,0:T(8,128)(2,1)}, bf16[8,2048]{1,0:T(8,128)(2,1)}, bf16[16,2048]{1,0:T(8,128)(2,1)}, bf16[8,2048]{1,0:T(8,128)(2,1)}) custom-call(bf16[16,64,128]{2,1,0:T(8,128)(2,1)S(1)} %all_to_all.10.back), custom_call_target="tpu_custom_call" | custom-call | tf_op jit(solution)/shard_map/pallas_call | solution.py:459
Async XLA Ops:
  2.8 26.1 %all-to-all-start = ((bf16[16,192,128]{2,1,0:T(8,128)(2,1)}), bf16[16,192,128]{2,1,0:T(8,128)(2,1)S(1)}, u32[]{:S(2)}, u32[]{:S(2)}) async-start(bf16[16,192,128]{2,1,0:T(8,128)(2,1)} %shard_map.174), calls=%async_computation | async-start | bytes 1572864 | tf_op jit(solution)/shard_map/all_to_all | solution.py:450

commit v3 on v2

--- a/solution.py
+++ b/solution.py
@@ -280,40 +280,42 @@
 
 
 def pack_kernel(n, *refs):
-    sources, packed, held, arrived = refs[0:12], refs[12], refs[13:25], refs[25]
+    sources, packed, held, arrived = refs[0:12], refs[12 : 12 + n], refs[12 + n : 24 + n], refs[24 + n]
     copies = [
         pltpu.make_async_copy(source, slot, arrived.at[i])
         for i, (source, slot) in enumerate(zip(sources, held))
     ]
     for copy in copies:
         copy.start()
+    me = lax.axis_index("seq")
     video, cross, audio = held[0:3], held[3:6], held[6:12]
     parts = video[0].shape[1] // n // LANES
     rows = cross[0].shape[0]
+
+    def group(ref, k, count, part):
+        at = pl.multiple_of(((me ^ k) * count + part) * LANES, LANES)
+        return ref[:, pl.ds(at, LANES)]
+
     at = 0
     for i, ref in enumerate(video):
         copies[i].wait()
         for part in range(parts):
-            for d in range(n):
-                packed[d, at : at + rows, :] = ref[:, (d * parts + part) * LANES : (d * parts + part + 1) * LANES]
+            for k in range(n):
+                packed[k][at : at + rows, :] = group(ref, k, parts, part)
             at += rows
     for i, ref in enumerate(cross):
         copies[3 + i].wait()
-        for d in range(n):
-            packed[d, at : at + rows, :] = ref[:, d * LANES : (d + 1) * LANES]
+        for k in range(n):
+            packed[k][at : at + rows, :] = group(ref, k, 1, 0)
         at += rows
     for i in range(0, 6, 2):
         copies[6 + i].wait()
         copies[7 + i].wait()
-        for d in range(n):
+        for k in range(n):
             pair = jnp.concatenate(
-                [
-                    audio[i][:, d * LANES : (d + 1) * LANES],
-                    audio[i + 1][:, d * LANES : (d + 1) * LANES],
-                ],
-                axis=0,
+                [group(audio[i], k, 1, 0), group(audio[i + 1], k, 1, 0)], axis=0
             )
-            packed[d, at : at + pair.shape[0], :] = pair
+            packed[k][at : at + rows, :] = pair
         at += rows
 
 
@@ -340,27 +342,33 @@
     return result
 
 
-def attend_kernel(n, rows, parts, video_len, audio_len, shift, got, done):
+def attend_kernel(n, rows, parts, video_len, audio_len, shift, *refs):
+    got, done = refs[:n], refs[n:]
     half = rows // 2
     tv, ta = n * rows, n * half
     ratio = tv // ta
     bits = ratio.bit_length() - 1
+    me = lax.axis_index("seq")
     video_valid, audio_valid, offset = video_len[0], audio_len[0], shift[0]
 
     def slab(at):
-        return got[:, at : at + rows, :].reshape(tv, LANES)
+        return jnp.concatenate([ref[at : at + rows, :] for ref in got], axis=0)
 
     def halves(at):
-        both = got[:, at : at + rows, :].astype(jnp.float32)
-        first = both[:, :half, :].reshape(ta, LANES).astype(jnp.bfloat16)
-        second = both[:, half:, :].reshape(ta, LANES).astype(jnp.bfloat16)
-        return first, second
+        both = [ref[at : at + rows, :].astype(jnp.float32) for ref in got]
+        first = jnp.concatenate([piece[:half] for piece in both], axis=0)
+        second = jnp.concatenate([piece[half:] for piece in both], axis=0)
+        return first.astype(jnp.bfloat16), second.astype(jnp.bfloat16)
 
     def places(q_count, k_count):
-        return (
-            lax.broadcasted_iota(jnp.int32, (q_count, k_count), 0),
-            lax.broadcasted_iota(jnp.int32, (q_count, k_count), 1),
+        return tuple(
+            lax.broadcasted_iota(jnp.int32, (q_count, k_count), axis) ^ (me * (count // n))
+            for axis, count in enumerate((q_count, k_count))
         )
+
+    def put(at, mixed):
+        for k in range(n):
+            done[k][at : at + rows, :] = mixed[k * rows : (k + 1) * rows].astype(jnp.bfloat16)
 
     q_at, k_at = places(tv, tv)
     permit = k_at < video_valid
@@ -372,7 +380,7 @@
             1.0 / math.sqrt(HDV),
             permit,
         )
-        done[:, h * rows : (h + 1) * rows, :] = mixed.astype(jnp.bfloat16).reshape(n, rows, LANES)
+        put(h * rows, mixed)
     at = 3 * parts * rows
     cross_query, cross_keys, cross_values = slab(at), slab(at + rows), slab(at + 2 * rows)
     at += 3 * rows
@@ -383,9 +391,7 @@
     q_at, k_at = places(tv, ta)
     center = jnp.clip((q_at >> bits) + offset, 0, audio_valid - 1)
     permit = (k_at < audio_valid) & (jnp.abs(k_at - center) <= 5 * ta // 8)
-    mixed = paired_mix(cross_query, sound_keys, sound_values, HDA, permit)
-    out = parts * rows
-    done[:, out : out + rows, :] = mixed.astype(jnp.bfloat16).reshape(n, rows, LANES)
+    put(parts * rows, paired_mix(cross_query, sound_keys, sound_values, HDA, permit))
 
     q_at, k_at = places(ta, ta)
     heard = paired_mix(audio_query, audio_keys, audio_values, HDA, k_at < audio_valid)
@@ -393,27 +399,38 @@
     center = jnp.clip((q_at - offset) * ratio, 0, video_valid - 1)
     permit = (k_at < video_valid) & (jnp.abs(k_at - center) <= tv // 8)
     listened = paired_mix(listen_query, cross_keys, cross_values, HDA, permit)
-    both = jnp.concatenate(
-        [heard.reshape(n, half, LANES), listened.reshape(n, half, LANES)], axis=1
-    )
-    out += rows
-    done[:, out : out + rows, :] = both.astype(jnp.bfloat16)
-
-
-def unpack_kernel(n, back, video_mixed, audio_mixed, video_cross, audio_cross):
+    for k in range(n):
+        both = jnp.concatenate(
+            [heard[k * half : (k + 1) * half], listened[k * half : (k + 1) * half]], axis=0
+        )
+        done[k][(parts + 1) * rows :, :] = both.astype(jnp.bfloat16)
+
+
+def unpack_kernel(n, *refs):
+    back, (video_mixed, audio_mixed, video_cross, audio_cross) = refs[:n], refs[n:]
     rows = video_mixed.shape[0]
     half = audio_mixed.shape[0]
     parts = video_mixed.shape[1] // n // LANES
-    for s in range(n):
+    me = lax.axis_index("seq")
+    for k in range(n):
         for h in range(parts):
-            at = (s * parts + h) * LANES
-            video_mixed[:, at : at + LANES] = back[s, h * rows : (h + 1) * rows, :]
-        at = s * LANES
+            at = pl.multiple_of(((me ^ k) * parts + h) * LANES, LANES)
+            video_mixed[:, pl.ds(at, LANES)] = back[k][h * rows : (h + 1) * rows, :]
+        at = pl.multiple_of((me ^ k) * LANES, LANES)
         out = parts * rows
-        video_cross[:, at : at + LANES] = back[s, out : out + rows, :]
-        both = back[s, out + rows : out + 2 * rows, :]
-        audio_mixed[:, at : at + LANES] = both[:half, :]
-        audio_cross[:, at : at + LANES] = both[half:, :]
+        video_cross[:, pl.ds(at, LANES)] = back[k][out : out + rows, :]
+        both = back[k][out + rows : out + 2 * rows, :]
+        audio_mixed[:, pl.ds(at, LANES)] = both[:half, :]
+        audio_cross[:, pl.ds(at, LANES)] = both[half:, :]
+
+
+def swap_pieces(pieces):
+    n = len(pieces)
+    order = sorted(range(1, n), key=lambda k: (k < n // 2, k))
+    moved = {0: pieces[0]}
+    for k in order:
+        moved[k] = lax.ppermute(pieces[k], "seq", [(i, i ^ k) for i in range(n)])
+    return [moved[k] for k in range(n)]
 
 
 def shards_packed(*arrays):
@@ -425,7 +442,7 @@
         video_length, audio_length, align_offset,
     ) = arrays
     n = lax.axis_size("seq")
-    rows, half = video_query.shape[0], audio_query.shape[0]
+    rows = video_query.shape[0]
     parts = video_query.shape[1] // n // LANES
     vmem = pl.BlockSpec(memory_space=pltpu.VMEM)
     smem = pl.BlockSpec(memory_space=pltpu.SMEM)
@@ -440,22 +457,22 @@
     )
     packed = pl.pallas_call(
         functools.partial(pack_kernel, n),
-        out_shape=jax.ShapeDtypeStruct((n, in_rows, LANES), jnp.bfloat16),
+        out_shape=(jax.ShapeDtypeStruct((in_rows, LANES), jnp.bfloat16),) * n,
         in_specs=[pl.BlockSpec(memory_space=pltpu.HBM)] * 12,
-        out_specs=vmem,
+        out_specs=(vmem,) * n,
         scratch_shapes=[pltpu.VMEM(source.shape, source.dtype) for source in sources]
         + [pltpu.SemaphoreType.DMA((12,))],
         compiler_params=pltpu.CompilerParams(vmem_limit_bytes=60 * 1024 * 1024),
     )(*sources)
-    got = lax.all_to_all(packed, "seq", split_axis=0, concat_axis=0, tiled=True)
+    got = swap_pieces(packed)
     done = pl.pallas_call(
         functools.partial(attend_kernel, n, rows, parts),
-        out_shape=jax.ShapeDtypeStruct((n, out_rows, LANES), jnp.bfloat16),
-        in_specs=[smem] * 3 + [vmem],
-        out_specs=vmem,
+        out_shape=(jax.ShapeDtypeStruct((out_rows, LANES), jnp.bfloat16),) * n,
+        in_specs=[smem] * 3 + [vmem] * n,
+        out_specs=(vmem,) * n,
         compiler_params=params,
-    )(video_length, audio_length, align_offset, got)
-    back = lax.all_to_all(done, "seq", split_axis=0, concat_axis=0, tiled=True)
+    )(video_length, audio_length, align_offset, *got)
+    back = swap_pieces(done)
     return pl.pallas_call(
         functools.partial(unpack_kernel, n),
         out_shape=(
@@ -464,10 +481,10 @@
             jax.ShapeDtypeStruct(cross_video_query.shape, jnp.bfloat16),
             jax.ShapeDtypeStruct(cross_audio_query.shape, jnp.bfloat16),
         ),
-        in_specs=[vmem],
+        in_specs=[vmem] * n,
         out_specs=(vmem,) * 4,
         compiler_params=params,
-    )(back)
+    )(*back)
 
 
 def shards(*arrays):
@@ -480,6 +497,8 @@
         and LANES % HDA == 0
         and rows == 2 * half
         and half % 8 == 0
+        and n & (n - 1) == 0
+        and half & (half - 1) == 0
     )
     return shards_packed(*arrays) if fits else shards_general(*arrays)
 

time: 46.6 us -> 60.6 us (1.30)
  starting transfers between devices: 7.4 us -> 45.9 us
  blocking collectives: 15.3 us -> 0 us
  waiting for transfers between devices: 16.8 us -> 6.74 us
  local copies, waits for them, and re-layouts: 0 us -> 0.8 us
    ppermute x0 -> x30, starting transfers between devices: none -> 45.9 us  [swap_pieces(): moved[k] = lax.ppermute(pieces[k], 'seq', [(i, i ^ k) for i in range(n)])]
    all_to_all x1 -> x0, waiting for transfers between devices: 16.8 us -> none  [shards_packed(): got = lax.all_to_all(packed, 'seq', split_axis=0, concat_axis=0, tiled=True)]
    all_to_all x1 -> x0, blocking collectives: 15.3 us -> none  [shards_packed(): back = lax.all_to_all(done, 'seq', split_axis=0, concat_axis=0, tiled=True)]
    all_to_all x1 -> x0, starting transfers between devices: 7.4 us -> none  [shards_packed(): got = lax.all_to_all(packed, 'seq', split_axis=0, concat_axis=0, tiled=True)]
    ppermute x0 -> x30, waiting for transfers between devices: none -> 6.74 us  [swap_pieces(): moved[k] = lax.ppermute(pieces[k], 'seq', [(i, i ^ k) for i in range(n)])]
    unnamed x0 -> x2, local copies, waits for them, and re-layouts: none -> 0.8 us
  transfers between devices with their start and end apart: 1 -> 30, of which waited for: 1 -> 3; matrix products, arithmetic and copies ran while one was open for 0% -> 0% of each run, Pallas kernels for 0% -> 0%
where the time goes in v3:
time: 60.6 us; the launch traced here: 60.4 us
  starting transfers between devices  45.9 us (76%)
  waiting for transfers between devices  6.74 us (11%)
  Pallas kernels  4.26 us (7%)
  between operations  2.66 us (4%)
  local copies, waits for them, and re-layouts  0.8 us (1%)
    ppermute x30, starting transfers between devices, swap_pieces(): moved[k] = lax.ppermute(pieces[k], 'seq', [(i, i ^ k) for i in range(n)])  45.9 us
    ppermute x30, waiting for transfers between devices, swap_pieces(): moved[k] = lax.ppermute(pieces[k], 'seq', [(i, i ^ k) for i in range(n)])  6.74 us
    pallas_call x1, Pallas kernels, shards_packed(): pl.pallas_call(functools.partial(pack_kernel, n), out_shape=(jax.ShapeDty...  2.18 us
    pallas_call x1, Pallas kernels, shards_packed(): pl.pallas_call(functools.partial(attend_kernel, n, rows, parts), out_shap...  1.33 us
  transfers between devices with their start and end apart: 30, of which 3 were waited for; matrix products, arithmetic and copies ran while one was open for 0% of the time, Pallas kernels for 0%

profile of v3, /device:TPU:0, one launch (start us, length us, event | category | flops | bytes accessed | tf_op | source)
XLA Modules:
  0.0 60.4 jit_solution(2211112953758875072)
XLA Ops:
  0.6 2.2 %shard_map.174 = (bf16[192,128]{1,0:T(8,128)(2,1)}, bf16[192,128]{1,0:T(8,128)(2,1)}, bf16[192,128]{1,0:T(8,128)(2,1)}, bf16[192,128]{1,0:T(8,128)(2,1)}, bf16[1...) custom-call(bf16[16,4096]{1,0:T(8,128)(2,1)} %refs_0_.1, ...), custom_call_target="tpu_custom_call" | custom-call | tf_op jit(solution)/shard_map/pallas_call | solution.py:458
  2.8 0.5 collective-permute-start
  3.3 2.6 %collective-permute-start.1 = (bf16[192,128]{1,0:T(8,128)(2,1)}, bf16[192,128]{1,0:T(8,128)(2,1)S(1)}, u32[]{:S(2)}, u32[]{:S(2)}) collective-permute-start(bf16[192,128]{1,0:T(8,128)(2,1)} %get-tuple-element.38), channel_id=1, source_target_pairs={{0,2},{1,3},{2,0},{3,1},{4,6},{5,7},{6,4},{7,5},{8,10},{9,11},{10,... | collective-permute-start | bytes 147464 | tf_op jit(solution)/shard_map/ppermute | solution.py:432
  5.9 0.1 collective-permute-start.2
  6.0 1.8 %collective-permute-start.3 = (bf16[192,128]{1,0:T(8,128)(2,1)}, bf16[192,128]{1,0:T(8,128)(2,1)S(1)}, u32[]{:S(2)}, u32[]{:S(2)}) collective-permute-start(bf16[192,128]{1,0:T(8,128)(2,1)} %get-tuple-element.40), channel_id=1, source_target_pairs={{0,4},{1,5},{2,6},{3,7},{4,0},{5,1},{6,2},{7,3},{8,12},{9,13},{10,... | collective-permute-start | bytes 147464 | tf_op jit(solution)/shard_map/ppermute | solution.py:432
  7.8 0.0 collective-permute-start.4
  7.8 0.0 collective-permute-done.refs_1_
  7.8 2.6 %collective-permute-start.5 = (bf16[192,128]{1,0:T(8,128)(2,1)}, bf16[192,128]{1,0:T(8,128)(2,1)S(1)}, u32[]{:S(2)}, u32[]{:S(2)}) collective-permute-start(bf16[192,128]{1,0:T(8,128)(2,1)} %get-tuple-element.42), channel_id=1, source_target_pairs={{0,6},{1,7},{2,4},{3,5},{4,2},{5,3},{6,0},{7,1},{8,14},{9,15},{10,... | collective-permute-start | bytes 147464 | tf_op jit(solution)/shard_map/ppermute | solution.py:432
  10.4 0.0 collective-permute-done.1.refs_2_
  10.4 0.1 collective-permute-start.6
  10.6 0.0 collective-permute-done.2.refs_3_
  10.6 2.6 %collective-permute-start.7 = (bf16[192,128]{1,0:T(8,128)(2,1)}, bf16[192,128]{1,0:T(8,128)(2,1)S(1)}, u32[]{:S(2)}, u32[]{:S(2)}) collective-permute-start(bf16[192,128]{1,0:T(8,128)(2,1)} %get-tuple-element.44), channel_id=1, source_target_pairs={{0,8},{1,9},{2,10},{3,11},{4,12},{5,13},{6,14},{7,15},{8,0},{9,1},... | collective-permute-start | bytes 147464 | tf_op jit(solution)/shard_map/ppermute | solution.py:432
  13.2 0.0 collective-permute-done.3.refs_4_
  13.2 0.9 %collective-permute-start.8 = (bf16[192,128]{1,0:T(8,128)(2,1)}, bf16[192,128]{1,0:T(8,128)(2,1)S(1)}, u32[]{:S(2)}, u32[]{:S(2)}) collective-permute-start(bf16[192,128]{1,0:T(8,128)(2,1)} %get-tuple-element.45), channel_id=1, source_target_pairs={{0,9},{1,8},{2,11},{3,10},{4,13},{5,12},{6,15},{7,14},{8,1},{9,0},... | collective-permute-start | bytes 147464 | tf_op jit(solution)/shard_map/ppermute | solution.py:432
  14.1 0.0 collective-permute-done.4.refs_5_
  14.1 2.7 %collective-permute-start.9 = (bf16[192,128]{1,0:T(8,128)(2,1)}, bf16[192,128]{1,0:T(8,128)(2,1)S(1)}, u32[]{:S(2)}, u32[]{:S(2)}) collective-permute-start(bf16[192,128]{1,0:T(8,128)(2,1)} %get-tuple-element.46), channel_id=1, source_target_pairs={{0,10},{1,11},{2,8},{3,9},{4,14},{5,15},{6,12},{7,13},{8,2},{9,3},... | collective-permute-start | bytes 147464 | tf_op jit(solution)/shard_map/ppermute | solution.py:432
  16.8 0.0 collective-permute-done.5.refs_6_
  16.8 0.6 collective-permute-start.10
  17.4 0.0 collective-permute-done.6.refs_7_
  17.4 3.1 %collective-permute-start.11 = (bf16[192,128]{1,0:T(8,128)(2,1)}, bf16[192,128]{1,0:T(8,128)(2,1)S(1)}, u32[]{:S(2)}, u32[]{:S(2)}) collective-permute-start(bf16[192,128]{1,0:T(8,128)(2,1)} %get-tuple-element.48), channel_id=1, source_target_pairs={{0,12},{1,13},{2,14},{3,15},{4,8},{5,9},{6,10},{7,11},{8,4},{9,5},... | collective-permute-start | bytes 147464 | tf_op jit(solution)/shard_map/ppermute | solution.py:432
  20.4 0.0 collective-permute-done.7.refs_8_
  20.4 0.8 %collective-permute-start.12 = (bf16[192,128]{1,0:T(8,128)(2,1)}, bf16[192,128]{1,0:T(8,128)(2,1)S(1)}, u32[]{:S(2)}, u32[]{:S(2)}) collective-permute-start(bf16[192,128]{1,0:T(8,128)(2,1)} %get-tuple-element.49), channel_id=1, source_target_pairs={{0,13},{1,12},{2,15},{3,14},{4,9},{5,8},{6,11},{7,10},{8,5},{9,4},... | collective-permute-start | bytes 147464 | tf_op jit(solution)/shard_map/ppermute | solution.py:432
  21.2 0.0 collective-permute-done.8.refs_9_
  21.2 4.2 %collective-permute-start.13 = (bf16[192,128]{1,0:T(8,128)(2,1)}, bf16[192,128]{1,0:T(8,128)(2,1)S(1)}, u32[]{:S(2)}, u32[]{:S(2)}) collective-permute-start(bf16[192,128]{1,0:T(8,128)(2,1)} %get-tuple-element.50), channel_id=1, source_target_pairs={{0,14},{1,15},{2,12},{3,13},{4,10},{5,11},{6,8},{7,9},{8,6},{9,7},... | collective-permute-start | bytes 147464 | tf_op jit(solution)/shard_map/ppermute | solution.py:432
  25.4 0.0 collective-permute-done.9.refs_10_
  25.4 2.9 %collective-permute-start.14 = (bf16[192,128]{1,0:T(8,128)(2,1)}, bf16[192,128]{1,0:T(8,128)(2,1)S(1)}, u32[]{:S(2)}, u32[]{:S(2)}) collective-permute-start(bf16[192,128]{1,0:T(8,128)(2,1)} %get-tuple-element.51), channel_id=1, source_target_pairs={{0,15},{1,14},{2,13},{3,12},{4,11},{5,10},{6,9},{7,8},{8,7},{9,6},... | collective-permute-start | bytes 147464 | tf_op jit(solution)/shard_map/ppermute | solution.py:432
  30.2 0.0 collective-permute-done.10.refs_11_
  30.2 0.0 collective-permute-done.11.refs_12_
  30.2 0.0 collective-permute-done.12.refs_13_
  30.2 0.0 collective-permute-done.13.refs_14_
  30.2 2.2 %collective-permute-done.14.refs_15_ = bf16[192,128]{1,0:T(8,128)(2,1)S(1)} collective-permute-done((bf16[192,128]{1,0:T(8,128)(2,1)}, bf16[192,128]{1,0:T(8,128)(2,1)S(1)}, u32[]{:S(2)}, u32[]{:S(2)}) %collective-permute-start.14) | collective-permute-done | bytes 49184 | tf_op jit(solution)/shard_map/ppermute | solution.py:432
  32.4 0.8 %copy-done = bf16[192,128]{1,0:T(8,128)(2,1)S(1)} copy-done((bf16[192,128]{1,0:T(8,128)(2,1)S(1)}, bf16[192,128]{1,0:T(8,128)(2,1)}, u32[]{:S(2)}) %copy-start) | copy-done | bytes 49176
  33.2 1.3 %shard_map.175 = (bf16[64,128]{1,0:T(8,128)(2,1)S(1)}, bf16[64,128]{1,0:T(8,128)(2,1)S(1)}, bf16[64,128]{1,0:T(8,128)(2,1)S(1)}, bf16[64,128]{1,0:T(8,128)(2,1)S...) custom-call(s32[1]{0:T(128)S(6)} %copy.19.video_len, ...), custom_call_target="tpu_custom_call" | custom-call | tf_op jit(solution)/shard_map/pallas_call | solution.py:468
  34.5 0.1 collective-permute-start.15
  34.7 0.3 collective-permute-start.16
  34.9 1.6 %collective-permute-start.17 = (bf16[64,128]{1,0:T(8,128)(2,1)S(1)}, bf16[64,128]{1,0:T(8,128)(2,1)S(1)}, u32[]{:S(2)}, u32[]{:S(2)}) collective-permute-start(bf16[64,128]{1,0:T(8,128)(2,1)S(1)} %get-tuple-element.55), channel_id=1, source_target_pairs={{0,3},{1,2},{2,1},{3,0},{4,7},{5,6},{6,5},{7,4},{8,11},{9,10},{10,... | collective-permute-start | bytes 49160 | tf_op jit(solution)/shard_map/ppermute | solution.py:432
  36.5 1.5 %collective-permute-start.18 = (bf16[64,128]{1,0:T(8,128)(2,1)S(1)}, bf16[64,128]{1,0:T(8,128)(2,1)S(1)}, u32[]{:S(2)}, u32[]{:S(2)}) collective-permute-start(bf16[64,128]{1,0:T(8,128)(2,1)S(1)} %get-tuple-element.56), channel_id=1, source_target_pairs={{0,4},{1,5},{2,6},{3,7},{4,0},{5,1},{6,2},{7,3},{8,12},{9,13},{10,... | collective-permute-start | bytes 49160 | tf_op jit(solution)/shard_map/ppermute | solution.py:432
  38.0 0.1 collective-permute-start.19
  38.2 0.0 collective-permute-done.15.refs_1_
  38.2 1.4 %collective-permute-start.20 = (bf16[64,128]{1,0:T(8,128)(2,1)S(1)}, bf16[64,128]{1,0:T(8,128)(2,1)S(1)}, u32[]{:S(2)}, u32[]{:S(2)}) collective-permute-start(bf16[64,128]{1,0:T(8,128)(2,1)S(1)} %get-tuple-element.58), channel_id=1, source_target_pairs={{0,6},{1,7},{2,4},{3,5},{4,2},{5,3},{6,0},{7,1},{8,14},{9,15},{10,... | collective-permute-start | bytes 49160 | tf_op jit(solution)/shard_map/ppermute | solution.py:432
  39.6 0.0 collective-permute-done.16.refs_2_
  39.6 1.3 %collective-permute-start.21 = (bf16[64,128]{1,0:T(8,128)(2,1)S(1)}, bf16[64,128]{1,0:T(8,128)(2,1)S(1)}, u32[]{:S(2)}, u32[]{:S(2)}) collective-permute-start(bf16[64,128]{1,0:T(8,128)(2,1)S(1)} %get-tuple-element.59), channel_id=1, source_target_pairs={{0,7},{1,6},{2,5},{3,4},{4,3},{5,2},{6,1},{7,0},{8,15},{9,14},{10,... | collective-permute-start | bytes 49160 | tf_op jit(solution)/shard_map/ppermute | solution.py:432
  40.9 0.0 collective-permute-done.17.refs_3_
  40.9 2.6 %collective-permute-start.22 = (bf16[64,128]{1,0:T(8,128)(2,1)S(1)}, bf16[64,128]{1,0:T(8,128)(2,1)S(1)}, u32[]{:S(2)}, u32[]{:S(2)}) collective-permute-start(bf16[64,128]{1,0:T(8,128)(2,1)S(1)} %get-tuple-element.60), channel_id=1, source_target_pairs={{0,8},{1,9},{2,10},{3,11},{4,12},{5,13},{6,14},{7,15},{8,0},{9,1},... | collective-permute-start | bytes 49160 | tf_op jit(solution)/shard_map/ppermute | solution.py:432
  43.5 0.0 collective-permute-done.18.refs_4_
  43.5 0.1 collective-permute-start.23
  43.6 0.0 collective-permute-done.19.refs_5_
  43.6 2.3 %collective-permute-start.24 = (bf16[64,128]{1,0:T(8,128)(2,1)S(1)}, bf16[64,128]{1,0:T(8,128)(2,1)S(1)}, u32[]{:S(2)}, u32[]{:S(2)}) collective-permute-start(bf16[64,128]{1,0:T(8,128)(2,1)S(1)} %get-tuple-element.62), channel_id=1, source_target_pairs={{0,10},{1,11},{2,8},{3,9},{4,14},{5,15},{6,12},{7,13},{8,2},{9,3},... | collective-permute-start | bytes 49160 | tf_op jit(solution)/shard_map/ppermute | solution.py:432
  45.9 0.0 collective-permute-done.20.refs_6_
  45.9 1.1 %collective-permute-start.25 = (bf16[64,128]{1,0:T(8,128)(2,1)S(1)}, bf16[64,128]{1,0:T(8,128)(2,1)S(1)}, u32[]{:S(2)}, u32[]{:S(2)}) collective-permute-start(bf16[64,128]{1,0:T(8,128)(2,1)S(1)} %get-tuple-element.63), channel_id=1, source_target_pairs={{0,11},{1,10},{2,9},{3,8},{4,15},{5,14},{6,13},{7,12},{8,3},{9,2},... | collective-permute-start | bytes 49160 | tf_op jit(solution)/shard_map/ppermute | solution.py:432
  47.1 0.0 collective-permute-done.21.refs_7_
  47.1 2.1 %collective-permute-start.26 = (bf16[64,128]{1,0:T(8,128)(2,1)S(1)}, bf16[64,128]{1,0:T(8,128)(2,1)S(1)}, u32[]{:S(2)}, u32[]{:S(2)}) collective-permute-start(bf16[64,128]{1,0:T(8,128)(2,1)S(1)} %get-tuple-element.64), channel_id=1, source_target_pairs={{0,12},{1,13},{2,14},{3,15},{4,8},{5,9},{6,10},{7,11},{8,4},{9,5},... | collective-permute-start | bytes 49160 | tf_op jit(solution)/shard_map/ppermute | solution.py:432
  49.2 0.0 collective-permute-done.22.refs_8_
  49.2 1.5 %collective-permute-start.27 = (bf16[64,128]{1,0:T(8,128)(2,1)S(1)}, bf16[64,128]{1,0:T(8,128)(2,1)S(1)}, u32[]{:S(2)}, u32[]{:S(2)}) collective-permute-start(bf16[64,128]{1,0:T(8,128)(2,1)S(1)} %get-tuple-element.65), channel_id=1, source_target_pairs={{0,13},{1,12},{2,15},{3,14},{4,9},{5,8},{6,11},{7,10},{8,5},{9,4},... | collective-permute-start | bytes 49160 | tf_op jit(solution)/shard_map/ppermute | solution.py:432
  50.7 0.0 collective-permute-done.23.refs_9_
  50.7 3.0 %collective-permute-start.28 = (bf16[64,128]{1,0:T(8,128)(2,1)S(1)}, bf16[64,128]{1,0:T(8,128)(2,1)S(1)}, u32[]{:S(2)}, u32[]{:S(2)}) collective-permute-start(bf16[64,128]{1,0:T(8,128)(2,1)S(1)} %get-tuple-element.66), channel_id=1, source_target_pairs={{0,14},{1,15},{2,12},{3,13},{4,10},{5,11},{6,8},{7,9},{8,6},{9,7},... | collective-permute-start | bytes 49160 | tf_op jit(solution)/shard_map/ppermute | solution.py:432
  53.7 0.0 collective-permute-done.24.refs_10_
  53.7 1.3 %collective-permute-start.29 = (bf16[64,128]{1,0:T(8,128)(2,1)S(1)}, bf16[64,128]{1,0:T(8,128)(2,1)S(1)}, u32[]{:S(2)}, u32[]{:S(2)}) collective-permute-start(bf16[64,128]{1,0:T(8,128)(2,1)S(1)} %get-tuple-element.67), channel_id=1, source_target_pairs={{0,15},{1,14},{2,13},{3,12},{4,11},{5,10},{6,9},{7,8},{8,7},{9,6},... | collective-permute-start | bytes 49160 | tf_op jit(solution)/shard_map/ppermute | solution.py:432
  55.1 0.0 collective-permute-done.25.refs_11_
  55.1 0.0 collective-permute-done.26.refs_12_
  55.1 0.0 collective-permute-done.27.refs_13_
  55.1 2.0 %collective-permute-done.28.refs_14_ = bf16[64,128]{1,0:T(8,128)(2,1)S(1)} collective-permute-done((bf16[64,128]{1,0:T(8,128)(2,1)S(1)}, bf16[64,128]{1,0:T(8,128)(2,1)S(1)}, u32[]{:S(2)}, u32[]{:S(2)}) %collective-permute-start.28) | collective-permute-done | bytes 16416 | tf_op jit(solution)/shard_map/ppermute | solution.py:432
  57.1 2.5 %collective-permute-done.29.refs_15_ = bf16[64,128]{1,0:T(8,128)(2,1)S(1)} collective-permute-done((bf16[64,128]{1,0:T(8,128)(2,1)S(1)}, bf16[64,128]{1,0:T(8,128)(2,1)S(1)}, u32[]{:S(2)}, u32[]{:S(2)}) %collective-permute-start.29) | collective-permute-done | bytes 16416 | tf_op jit(solution)/shard_map/ppermute | solution.py:432
  59.6 0.8 %shard_map.176 = (bf16[16,4096]{1,0:T(8,128)(2,1)}, bf16[8,2048]{1,0:T(8,128)(2,1)}, bf16[16,2048]{1,0:T(8,128)(2,1)}, bf16[8,2048]{1,0:T(8,128)(2,1)}) custom-call(bf16[64,128]{1,0:T(8,128)(2,1)S(1)} %get-tuple-element.52.refs_0_, bf16[64,128]{1,0:T(8,128)(2,1)S(1)} %collective-permute-done.15.refs_1_, bf16[64,128]{1,0:T(8,128)(2,1)S(1)} %collective-permute-done.16.refs_2_, ...), custom_call_target="tpu_custom_call" | custom-call | tf_op jit(solution)/shard_map/pallas_call | solution.py:476
  (1 shorter events, 0.0 us)
Async XLA Ops:
  2.8 5.0 %collective-permute-start = (bf16[192,128]{1,0:T(8,128)(2,1)}, bf16[192,128]{1,0:T(8,128)(2,1)S(1)}, u32[]{:S(2)}, u32[]{:S(2)}) collective-permute-start(bf16[192,128]{1,0:T(8,128)(2,1)} %get-tuple-element.37), channel_id=1, source_target_pairs={{0,1},{1,0},{2,3},{3,2},{4,5},{5,4},{6,7},{7,6},{8,9},{9,8},{10,11... | collective-permute-start | bytes 147464 | tf_op jit(solution)/shard_map/ppermute | solution.py:432
  3.3 7.1 %collective-permute-start.1 = (bf16[192,128]{1,0:T(8,128)(2,1)}, bf16[192,128]{1,0:T(8,128)(2,1)S(1)}, u32[]{:S(2)}, u32[]{:S(2)}) collective-permute-start(bf16[192,128]{1,0:T(8,128)(2,1)} %get-tuple-element.38), channel_id=1, source_target_pairs={{0,2},{1,3},{2,0},{3,1},{4,6},{5,7},{6,4},{7,5},{8,10},{9,11},{10,... | collective-permute-start | bytes 147464 | tf_op jit(solution)/shard_map/ppermute | solution.py:432
  5.9 4.6 %collective-permute-start.2 = (bf16[192,128]{1,0:T(8,128)(2,1)}, bf16[192,128]{1,0:T(8,128)(2,1)S(1)}, u32[]{:S(2)}, u32[]{:S(2)}) collective-permute-start(bf16[192,128]{1,0:T(8,128)(2,1)} %get-tuple-element.39), channel_id=1, source_target_pairs={{0,3},{1,2},{2,1},{3,0},{4,7},{5,6},{6,5},{7,4},{8,11},{9,10},{10,... | collective-permute-start | bytes 147464 | tf_op jit(solution)/shard_map/ppermute | solution.py:432
  6.0 7.2 %collective-permute-start.3 = (bf16[192,128]{1,0:T(8,128)(2,1)}, bf16[192,128]{1,0:T(8,128)(2,1)S(1)}, u32[]{:S(2)}, u32[]{:S(2)}) collective-permute-start(bf16[192,128]{1,0:T(8,128)(2,1)} %get-tuple-element.40), channel_id=1, source_target_pairs={{0,4},{1,5},{2,6},{3,7},{4,0},{5,1},{6,2},{7,3},{8,12},{9,13},{10,... | collective-permute-start | bytes 147464 | tf_op jit(solution)/shard_map/ppermute | solution.py:432
  7.8 6.3 %collective-permute-start.4 = (bf16[192,128]{1,0:T(8,128)(2,1)}, bf16[192,128]{1,0:T(8,128)(2,1)S(1)}, u32[]{:S(2)}, u32[]{:S(2)}) collective-permute-start(bf16[192,128]{1,0:T(8,128)(2,1)} %get-tuple-element.41), channel_id=1, source_target_pairs={{0,5},{1,4},{2,7},{3,6},{4,1},{5,0},{6,3},{7,2},{8,13},{9,12},{10,... | collective-permute-start | bytes 147464 | tf_op jit(solution)/shard_map/ppermute | solution.py:432
  7.8 9.0 %collective-permute-start.5 = (bf16[192,128]{1,0:T(8,128)(2,1)}, bf16[192,128]{1,0:T(8,128)(2,1)S(1)}, u32[]{:S(2)}, u32[]{:S(2)}) collective-permute-start(bf16[192,128]{1,0:T(8,128)(2,1)} %get-tuple-element.42), channel_id=1, source_target_pairs={{0,6},{1,7},{2,4},{3,5},{4,2},{5,3},{6,0},{7,1},{8,14},{9,15},{10,... | collective-permute-start | bytes 147464 | tf_op jit(solution)/shard_map/ppermute | solution.py:432
  10.4 6.9 %collective-permute-start.6 = (bf16[192,128]{1,0:T(8,128)(2,1)}, bf16[192,128]{1,0:T(8,128)(2,1)S(1)}, u32[]{:S(2)}, u32[]{:S(2)}) collective-permute-start(bf16[192,128]{1,0:T(8,128)(2,1)} %get-tuple-element.43), channel_id=1, source_target_pairs={{0,7},{1,6},{2,5},{3,4},{4,3},{5,2},{6,1},{7,0},{8,15},{9,14},{10,... | collective-permute-start | bytes 147464 | tf_op jit(solution)/shard_map/ppermute | solution.py:432
  10.6 9.9 %collective-permute-start.7 = (bf16[192,128]{1,0:T(8,128)(2,1)}, bf16[192,128]{1,0:T(8,128)(2,1)S(1)}, u32[]{:S(2)}, u32[]{:S(2)}) collective-permute-start(bf16[192,128]{1,0:T(8,128)(2,1)} %get-tuple-element.44), channel_id=1, source_target_pairs={{0,8},{1,9},{2,10},{3,11},{4,12},{5,13},{6,14},{7,15},{8,0},{9,1},... | collective-permute-start | bytes 147464 | tf_op jit(solution)/shard_map/ppermute | solution.py:432
  13.2 8.0 %collective-permute-start.8 = (bf16[192,128]{1,0:T(8,128)(2,1)}, bf16[192,128]{1,0:T(8,128)(2,1)S(1)}, u32[]{:S(2)}, u32[]{:S(2)}) collective-permute-start(bf16[192,128]{1,0:T(8,128)(2,1)} %get-tuple-element.45), channel_id=1, source_target_pairs={{0,9},{1,8},{2,11},{3,10},{4,13},{5,12},{6,15},{7,14},{8,1},{9,0},... | collective-permute-start | bytes 147464 | tf_op jit(solution)/shard_map/ppermute | solution.py:432
  14.1 11.3 %collective-permute-start.9 = (bf16[192,128]{1,0:T(8,128)(2,1)}, bf16[192,128]{1,0:T(8,128)(2,1)S(1)}, u32[]{:S(2)}, u32[]{:S(2)}) collective-permute-start(bf16[192,128]{1,0:T(8,128)(2,1)} %get-tuple-element.46), channel_id=1, source_target_pairs={{0,10},{1,11},{2,8},{3,9},{4,14},{5,15},{6,12},{7,13},{8,2},{9,3},... | collective-permute-start | bytes 147464 | tf_op jit(solution)/shard_map/ppermute | solution.py:432
  16.8 13.4 %collective-permute-start.10 = (bf16[192,128]{1,0:T(8,128)(2,1)}, bf16[192,128]{1,0:T(8,128)(2,1)S(1)}, u32[]{:S(2)}, u32[]{:S(2)}) collective-permute-start(bf16[192,128]{1,0:T(8,128)(2,1)} %get-tuple-element.47), channel_id=1, source_target_pairs={{0,11},{1,10},{2,9},{3,8},{4,15},{5,14},{6,13},{7,12},{8,3},{9,2},... | collective-permute-start | bytes 147464 | tf_op jit(solution)/shard_map/ppermute | solution.py:432
  17.4 12.9 %collective-permute-start.11 = (bf16[192,128]{1,0:T(8,128)(2,1)}, bf16[192,128]{1,0:T(8,128)(2,1)S(1)}, u32[]{:S(2)}, u32[]{:S(2)}) collective-permute-start(bf16[192,128]{1,0:T(8,128)(2,1)} %get-tuple-element.48), channel_id=1, source_target_pairs={{0,12},{1,13},{2,14},{3,15},{4,8},{5,9},{6,10},{7,11},{8,4},{9,5},... | collective-permute-start | bytes 147464 | tf_op jit(solution)/shard_map/ppermute | solution.py:432
  20.4 9.8 %collective-permute-start.12 = (bf16[192,128]{1,0:T(8,128)(2,1)}, bf16[192,128]{1,0:T(8,128)(2,1)S(1)}, u32[]{:S(2)}, u32[]{:S(2)}) collective-permute-start(bf16[192,128]{1,0:T(8,128)(2,1)} %get-tuple-element.49), channel_id=1, source_target_pairs={{0,13},{1,12},{2,15},{3,14},{4,9},{5,8},{6,11},{7,10},{8,5},{9,4},... | collective-permute-start | bytes 147464 | tf_op jit(solution)/shard_map/ppermute | solution.py:432
  21.2 9.0 %collective-permute-start.13 = (bf16[192,128]{1,0:T(8,128)(2,1)}, bf16[192,128]{1,0:T(8,128)(2,1)S(1)}, u32[]{:S(2)}, u32[]{:S(2)}) collective-permute-start(bf16[192,128]{1,0:T(8,128)(2,1)} %get-tuple-element.50), channel_id=1, source_target_pairs={{0,14},{1,15},{2,12},{3,13},{4,10},{5,11},{6,8},{7,9},{8,6},{9,7},... | collective-permute-start | bytes 147464 | tf_op jit(solution)/shard_map/ppermute | solution.py:432
  25.4 7.0 %collective-permute-start.14 = (bf16[192,128]{1,0:T(8,128)(2,1)}, bf16[192,128]{1,0:T(8,128)(2,1)S(1)}, u32[]{:S(2)}, u32[]{:S(2)}) collective-permute-start(bf16[192,128]{1,0:T(8,128)(2,1)} %get-tuple-element.51), channel_id=1, source_target_pairs={{0,15},{1,14},{2,13},{3,12},{4,11},{5,10},{6,9},{7,8},{8,7},{9,6},... | collective-permute-start | bytes 147464 | tf_op jit(solution)/shard_map/ppermute | solution.py:432
  32.4 0.8 %copy-start = (bf16[192,128]{1,0:T(8,128)(2,1)S(1)}, bf16[192,128]{1,0:T(8,128)(2,1)}, u32[]{:S(2)}) copy-start(bf16[192,128]{1,0:T(8,128)(2,1)} %get-tuple-element.36.refs_0_) | copy-start | bytes 147460
  34.5 3.6 %collective-permute-start.15 = (bf16[64,128]{1,0:T(8,128)(2,1)S(1)}, bf16[64,128]{1,0:T(8,128)(2,1)S(1)}, u32[]{:S(2)}, u32[]{:S(2)}) collective-permute-start(bf16[64,128]{1,0:T(8,128)(2,1)S(1)} %get-tuple-element.53), channel_id=1, source_target_pairs={{0,1},{1,0},{2,3},{3,2},{4,5},{5,4},{6,7},{7,6},{8,9},{9,8},{10,11... | collective-permute-start | bytes 49160 | tf_op jit(solution)/shard_map/ppermute | solution.py:432
  34.7 4.9 %collective-permute-start.16 = (bf16[64,128]{1,0:T(8,128)(2,1)S(1)}, bf16[64,128]{1,0:T(8,128)(2,1)S(1)}, u32[]{:S(2)}, u32[]{:S(2)}) collective-permute-start(bf16[64,128]{1,0:T(8,128)(2,1)S(1)} %get-tuple-element.54), channel_id=1, source_target_pairs={{0,2},{1,3},{2,0},{3,1},{4,6},{5,7},{6,4},{7,5},{8,10},{9,11},{10,... | collective-permute-start | bytes 49160 | tf_op jit(solution)/shard_map/ppermute | solution.py:432
  34.9 6.0 %collective-permute-start.17 = (bf16[64,128]{1,0:T(8,128)(2,1)S(1)}, bf16[64,128]{1,0:T(8,128)(2,1)S(1)}, u32[]{:S(2)}, u32[]{:S(2)}) collective-permute-start(bf16[64,128]{1,0:T(8,128)(2,1)S(1)} %get-tuple-element.55), channel_id=1, source_target_pairs={{0,3},{1,2},{2,1},{3,0},{4,7},{5,6},{6,5},{7,4},{8,11},{9,10},{10,... | collective-permute-start | bytes 49160 | tf_op jit(solution)/shard_map/ppermute | solution.py:432
  36.5 7.0 %collective-permute-start.18 = (bf16[64,128]{1,0:T(8,128)(2,1)S(1)}, bf16[64,128]{1,0:T(8,128)(2,1)S(1)}, u32[]{:S(2)}, u32[]{:S(2)}) collective-permute-start(bf16[64,128]{1,0:T(8,128)(2,1)S(1)} %get-tuple-element.56), channel_id=1, source_target_pairs={{0,4},{1,5},{2,6},{3,7},{4,0},{5,1},{6,2},{7,3},{8,12},{9,13},{10,... | collective-permute-start | bytes 49160 | tf_op jit(solution)/shard_map/ppermute | solution.py:432
  38.0 5.6 %collective-permute-start.19 = (bf16[64,128]{1,0:T(8,128)(2,1)S(1)}, bf16[64,128]{1,0:T(8,128)(2,1)S(1)}, u32[]{:S(2)}, u32[]{:S(2)}) collective-permute-start(bf16[64,128]{1,0:T(8,128)(2,1)S(1)} %get-tuple-element.57), channel_id=1, source_target_pairs={{0,5},{1,4},{2,7},{3,6},{4,1},{5,0},{6,3},{7,2},{8,13},{9,12},{10,... | collective-permute-start | bytes 49160 | tf_op jit(solution)/shard_map/ppermute | solution.py:432
  38.2 7.8 %collective-permute-start.20 = (bf16[64,128]{1,0:T(8,128)(2,1)S(1)}, bf16[64,128]{1,0:T(8,128)(2,1)S(1)}, u32[]{:S(2)}, u32[]{:S(2)}) collective-permute-start(bf16[64,128]{1,0:T(8,128)(2,1)S(1)} %get-tuple-element.58), channel_id=1, source_target_pairs={{0,6},{1,7},{2,4},{3,5},{4,2},{5,3},{6,0},{7,1},{8,14},{9,15},{10,... | collective-permute-start | bytes 49160 | tf_op jit(solution)/shard_map/ppermute | solution.py:432
  39.6 7.5 %collective-permute-start.21 = (bf16[64,128]{1,0:T(8,128)(2,1)S(1)}, bf16[64,128]{1,0:T(8,128)(2,1)S(1)}, u32[]{:S(2)}, u32[]{:S(2)}) collective-permute-start(bf16[64,128]{1,0:T(8,128)(2,1)S(1)} %get-tuple-element.59), channel_id=1, source_target_pairs={{0,7},{1,6},{2,5},{3,4},{4,3},{5,2},{6,1},{7,0},{8,15},{9,14},{10,... | collective-permute-start | bytes 49160 | tf_op jit(solution)/shard_map/ppermute | solution.py:432
  40.9 8.3 %collective-permute-start.22 = (bf16[64,128]{1,0:T(8,128)(2,1)S(1)}, bf16[64,128]{1,0:T(8,128)(2,1)S(1)}, u32[]{:S(2)}, u32[]{:S(2)}) collective-permute-start(bf16[64,128]{1,0:T(8,128)(2,1)S(1)} %get-tuple-element.60), channel_id=1, source_target_pairs={{0,8},{1,9},{2,10},{3,11},{4,12},{5,13},{6,14},{7,15},{8,0},{9,1},... | collective-permute-start | bytes 49160 | tf_op jit(solution)/shard_map/ppermute | solution.py:432
  43.5 7.2 %collective-permute-start.23 = (bf16[64,128]{1,0:T(8,128)(2,1)S(1)}, bf16[64,128]{1,0:T(8,128)(2,1)S(1)}, u32[]{:S(2)}, u32[]{:S(2)}) collective-permute-start(bf16[64,128]{1,0:T(8,128)(2,1)S(1)} %get-tuple-element.61), channel_id=1, source_target_pairs={{0,9},{1,8},{2,11},{3,10},{4,13},{5,12},{6,15},{7,14},{8,1},{9,0},... | collective-permute-start | bytes 49160 | tf_op jit(solution)/shard_map/ppermute | solution.py:432
  43.6 10.2 %collective-permute-start.24 = (bf16[64,128]{1,0:T(8,128)(2,1)S(1)}, bf16[64,128]{1,0:T(8,128)(2,1)S(1)}, u32[]{:S(2)}, u32[]{:S(2)}) collective-permute-start(bf16[64,128]{1,0:T(8,128)(2,1)S(1)} %get-tuple-element.62), channel_id=1, source_target_pairs={{0,10},{1,11},{2,8},{3,9},{4,14},{5,15},{6,12},{7,13},{8,2},{9,3},... | collective-permute-start | bytes 49160 | tf_op jit(solution)/shard_map/ppermute | solution.py:432
  45.9 9.1 %collective-permute-start.25 = (bf16[64,128]{1,0:T(8,128)(2,1)S(1)}, bf16[64,128]{1,0:T(8,128)(2,1)S(1)}, u32[]{:S(2)}, u32[]{:S(2)}) collective-permute-start(bf16[64,128]{1,0:T(8,128)(2,1)S(1)} %get-tuple-element.63), channel_id=1, source_target_pairs={{0,11},{1,10},{2,9},{3,8},{4,15},{5,14},{6,13},{7,12},{8,3},{9,2},... | collective-permute-start | bytes 49160 | tf_op jit(solution)/shard_map/ppermute | solution.py:432
  47.1 8.0 %collective-permute-start.26 = (bf16[64,128]{1,0:T(8,128)(2,1)S(1)}, bf16[64,128]{1,0:T(8,128)(2,1)S(1)}, u32[]{:S(2)}, u32[]{:S(2)}) collective-permute-start(bf16[64,128]{1,0:T(8,128)(2,1)S(1)} %get-tuple-element.64), channel_id=1, source_target_pairs={{0,12},{1,13},{2,14},{3,15},{4,8},{5,9},{6,10},{7,11},{8,4},{9,5},... | collective-permute-start | bytes 49160 | tf_op jit(solution)/shard_map/ppermute | solution.py:432
  49.2 5.9 %collective-permute-start.27 = (bf16[64,128]{1,0:T(8,128)(2,1)S(1)}, bf16[64,128]{1,0:T(8,128)(2,1)S(1)}, u32[]{:S(2)}, u32[]{:S(2)}) collective-permute-start(bf16[64,128]{1,0:T(8,128)(2,1)S(1)} %get-tuple-element.65), channel_id=1, source_target_pairs={{0,13},{1,12},{2,15},{3,14},{4,9},{5,8},{6,11},{7,10},{8,5},{9,4},... | collective-permute-start | bytes 49160 | tf_op jit(solution)/shard_map/ppermute | solution.py:432
  50.7 6.4 %collective-permute-start.28 = (bf16[64,128]{1,0:T(8,128)(2,1)S(1)}, bf16[64,128]{1,0:T(8,128)(2,1)S(1)}, u32[]{:S(2)}, u32[]{:S(2)}) collective-permute-start(bf16[64,128]{1,0:T(8,128)(2,1)S(1)} %get-tuple-element.66), channel_id=1, source_target_pairs={{0,14},{1,15},{2,12},{3,13},{4,10},{5,11},{6,8},{7,9},{8,6},{9,7},... | collective-permute-start | bytes 49160 | tf_op jit(solution)/shard_map/ppermute | solution.py:432
  53.7 5.9 %collective-permute-start.29 = (bf16[64,128]{1,0:T(8,128)(2,1)S(1)}, bf16[64,128]{1,0:T(8,128)(2,1)S(1)}, u32[]{:S(2)}, u32[]{:S(2)}) collective-permute-start(bf16[64,128]{1,0:T(8,128)(2,1)S(1)} %get-tuple-element.67), channel_id=1, source_target_pairs={{0,15},{1,14},{2,13},{3,12},{4,11},{5,10},{6,9},{7,8},{8,7},{9,6},... | collective-permute-start | bytes 49160 | tf_op jit(solution)/shard_map/ppermute | solution.py:432

commit v4 on v2

--- a/solution.py
+++ b/solution.py
@@ -279,42 +279,45 @@
 LANES = 128
 
 
-def pack_kernel(n, *refs):
-    sources, packed, held, arrived = refs[0:12], refs[12], refs[13:25], refs[25]
+def by_step(items):
+    return [items[-j % len(items)] for j in range(len(items))]
+
+
+def pack_kernel(chips, *refs):
+    sources, refs = refs[:12], refs[12:]
+    packed, held, arrived = by_step(refs[:chips]), refs[chips : chips + 12], refs[chips + 12]
     copies = [
         pltpu.make_async_copy(source, slot, arrived.at[i])
         for i, (source, slot) in enumerate(zip(sources, held))
     ]
     for copy in copies:
         copy.start()
+    chip = lax.axis_index("seq") // 2
     video, cross, audio = held[0:3], held[3:6], held[6:12]
-    parts = video[0].shape[1] // n // LANES
-    rows = cross[0].shape[0]
+    rows = video[0].shape[0]
+
+    def group(ref, j, part):
+        width = ref.shape[1] // chips
+        at = pl.multiple_of((chip ^ j) * width + part * LANES, LANES)
+        return ref[:, pl.ds(at, LANES)]
+
     at = 0
-    for i, ref in enumerate(video):
+    for i, ref in enumerate(video + cross):
         copies[i].wait()
-        for part in range(parts):
-            for d in range(n):
-                packed[d, at : at + rows, :] = ref[:, (d * parts + part) * LANES : (d * parts + part + 1) * LANES]
+        for part in range(ref.shape[1] // chips // LANES):
+            for j in range(chips):
+                packed[j][at : at + rows, :] = group(ref, j, part)
             at += rows
-    for i, ref in enumerate(cross):
-        copies[3 + i].wait()
-        for d in range(n):
-            packed[d, at : at + rows, :] = ref[:, d * LANES : (d + 1) * LANES]
-        at += rows
     for i in range(0, 6, 2):
         copies[6 + i].wait()
         copies[7 + i].wait()
-        for d in range(n):
-            pair = jnp.concatenate(
-                [
-                    audio[i][:, d * LANES : (d + 1) * LANES],
-                    audio[i + 1][:, d * LANES : (d + 1) * LANES],
-                ],
-                axis=0,
-            )
-            packed[d, at : at + pair.shape[0], :] = pair
-        at += rows
+        for part in range(audio[i].shape[1] // chips // LANES):
+            for j in range(chips):
+                pair = jnp.concatenate(
+                    [group(audio[i], j, part), group(audio[i + 1], j, part)], axis=0
+                )
+                packed[j][at : at + rows, :] = pair
+            at += rows
 
 
 def softmax_mix(query, key, value, scale, permit):
@@ -340,80 +343,102 @@
     return result
 
 
-def attend_kernel(n, rows, parts, video_len, audio_len, shift, got, done):
+def attend_kernel(chips, rows, parts, pairs, video_len, audio_len, shift, *refs):
+    own, other, done = (by_step(refs[i * chips : (i + 1) * chips]) for i in range(3))
+    every = [ref for both in zip(own, other) for ref in both]
     half = rows // 2
-    tv, ta = n * rows, n * half
+    tv, ta = 2 * chips * rows, 2 * chips * half
     ratio = tv // ta
     bits = ratio.bit_length() - 1
+    me = lax.axis_index("seq")
     video_valid, audio_valid, offset = video_len[0], audio_len[0], shift[0]
 
-    def slab(at):
-        return got[:, at : at + rows, :].reshape(tv, LANES)
-
-    def halves(at):
-        both = got[:, at : at + rows, :].astype(jnp.float32)
-        first = both[:, :half, :].reshape(ta, LANES).astype(jnp.bfloat16)
-        second = both[:, half:, :].reshape(ta, LANES).astype(jnp.bfloat16)
-        return first, second
-
-    def places(q_count, k_count):
-        return (
-            lax.broadcasted_iota(jnp.int32, (q_count, k_count), 0),
-            lax.broadcasted_iota(jnp.int32, (q_count, k_count), 1),
-        )
-
-    q_at, k_at = places(tv, tv)
+    def slab(refs, at):
+        return jnp.concatenate([ref[at : at + rows, :] for ref in refs], axis=0)
+
+    def side(refs, at, second):
+        wide = [ref[at : at + rows, :].astype(jnp.float32) for ref in refs]
+        taken = [piece[half:] if second else piece[:half] for piece in wide]
+        return jnp.concatenate(taken, axis=0).astype(jnp.bfloat16)
+
+    def places(q_step, k_step):
+        q_at = lax.broadcasted_iota(jnp.int32, (chips * q_step, 2 * chips * k_step), 0)
+        q_at = (q_at // q_step * (2 * q_step) + q_at % q_step) ^ (me * q_step)
+        k_at = lax.broadcasted_iota(jnp.int32, (chips * q_step, 2 * chips * k_step), 1)
+        return q_at, k_at ^ (me * k_step)
+
+    def put(at, mixed):
+        for j in range(chips):
+            done[j][at : at + rows, :] = mixed[j * rows : (j + 1) * rows].astype(jnp.bfloat16)
+
+    q_at, k_at = places(rows, rows)
     permit = k_at < video_valid
     for h in range(parts):
         mixed = softmax_mix(
-            slab(h * rows),
-            slab((parts + h) * rows),
-            slab((2 * parts + h) * rows),
+            slab(own, h * rows),
+            slab(every, (parts + h) * rows),
+            slab(every, (2 * parts + h) * rows),
             1.0 / math.sqrt(HDV),
             permit,
         )
-        done[:, h * rows : (h + 1) * rows, :] = mixed.astype(jnp.bfloat16).reshape(n, rows, LANES)
-    at = 3 * parts * rows
-    cross_query, cross_keys, cross_values = slab(at), slab(at + rows), slab(at + 2 * rows)
-    at += 3 * rows
-    audio_query, audio_keys = halves(at)
-    audio_values, listen_query = halves(at + rows)
-    sound_keys, sound_values = halves(at + 2 * rows)
-
-    q_at, k_at = places(tv, ta)
+        put(h * rows, mixed)
+
+    cross = 3 * parts * rows
+    audio = cross + 3 * pairs * rows
+    q_at, k_at = places(rows, half)
     center = jnp.clip((q_at >> bits) + offset, 0, audio_valid - 1)
-    permit = (k_at < audio_valid) & (jnp.abs(k_at - center) <= 5 * ta // 8)
-    mixed = paired_mix(cross_query, sound_keys, sound_values, HDA, permit)
-    out = parts * rows
-    done[:, out : out + rows, :] = mixed.astype(jnp.bfloat16).reshape(n, rows, LANES)
-
-    q_at, k_at = places(ta, ta)
-    heard = paired_mix(audio_query, audio_keys, audio_values, HDA, k_at < audio_valid)
-    q_at, k_at = places(ta, tv)
+    toward_video = (k_at < audio_valid) & (jnp.abs(k_at - center) <= 5 * ta // 8)
+    q_at, k_at = places(half, half)
+    within_audio = k_at < audio_valid
+    q_at, k_at = places(half, rows)
     center = jnp.clip((q_at - offset) * ratio, 0, video_valid - 1)
-    permit = (k_at < video_valid) & (jnp.abs(k_at - center) <= tv // 8)
-    listened = paired_mix(listen_query, cross_keys, cross_values, HDA, permit)
-    both = jnp.concatenate(
-        [heard.reshape(n, half, LANES), listened.reshape(n, half, LANES)], axis=1
-    )
-    out += rows
-    done[:, out : out + rows, :] = both.astype(jnp.bfloat16)
-
-
-def unpack_kernel(n, back, video_mixed, audio_mixed, video_cross, audio_cross):
+    toward_audio = (k_at < video_valid) & (jnp.abs(k_at - center) <= tv // 8)
+    for p in range(pairs):
+        at = cross + p * rows
+        cross_query = slab(own, at)
+        cross_keys = slab(every, at + pairs * rows)
+        cross_values = slab(every, at + 2 * pairs * rows)
+        at = audio + p * rows
+        audio_query, audio_keys = side(own, at, False), side(every, at, True)
+        at += pairs * rows
+        audio_values, listen_query = side(every, at, False), side(own, at, True)
+        at += pairs * rows
+        sound_keys, sound_values = side(every, at, False), side(every, at, True)
+        out = (parts + p) * rows
+        put(out, paired_mix(cross_query, sound_keys, sound_values, HDA, toward_video))
+        heard = paired_mix(audio_query, audio_keys, audio_values, HDA, within_audio)
+        listened = paired_mix(listen_query, cross_keys, cross_values, HDA, toward_audio)
+        out += pairs * rows
+        for j in range(chips):
+            both = jnp.concatenate(
+                [heard[j * half : (j + 1) * half], listened[j * half : (j + 1) * half]], axis=0
+            )
+            done[j][out : out + rows, :] = both.astype(jnp.bfloat16)
+
+
+def unpack_kernel(chips, *refs):
+    back, (video_mixed, audio_mixed, video_cross, audio_cross) = by_step(refs[:chips]), refs[chips:]
     rows = video_mixed.shape[0]
     half = audio_mixed.shape[0]
-    parts = video_mixed.shape[1] // n // LANES
-    for s in range(n):
+    parts = video_mixed.shape[1] // chips // LANES
+    pairs = audio_mixed.shape[1] // chips // LANES
+    chip = lax.axis_index("seq") // 2
+    for j in range(chips):
         for h in range(parts):
-            at = (s * parts + h) * LANES
-            video_mixed[:, at : at + LANES] = back[s, h * rows : (h + 1) * rows, :]
-        at = s * LANES
-        out = parts * rows
-        video_cross[:, at : at + LANES] = back[s, out : out + rows, :]
-        both = back[s, out + rows : out + 2 * rows, :]
-        audio_mixed[:, at : at + LANES] = both[:half, :]
-        audio_cross[:, at : at + LANES] = both[half:, :]
+            at = pl.multiple_of(((chip ^ j) * parts + h) * LANES, LANES)
+            video_mixed[:, pl.ds(at, LANES)] = back[j][h * rows : (h + 1) * rows, :]
+        for p in range(pairs):
+            at = pl.multiple_of(((chip ^ j) * pairs + p) * LANES, LANES)
+            out = (parts + p) * rows
+            video_cross[:, pl.ds(at, LANES)] = back[j][out : out + rows, :]
+            out += pairs * rows
+            both = back[j][out : out + rows, :]
+            audio_mixed[:, pl.ds(at, LANES)] = both[:half, :]
+            audio_cross[:, pl.ds(at, LANES)] = both[half:, :]
+
+
+def swap(piece, n, step):
+    return lax.ppermute(piece, "seq", [(i, i ^ step) for i in range(n)])
 
 
 def shards_packed(*arrays):
@@ -425,13 +450,15 @@
         video_length, audio_length, align_offset,
     ) = arrays
     n = lax.axis_size("seq")
-    rows, half = video_query.shape[0], audio_query.shape[0]
-    parts = video_query.shape[1] // n // LANES
+    chips = n // 2
+    rows = video_query.shape[0]
+    parts = video_query.shape[1] // chips // LANES
+    pairs = audio_query.shape[1] // chips // LANES
     vmem = pl.BlockSpec(memory_space=pltpu.VMEM)
     smem = pl.BlockSpec(memory_space=pltpu.SMEM)
     params = pltpu.CompilerParams(vmem_limit_bytes=32 * 1024 * 1024)
-    in_rows = (3 * parts + 6) * rows
-    out_rows = (parts + 2) * rows
+    in_rows = (3 * parts + 6 * pairs) * rows
+    out_rows = (parts + 2 * pairs) * rows
     sources = (
         video_query, video_keys, video_values,
         cross_video_query, cross_video_keys, cross_video_values,
@@ -439,47 +466,57 @@
         cross_audio_query, cross_audio_keys, cross_audio_values,
     )
     packed = pl.pallas_call(
-        functools.partial(pack_kernel, n),
-        out_shape=jax.ShapeDtypeStruct((n, in_rows, LANES), jnp.bfloat16),
+        functools.partial(pack_kernel, chips),
+        out_shape=(jax.ShapeDtypeStruct((in_rows, LANES), jnp.bfloat16),) * chips,
         in_specs=[pl.BlockSpec(memory_space=pltpu.HBM)] * 12,
-        out_specs=vmem,
+        out_specs=(vmem,) * chips,
         scratch_shapes=[pltpu.VMEM(source.shape, source.dtype) for source in sources]
         + [pltpu.SemaphoreType.DMA((12,))],
         compiler_params=pltpu.CompilerParams(vmem_limit_bytes=60 * 1024 * 1024),
     )(*sources)
-    got = lax.all_to_all(packed, "seq", split_axis=0, concat_axis=0, tiled=True)
+    packed = by_step(packed)
+    own = packed[:1] + [swap(packed[j], n, 2 * j) for j in range(1, chips)]
+    other = [swap(piece, n, 1) for piece in own]
     done = pl.pallas_call(
-        functools.partial(attend_kernel, n, rows, parts),
-        out_shape=jax.ShapeDtypeStruct((n, out_rows, LANES), jnp.bfloat16),
-        in_specs=[smem] * 3 + [vmem],
-        out_specs=vmem,
+        functools.partial(attend_kernel, chips, rows, parts, pairs),
+        out_shape=(jax.ShapeDtypeStruct((out_rows, LANES), jnp.bfloat16),) * chips,
+        in_specs=[smem] * 3 + [vmem] * (2 * chips),
+        out_specs=(vmem,) * chips,
         compiler_params=params,
-    )(video_length, audio_length, align_offset, got)
-    back = lax.all_to_all(done, "seq", split_axis=0, concat_axis=0, tiled=True)
+    )(
+        video_length, audio_length, align_offset,
+        *by_step(own), *by_step(other),
+    )
+    done = by_step(done)
+    back = done[:1] + [swap(done[j], n, 2 * j) for j in range(1, chips)]
     return pl.pallas_call(
-        functools.partial(unpack_kernel, n),
+        functools.partial(unpack_kernel, chips),
         out_shape=(
             jax.ShapeDtypeStruct(video_query.shape, jnp.bfloat16),
             jax.ShapeDtypeStruct(audio_query.shape, jnp.bfloat16),
             jax.ShapeDtypeStruct(cross_video_query.shape, jnp.bfloat16),
             jax.ShapeDtypeStruct(cross_audio_query.shape, jnp.bfloat16),
         ),
-        in_specs=[vmem],
+        in_specs=[vmem] * chips,
         out_specs=(vmem,) * 4,
         compiler_params=params,
-    )(back)
+    )(*by_step(back))
 
 
 def shards(*arrays):
     n = lax.axis_size("seq")
     rows, half = arrays[0].shape[0], arrays[3].shape[0]
+    chips = max(n // 2, 1)
     fits = (
-        arrays[0].shape[1] % (n * LANES) == 0
-        and arrays[3].shape[1] == n * LANES
+        n % 2 == 0
+        and n & (n - 1) == 0
+        and arrays[0].shape[1] % (chips * LANES) == 0
+        and arrays[3].shape[1] % (chips * LANES) == 0
         and HDV == LANES
         and LANES % HDA == 0
         and rows == 2 * half
         and half % 8 == 0
+        and half & (half - 1) == 0
     )
     return shards_packed(*arrays) if fits else shards_general(*arrays)
 

time: 46.6 us -> 48.5 us (1.041)
  starting transfers between devices: 7.4 us -> 31.9 us
  blocking collectives: 15.3 us -> 0 us
  waiting for transfers between devices: 16.8 us -> 6.81 us
  Pallas kernels: 4.19 us -> 6.06 us
  local copies, waits for them, and re-layouts: 0 us -> 0.89 us
    ppermute x0 -> x22, starting transfers between devices: none -> 31.9 us  [swap(): return lax.ppermute(piece, 'seq', [(i, i ^ step) for i in range(n)])]
    all_to_all x1 -> x0, waiting for transfers between devices: 16.8 us -> none  [shards_packed(): got = lax.all_to_all(packed, 'seq', split_axis=0, concat_axis=0, tiled=True)]
    all_to_all x1 -> x0, blocking collectives: 15.3 us -> none  [shards_packed(): back = lax.all_to_all(done, 'seq', split_axis=0, concat_axis=0, tiled=True)]
    all_to_all x1 -> x0, starting transfers between devices: 7.4 us -> none  [shards_packed(): got = lax.all_to_all(packed, 'seq', split_axis=0, concat_axis=0, tiled=True)]
    ppermute x0 -> x22, waiting for transfers between devices: none -> 6.81 us  [swap(): return lax.ppermute(piece, 'seq', [(i, i ^ step) for i in range(n)])]
    pallas_call x3, Pallas kernels: 4.19 us -> 6.06 us  [the longest x1 3.14 us: shards_packed(): pl.pallas_call(functools.partial(attend_kernel, chips, rows, parts, pairs...]
    unnamed x0 -> x2, local copies, waits for them, and re-layouts: none -> 0.89 us
  transfers between devices with their start and end apart: 1 -> 22, of which waited for: 1 -> 5; matrix products, arithmetic and copies ran while one was open for 0% -> 0% of each run, Pallas kernels for 0% -> 0%
where the time goes in v4:
time: 48.5 us; the launch traced here: 48.3 us
  starting transfers between devices  31.9 us (66%)
  waiting for transfers between devices  6.81 us (14%)
  Pallas kernels  6.06 us (12%)
  between operations  2.66 us (5%)
  local copies, waits for them, and re-layouts  0.89 us (2%)
    ppermute x22, starting transfers between devices, swap(): return lax.ppermute(piece, 'seq', [(i, i ^ step) for i in range(n)])  31.9 us
    ppermute x22, waiting for transfers between devices, swap(): return lax.ppermute(piece, 'seq', [(i, i ^ step) for i in range(n)])  6.81 us
    pallas_call x1, Pallas kernels, shards_packed(): pl.pallas_call(functools.partial(attend_kernel, chips, rows, parts, pairs...  3.14 us
    pallas_call x1, Pallas kernels, shards_packed(): pl.pallas_call(functools.partial(pack_kernel, chips), out_shape=(jax.Shap...  2.17 us
  transfers between devices with their start and end apart: 22, of which 5 were waited for; matrix products, arithmetic and copies ran while one was open for 0% of the time, Pallas kernels for 0%

profile of v4, /device:TPU:0, one launch (start us, length us, event | category | flops | bytes accessed | tf_op | source)
XLA Modules:
  0.0 48.3 jit_solution(16562996583099727208)
XLA Ops:
  0.6 2.2 %shard_map.174 = (bf16[384,128]{1,0:T(8,128)(2,1)}, bf16[384,128]{1,0:T(8,128)(2,1)}, bf16[384,128]{1,0:T(8,128)(2,1)}, bf16[384,128]{1,0:T(8,128)(2,1)}, bf16[3...) custom-call(bf16[16,4096]{1,0:T(8,128)(2,1)} %refs_0_.1, ...), custom_call_target="tpu_custom_call" | custom-call | tf_op jit(solution)/shard_map/pallas_call | solution.py:468
  2.8 6.1 %collective-permute-start = (bf16[384,128]{1,0:T(8,128)(2,1)}, bf16[384,128]{1,0:T(8,128)(2,1)S(1)}, u32[]{:S(2)}, u32[]{:S(2)}) collective-permute-start(bf16[384,128]{1,0:T(8,128)(2,1)} %get-tuple-element.21), channel_id=1, source_target_pairs={{0,14},{1,15},{2,12},{3,13},{4,10},{5,11},{6,8},{7,9},{8,6},{9,7},... | collective-permute-start | bytes 294920 | tf_op jit(solution)/shard_map/ppermute | solution.py:441
  8.9 0.2 collective-permute-start.1
  9.1 0.7 %collective-permute-start.2 = (bf16[384,128]{1,0:T(8,128)(2,1)}, bf16[384,128]{1,0:T(8,128)(2,1)S(1)}, u32[]{:S(2)}, u32[]{:S(2)}) collective-permute-start(bf16[384,128]{1,0:T(8,128)(2,1)} %get-tuple-element.23), channel_id=1, source_target_pairs={{0,10},{1,11},{2,8},{3,9},{4,14},{5,15},{6,12},{7,13},{8,2},{9,3},... | collective-permute-start | bytes 294920 | tf_op jit(solution)/shard_map/ppermute | solution.py:441
  9.8 2.0 %collective-permute-start.3 = (bf16[384,128]{1,0:T(8,128)(2,1)}, bf16[384,128]{1,0:T(8,128)(2,1)S(1)}, u32[]{:S(2)}, u32[]{:S(2)}) collective-permute-start(bf16[384,128]{1,0:T(8,128)(2,1)} %get-tuple-element.24), channel_id=1, source_target_pairs={{0,8},{1,9},{2,10},{3,11},{4,12},{5,13},{6,14},{7,15},{8,0},{9,1},... | collective-permute-start | bytes 294920 | tf_op jit(solution)/shard_map/ppermute | solution.py:441
  11.9 2.3 %collective-permute-start.4 = (bf16[384,128]{1,0:T(8,128)(2,1)}, bf16[384,128]{1,0:T(8,128)(2,1)S(1)}, u32[]{:S(2)}, u32[]{:S(2)}) collective-permute-start(bf16[384,128]{1,0:T(8,128)(2,1)} %get-tuple-element.25), channel_id=1, source_target_pairs={{0,6},{1,7},{2,4},{3,5},{4,2},{5,3},{6,0},{7,1},{8,14},{9,15},{10,... | collective-permute-start | bytes 294920 | tf_op jit(solution)/shard_map/ppermute | solution.py:441
  14.2 0.0 collective-permute-done.refs_1_
  14.2 6.8 %collective-permute-start.5 = (bf16[384,128]{1,0:T(8,128)(2,1)}, bf16[384,128]{1,0:T(8,128)(2,1)S(1)}, u32[]{:S(2)}, u32[]{:S(2)}) collective-permute-start(bf16[384,128]{1,0:T(8,128)(2,1)} %get-tuple-element.26), channel_id=1, source_target_pairs={{0,4},{1,5},{2,6},{3,7},{4,0},{5,1},{6,2},{7,3},{8,12},{9,13},{10,... | collective-permute-start | bytes 294920 | tf_op jit(solution)/shard_map/ppermute | solution.py:441
  21.0 0.0 collective-permute-done.1.refs_2_
  21.0 1.0 %collective-permute-start.6 = (bf16[384,128]{1,0:T(8,128)(2,1)}, bf16[384,128]{1,0:T(8,128)(2,1)S(1)}, u32[]{:S(2)}, u32[]{:S(2)}) collective-permute-start(bf16[384,128]{1,0:T(8,128)(2,1)} %get-tuple-element.27), channel_id=1, source_target_pairs={{0,2},{1,3},{2,0},{3,1},{4,6},{5,7},{6,4},{7,5},{8,10},{9,11},{10,... | collective-permute-start | bytes 294920 | tf_op jit(solution)/shard_map/ppermute | solution.py:441
  21.9 2.8 %collective-permute-done.2.refs_3_ = bf16[384,128]{1,0:T(8,128)(2,1)S(1)} collective-permute-done((bf16[384,128]{1,0:T(8,128)(2,1)}, bf16[384,128]{1,0:T(8,128)(2,1)S(1)}, u32[]{:S(2)}, u32[]{:S(2)}) %collective-permute-start.2) | collective-permute-done | bytes 98336 | tf_op jit(solution)/shard_map/ppermute | solution.py:441
  24.7 0.0 collective-permute-start.7
  24.7 1.1 %collective-permute-done.3.refs_4_ = bf16[384,128]{1,0:T(8,128)(2,1)S(1)} collective-permute-done((bf16[384,128]{1,0:T(8,128)(2,1)}, bf16[384,128]{1,0:T(8,128)(2,1)S(1)}, u32[]{:S(2)}, u32[]{:S(2)}) %collective-permute-start.3) | collective-permute-done | bytes 98336 | tf_op jit(solution)/shard_map/ppermute | solution.py:441
  25.9 0.0 collective-permute-start.8
  25.9 0.0 collective-permute-done.4.refs_5_
  25.9 0.5 %collective-permute-start.9 = (bf16[384,128]{1,0:T(8,128)(2,1)S(1)}, bf16[384,128]{1,0:T(8,128)(2,1)S(1)}, u32[]{:S(2)}, u32[]{:S(2)}) collective-permute-start(bf16[384,128]{1,0:T(8,128)(2,1)S(1)} %collective-permute-done.1.refs_2_), channel_id=1, source_target_pairs={{0,1},{1,0},{2,3},{3,2},{4,5},{5,4},{6,7},{7,6},{8,9},{9,8},{10,11... | collective-permute-start | bytes 294920 | tf_op jit(solution)/shard_map/ppermute | solution.py:441
  26.4 0.4 collective-permute-done.5.refs_6_
  26.8 0.0 collective-permute-start.10
  26.8 0.0 collective-permute-done.6.refs_7_
  26.8 0.5 %collective-permute-start.11 = (bf16[384,128]{1,0:T(8,128)(2,1)S(1)}, bf16[384,128]{1,0:T(8,128)(2,1)S(1)}, u32[]{:S(2)}, u32[]{:S(2)}) collective-permute-start(bf16[384,128]{1,0:T(8,128)(2,1)S(1)} %collective-permute-done.3.refs_4_), channel_id=1, source_target_pairs={{0,1},{1,0},{2,3},{3,2},{4,5},{5,4},{6,7},{7,6},{8,9},{9,8},{10,11... | collective-permute-start | bytes 294920 | tf_op jit(solution)/shard_map/ppermute | solution.py:441
  27.4 0.0 collective-permute-done.7.refs_8_
  27.4 0.1 collective-permute-start.12
  27.4 0.0 collective-permute-done.8.refs_9_
  27.4 0.4 collective-permute-start.13
  27.9 0.0 collective-permute-done.9.refs_10_
  27.9 0.1 collective-permute-start.14
  29.9 0.0 collective-permute-done.10.refs_11_
  29.9 0.0 collective-permute-done.11.refs_12_
  29.9 0.0 collective-permute-done.12.refs_13_
  29.9 0.0 collective-permute-done.13.refs_14_
  29.9 0.0 collective-permute-done.14.refs_15_
  29.9 0.0 copy-start
  30.0 0.9 %copy-done = bf16[384,128]{1,0:T(8,128)(2,1)S(1)} copy-done((bf16[384,128]{1,0:T(8,128)(2,1)S(1)}, bf16[384,128]{1,0:T(8,128)(2,1)}, u32[]{:S(2)}) %copy-start) | copy-done | bytes 98328
  30.8 3.1 %shard_map.175 = (bf16[128,128]{1,0:T(8,128)(2,1)S(1)}, bf16[128,128]{1,0:T(8,128)(2,1)S(1)}, bf16[128,128]{1,0:T(8,128)(2,1)S(1)}, bf16[128,128]{1,0:T(8,128)(2...) custom-call(s32[1]{0:T(128)S(6)} %copy.19.video_len, ...), custom_call_target="tpu_custom_call" | custom-call | tf_op jit(solution)/shard_map/pallas_call | solution.py:480
  34.0 2.6 %collective-permute-start.15 = (bf16[128,128]{1,0:T(8,128)(2,1)S(1)}, bf16[128,128]{1,0:T(8,128)(2,1)S(1)}, u32[]{:S(2)}, u32[]{:S(2)}) collective-permute-start(bf16[128,128]{1,0:T(8,128)(2,1)S(1)} %get-tuple-element.29), channel_id=1, source_target_pairs={{0,14},{1,15},{2,12},{3,13},{4,10},{5,11},{6,8},{7,9},{8,6},{9,7},... | collective-permute-start | bytes 98312 | tf_op jit(solution)/shard_map/ppermute | solution.py:441
  36.5 1.3 %collective-permute-start.16 = (bf16[128,128]{1,0:T(8,128)(2,1)S(1)}, bf16[128,128]{1,0:T(8,128)(2,1)S(1)}, u32[]{:S(2)}, u32[]{:S(2)}) collective-permute-start(bf16[128,128]{1,0:T(8,128)(2,1)S(1)} %get-tuple-element.30), channel_id=1, source_target_pairs={{0,12},{1,13},{2,14},{3,15},{4,8},{5,9},{6,10},{7,11},{8,4},{9,5},... | collective-permute-start | bytes 98312 | tf_op jit(solution)/shard_map/ppermute | solution.py:441
  37.8 1.4 %collective-permute-start.17 = (bf16[128,128]{1,0:T(8,128)(2,1)S(1)}, bf16[128,128]{1,0:T(8,128)(2,1)S(1)}, u32[]{:S(2)}, u32[]{:S(2)}) collective-permute-start(bf16[128,128]{1,0:T(8,128)(2,1)S(1)} %get-tuple-element.31), channel_id=1, source_target_pairs={{0,10},{1,11},{2,8},{3,9},{4,14},{5,15},{6,12},{7,13},{8,2},{9,3},... | collective-permute-start | bytes 98312 | tf_op jit(solution)/shard_map/ppermute | solution.py:441
  39.2 2.5 %collective-permute-start.18 = (bf16[128,128]{1,0:T(8,128)(2,1)S(1)}, bf16[128,128]{1,0:T(8,128)(2,1)S(1)}, u32[]{:S(2)}, u32[]{:S(2)}) collective-permute-start(bf16[128,128]{1,0:T(8,128)(2,1)S(1)} %get-tuple-element.32), channel_id=1, source_target_pairs={{0,8},{1,9},{2,10},{3,11},{4,12},{5,13},{6,14},{7,15},{8,0},{9,1},... | collective-permute-start | bytes 98312 | tf_op jit(solution)/shard_map/ppermute | solution.py:441
  41.7 0.1 collective-permute-start.19
  41.8 0.0 collective-permute-done.15.refs_1_
  41.8 1.8 %collective-permute-start.20 = (bf16[128,128]{1,0:T(8,128)(2,1)S(1)}, bf16[128,128]{1,0:T(8,128)(2,1)S(1)}, u32[]{:S(2)}, u32[]{:S(2)}) collective-permute-start(bf16[128,128]{1,0:T(8,128)(2,1)S(1)} %get-tuple-element.34), channel_id=1, source_target_pairs={{0,4},{1,5},{2,6},{3,7},{4,0},{5,1},{6,2},{7,3},{8,12},{9,13},{10,... | collective-permute-start | bytes 98312 | tf_op jit(solution)/shard_map/ppermute | solution.py:441
  43.7 0.0 collective-permute-done.16.refs_2_
  43.7 1.5 %collective-permute-start.21 = (bf16[128,128]{1,0:T(8,128)(2,1)S(1)}, bf16[128,128]{1,0:T(8,128)(2,1)S(1)}, u32[]{:S(2)}, u32[]{:S(2)}) collective-permute-start(bf16[128,128]{1,0:T(8,128)(2,1)S(1)} %get-tuple-element.35), channel_id=1, source_target_pairs={{0,2},{1,3},{2,0},{3,1},{4,6},{5,7},{6,4},{7,5},{8,10},{9,11},{10,... | collective-permute-start | bytes 98312 | tf_op jit(solution)/shard_map/ppermute | solution.py:441
  45.2 0.0 collective-permute-done.17.refs_3_
  45.2 0.0 collective-permute-done.18.refs_4_
  45.2 1.3 %collective-permute-done.19.refs_5_ = bf16[128,128]{1,0:T(8,128)(2,1)S(1)} collective-permute-done((bf16[128,128]{1,0:T(8,128)(2,1)S(1)}, bf16[128,128]{1,0:T(8,128)(2,1)S(1)}, u32[]{:S(2)}, u32[]{:S(2)}) %collective-permute-start.19) | collective-permute-done | bytes 32800 | tf_op jit(solution)/shard_map/ppermute | solution.py:441
  46.5 0.0 collective-permute-done.20.refs_6_
  46.5 1.1 %collective-permute-done.21.refs_7_ = bf16[128,128]{1,0:T(8,128)(2,1)S(1)} collective-permute-done((bf16[128,128]{1,0:T(8,128)(2,1)S(1)}, bf16[128,128]{1,0:T(8,128)(2,1)S(1)}, u32[]{:S(2)}, u32[]{:S(2)}) %collective-permute-start.21) | collective-permute-done | bytes 32800 | tf_op jit(solution)/shard_map/ppermute | solution.py:441
  47.6 0.8 %shard_map.176 = (bf16[16,4096]{1,0:T(8,128)(2,1)}, bf16[8,2048]{1,0:T(8,128)(2,1)}, bf16[16,2048]{1,0:T(8,128)(2,1)}, bf16[8,2048]{1,0:T(8,128)(2,1)}) custom-call(bf16[128,128]{1,0:T(8,128)(2,1)S(1)} %get-tuple-element.28.refs_0_, bf16[128,128]{1,0:T(8,128)(2,1)S(1)} %collective-permute-done.15.refs_1_, ...), custom_call_target="tpu_custom_call" | custom-call | tf_op jit(solution)/shard_map/pallas_call | solution.py:492
Async XLA Ops:
  2.8 11.4 %collective-permute-start = (bf16[384,128]{1,0:T(8,128)(2,1)}, bf16[384,128]{1,0:T(8,128)(2,1)S(1)}, u32[]{:S(2)}, u32[]{:S(2)}) collective-permute-start(bf16[384,128]{1,0:T(8,128)(2,1)} %get-tuple-element.21), channel_id=1, source_target_pairs={{0,14},{1,15},{2,12},{3,13},{4,10},{5,11},{6,8},{7,9},{8,6},{9,7},... | collective-permute-start | bytes 294920 | tf_op jit(solution)/shard_map/ppermute | solution.py:441
  8.9 12.1 %collective-permute-start.1 = (bf16[384,128]{1,0:T(8,128)(2,1)}, bf16[384,128]{1,0:T(8,128)(2,1)S(1)}, u32[]{:S(2)}, u32[]{:S(2)}) collective-permute-start(bf16[384,128]{1,0:T(8,128)(2,1)} %get-tuple-element.22), channel_id=1, source_target_pairs={{0,12},{1,13},{2,14},{3,15},{4,8},{5,9},{6,10},{7,11},{8,4},{9,5},... | collective-permute-start | bytes 294920 | tf_op jit(solution)/shard_map/ppermute | solution.py:441
  9.1 15.6 %collective-permute-start.2 = (bf16[384,128]{1,0:T(8,128)(2,1)}, bf16[384,128]{1,0:T(8,128)(2,1)S(1)}, u32[]{:S(2)}, u32[]{:S(2)}) collective-permute-start(bf16[384,128]{1,0:T(8,128)(2,1)} %get-tuple-element.23), channel_id=1, source_target_pairs={{0,10},{1,11},{2,8},{3,9},{4,14},{5,15},{6,12},{7,13},{8,2},{9,3},... | collective-permute-start | bytes 294920 | tf_op jit(solution)/shard_map/ppermute | solution.py:441
  9.8 16.0 %collective-permute-start.3 = (bf16[384,128]{1,0:T(8,128)(2,1)}, bf16[384,128]{1,0:T(8,128)(2,1)S(1)}, u32[]{:S(2)}, u32[]{:S(2)}) collective-permute-start(bf16[384,128]{1,0:T(8,128)(2,1)} %get-tuple-element.24), channel_id=1, source_target_pairs={{0,8},{1,9},{2,10},{3,11},{4,12},{5,13},{6,14},{7,15},{8,0},{9,1},... | collective-permute-start | bytes 294920 | tf_op jit(solution)/shard_map/ppermute | solution.py:441
  11.9 14.0 %collective-permute-start.4 = (bf16[384,128]{1,0:T(8,128)(2,1)}, bf16[384,128]{1,0:T(8,128)(2,1)S(1)}, u32[]{:S(2)}, u32[]{:S(2)}) collective-permute-start(bf16[384,128]{1,0:T(8,128)(2,1)} %get-tuple-element.25), channel_id=1, source_target_pairs={{0,6},{1,7},{2,4},{3,5},{4,2},{5,3},{6,0},{7,1},{8,14},{9,15},{10,... | collective-permute-start | bytes 294920 | tf_op jit(solution)/shard_map/ppermute | solution.py:441
  14.2 12.7 %collective-permute-start.5 = (bf16[384,128]{1,0:T(8,128)(2,1)}, bf16[384,128]{1,0:T(8,128)(2,1)S(1)}, u32[]{:S(2)}, u32[]{:S(2)}) collective-permute-start(bf16[384,128]{1,0:T(8,128)(2,1)} %get-tuple-element.26), channel_id=1, source_target_pairs={{0,4},{1,5},{2,6},{3,7},{4,0},{5,1},{6,2},{7,3},{8,12},{9,13},{10,... | collective-permute-start | bytes 294920 | tf_op jit(solution)/shard_map/ppermute | solution.py:441
  21.0 5.9 %collective-permute-start.6 = (bf16[384,128]{1,0:T(8,128)(2,1)}, bf16[384,128]{1,0:T(8,128)(2,1)S(1)}, u32[]{:S(2)}, u32[]{:S(2)}) collective-permute-start(bf16[384,128]{1,0:T(8,128)(2,1)} %get-tuple-element.27), channel_id=1, source_target_pairs={{0,2},{1,3},{2,0},{3,1},{4,6},{5,7},{6,4},{7,5},{8,10},{9,11},{10,... | collective-permute-start | bytes 294920 | tf_op jit(solution)/shard_map/ppermute | solution.py:441
  24.7 2.6 %collective-permute-start.7 = (bf16[384,128]{1,0:T(8,128)(2,1)}, bf16[384,128]{1,0:T(8,128)(2,1)S(1)}, u32[]{:S(2)}, u32[]{:S(2)}) collective-permute-start(bf16[384,128]{1,0:T(8,128)(2,1)} %get-tuple-element.20.refs_0_), channel_id=1, source_target_pairs={{0,1},{1,0},{2,3},{3,2},{4,5},{5,4},{6,7},{7,6},{8,9},{9,8},{10,11... | collective-permute-start | bytes 294920 | tf_op jit(solution)/shard_map/ppermute | solution.py:441
  25.9 1.5 %collective-permute-start.8 = (bf16[384,128]{1,0:T(8,128)(2,1)S(1)}, bf16[384,128]{1,0:T(8,128)(2,1)S(1)}, u32[]{:S(2)}, u32[]{:S(2)}) collective-permute-start(bf16[384,128]{1,0:T(8,128)(2,1)S(1)} %collective-permute-done.refs_1_), channel_id=1, source_target_pairs={{0,1},{1,0},{2,3},{3,2},{4,5},{5,4},{6,7},{7,6},{8,9},{9,8},{10,11... | collective-permute-start | bytes 294920 | tf_op jit(solution)/shard_map/ppermute | solution.py:441
  25.9 2.0 %collective-permute-start.9 = (bf16[384,128]{1,0:T(8,128)(2,1)S(1)}, bf16[384,128]{1,0:T(8,128)(2,1)S(1)}, u32[]{:S(2)}, u32[]{:S(2)}) collective-permute-start(bf16[384,128]{1,0:T(8,128)(2,1)S(1)} %collective-permute-done.1.refs_2_), channel_id=1, source_target_pairs={{0,1},{1,0},{2,3},{3,2},{4,5},{5,4},{6,7},{7,6},{8,9},{9,8},{10,11... | collective-permute-start | bytes 294920 | tf_op jit(solution)/shard_map/ppermute | solution.py:441
  26.8 3.1 %collective-permute-start.10 = (bf16[384,128]{1,0:T(8,128)(2,1)S(1)}, bf16[384,128]{1,0:T(8,128)(2,1)S(1)}, u32[]{:S(2)}, u32[]{:S(2)}) collective-permute-start(bf16[384,128]{1,0:T(8,128)(2,1)S(1)} %collective-permute-done.2.refs_3_), channel_id=1, source_target_pairs={{0,1},{1,0},{2,3},{3,2},{4,5},{5,4},{6,7},{7,6},{8,9},{9,8},{10,11... | collective-permute-start | bytes 294920 | tf_op jit(solution)/shard_map/ppermute | solution.py:441
  26.8 3.1 %collective-permute-start.11 = (bf16[384,128]{1,0:T(8,128)(2,1)S(1)}, bf16[384,128]{1,0:T(8,128)(2,1)S(1)}, u32[]{:S(2)}, u32[]{:S(2)}) collective-permute-start(bf16[384,128]{1,0:T(8,128)(2,1)S(1)} %collective-permute-done.3.refs_4_), channel_id=1, source_target_pairs={{0,1},{1,0},{2,3},{3,2},{4,5},{5,4},{6,7},{7,6},{8,9},{9,8},{10,11... | collective-permute-start | bytes 294920 | tf_op jit(solution)/shard_map/ppermute | solution.py:441
  27.4 2.6 %collective-permute-start.12 = (bf16[384,128]{1,0:T(8,128)(2,1)S(1)}, bf16[384,128]{1,0:T(8,128)(2,1)S(1)}, u32[]{:S(2)}, u32[]{:S(2)}) collective-permute-start(bf16[384,128]{1,0:T(8,128)(2,1)S(1)} %collective-permute-done.4.refs_5_), channel_id=1, source_target_pairs={{0,1},{1,0},{2,3},{3,2},{4,5},{5,4},{6,7},{7,6},{8,9},{9,8},{10,11... | collective-permute-start | bytes 294920 | tf_op jit(solution)/shard_map/ppermute | solution.py:441
  27.4 2.5 %collective-permute-start.13 = (bf16[384,128]{1,0:T(8,128)(2,1)S(1)}, bf16[384,128]{1,0:T(8,128)(2,1)S(1)}, u32[]{:S(2)}, u32[]{:S(2)}) collective-permute-start(bf16[384,128]{1,0:T(8,128)(2,1)S(1)} %collective-permute-done.5.refs_6_), channel_id=1, source_target_pairs={{0,1},{1,0},{2,3},{3,2},{4,5},{5,4},{6,7},{7,6},{8,9},{9,8},{10,11... | collective-permute-start | bytes 294920 | tf_op jit(solution)/shard_map/ppermute | solution.py:441
  27.9 2.1 %collective-permute-start.14 = (bf16[384,128]{1,0:T(8,128)(2,1)S(1)}, bf16[384,128]{1,0:T(8,128)(2,1)S(1)}, u32[]{:S(2)}, u32[]{:S(2)}) collective-permute-start(bf16[384,128]{1,0:T(8,128)(2,1)S(1)} %collective-permute-done.6.refs_7_), channel_id=1, source_target_pairs={{0,1},{1,0},{2,3},{3,2},{4,5},{5,4},{6,7},{7,6},{8,9},{9,8},{10,11... | collective-permute-start | bytes 294920 | tf_op jit(solution)/shard_map/ppermute | solution.py:441
  29.9 0.9 %copy-start = (bf16[384,128]{1,0:T(8,128)(2,1)S(1)}, bf16[384,128]{1,0:T(8,128)(2,1)}, u32[]{:S(2)}) copy-start(bf16[384,128]{1,0:T(8,128)(2,1)} %get-tuple-element.20.refs_0_) | copy-start | bytes 294916
  34.0 7.9 %collective-permute-start.15 = (bf16[128,128]{1,0:T(8,128)(2,1)S(1)}, bf16[128,128]{1,0:T(8,128)(2,1)S(1)}, u32[]{:S(2)}, u32[]{:S(2)}) collective-permute-start(bf16[128,128]{1,0:T(8,128)(2,1)S(1)} %get-tuple-element.29), channel_id=1, source_target_pairs={{0,14},{1,15},{2,12},{3,13},{4,10},{5,11},{6,8},{7,9},{8,6},{9,7},... | collective-permute-start | bytes 98312 | tf_op jit(solution)/shard_map/ppermute | solution.py:441
  36.5 7.1 %collective-permute-start.16 = (bf16[128,128]{1,0:T(8,128)(2,1)S(1)}, bf16[128,128]{1,0:T(8,128)(2,1)S(1)}, u32[]{:S(2)}, u32[]{:S(2)}) collective-permute-start(bf16[128,128]{1,0:T(8,128)(2,1)S(1)} %get-tuple-element.30), channel_id=1, source_target_pairs={{0,12},{1,13},{2,14},{3,15},{4,8},{5,9},{6,10},{7,11},{8,4},{9,5},... | collective-permute-start | bytes 98312 | tf_op jit(solution)/shard_map/ppermute | solution.py:441
  37.8 7.4 %collective-permute-start.17 = (bf16[128,128]{1,0:T(8,128)(2,1)S(1)}, bf16[128,128]{1,0:T(8,128)(2,1)S(1)}, u32[]{:S(2)}, u32[]{:S(2)}) collective-permute-start(bf16[128,128]{1,0:T(8,128)(2,1)S(1)} %get-tuple-element.31), channel_id=1, source_target_pairs={{0,10},{1,11},{2,8},{3,9},{4,14},{5,15},{6,12},{7,13},{8,2},{9,3},... | collective-permute-start | bytes 98312 | tf_op jit(solution)/shard_map/ppermute | solution.py:441
  39.2 6.0 %collective-permute-start.18 = (bf16[128,128]{1,0:T(8,128)(2,1)S(1)}, bf16[128,128]{1,0:T(8,128)(2,1)S(1)}, u32[]{:S(2)}, u32[]{:S(2)}) collective-permute-start(bf16[128,128]{1,0:T(8,128)(2,1)S(1)} %get-tuple-element.32), channel_id=1, source_target_pairs={{0,8},{1,9},{2,10},{3,11},{4,12},{5,13},{6,14},{7,15},{8,0},{9,1},... | collective-permute-start | bytes 98312 | tf_op jit(solution)/shard_map/ppermute | solution.py:441
  41.7 4.8 %collective-permute-start.19 = (bf16[128,128]{1,0:T(8,128)(2,1)S(1)}, bf16[128,128]{1,0:T(8,128)(2,1)S(1)}, u32[]{:S(2)}, u32[]{:S(2)}) collective-permute-start(bf16[128,128]{1,0:T(8,128)(2,1)S(1)} %get-tuple-element.33), channel_id=1, source_target_pairs={{0,6},{1,7},{2,4},{3,5},{4,2},{5,3},{6,0},{7,1},{8,14},{9,15},{10,... | collective-permute-start | bytes 98312 | tf_op jit(solution)/shard_map/ppermute | solution.py:441
  41.8 4.7 %collective-permute-start.20 = (bf16[128,128]{1,0:T(8,128)(2,1)S(1)}, bf16[128,128]{1,0:T(8,128)(2,1)S(1)}, u32[]{:S(2)}, u32[]{:S(2)}) collective-permute-start(bf16[128,128]{1,0:T(8,128)(2,1)S(1)} %get-tuple-element.34), channel_id=1, source_target_pairs={{0,4},{1,5},{2,6},{3,7},{4,0},{5,1},{6,2},{7,3},{8,12},{9,13},{10,... | collective-permute-start | bytes 98312 | tf_op jit(solution)/shard_map/ppermute | solution.py:441
  43.7 3.9 %collective-permute-start.21 = (bf16[128,128]{1,0:T(8,128)(2,1)S(1)}, bf16[128,128]{1,0:T(8,128)(2,1)S(1)}, u32[]{:S(2)}, u32[]{:S(2)}) collective-permute-start(bf16[128,128]{1,0:T(8,128)(2,1)S(1)} %get-tuple-element.35), channel_id=1, source_target_pairs={{0,2},{1,3},{2,0},{3,1},{4,6},{5,7},{6,4},{7,5},{8,10},{9,11},{10,... | collective-permute-start | bytes 98312 | tf_op jit(solution)/shard_map/ppermute | solution.py:441

commit v5 on v2

--- a/solution.py
+++ b/solution.py
@@ -279,32 +279,34 @@
 LANES = 128
 
 
-def pack_kernel(n, *refs):
-    sources, packed, held, arrived = refs[0:12], refs[12], refs[13:25], refs[25]
+def fetch(sources, held, arrived):
     copies = [
         pltpu.make_async_copy(source, slot, arrived.at[i])
         for i, (source, slot) in enumerate(zip(sources, held))
     ]
     for copy in copies:
         copy.start()
-    video, cross, audio = held[0:3], held[3:6], held[6:12]
-    parts = video[0].shape[1] // n // LANES
+    return copies
+
+
+def by_step(items):
+    return [items[-j % len(items)] for j in range(len(items))]
+
+
+def pack_small(n, *refs):
+    sources, packed, held, arrived = refs[:9], refs[9], refs[10:19], refs[19]
+    copies = fetch(sources, held, arrived)
+    cross, audio = held[:3], held[3:]
     rows = cross[0].shape[0]
     at = 0
-    for i, ref in enumerate(video):
+    for i, ref in enumerate(cross):
         copies[i].wait()
-        for part in range(parts):
-            for d in range(n):
-                packed[d, at : at + rows, :] = ref[:, (d * parts + part) * LANES : (d * parts + part + 1) * LANES]
-            at += rows
-    for i, ref in enumerate(cross):
-        copies[3 + i].wait()
         for d in range(n):
             packed[d, at : at + rows, :] = ref[:, d * LANES : (d + 1) * LANES]
         at += rows
     for i in range(0, 6, 2):
-        copies[6 + i].wait()
-        copies[7 + i].wait()
+        copies[3 + i].wait()
+        copies[4 + i].wait()
         for d in range(n):
             pair = jnp.concatenate(
                 [
@@ -313,8 +315,33 @@
                 ],
                 axis=0,
             )
-            packed[d, at : at + pair.shape[0], :] = pair
+            packed[d, at : at + rows, :] = pair
         at += rows
+
+
+def pack_video(chips, *refs):
+    sources, refs = refs[:3], refs[4:]
+    packed, held, arrived = by_step(refs[:chips]), refs[chips : chips + 3], refs[chips + 3]
+    copies = fetch(sources, held, arrived)
+    chip = lax.axis_index("seq") // 2
+    side = chips // 2
+    rows, width = held[0].shape[0], held[0].shape[1] // side
+    tiles = width // LANES
+    for i, ref in enumerate(held):
+        copies[i].wait()
+        for t in range(tiles):
+            for j in range(chips):
+                if j >= side and i == 0:
+                    continue
+                at = ((i if j < side else i - 1) * tiles + t) * rows
+                column = pl.multiple_of(((chip ^ j) % side) * width + t * LANES, LANES)
+                packed[j][at : at + rows, :] = ref[:, pl.ds(column, LANES)]
+
+
+def keep_kernel(source, kept, arrived):
+    copy = pltpu.make_async_copy(source, kept, arrived)
+    copy.start()
+    copy.wait()
 
 
 def softmax_mix(query, key, value, scale, permit):
@@ -340,12 +367,42 @@
     return result
 
 
-def attend_kernel(n, rows, parts, video_len, audio_len, shift, got, done):
+def attend_video(chips, tiles, video_len, *refs):
+    side = chips // 2
+    own, other = by_step(refs[:chips]), by_step(refs[chips : 2 * chips])
+    done = by_step(refs[2 * chips : 2 * chips + side])
+    length, arrived = refs[2 * chips + side :]
+    copy = pltpu.make_async_copy(video_len, length, arrived)
+    copy.start()
+    rows = own[0].shape[0] // (3 * tiles)
+    me = lax.axis_index("seq")
+    slot = lax.broadcasted_iota(jnp.int32, (side * rows, 2 * chips * rows), 1)
+    k_at = slot ^ (me * rows)
+    copy.wait()
+    permit = k_at < length[0]
+
+    def gather(kind, t):
+        pieces = []
+        for j in range(chips):
+            at = ((kind if j < side else kind - 1) * tiles + t) * rows
+            pieces += [own[j][at : at + rows, :], other[j][at : at + rows, :]]
+        return jnp.concatenate(pieces, axis=0)
+
+    for t in range(tiles):
+        query = jnp.concatenate([own[j][t * rows : (t + 1) * rows, :] for j in range(side)], axis=0)
+        mixed = softmax_mix(query, gather(1, t), gather(2, t), 1.0 / math.sqrt(HDV), permit)
+        for j in range(side):
+            done[j][t * rows : (t + 1) * rows, :] = mixed[j * rows : (j + 1) * rows].astype(
+                jnp.bfloat16
+            )
+
+
+def attend_small(n, rows, video_len, audio_len, shift, got, done, *scratch):
+    copies = fetch((video_len, audio_len, shift), scratch[:3], scratch[3])
     half = rows // 2
     tv, ta = n * rows, n * half
     ratio = tv // ta
     bits = ratio.bit_length() - 1
-    video_valid, audio_valid, offset = video_len[0], audio_len[0], shift[0]
 
     def slab(at):
         return got[:, at : at + rows, :].reshape(tv, LANES)
@@ -362,30 +419,19 @@
             lax.broadcasted_iota(jnp.int32, (q_count, k_count), 1),
         )
 
-    q_at, k_at = places(tv, tv)
-    permit = k_at < video_valid
-    for h in range(parts):
-        mixed = softmax_mix(
-            slab(h * rows),
-            slab((parts + h) * rows),
-            slab((2 * parts + h) * rows),
-            1.0 / math.sqrt(HDV),
-            permit,
-        )
-        done[:, h * rows : (h + 1) * rows, :] = mixed.astype(jnp.bfloat16).reshape(n, rows, LANES)
-    at = 3 * parts * rows
-    cross_query, cross_keys, cross_values = slab(at), slab(at + rows), slab(at + 2 * rows)
-    at += 3 * rows
-    audio_query, audio_keys = halves(at)
-    audio_values, listen_query = halves(at + rows)
-    sound_keys, sound_values = halves(at + 2 * rows)
+    cross_query, cross_keys, cross_values = slab(0), slab(rows), slab(2 * rows)
+    audio_query, audio_keys = halves(3 * rows)
+    audio_values, listen_query = halves(4 * rows)
+    sound_keys, sound_values = halves(5 * rows)
+    for copy in copies:
+        copy.wait()
+    video_valid, audio_valid, offset = (ref[0] for ref in scratch[:3])
 
     q_at, k_at = places(tv, ta)
     center = jnp.clip((q_at >> bits) + offset, 0, audio_valid - 1)
     permit = (k_at < audio_valid) & (jnp.abs(k_at - center) <= 5 * ta // 8)
     mixed = paired_mix(cross_query, sound_keys, sound_values, HDA, permit)
-    out = parts * rows
-    done[:, out : out + rows, :] = mixed.astype(jnp.bfloat16).reshape(n, rows, LANES)
+    done[:, :rows, :] = mixed.astype(jnp.bfloat16).reshape(n, rows, LANES)
 
     q_at, k_at = places(ta, ta)
     heard = paired_mix(audio_query, audio_keys, audio_values, HDA, k_at < audio_valid)
@@ -396,24 +442,31 @@
     both = jnp.concatenate(
         [heard.reshape(n, half, LANES), listened.reshape(n, half, LANES)], axis=1
     )
-    out += rows
-    done[:, out : out + rows, :] = both.astype(jnp.bfloat16)
-
-
-def unpack_kernel(n, back, video_mixed, audio_mixed, video_cross, audio_cross):
-    rows = video_mixed.shape[0]
-    half = audio_mixed.shape[0]
-    parts = video_mixed.shape[1] // n // LANES
+    done[:, rows:, :] = both.astype(jnp.bfloat16)
+
+
+def unpack_small(n, back, audio_mixed, video_cross, audio_cross):
+    rows, half = video_cross.shape[0], audio_mixed.shape[0]
     for s in range(n):
-        for h in range(parts):
-            at = (s * parts + h) * LANES
-            video_mixed[:, at : at + LANES] = back[s, h * rows : (h + 1) * rows, :]
         at = s * LANES
-        out = parts * rows
-        video_cross[:, at : at + LANES] = back[s, out : out + rows, :]
-        both = back[s, out + rows : out + 2 * rows, :]
+        video_cross[:, at : at + LANES] = back[s, :rows, :]
+        both = back[s, rows:, :]
         audio_mixed[:, at : at + LANES] = both[:half, :]
         audio_cross[:, at : at + LANES] = both[half:, :]
+
+
+def unpack_video(side, *refs):
+    back, video_mixed = by_step(refs[:side]), refs[side]
+    rows, width = video_mixed.shape[0], video_mixed.shape[1] // side
+    chip = lax.axis_index("seq") // 2
+    for j in range(side):
+        for t in range(width // LANES):
+            column = pl.multiple_of(((chip ^ j) % side) * width + t * LANES, LANES)
+            video_mixed[:, pl.ds(column, LANES)] = back[j][t * rows : (t + 1) * rows, :]
+
+
+def swap(piece, n, step):
+    return lax.ppermute(piece, "seq", [(i, i ^ step) for i in range(n)])
 
 
 def shards_packed(*arrays):
@@ -425,61 +478,117 @@
         video_length, audio_length, align_offset,
     ) = arrays
     n = lax.axis_size("seq")
-    rows, half = video_query.shape[0], audio_query.shape[0]
-    parts = video_query.shape[1] // n // LANES
+    chips, side = n // 2, n // 4
+    rows = video_query.shape[0]
+    tiles = video_query.shape[1] // side // LANES
     vmem = pl.BlockSpec(memory_space=pltpu.VMEM)
-    smem = pl.BlockSpec(memory_space=pltpu.SMEM)
+    hbm = pl.BlockSpec(memory_space=pltpu.HBM)
     params = pltpu.CompilerParams(vmem_limit_bytes=32 * 1024 * 1024)
-    in_rows = (3 * parts + 6) * rows
-    out_rows = (parts + 2) * rows
-    sources = (
-        video_query, video_keys, video_values,
+    first = pltpu.CompilerParams(vmem_limit_bytes=60 * 1024 * 1024)
+    one = pltpu.SMEM((1,), jnp.int32)
+
+    def buffer(*shape):
+        return jax.ShapeDtypeStruct(shape, jnp.bfloat16)
+
+    def staging(sources):
+        return [pltpu.VMEM(source.shape, source.dtype) for source in sources] + [
+            pltpu.SemaphoreType.DMA((len(sources),))
+        ]
+
+    small = (
         cross_video_query, cross_video_keys, cross_video_values,
         audio_query, audio_keys, audio_values,
         cross_audio_query, cross_audio_keys, cross_audio_values,
     )
+    packed_small = pl.pallas_call(
+        functools.partial(pack_small, n),
+        out_shape=buffer(n, 6 * rows, LANES),
+        in_specs=[hbm] * 9,
+        out_specs=vmem,
+        scratch_shapes=staging(small),
+        compiler_params=first,
+    )(*small)
+    got = lax.all_to_all(packed_small, "seq", split_axis=0, concat_axis=0, tiled=True)
+
+    video = (video_query, video_keys, video_values)
     packed = pl.pallas_call(
-        functools.partial(pack_kernel, n),
-        out_shape=jax.ShapeDtypeStruct((n, in_rows, LANES), jnp.bfloat16),
-        in_specs=[pl.BlockSpec(memory_space=pltpu.HBM)] * 12,
+        functools.partial(pack_video, chips),
+        out_shape=by_step(
+            [buffer((3 if j < side else 2) * tiles * rows, LANES) for j in range(chips)]
+        ),
+        in_specs=[hbm] * 4,
+        out_specs=[vmem] * chips,
+        scratch_shapes=staging(video),
+        compiler_params=first,
+    )(*video, packed_small)
+    packed = by_step(packed)
+    moved = [swap(packed[j], n, 2 * j) for j in range(1, chips)]
+    kept = pl.pallas_call(
+        keep_kernel,
+        out_shape=packed[0],
+        in_specs=[hbm],
         out_specs=vmem,
-        scratch_shapes=[pltpu.VMEM(source.shape, source.dtype) for source in sources]
-        + [pltpu.SemaphoreType.DMA((12,))],
-        compiler_params=pltpu.CompilerParams(vmem_limit_bytes=60 * 1024 * 1024),
-    )(*sources)
-    got = lax.all_to_all(packed, "seq", split_axis=0, concat_axis=0, tiled=True)
-    done = pl.pallas_call(
-        functools.partial(attend_kernel, n, rows, parts),
-        out_shape=jax.ShapeDtypeStruct((n, out_rows, LANES), jnp.bfloat16),
-        in_specs=[smem] * 3 + [vmem],
+        scratch_shapes=[pltpu.SemaphoreType.DMA],
+        compiler_params=params,
+    )(packed[0])
+    own = [kept] + moved
+    other = [swap(piece, n, 1) for piece in packed[:1] + moved]
+
+    done_small = pl.pallas_call(
+        functools.partial(attend_small, n, rows),
+        out_shape=buffer(n, 2 * rows, LANES),
+        in_specs=[hbm] * 3 + [vmem],
+        out_specs=vmem,
+        scratch_shapes=[one] * 3 + [pltpu.SemaphoreType.DMA((3,))],
+        compiler_params=params,
+    )(video_length, audio_length, align_offset, got)
+    back_small = lax.all_to_all(done_small, "seq", split_axis=0, concat_axis=0, tiled=True)
+
+    done = by_step(
+        pl.pallas_call(
+            functools.partial(attend_video, chips, tiles),
+            out_shape=[buffer(tiles * rows, LANES)] * side,
+            in_specs=[hbm] + [vmem] * (2 * chips),
+            out_specs=[vmem] * side,
+            scratch_shapes=[one, pltpu.SemaphoreType.DMA],
+            compiler_params=params,
+        )(video_length, *by_step(own), *by_step(other))
+    )
+    back = done[:1] + [swap(done[j], n, 2 * j) for j in range(1, side)]
+    audio_mixed, video_cross, audio_cross = pl.pallas_call(
+        functools.partial(unpack_small, n),
+        out_shape=(
+            buffer(*audio_query.shape),
+            buffer(*cross_video_query.shape),
+            buffer(*cross_audio_query.shape),
+        ),
+        in_specs=[vmem],
+        out_specs=(vmem,) * 3,
+        compiler_params=params,
+    )(back_small)
+    video_mixed = pl.pallas_call(
+        functools.partial(unpack_video, side),
+        out_shape=buffer(*video_query.shape),
+        in_specs=[vmem] * side,
         out_specs=vmem,
         compiler_params=params,
-    )(video_length, audio_length, align_offset, got)
-    back = lax.all_to_all(done, "seq", split_axis=0, concat_axis=0, tiled=True)
-    return pl.pallas_call(
-        functools.partial(unpack_kernel, n),
-        out_shape=(
-            jax.ShapeDtypeStruct(video_query.shape, jnp.bfloat16),
-            jax.ShapeDtypeStruct(audio_query.shape, jnp.bfloat16),
-            jax.ShapeDtypeStruct(cross_video_query.shape, jnp.bfloat16),
-            jax.ShapeDtypeStruct(cross_audio_query.shape, jnp.bfloat16),
-        ),
-        in_specs=[vmem],
-        out_specs=(vmem,) * 4,
-        compiler_params=params,
-    )(back)
+    )(*by_step(back))
+    return (video_mixed, audio_mixed, video_cross, audio_cross)
 
 
 def shards(*arrays):
     n = lax.axis_size("seq")
     rows, half = arrays[0].shape[0], arrays[3].shape[0]
     fits = (
-        arrays[0].shape[1] % (n * LANES) == 0
+        n % 4 == 0
+        and n & (n - 1) == 0
+        and arrays[0].shape[1] % (n // 4 * LANES) == 0
         and arrays[3].shape[1] == n * LANES
         and HDV == LANES
         and LANES % HDA == 0
         and rows == 2 * half
         and half % 8 == 0
+        and half & (half - 1) == 0
     )
     return shards_packed(*arrays) if fits else shards_general(*arrays)
 

time: 46.6 us -> 56.8 us (1.22)
  starting transfers between devices: 7.4 us -> 35.1 us
  blocking collectives: 15.3 us -> 0 us
  waiting for transfers between devices: 16.8 us -> 8.25 us
  Pallas kernels: 4.19 us -> 10.3 us
    ppermute x0 -> x18, starting transfers between devices: none -> 20.9 us  [swap(): return lax.ppermute(piece, 'seq', [(i, i ^ step) for i in range(n)])]
    all_to_all x1 -> x2, waiting for transfers between devices: 16.8 us -> 0.01 us  [the longest x1 0.01 us: shards_packed(): lax.all_to_all(done_small, 'seq', split_axis=0, concat_axis=0, tiled=True)]
    all_to_all x1 -> x0, blocking collectives: 15.3 us -> none  [shards_packed(): back = lax.all_to_all(done, 'seq', split_axis=0, concat_axis=0, tiled=True)]
    ppermute x0 -> x18, waiting for transfers between devices: none -> 8.25 us  [swap(): return lax.ppermute(piece, 'seq', [(i, i ^ step) for i in range(n)])]
    all_to_all x1 -> x2, starting transfers between devices: 7.4 us -> 14.2 us  [the longest x1 7.4 us: shards_packed(): lax.all_to_all(packed_small, 'seq', split_axis=0, concat_axis=0, tiled=True)]
    pallas_call x3 -> x7, Pallas kernels: 4.19 us -> 10.3 us  [the longest x1 2.6 us: shards_packed(): pl.pallas_call(functools.partial(attend_video, chips, tiles), out_shape=[...]
  transfers between devices with their start and end apart: 1 -> 20, of which waited for: 1 -> 7; matrix products, arithmetic and copies ran while one was open for 0% -> 0% of each run, Pallas kernels for 0% -> 14%
where the time goes in v5:
time: 56.8 us; the launch traced here: 56.4 us
  starting transfers between devices  35.1 us (62%)
  Pallas kernels  10.3 us (18%)
  waiting for transfers between devices  8.25 us (15%)
  between operations  2.71 us (5%)
    ppermute x18, starting transfers between devices, swap(): return lax.ppermute(piece, 'seq', [(i, i ^ step) for i in range(n)])  20.9 us
    ppermute x18, waiting for transfers between devices, swap(): return lax.ppermute(piece, 'seq', [(i, i ^ step) for i in range(n)])  8.25 us
    all_to_all x1, starting transfers between devices, shards_packed(): lax.all_to_all(packed_small, 'seq', split_axis=0, concat_axis=0, tiled=True)  7.4 us
    all_to_all x1, starting transfers between devices, shards_packed(): lax.all_to_all(done_small, 'seq', split_axis=0, concat_axis=0, tiled=True)  6.78 us
    pallas_call x1, Pallas kernels, shards_packed(): pl.pallas_call(functools.partial(attend_video, chips, tiles), out_shape=[...  2.6 us
    pallas_call x1, Pallas kernels, shards_packed(): pl.pallas_call(functools.partial(attend_small, n, rows), out_shape=buffer...  2.43 us
    pallas_call x1, Pallas kernels, shards_packed(): pl.pallas_call(functools.partial(pack_video, chips), out_shape=by_step([b...  1.96 us
    pallas_call x1, Pallas kernels, shards_packed(): pl.pallas_call(functools.partial(pack_small, n), out_shape=buffer(n, 6 *...  1.8 us
  transfers between devices with their start and end apart: 20, of which 7 were waited for; matrix products, arithmetic and copies ran while one was open for 0% of the time, Pallas kernels for 14%

profile of v5, /device:TPU:0, one launch (start us, length us, event | category | flops | bytes accessed | tf_op | source)
XLA Modules:
  0.0 56.4 jit_solution(4647121292534585067)
XLA Ops:
  0.6 1.8 %shard_map.174.refs_3_ = bf16[16,96,128]{2,1,0:T(8,128)(2,1)} custom-call(bf16[16,2048]{1,0:T(8,128)(2,1)} %refs_0_.2, bf16[16,2048]{1,0:T(8,128)(2,1)} %refs_1_.2, bf16[16,2048]{1,0:T(8,128)(2,1)} %refs_2_.2, bf16[8,2048]{1,0:T(8,128)(2,1)} %refs_3_.1, bf16[8,2048]{1,0:T(8,128)(2,1)} %refs_4_.1, bf16[8,2048]{1,0:T(8,128)(2,1)} %refs_5_.1, ...), custom_call_target="tpu_custom_call" | custom-call | tf_op jit(solution)/shard_map/pallas_call | solution.py:503
  2.4 7.4 %all-to-all-start = ((bf16[16,96,128]{2,1,0:T(8,128)(2,1)}), bf16[16,96,128]{2,1,0:T(8,128)(2,1)S(1)}, u32[]{:S(2)}, u32[]{:S(2)}) async-start(bf16[16,96,128]{2,1,0:T(8,128)(2,1)} %shard_map.174.refs_3_), calls=%async_computation | async-start | bytes 786432 | tf_op jit(solution)/shard_map/all_to_all | solution.py:511
  9.8 2.0 %shard_map.175 = (bf16[384,128]{1,0:T(8,128)(2,1)}, bf16[256,128]{1,0:T(8,128)(2,1)}, bf16[256,128]{1,0:T(8,128)(2,1)}, bf16[256,128]{1,0:T(8,128)(2,1)}, bf16[2...) custom-call(bf16[16,4096]{1,0:T(8,128)(2,1)} %refs_0_.3, ...), custom_call_target="tpu_custom_call" | custom-call | tf_op jit(solution)/shard_map/pallas_call | solution.py:514
  11.8 4.7 %collective-permute-start = (bf16[256,128]{1,0:T(8,128)(2,1)}, bf16[256,128]{1,0:T(8,128)(2,1)S(1)}, u32[]{:S(2)}, u32[]{:S(2)}) collective-permute-start(bf16[256,128]{1,0:T(8,128)(2,1)} %get-tuple-element.20), channel_id=1, source_target_pairs={{0,14},{1,15},{2,12},{3,13},{4,10},{5,11},{6,8},{7,9},{8,6},{9,7},... | collective-permute-start | bytes 196616 | tf_op jit(solution)/shard_map/ppermute | solution.py:469
  16.5 0.6 collective-permute-start.1
  17.1 0.6 %collective-permute-start.2 = (bf16[256,128]{1,0:T(8,128)(2,1)}, bf16[256,128]{1,0:T(8,128)(2,1)S(1)}, u32[]{:S(2)}, u32[]{:S(2)}) collective-permute-start(bf16[256,128]{1,0:T(8,128)(2,1)} %get-tuple-element.22), channel_id=1, source_target_pairs={{0,10},{1,11},{2,8},{3,9},{4,14},{5,15},{6,12},{7,13},{8,2},{9,3},... | collective-permute-start | bytes 196616 | tf_op jit(solution)/shard_map/ppermute | solution.py:469
  17.6 4.2 %collective-permute-start.4 = (bf16[384,128]{1,0:T(8,128)(2,1)}, bf16[384,128]{1,0:T(8,128)(2,1)S(1)}, u32[]{:S(2)}, u32[]{:S(2)}) collective-permute-start(bf16[384,128]{1,0:T(8,128)(2,1)} %get-tuple-element.24), channel_id=1, source_target_pairs={{0,6},{1,7},{2,4},{3,5},{4,2},{5,3},{6,0},{7,1},{8,14},{9,15},{10,... | collective-permute-start | bytes 294920 | tf_op jit(solution)/shard_map/ppermute | solution.py:469
  23.7 0.0 all-to-all-done.got
  23.7 0.0 copy-start.2
  23.8 2.4 %shard_map.179 = bf16[16,32,128]{2,1,0:T(8,128)(2,1)} custom-call(s32[1]{0:T(128)S(6)} %copy.19.video_len, s32[1]{0:T(128)S(6)} %copy.20.audio_len, s32[1]{0:T(128)S(6)} %copy.21.shift, bf16[16,96,128]{2,1,0:T(8,128)(2,1)S(1)} %all-to-all-done.got), custom_call_target="tpu_custom_call" | custom-call | tf_op jit(solution)/shard_map/pallas_call | solution.py:537
  26.2 0.0 copy-start.3
  26.2 0.0 copy-start.1
  26.2 0.0 copy-start
  26.2 6.8 %all-to-all-start.1 = ((bf16[16,32,128]{2,1,0:T(8,128)(2,1)}), bf16[16,32,128]{2,1,0:T(8,128)(2,1)S(1)}, u32[]{:S(2)}, u32[]{:S(2)}) async-start(bf16[16,32,128]{2,1,0:T(8,128)(2,1)} %shard_map.179), calls=%async_computation.1 | async-start | bytes 262144 | tf_op jit(solution)/shard_map/all_to_all | solution.py:545
  33.0 0.0 copy-done.3
  33.0 2.9 %collective-permute-start.3 = (bf16[256,128]{1,0:T(8,128)(2,1)S(1)}, bf16[256,128]{1,0:T(8,128)(2,1)S(1)}, u32[]{:S(2)}, u32[]{:S(2)}) collective-permute-start(bf16[256,128]{1,0:T(8,128)(2,1)S(1)} %copy-done.3), channel_id=1, source_target_pairs={{0,8},{1,9},{2,10},{3,11},{4,12},{5,13},{6,14},{7,15},{8,0},{9,1},... | collective-permute-start | bytes 196616 | tf_op jit(solution)/shard_map/ppermute | solution.py:469
  35.9 0.0 collective-permute-done.refs_1_
  35.9 0.0 copy-done.2
  35.9 1.5 %collective-permute-start.5 = (bf16[384,128]{1,0:T(8,128)(2,1)S(1)}, bf16[384,128]{1,0:T(8,128)(2,1)S(1)}, u32[]{:S(2)}, u32[]{:S(2)}) collective-permute-start(bf16[384,128]{1,0:T(8,128)(2,1)S(1)} %copy-done.2), channel_id=1, source_target_pairs={{0,4},{1,5},{2,6},{3,7},{4,0},{5,1},{6,2},{7,3},{8,12},{9,13},{10,... | collective-permute-start | bytes 294920 | tf_op jit(solution)/shard_map/ppermute | solution.py:469
  37.4 0.0 collective-permute-done.1.refs_2_
  37.4 0.0 copy-done.1
  37.4 1.5 %collective-permute-start.6 = (bf16[384,128]{1,0:T(8,128)(2,1)S(1)}, bf16[384,128]{1,0:T(8,128)(2,1)S(1)}, u32[]{:S(2)}, u32[]{:S(2)}) collective-permute-start(bf16[384,128]{1,0:T(8,128)(2,1)S(1)} %copy-done.1), channel_id=1, source_target_pairs={{0,2},{1,3},{2,0},{3,1},{4,6},{5,7},{6,4},{7,5},{8,10},{9,11},{10,... | collective-permute-start | bytes 294920 | tf_op jit(solution)/shard_map/ppermute | solution.py:469
  38.9 0.0 collective-permute-done.2.refs_3_
  38.9 0.0 copy-done
  38.9 0.0 collective-permute-start.7
  38.9 3.8 %collective-permute-done.3.refs_4_ = bf16[256,128]{1,0:T(8,128)(2,1)S(1)} collective-permute-done((bf16[256,128]{1,0:T(8,128)(2,1)S(1)}, bf16[256,128]{1,0:T(8,128)(2,1)S(1)}, u32[]{:S(2)}, u32[]{:S(2)}) %collective-permute-start.3) | collective-permute-done | bytes 65568 | tf_op jit(solution)/shard_map/ppermute | solution.py:469
  42.7 0.0 collective-permute-start.8
  42.7 0.0 collective-permute-done.4.refs_5_
  42.7 0.5 collective-permute-start.9
  43.2 0.0 collective-permute-done.5.refs_6_
  43.2 0.1 collective-permute-start.12
  43.2 0.0 collective-permute-done.6.refs_7_
  43.2 0.4 collective-permute-start.13
  43.7 0.0 collective-permute-done.7.refs_8_
  43.7 0.1 collective-permute-start.14
  43.8 0.1 collective-permute-done.8.refs_9_
  43.9 0.3 collective-permute-start.10
  44.2 0.0 collective-permute-done.9.refs_10_
  44.2 0.2 collective-permute-start.11
  44.4 0.1 shard_map.176.refs_0_
  44.5 0.6 %collective-permute-done.10.refs_11_ = bf16[256,128]{1,0:T(8,128)(2,1)S(1)} collective-permute-done((bf16[256,128]{1,0:T(8,128)(2,1)S(1)}, bf16[256,128]{1,0:T(8,128)(2,1)S(1)}, u32[]{:S(2)}, u32[]{:S(2)}) %collective-permute-start.10) | collective-permute-done | bytes 65568 | tf_op jit(solution)/shard_map/ppermute | solution.py:469
  45.2 0.3 collective-permute-done.11.refs_12_
  45.5 0.0 collective-permute-done.12.refs_13_
  45.5 0.0 collective-permute-done.13.refs_14_
  45.5 0.0 collective-permute-done.14.refs_15_
  45.5 2.6 %shard_map.177 = (bf16[128,128]{1,0:T(8,128)(2,1)S(1)}, bf16[128,128]{1,0:T(8,128)(2,1)S(1)}, bf16[128,128]{1,0:T(8,128)(2,1)S(1)}, bf16[128,128]{1,0:T(8,128)(2,1)S(1)}) custom-call(s32[1]{0:T(128)S(6)} %copy.19.video_len, bf16[384,128]{1,0:T(8,128)(2,1)S(1)} %shard_map.176.refs_0_, bf16[256,128]{1,0:T(8,128)(2,1)S(1)} %collective-permute-done.refs_1_, ...), custom_call_target="tpu_custom_call" | custom-call | tf_op jit(solution)/shard_map/pallas_call | solution.py:548
  48.1 0.8 %collective-permute-start.15 = (bf16[128,128]{1,0:T(8,128)(2,1)S(1)}, bf16[128,128]{1,0:T(8,128)(2,1)S(1)}, u32[]{:S(2)}, u32[]{:S(2)}) collective-permute-start(bf16[128,128]{1,0:T(8,128)(2,1)S(1)} %get-tuple-element.28), channel_id=1, source_target_pairs={{0,6},{1,7},{2,4},{3,5},{4,2},{5,3},{6,0},{7,1},{8,14},{9,15},{10,... | collective-permute-start | bytes 98312 | tf_op jit(solution)/shard_map/ppermute | solution.py:469
  48.9 2.2 %collective-permute-start.16 = (bf16[128,128]{1,0:T(8,128)(2,1)S(1)}, bf16[128,128]{1,0:T(8,128)(2,1)S(1)}, u32[]{:S(2)}, u32[]{:S(2)}) collective-permute-start(bf16[128,128]{1,0:T(8,128)(2,1)S(1)} %get-tuple-element.29), channel_id=1, source_target_pairs={{0,4},{1,5},{2,6},{3,7},{4,0},{5,1},{6,2},{7,3},{8,12},{9,13},{10,... | collective-permute-start | bytes 98312 | tf_op jit(solution)/shard_map/ppermute | solution.py:469
  51.1 0.6 %collective-permute-start.17 = (bf16[128,128]{1,0:T(8,128)(2,1)S(1)}, bf16[128,128]{1,0:T(8,128)(2,1)S(1)}, u32[]{:S(2)}, u32[]{:S(2)}) collective-permute-start(bf16[128,128]{1,0:T(8,128)(2,1)S(1)} %get-tuple-element.30), channel_id=1, source_target_pairs={{0,2},{1,3},{2,0},{3,1},{4,6},{5,7},{6,4},{7,5},{8,10},{9,11},{10,... | collective-permute-start | bytes 98312 | tf_op jit(solution)/shard_map/ppermute | solution.py:469
  51.6 1.3 %collective-permute-done.15.refs_1_ = bf16[128,128]{1,0:T(8,128)(2,1)S(1)} collective-permute-done((bf16[128,128]{1,0:T(8,128)(2,1)S(1)}, bf16[128,128]{1,0:T(8,128)(2,1)S(1)}, u32[]{:S(2)}, u32[]{:S(2)}) %collective-permute-start.15) | collective-permute-done | bytes 32800 | tf_op jit(solution)/shard_map/ppermute | solution.py:469
  53.0 0.3 collective-permute-done.16.refs_2_
  53.3 1.7 %collective-permute-done.17.refs_3_ = bf16[128,128]{1,0:T(8,128)(2,1)S(1)} collective-permute-done((bf16[128,128]{1,0:T(8,128)(2,1)S(1)}, bf16[128,128]{1,0:T(8,128)(2,1)S(1)}, u32[]{:S(2)}, u32[]{:S(2)}) %collective-permute-start.17) | collective-permute-done | bytes 32800 | tf_op jit(solution)/shard_map/ppermute | solution.py:469
  55.0 0.7 %shard_map.178 = bf16[16,4096]{1,0:T(8,128)(2,1)} custom-call(bf16[128,128]{1,0:T(8,128)(2,1)S(1)} %get-tuple-element.27.refs_0_, bf16[128,128]{1,0:T(8,128)(2,1)S(1)} %collective-permute-done.15.refs_1_, bf16[128,128]{1,0:T(8,128)(2,1)S(1)} %collective-permute-done.16.refs_2_, bf16[128,128]{1,0:T(8,128)(2,1)S(1)} %collective-permute-done.17.refs_3_), custom_call_target="tpu_custom_call" | custom-call | tf_op jit(solution)/shard_map/pallas_call | solution.py:569
  55.7 0.0 all-to-all-done.1.back
  55.7 0.7 %shard_map.180 = (bf16[8,2048]{1,0:T(8,128)(2,1)}, bf16[16,2048]{1,0:T(8,128)(2,1)}, bf16[8,2048]{1,0:T(8,128)(2,1)}) custom-call(bf16[16,32,128]{2,1,0:T(8,128)(2,1)S(1)} %all-to-all-done.1.back), custom_call_target="tpu_custom_call" | custom-call | tf_op jit(solution)/shard_map/pallas_call | solution.py:558
Async XLA Ops:
  2.4 21.3 %all-to-all-start = ((bf16[16,96,128]{2,1,0:T(8,128)(2,1)}), bf16[16,96,128]{2,1,0:T(8,128)(2,1)S(1)}, u32[]{:S(2)}, u32[]{:S(2)}) async-start(bf16[16,96,128]{2,1,0:T(8,128)(2,1)} %shard_map.174.refs_3_), calls=%async_computation | async-start | bytes 786432 | tf_op jit(solution)/shard_map/all_to_all | solution.py:511
  11.8 24.1 %collective-permute-start = (bf16[256,128]{1,0:T(8,128)(2,1)}, bf16[256,128]{1,0:T(8,128)(2,1)S(1)}, u32[]{:S(2)}, u32[]{:S(2)}) collective-permute-start(bf16[256,128]{1,0:T(8,128)(2,1)} %get-tuple-element.20), channel_id=1, source_target_pairs={{0,14},{1,15},{2,12},{3,13},{4,10},{5,11},{6,8},{7,9},{8,6},{9,7},... | collective-permute-start | bytes 196616 | tf_op jit(solution)/shard_map/ppermute | solution.py:469
  16.5 20.9 %collective-permute-start.1 = (bf16[256,128]{1,0:T(8,128)(2,1)}, bf16[256,128]{1,0:T(8,128)(2,1)S(1)}, u32[]{:S(2)}, u32[]{:S(2)}) collective-permute-start(bf16[256,128]{1,0:T(8,128)(2,1)} %get-tuple-element.21), channel_id=1, source_target_pairs={{0,12},{1,13},{2,14},{3,15},{4,8},{5,9},{6,10},{7,11},{8,4},{9,5},... | collective-permute-start | bytes 196616 | tf_op jit(solution)/shard_map/ppermute | solution.py:469
  17.1 21.8 %collective-permute-start.2 = (bf16[256,128]{1,0:T(8,128)(2,1)}, bf16[256,128]{1,0:T(8,128)(2,1)S(1)}, u32[]{:S(2)}, u32[]{:S(2)}) collective-permute-start(bf16[256,128]{1,0:T(8,128)(2,1)} %get-tuple-element.22), channel_id=1, source_target_pairs={{0,10},{1,11},{2,8},{3,9},{4,14},{5,15},{6,12},{7,13},{8,2},{9,3},... | collective-permute-start | bytes 196616 | tf_op jit(solution)/shard_map/ppermute | solution.py:469
  17.6 25.0 %collective-permute-start.4 = (bf16[384,128]{1,0:T(8,128)(2,1)}, bf16[384,128]{1,0:T(8,128)(2,1)S(1)}, u32[]{:S(2)}, u32[]{:S(2)}) collective-permute-start(bf16[384,128]{1,0:T(8,128)(2,1)} %get-tuple-element.24), channel_id=1, source_target_pairs={{0,6},{1,7},{2,4},{3,5},{4,2},{5,3},{6,0},{7,1},{8,14},{9,15},{10,... | collective-permute-start | bytes 294920 | tf_op jit(solution)/shard_map/ppermute | solution.py:469
  23.7 12.2 %copy-start.2 = (bf16[384,128]{1,0:T(8,128)(2,1)S(1)}, bf16[384,128]{1,0:T(8,128)(2,1)}, u32[]{:S(2)}) copy-start(bf16[384,128]{1,0:T(8,128)(2,1)} %get-tuple-element.25) | copy-start | bytes 294916
  26.2 6.8 %copy-start.3 = (bf16[256,128]{1,0:T(8,128)(2,1)S(1)}, bf16[256,128]{1,0:T(8,128)(2,1)}, u32[]{:S(2)}) copy-start(bf16[256,128]{1,0:T(8,128)(2,1)} %get-tuple-element.23) | copy-start | bytes 196612
  26.2 11.2 %copy-start.1 = (bf16[384,128]{1,0:T(8,128)(2,1)S(1)}, bf16[384,128]{1,0:T(8,128)(2,1)}, u32[]{:S(2)}) copy-start(bf16[384,128]{1,0:T(8,128)(2,1)} %get-tuple-element.26) | copy-start | bytes 294916
  26.2 12.7 %copy-start = (bf16[384,128]{1,0:T(8,128)(2,1)S(1)}, bf16[384,128]{1,0:T(8,128)(2,1)}, u32[]{:S(2)}) copy-start(bf16[384,128]{1,0:T(8,128)(2,1)} %get-tuple-element.19.source) | copy-start | bytes 294916
  26.2 29.5 %all-to-all-start.1 = ((bf16[16,32,128]{2,1,0:T(8,128)(2,1)}), bf16[16,32,128]{2,1,0:T(8,128)(2,1)S(1)}, u32[]{:S(2)}, u32[]{:S(2)}) async-start(bf16[16,32,128]{2,1,0:T(8,128)(2,1)} %shard_map.179), calls=%async_computation.1 | async-start | bytes 262144 | tf_op jit(solution)/shard_map/all_to_all | solution.py:545
  33.0 9.6 %collective-permute-start.3 = (bf16[256,128]{1,0:T(8,128)(2,1)S(1)}, bf16[256,128]{1,0:T(8,128)(2,1)S(1)}, u32[]{:S(2)}, u32[]{:S(2)}) collective-permute-start(bf16[256,128]{1,0:T(8,128)(2,1)S(1)} %copy-done.3), channel_id=1, source_target_pairs={{0,8},{1,9},{2,10},{3,11},{4,12},{5,13},{6,14},{7,15},{8,0},{9,1},... | collective-permute-start | bytes 196616 | tf_op jit(solution)/shard_map/ppermute | solution.py:469
  35.9 7.3 %collective-permute-start.5 = (bf16[384,128]{1,0:T(8,128)(2,1)S(1)}, bf16[384,128]{1,0:T(8,128)(2,1)S(1)}, u32[]{:S(2)}, u32[]{:S(2)}) collective-permute-start(bf16[384,128]{1,0:T(8,128)(2,1)S(1)} %copy-done.2), channel_id=1, source_target_pairs={{0,4},{1,5},{2,6},{3,7},{4,0},{5,1},{6,2},{7,3},{8,12},{9,13},{10,... | collective-permute-start | bytes 294920 | tf_op jit(solution)/shard_map/ppermute | solution.py:469
  37.4 5.9 %collective-permute-start.6 = (bf16[384,128]{1,0:T(8,128)(2,1)S(1)}, bf16[384,128]{1,0:T(8,128)(2,1)S(1)}, u32[]{:S(2)}, u32[]{:S(2)}) collective-permute-start(bf16[384,128]{1,0:T(8,128)(2,1)S(1)} %copy-done.1), channel_id=1, source_target_pairs={{0,2},{1,3},{2,0},{3,1},{4,6},{5,7},{6,4},{7,5},{8,10},{9,11},{10,... | collective-permute-start | bytes 294920 | tf_op jit(solution)/shard_map/ppermute | solution.py:469
  38.9 4.8 %collective-permute-start.7 = (bf16[384,128]{1,0:T(8,128)(2,1)S(1)}, bf16[384,128]{1,0:T(8,128)(2,1)S(1)}, u32[]{:S(2)}, u32[]{:S(2)}) collective-permute-start(bf16[384,128]{1,0:T(8,128)(2,1)S(1)} %copy-done), channel_id=1, source_target_pairs={{0,1},{1,0},{2,3},{3,2},{4,5},{5,4},{6,7},{7,6},{8,9},{9,8},{10,11... | collective-permute-start | bytes 294920 | tf_op jit(solution)/shard_map/ppermute | solution.py:469
  42.7 1.3 %collective-permute-start.8 = (bf16[256,128]{1,0:T(8,128)(2,1)S(1)}, bf16[256,128]{1,0:T(8,128)(2,1)S(1)}, u32[]{:S(2)}, u32[]{:S(2)}) collective-permute-start(bf16[256,128]{1,0:T(8,128)(2,1)S(1)} %collective-permute-done.refs_1_), channel_id=1, source_target_pairs={{0,1},{1,0},{2,3},{3,2},{4,5},{5,4},{6,7},{7,6},{8,9},{9,8},{10,11... | collective-permute-start | bytes 196616 | tf_op jit(solution)/shard_map/ppermute | solution.py:469
  42.7 1.5 %collective-permute-start.9 = (bf16[256,128]{1,0:T(8,128)(2,1)S(1)}, bf16[256,128]{1,0:T(8,128)(2,1)S(1)}, u32[]{:S(2)}, u32[]{:S(2)}) collective-permute-start(bf16[256,128]{1,0:T(8,128)(2,1)S(1)} %collective-permute-done.1.refs_2_), channel_id=1, source_target_pairs={{0,1},{1,0},{2,3},{3,2},{4,5},{5,4},{6,7},{7,6},{8,9},{9,8},{10,11... | collective-permute-start | bytes 196616 | tf_op jit(solution)/shard_map/ppermute | solution.py:469
  43.2 2.3 %collective-permute-start.12 = (bf16[384,128]{1,0:T(8,128)(2,1)S(1)}, bf16[384,128]{1,0:T(8,128)(2,1)S(1)}, u32[]{:S(2)}, u32[]{:S(2)}) collective-permute-start(bf16[384,128]{1,0:T(8,128)(2,1)S(1)} %collective-permute-done.4.refs_5_), channel_id=1, source_target_pairs={{0,1},{1,0},{2,3},{3,2},{4,5},{5,4},{6,7},{7,6},{8,9},{9,8},{10,11... | collective-permute-start | bytes 294920 | tf_op jit(solution)/shard_map/ppermute | solution.py:469
  43.2 2.2 %collective-permute-start.13 = (bf16[384,128]{1,0:T(8,128)(2,1)S(1)}, bf16[384,128]{1,0:T(8,128)(2,1)S(1)}, u32[]{:S(2)}, u32[]{:S(2)}) collective-permute-start(bf16[384,128]{1,0:T(8,128)(2,1)S(1)} %collective-permute-done.5.refs_6_), channel_id=1, source_target_pairs={{0,1},{1,0},{2,3},{3,2},{4,5},{5,4},{6,7},{7,6},{8,9},{9,8},{10,11... | collective-permute-start | bytes 294920 | tf_op jit(solution)/shard_map/ppermute | solution.py:469
  43.7 1.8 %collective-permute-start.14 = (bf16[384,128]{1,0:T(8,128)(2,1)S(1)}, bf16[384,128]{1,0:T(8,128)(2,1)S(1)}, u32[]{:S(2)}, u32[]{:S(2)}) collective-permute-start(bf16[384,128]{1,0:T(8,128)(2,1)S(1)} %collective-permute-done.6.refs_7_), channel_id=1, source_target_pairs={{0,1},{1,0},{2,3},{3,2},{4,5},{5,4},{6,7},{7,6},{8,9},{9,8},{10,11... | collective-permute-start | bytes 294920 | tf_op jit(solution)/shard_map/ppermute | solution.py:469
  43.9 1.3 %collective-permute-start.10 = (bf16[256,128]{1,0:T(8,128)(2,1)S(1)}, bf16[256,128]{1,0:T(8,128)(2,1)S(1)}, u32[]{:S(2)}, u32[]{:S(2)}) collective-permute-start(bf16[256,128]{1,0:T(8,128)(2,1)S(1)} %collective-permute-done.2.refs_3_), channel_id=1, source_target_pairs={{0,1},{1,0},{2,3},{3,2},{4,5},{5,4},{6,7},{7,6},{8,9},{9,8},{10,11... | collective-permute-start | bytes 196616 | tf_op jit(solution)/shard_map/ppermute | solution.py:469
  44.2 1.3 %collective-permute-start.11 = (bf16[256,128]{1,0:T(8,128)(2,1)S(1)}, bf16[256,128]{1,0:T(8,128)(2,1)S(1)}, u32[]{:S(2)}, u32[]{:S(2)}) collective-permute-start(bf16[256,128]{1,0:T(8,128)(2,1)S(1)} %collective-permute-done.3.refs_4_), channel_id=1, source_target_pairs={{0,1},{1,0},{2,3},{3,2},{4,5},{5,4},{6,7},{7,6},{8,9},{9,8},{10,11... | collective-permute-start | bytes 196616 | tf_op jit(solution)/shard_map/ppermute | solution.py:469
  48.1 4.9 %collective-permute-start.15 = (bf16[128,128]{1,0:T(8,128)(2,1)S(1)}, bf16[128,128]{1,0:T(8,128)(2,1)S(1)}, u32[]{:S(2)}, u32[]{:S(2)}) collective-permute-start(bf16[128,128]{1,0:T(8,128)(2,1)S(1)} %get-tuple-element.28), channel_id=1, source_target_pairs={{0,6},{1,7},{2,4},{3,5},{4,2},{5,3},{6,0},{7,1},{8,14},{9,15},{10,... | collective-permute-start | bytes 98312 | tf_op jit(solution)/shard_map/ppermute | solution.py:469
  48.9 4.4 %collective-permute-start.16 = (bf16[128,128]{1,0:T(8,128)(2,1)S(1)}, bf16[128,128]{1,0:T(8,128)(2,1)S(1)}, u32[]{:S(2)}, u32[]{:S(2)}) collective-permute-start(bf16[128,128]{1,0:T(8,128)(2,1)S(1)} %get-tuple-element.29), channel_id=1, source_target_pairs={{0,4},{1,5},{2,6},{3,7},{4,0},{5,1},{6,2},{7,3},{8,12},{9,13},{10,... | collective-permute-start | bytes 98312 | tf_op jit(solution)/shard_map/ppermute | solution.py:469
  51.1 3.9 %collective-permute-start.17 = (bf16[128,128]{1,0:T(8,128)(2,1)S(1)}, bf16[128,128]{1,0:T(8,128)(2,1)S(1)}, u32[]{:S(2)}, u32[]{:S(2)}) collective-permute-start(bf16[128,128]{1,0:T(8,128)(2,1)S(1)} %get-tuple-element.30), channel_id=1, source_target_pairs={{0,2},{1,3},{2,0},{3,1},{4,6},{5,7},{6,4},{7,5},{8,10},{9,11},{10,... | collective-permute-start | bytes 98312 | tf_op jit(solution)/shard_map/ppermute | solution.py:469

commit v6 on v4

--- a/solution.py
+++ b/solution.py
@@ -279,19 +279,24 @@
 LANES = 128
 
 
-def by_step(items):
-    return [items[-j % len(items)] for j in range(len(items))]
-
-
-def pack_kernel(chips, *refs):
-    sources, refs = refs[:12], refs[12:]
-    packed, held, arrived = by_step(refs[:chips]), refs[chips : chips + 12], refs[chips + 12]
+def fetch(sources, held, arrived):
     copies = [
         pltpu.make_async_copy(source, slot, arrived.at[i])
         for i, (source, slot) in enumerate(zip(sources, held))
     ]
     for copy in copies:
         copy.start()
+    return copies
+
+
+def by_step(items):
+    return [items[-j % len(items)] for j in range(len(items))]
+
+
+def pack_kernel(chips, *refs):
+    sources, refs = refs[:12], refs[12:]
+    packed, held, arrived = by_step(refs[:chips]), refs[chips : chips + 12], refs[chips + 12]
+    copies = fetch(sources, held, arrived)
     chip = lax.axis_index("seq") // 2
     video, cross, audio = held[0:3], held[3:6], held[6:12]
     rows = video[0].shape[0]
@@ -320,6 +325,15 @@
             at += rows
 
 
+def keep_kernel(source, video_len, audio_len, shift, after, kept, bounds, *scratch):
+    held, arrived = scratch[:3], scratch[3]
+    copies = fetch((source, video_len, audio_len, shift), (kept, *held), arrived)
+    for copy in copies:
+        copy.wait()
+    row = lax.broadcasted_iota(jnp.int32, bounds.shape, 0)
+    bounds[...] = jnp.where(row == 0, held[0][0], jnp.where(row == 1, held[1][0], held[2][0]))
+
+
 def softmax_mix(query, key, value, scale, permit):
     scores = lax.dot_general(
         query, key, (((1,), (1,)), ((), ())), preferred_element_type=jnp.float32
@@ -343,41 +357,65 @@
     return result
 
 
-def attend_kernel(chips, rows, parts, pairs, video_len, audio_len, shift, *refs):
-    own, other, done = (by_step(refs[i * chips : (i + 1) * chips]) for i in range(3))
+def shares(chips):
+    turn = chips // 4
+    first = [j for j in range(chips) if (j // turn ^ j // (2 * turn)) % 2 == 0]
+    return [(j, j ^ turn) for j in first]
+
+
+def attend_kernel(chips, rows, parts, pairs, bounds, *refs):
+    own, other = by_step(refs[:chips]), by_step(refs[chips : 2 * chips])
+    done = refs[2 * chips :]
+    share = shares(chips)
     every = [ref for both in zip(own, other) for ref in both]
     half = rows // 2
     tv, ta = 2 * chips * rows, 2 * chips * half
-    ratio = tv // ta
-    bits = ratio.bit_length() - 1
+    bits = (tv // ta).bit_length() - 1
     me = lax.axis_index("seq")
-    video_valid, audio_valid, offset = video_len[0], audio_len[0], shift[0]
-
-    def slab(refs, at):
-        return jnp.concatenate([ref[at : at + rows, :] for ref in refs], axis=0)
-
-    def side(refs, at, second):
-        wide = [ref[at : at + rows, :].astype(jnp.float32) for ref in refs]
-        taken = [piece[half:] if second else piece[:half] for piece in wide]
-        return jnp.concatenate(taken, axis=0).astype(jnp.bfloat16)
+    core, home = me % 2, me // 2 * 2
+    video_valid, audio_valid, offset = (bounds[i : i + 1, 0:1] for i in range(3))
+
+    def slab(at):
+        return jnp.concatenate([ref[at : at + rows, :] for ref in every], axis=0)
+
+    def asked(at):
+        pieces = []
+        for zero, one in share:
+            for c in range(2):
+                low = (own, other)[c][zero][at : at + rows, :]
+                high = (other, own)[c][one][at : at + rows, :]
+                pieces.append(jnp.where(core == 0, low, high))
+        return jnp.concatenate(pieces, axis=0)
+
+    def split(wide):
+        wide = wide.astype(jnp.float32).reshape(-1, rows, LANES)
+        first = wide[:, :half, :].reshape(-1, LANES).astype(jnp.bfloat16)
+        second = wide[:, half:, :].reshape(-1, LANES).astype(jnp.bfloat16)
+        return first, second
 
     def places(q_step, k_step):
-        q_at = lax.broadcasted_iota(jnp.int32, (chips * q_step, 2 * chips * k_step), 0)
-        q_at = (q_at // q_step * (2 * q_step) + q_at % q_step) ^ (me * q_step)
-        k_at = lax.broadcasted_iota(jnp.int32, (chips * q_step, 2 * chips * k_step), 1)
-        return q_at, k_at ^ (me * k_step)
+        shape = (chips * q_step, 2 * chips * k_step)
+        k_at = lax.broadcasted_iota(jnp.int32, shape, 1) ^ (me * k_step)
+        starts = []
+        for zero, one in share:
+            chip = home ^ jnp.where(core == 0, 2 * zero, 2 * one)
+            starts.append(lax.broadcasted_iota(jnp.int32, (2 * q_step, 1), 0) + chip * q_step)
+        return jnp.concatenate(starts, axis=0), k_at
 
     def put(at, mixed):
-        for j in range(chips):
-            done[j][at : at + rows, :] = mixed[j * rows : (j + 1) * rows].astype(jnp.bfloat16)
+        count = done[0].shape[0] // 2
+        for u in range(len(share)):
+            for c in range(2):
+                piece = mixed[(2 * u + c) * rows : (2 * u + c + 1) * rows]
+                done[u][c * count + at : c * count + at + rows, :] = piece.astype(jnp.bfloat16)
 
     q_at, k_at = places(rows, rows)
     permit = k_at < video_valid
     for h in range(parts):
         mixed = softmax_mix(
-            slab(own, h * rows),
-            slab(every, (parts + h) * rows),
-            slab(every, (2 * parts + h) * rows),
+            asked(h * rows),
+            slab((parts + h) * rows),
+            slab((2 * parts + h) * rows),
             1.0 / math.sqrt(HDV),
             permit,
         )
@@ -391,50 +429,61 @@
     q_at, k_at = places(half, half)
     within_audio = k_at < audio_valid
     q_at, k_at = places(half, rows)
-    center = jnp.clip((q_at - offset) * ratio, 0, video_valid - 1)
+    center = jnp.clip((q_at - offset) << bits, 0, video_valid - 1)
     toward_audio = (k_at < video_valid) & (jnp.abs(k_at - center) <= tv // 8)
     for p in range(pairs):
         at = cross + p * rows
-        cross_query = slab(own, at)
-        cross_keys = slab(every, at + pairs * rows)
-        cross_values = slab(every, at + 2 * pairs * rows)
+        cross_query = asked(at)
+        cross_keys = slab(at + pairs * rows)
+        cross_values = slab(at + 2 * pairs * rows)
         at = audio + p * rows
-        audio_query, audio_keys = side(own, at, False), side(every, at, True)
+        audio_query = split(asked(at))[0]
+        audio_keys = split(slab(at))[1]
         at += pairs * rows
-        audio_values, listen_query = side(every, at, False), side(own, at, True)
+        audio_values = split(slab(at))[0]
+        listen_query = split(asked(at))[1]
         at += pairs * rows
-        sound_keys, sound_values = side(every, at, False), side(every, at, True)
+        sound_keys, sound_values = split(slab(at))
         out = (parts + p) * rows
         put(out, paired_mix(cross_query, sound_keys, sound_values, HDA, toward_video))
         heard = paired_mix(audio_query, audio_keys, audio_values, HDA, within_audio)
         listened = paired_mix(listen_query, cross_keys, cross_values, HDA, toward_audio)
-        out += pairs * rows
-        for j in range(chips):
-            both = jnp.concatenate(
-                [heard[j * half : (j + 1) * half], listened[j * half : (j + 1) * half]], axis=0
-            )
-            done[j][out : out + rows, :] = both.astype(jnp.bfloat16)
+        both = jnp.concatenate(
+            [heard.reshape(-1, half, LANES), listened.reshape(-1, half, LANES)], axis=1
+        )
+        put(out + pairs * rows, both.reshape(-1, LANES))
 
 
 def unpack_kernel(chips, *refs):
-    back, (video_mixed, audio_mixed, video_cross, audio_cross) = by_step(refs[:chips]), refs[chips:]
+    share = shares(chips)
+    back, other = refs[: len(share)], refs[len(share) : 2 * len(share)]
+    video_mixed, audio_mixed, video_cross, audio_cross = refs[2 * len(share) :]
     rows = video_mixed.shape[0]
     half = audio_mixed.shape[0]
     parts = video_mixed.shape[1] // chips // LANES
     pairs = audio_mixed.shape[1] // chips // LANES
-    chip = lax.axis_index("seq") // 2
-    for j in range(chips):
-        for h in range(parts):
-            at = pl.multiple_of(((chip ^ j) * parts + h) * LANES, LANES)
-            video_mixed[:, pl.ds(at, LANES)] = back[j][h * rows : (h + 1) * rows, :]
-        for p in range(pairs):
-            at = pl.multiple_of(((chip ^ j) * pairs + p) * LANES, LANES)
-            out = (parts + p) * rows
-            video_cross[:, pl.ds(at, LANES)] = back[j][out : out + rows, :]
-            out += pairs * rows
-            both = back[j][out : out + rows, :]
-            audio_mixed[:, pl.ds(at, LANES)] = both[:half, :]
-            audio_cross[:, pl.ds(at, LANES)] = both[half:, :]
+    me = lax.axis_index("seq")
+    core, home = me % 2, me // 2
+    for u, (zero, one) in enumerate(share):
+        for ref, chip in (
+            (back[u], home ^ jnp.where(core == 0, zero, one)),
+            (other[u], home ^ jnp.where(core == 0, one, zero)),
+        ):
+            base = pl.multiple_of(core * (ref.shape[0] // 2), 16)
+
+            def piece(at):
+                return ref[pl.ds(base + at, rows), :]
+
+            for h in range(parts):
+                at = pl.multiple_of((chip * parts + h) * LANES, LANES)
+                video_mixed[:, pl.ds(at, LANES)] = piece(h * rows)
+            for p in range(pairs):
+                at = pl.multiple_of((chip * pairs + p) * LANES, LANES)
+                out = (parts + p) * rows
+                video_cross[:, pl.ds(at, LANES)] = piece(out)
+                both = piece(out + pairs * rows)
+                audio_mixed[:, pl.ds(at, LANES)] = both[:half, :]
+                audio_cross[:, pl.ds(at, LANES)] = both[half:, :]
 
 
 def swap(piece, n, step):
@@ -455,10 +504,12 @@
     parts = video_query.shape[1] // chips // LANES
     pairs = audio_query.shape[1] // chips // LANES
     vmem = pl.BlockSpec(memory_space=pltpu.VMEM)
-    smem = pl.BlockSpec(memory_space=pltpu.SMEM)
+    hbm = pl.BlockSpec(memory_space=pltpu.HBM)
     params = pltpu.CompilerParams(vmem_limit_bytes=32 * 1024 * 1024)
-    in_rows = (3 * parts + 6 * pairs) * rows
-    out_rows = (parts + 2 * pairs) * rows
+
+    def buffer(*shape):
+        return jax.ShapeDtypeStruct(shape, jnp.bfloat16)
+
     sources = (
         video_query, video_keys, video_values,
         cross_video_query, cross_video_keys, cross_video_values,
@@ -467,48 +518,57 @@
     )
     packed = pl.pallas_call(
         functools.partial(pack_kernel, chips),
-        out_shape=(jax.ShapeDtypeStruct((in_rows, LANES), jnp.bfloat16),) * chips,
-        in_specs=[pl.BlockSpec(memory_space=pltpu.HBM)] * 12,
-        out_specs=(vmem,) * chips,
+        out_shape=[buffer((3 * parts + 6 * pairs) * rows, LANES)] * chips,
+        in_specs=[hbm] * 12,
+        out_specs=[vmem] * chips,
         scratch_shapes=[pltpu.VMEM(source.shape, source.dtype) for source in sources]
         + [pltpu.SemaphoreType.DMA((12,))],
         compiler_params=pltpu.CompilerParams(vmem_limit_bytes=60 * 1024 * 1024),
     )(*sources)
     packed = by_step(packed)
-    own = packed[:1] + [swap(packed[j], n, 2 * j) for j in range(1, chips)]
+    moved = [swap(packed[j], n, 2 * j) for j in range(1, chips)]
+    kept, bounds = pl.pallas_call(
+        keep_kernel,
+        out_shape=(packed[0], jax.ShapeDtypeStruct((8, LANES), jnp.int32)),
+        in_specs=[hbm] * 4 + [pl.BlockSpec(memory_space=pl.ANY)],
+        out_specs=(vmem, vmem),
+        scratch_shapes=[pltpu.SMEM((1,), jnp.int32)] * 3 + [pltpu.SemaphoreType.DMA((4,))],
+        compiler_params=params,
+    )(packed[0], video_length, audio_length, align_offset, moved[-1])
+    own = [kept] + moved
     other = [swap(piece, n, 1) for piece in own]
+    share = shares(chips)
     done = pl.pallas_call(
         functools.partial(attend_kernel, chips, rows, parts, pairs),
-        out_shape=(jax.ShapeDtypeStruct((out_rows, LANES), jnp.bfloat16),) * chips,
-        in_specs=[smem] * 3 + [vmem] * (2 * chips),
-        out_specs=(vmem,) * chips,
+        out_shape=[buffer(2 * (parts + 2 * pairs) * rows, LANES)] * len(share),
+        in_specs=[vmem] * (1 + 2 * chips),
+        out_specs=[vmem] * len(share),
         compiler_params=params,
-    )(
-        video_length, audio_length, align_offset,
-        *by_step(own), *by_step(other),
-    )
-    done = by_step(done)
-    back = done[:1] + [swap(done[j], n, 2 * j) for j in range(1, chips)]
+    )(bounds, *by_step(own), *by_step(other))
+    back = [
+        lax.ppermute(piece, "seq", [(i, i ^ 2 * pair[i % 2]) for i in range(n)])
+        for piece, pair in zip(done, share)
+    ]
     return pl.pallas_call(
         functools.partial(unpack_kernel, chips),
         out_shape=(
-            jax.ShapeDtypeStruct(video_query.shape, jnp.bfloat16),
-            jax.ShapeDtypeStruct(audio_query.shape, jnp.bfloat16),
-            jax.ShapeDtypeStruct(cross_video_query.shape, jnp.bfloat16),
-            jax.ShapeDtypeStruct(cross_audio_query.shape, jnp.bfloat16),
-        ),
-        in_specs=[vmem] * chips,
+            buffer(*video_query.shape),
+            buffer(*audio_query.shape),
+            buffer(*cross_video_query.shape),
+            buffer(*cross_audio_query.shape),
+        ),
+        in_specs=[vmem] * (2 * len(share)),
         out_specs=(vmem,) * 4,
         compiler_params=params,
-    )(*by_step(back))
+    )(*back, *[swap(piece, n, 1) for piece in back])
 
 
 def shards(*arrays):
     n = lax.axis_size("seq")
+    chips = max(n // 2, 1)
     rows, half = arrays[0].shape[0], arrays[3].shape[0]
-    chips = max(n // 2, 1)
     fits = (
-        n % 2 == 0
+        n % 8 == 0
         and n & (n - 1) == 0
         and arrays[0].shape[1] % (chips * LANES) == 0
         and arrays[3].shape[1] % (chips * LANES) == 0

time: 48.5 us -> 47.1 us (0.971)
  starting transfers between devices: 31.9 us -> 27.7 us
  waiting for transfers between devices: 6.81 us -> 8.59 us
  Pallas kernels: 6.06 us -> 6.84 us
    ppermute x22 -> x19, starting transfers between devices: 31.9 us -> 21.7 us  [swap(): return lax.ppermute(piece, 'seq', [(i, i ^ step) for i in range(n)])]
    ppermute x0 -> x4, starting transfers between devices: none -> 6.02 us  [shards_packed(): lax.ppermute(piece, 'seq', [(i, i ^ 2 * pair[i % 2]) for i in range(n)])]
    ppermute x0 -> x4, waiting for transfers between devices: none -> 3.26 us  [shards_packed(): lax.ppermute(piece, 'seq', [(i, i ^ 2 * pair[i % 2]) for i in range(n)])]
    ppermute x22 -> x19, waiting for transfers between devices: 6.81 us -> 5.33 us  [swap(): return lax.ppermute(piece, 'seq', [(i, i ^ step) for i in range(n)])]
    pallas_call x2 -> x3, Pallas kernels: 2.92 us -> 3.66 us  [the longest x1 2.18 us: shards_packed(): pl.pallas_call(functools.partial(pack_kernel, chips), out_shape=[buffer((...]
    unnamed x2 -> x4, local copies, waits for them, and re-layouts: 0.89 us -> 1.06 us
  transfers between devices with their start and end apart: 22 -> 23, of which waited for: 5 -> 11; matrix products, arithmetic and copies ran while one was open for 0% -> 0% of each run, Pallas kernels for 0% -> 2%
where the time goes in v6:
time: 47.1 us; the launch traced here: 46.9 us
  starting transfers between devices  27.7 us (59%)
  waiting for transfers between devices  8.59 us (18%)
  Pallas kernels  6.84 us (15%)
  between operations  2.66 us (6%)
  local copies, waits for them, and re-layouts  1.06 us (2%)
    ppermute x19, starting transfers between devices, swap(): return lax.ppermute(piece, 'seq', [(i, i ^ step) for i in range(n)])  21.7 us
    ppermute x4, starting transfers between devices, shards_packed(): lax.ppermute(piece, 'seq', [(i, i ^ 2 * pair[i % 2]) for i in range(n)])  6.02 us
    ppermute x19, waiting for transfers between devices, swap(): return lax.ppermute(piece, 'seq', [(i, i ^ step) for i in range(n)])  5.33 us
    ppermute x4, waiting for transfers between devices, shards_packed(): lax.ppermute(piece, 'seq', [(i, i ^ 2 * pair[i % 2]) for i in range(n)])  3.26 us
    pallas_call x1, Pallas kernels, shards_packed(): pl.pallas_call(functools.partial(attend_kernel, chips, rows, parts, pairs...  3.18 us
    pallas_call x1, Pallas kernels, shards_packed(): pl.pallas_call(functools.partial(pack_kernel, chips), out_shape=[buffer((...  2.18 us
    unnamed x4, local copies, waits for them, and re-layouts  1.06 us
  transfers between devices with their start and end apart: 23, of which 11 were waited for; matrix products, arithmetic and copies ran while one was open for 0% of the time, Pallas kernels for 2%

profile of v6, /device:TPU:0, one launch (start us, length us, event | category | flops | bytes accessed | tf_op | source)
XLA Modules:
  0.0 46.9 jit_solution(16369557047452175835)
XLA Ops:
  0.6 2.2 %shard_map.174 = (bf16[384,128]{1,0:T(8,128)(2,1)}, bf16[384,128]{1,0:T(8,128)(2,1)}, bf16[384,128]{1,0:T(8,128)(2,1)}, bf16[384,128]{1,0:T(8,128)(2,1)}, bf16[3...) custom-call(bf16[16,4096]{1,0:T(8,128)(2,1)} %refs_0_.1, ...), custom_call_target="tpu_custom_call" | custom-call | tf_op jit(solution)/shard_map/pallas_call | solution.py:519
  2.8 6.1 %collective-permute-start = (bf16[384,128]{1,0:T(8,128)(2,1)}, bf16[384,128]{1,0:T(8,128)(2,1)S(1)}, u32[]{:S(2)}, u32[]{:S(2)}) collective-permute-start(bf16[384,128]{1,0:T(8,128)(2,1)} %get-tuple-element.19), channel_id=1, source_target_pairs={{0,14},{1,15},{2,12},{3,13},{4,10},{5,11},{6,8},{7,9},{8,6},{9,7},... | collective-permute-start | bytes 294920 | tf_op jit(solution)/shard_map/ppermute | solution.py:490
  8.9 0.2 collective-permute-start.1
  9.1 0.7 %collective-permute-start.2 = (bf16[384,128]{1,0:T(8,128)(2,1)}, bf16[384,128]{1,0:T(8,128)(2,1)S(1)}, u32[]{:S(2)}, u32[]{:S(2)}) collective-permute-start(bf16[384,128]{1,0:T(8,128)(2,1)} %get-tuple-element.23), channel_id=1, source_target_pairs={{0,10},{1,11},{2,8},{3,9},{4,14},{5,15},{6,12},{7,13},{8,2},{9,3},... | collective-permute-start | bytes 294920 | tf_op jit(solution)/shard_map/ppermute | solution.py:490
  9.9 2.0 %collective-permute-start.3 = (bf16[384,128]{1,0:T(8,128)(2,1)}, bf16[384,128]{1,0:T(8,128)(2,1)S(1)}, u32[]{:S(2)}, u32[]{:S(2)}) collective-permute-start(bf16[384,128]{1,0:T(8,128)(2,1)} %get-tuple-element.24), channel_id=1, source_target_pairs={{0,8},{1,9},{2,10},{3,11},{4,12},{5,13},{6,14},{7,15},{8,0},{9,1},... | collective-permute-start | bytes 294920 | tf_op jit(solution)/shard_map/ppermute | solution.py:490
  11.9 2.3 %collective-permute-start.4 = (bf16[384,128]{1,0:T(8,128)(2,1)}, bf16[384,128]{1,0:T(8,128)(2,1)S(1)}, u32[]{:S(2)}, u32[]{:S(2)}) collective-permute-start(bf16[384,128]{1,0:T(8,128)(2,1)} %get-tuple-element.25), channel_id=1, source_target_pairs={{0,6},{1,7},{2,4},{3,5},{4,2},{5,3},{6,0},{7,1},{8,14},{9,15},{10,... | collective-permute-start | bytes 294920 | tf_op jit(solution)/shard_map/ppermute | solution.py:490
  16.1 0.0 collective-permute-done.after.refs_1_
  16.1 4.8 %collective-permute-start.5 = (bf16[384,128]{1,0:T(8,128)(2,1)}, bf16[384,128]{1,0:T(8,128)(2,1)S(1)}, u32[]{:S(2)}, u32[]{:S(2)}) collective-permute-start(bf16[384,128]{1,0:T(8,128)(2,1)} %get-tuple-element.26), channel_id=1, source_target_pairs={{0,4},{1,5},{2,6},{3,7},{4,0},{5,1},{6,2},{7,3},{8,12},{9,13},{10,... | collective-permute-start | bytes 294920 | tf_op jit(solution)/shard_map/ppermute | solution.py:490
  21.0 0.0 copy-start
  21.0 0.9 %copy-done = bf16[384,128]{1,0:T(8,128)(2,1)S(1)} copy-done((bf16[384,128]{1,0:T(8,128)(2,1)S(1)}, bf16[384,128]{1,0:T(8,128)(2,1)}, u32[]{:S(2)}) %copy-start) | copy-done | bytes 98328
  21.9 0.0 copy-start.1
  21.9 0.7 %shard_map.175 = (bf16[384,128]{1,0:T(8,128)(2,1)S(1)}, s32[8,128]{1,0:T(8,128)S(1)}) custom-call(bf16[384,128]{1,0:T(8,128)(2,1)S(1)} %copy-done, s32[1]{0:T(128)S(6)} %copy.19.video_len, s32[1]{0:T(128)S(6)} %copy.20.audio_len, s32[1]{0:T(128)S(6)} %copy.21.shift, bf16[384,128]{1,0:T(8,128)(2,1)S(1)} %collective-permute-done.after.refs_1_), custom_call_target="tpu_custom_call" | custom-call | tf_op jit(solution)/shard_map/pallas_call | solution.py:530
  22.6 0.0 collective-permute-done.1.refs_2_
  22.6 0.2 copy-done.1
  22.8 1.0 %collective-permute-start.6 = (bf16[384,128]{1,0:T(8,128)(2,1)S(1)}, bf16[384,128]{1,0:T(8,128)(2,1)S(1)}, u32[]{:S(2)}, u32[]{:S(2)}) collective-permute-start(bf16[384,128]{1,0:T(8,128)(2,1)S(1)} %copy-done.1), channel_id=1, source_target_pairs={{0,2},{1,3},{2,0},{3,1},{4,6},{5,7},{6,4},{7,5},{8,10},{9,11},{10,... | collective-permute-start | bytes 294920 | tf_op jit(solution)/shard_map/ppermute | solution.py:490
  23.7 1.0 %collective-permute-done.2.refs_3_ = bf16[384,128]{1,0:T(8,128)(2,1)S(1)} collective-permute-done((bf16[384,128]{1,0:T(8,128)(2,1)}, bf16[384,128]{1,0:T(8,128)(2,1)S(1)}, u32[]{:S(2)}, u32[]{:S(2)}) %collective-permute-start.2) | collective-permute-done | bytes 98336 | tf_op jit(solution)/shard_map/ppermute | solution.py:490
  24.8 0.0 collective-permute-start.7
  24.8 1.1 %collective-permute-done.3.refs_4_ = bf16[384,128]{1,0:T(8,128)(2,1)S(1)} collective-permute-done((bf16[384,128]{1,0:T(8,128)(2,1)}, bf16[384,128]{1,0:T(8,128)(2,1)S(1)}, u32[]{:S(2)}, u32[]{:S(2)}) %collective-permute-start.3) | collective-permute-done | bytes 98336 | tf_op jit(solution)/shard_map/ppermute | solution.py:490
  25.9 0.0 collective-permute-start.8
  25.9 0.0 collective-permute-done.4.refs_5_
  25.9 0.5 %collective-permute-start.9 = (bf16[384,128]{1,0:T(8,128)(2,1)S(1)}, bf16[384,128]{1,0:T(8,128)(2,1)S(1)}, u32[]{:S(2)}, u32[]{:S(2)}) collective-permute-start(bf16[384,128]{1,0:T(8,128)(2,1)S(1)} %collective-permute-done.1.refs_2_), channel_id=1, source_target_pairs={{0,1},{1,0},{2,3},{3,2},{4,5},{5,4},{6,7},{7,6},{8,9},{9,8},{10,11... | collective-permute-start | bytes 294920 | tf_op jit(solution)/shard_map/ppermute | solution.py:490
  26.4 0.4 collective-permute-done.5.refs_6_
  26.9 0.0 collective-permute-start.10
  26.9 0.5 %collective-permute-done.6.refs_7_ = bf16[384,128]{1,0:T(8,128)(2,1)S(1)} collective-permute-done((bf16[384,128]{1,0:T(8,128)(2,1)S(1)}, bf16[384,128]{1,0:T(8,128)(2,1)S(1)}, u32[]{:S(2)}, u32[]{:S(2)}) %collective-permute-start.6) | collective-permute-done | bytes 98336 | tf_op jit(solution)/shard_map/ppermute | solution.py:490
  27.4 0.0 collective-permute-start.11
  27.4 0.0 collective-permute-done.7.refs_8_
  27.4 0.5 %collective-permute-start.12 = (bf16[384,128]{1,0:T(8,128)(2,1)S(1)}, bf16[384,128]{1,0:T(8,128)(2,1)S(1)}, u32[]{:S(2)}, u32[]{:S(2)}) collective-permute-start(bf16[384,128]{1,0:T(8,128)(2,1)S(1)} %collective-permute-done.4.refs_5_), channel_id=1, source_target_pairs={{0,1},{1,0},{2,3},{3,2},{4,5},{5,4},{6,7},{7,6},{8,9},{9,8},{10,11... | collective-permute-start | bytes 294920 | tf_op jit(solution)/shard_map/ppermute | solution.py:490
  27.9 0.0 collective-permute-done.8.refs_9_
  27.9 0.1 collective-permute-start.13
  28.0 0.0 collective-permute-done.9.refs_10_
  28.0 0.4 collective-permute-start.14
  28.4 0.0 collective-permute-done.10.refs_11_
  28.4 0.3 collective-permute-done.11.refs_12_
  28.7 0.2 collective-permute-done.12.refs_13_
  28.8 0.4 collective-permute-done.13.refs_14_
  29.2 0.2 collective-permute-done.14.refs_15_
  29.4 3.2 %shard_map.176 = (bf16[256,128]{1,0:T(8,128)(2,1)S(1)}, bf16[256,128]{1,0:T(8,128)(2,1)S(1)}, bf16[256,128]{1,0:T(8,128)(2,1)S(1)}, bf16[256,128]{1,0:T(8,128)(2,1)S(1)}) custom-call(s32[8,128]{1,0:T(8,128)S(1)} %get-tuple-element.20.bounds, bf16[384,128]{1,0:T(8,128)(2,1)S(1)} %get-tuple-element.21.refs_0_, ...), custom_call_target="tpu_custom_call" | custom-call | tf_op jit(solution)/shard_map/pallas_call | solution.py:541
  32.5 0.7 %collective-permute-start.15 = (bf16[256,128]{1,0:T(8,128)(2,1)S(1)}, bf16[256,128]{1,0:T(8,128)(2,1)S(1)}, u32[]{:S(2)}, u32[]{:S(2)}) collective-permute-start(bf16[256,128]{1,0:T(8,128)(2,1)S(1)} %get-tuple-element.28), channel_id=1, source_target_pairs={{0,0},{1,5},{2,2},{3,7},{4,4},{5,1},{6,6},{7,3},{8,8},{9,13},{10,1... | collective-permute-start | bytes 196616 | tf_op jit(solution)/shard_map/ppermute | solution.py:549
  33.2 1.0 %collective-permute-start.16 = (bf16[256,128]{1,0:T(8,128)(2,1)S(1)}, bf16[256,128]{1,0:T(8,128)(2,1)S(1)}, u32[]{:S(2)}, u32[]{:S(2)}) collective-permute-start(bf16[256,128]{1,0:T(8,128)(2,1)S(1)} %get-tuple-element.29), channel_id=1, source_target_pairs={{0,2},{1,7},{2,0},{3,5},{4,6},{5,3},{6,4},{7,1},{8,10},{9,15},{10,... | collective-permute-start | bytes 196616 | tf_op jit(solution)/shard_map/ppermute | solution.py:549
  34.2 3.2 %collective-permute-start.17 = (bf16[256,128]{1,0:T(8,128)(2,1)S(1)}, bf16[256,128]{1,0:T(8,128)(2,1)S(1)}, u32[]{:S(2)}, u32[]{:S(2)}) collective-permute-start(bf16[256,128]{1,0:T(8,128)(2,1)S(1)} %get-tuple-element.30), channel_id=1, source_target_pairs={{0,12},{1,9},{2,14},{3,11},{4,8},{5,13},{6,10},{7,15},{8,4},{9,1},... | collective-permute-start | bytes 196616 | tf_op jit(solution)/shard_map/ppermute | solution.py:549
  37.4 1.1 %collective-permute-start.18 = (bf16[256,128]{1,0:T(8,128)(2,1)S(1)}, bf16[256,128]{1,0:T(8,128)(2,1)S(1)}, u32[]{:S(2)}, u32[]{:S(2)}) collective-permute-start(bf16[256,128]{1,0:T(8,128)(2,1)S(1)} %get-tuple-element.31), channel_id=1, source_target_pairs={{0,14},{1,11},{2,12},{3,9},{4,10},{5,15},{6,8},{7,13},{8,6},{9,3},... | collective-permute-start | bytes 196616 | tf_op jit(solution)/shard_map/ppermute | solution.py:549
  38.6 0.0 collective-permute-done.15.refs_0_
  38.6 1.0 %collective-permute-start.19 = (bf16[256,128]{1,0:T(8,128)(2,1)S(1)}, bf16[256,128]{1,0:T(8,128)(2,1)S(1)}, u32[]{:S(2)}, u32[]{:S(2)}) collective-permute-start(bf16[256,128]{1,0:T(8,128)(2,1)S(1)} %collective-permute-done.15.refs_0_), channel_id=1, source_target_pairs={{0,1},{1,0},{2,3},{3,2},{4,5},{5,4},{6,7},{7,6},{8,9},{9,8},{10,11... | collective-permute-start | bytes 196616 | tf_op jit(solution)/shard_map/ppermute | solution.py:490
  39.6 0.0 collective-permute-done.16.refs_1_
  39.6 0.1 collective-permute-start.20
  39.7 0.7 %collective-permute-done.17.refs_2_ = bf16[256,128]{1,0:T(8,128)(2,1)S(1)} collective-permute-done((bf16[256,128]{1,0:T(8,128)(2,1)S(1)}, bf16[256,128]{1,0:T(8,128)(2,1)S(1)}, u32[]{:S(2)}, u32[]{:S(2)}) %collective-permute-start.17) | collective-permute-done | bytes 65568 | tf_op jit(solution)/shard_map/ppermute | solution.py:549
  40.3 1.9 %collective-permute-start.21 = (bf16[256,128]{1,0:T(8,128)(2,1)S(1)}, bf16[256,128]{1,0:T(8,128)(2,1)S(1)}, u32[]{:S(2)}, u32[]{:S(2)}) collective-permute-start(bf16[256,128]{1,0:T(8,128)(2,1)S(1)} %collective-permute-done.17.refs_2_), channel_id=1, source_target_pairs={{0,1},{1,0},{2,3},{3,2},{4,5},{5,4},{6,7},{7,6},{8,9},{9,8},{10,11... | collective-permute-start | bytes 196616 | tf_op jit(solution)/shard_map/ppermute | solution.py:490
  42.2 2.6 %collective-permute-done.18.refs_3_ = bf16[256,128]{1,0:T(8,128)(2,1)S(1)} collective-permute-done((bf16[256,128]{1,0:T(8,128)(2,1)S(1)}, bf16[256,128]{1,0:T(8,128)(2,1)S(1)}, u32[]{:S(2)}, u32[]{:S(2)}) %collective-permute-start.18) | collective-permute-done | bytes 65568 | tf_op jit(solution)/shard_map/ppermute | solution.py:549
  44.8 0.0 collective-permute-start.22
  44.8 0.0 collective-permute-done.19.refs_4_
  44.8 0.0 collective-permute-done.20.refs_5_
  44.8 0.0 collective-permute-done.21.refs_6_
  44.9 1.2 %collective-permute-done.22.refs_7_ = bf16[256,128]{1,0:T(8,128)(2,1)S(1)} collective-permute-done((bf16[256,128]{1,0:T(8,128)(2,1)S(1)}, bf16[256,128]{1,0:T(8,128)(2,1)S(1)}, u32[]{:S(2)}, u32[]{:S(2)}) %collective-permute-start.22) | collective-permute-done | bytes 65568 | tf_op jit(solution)/shard_map/ppermute | solution.py:490
  46.1 0.8 %shard_map.177 = (bf16[16,4096]{1,0:T(8,128)(2,1)}, bf16[8,2048]{1,0:T(8,128)(2,1)}, bf16[16,2048]{1,0:T(8,128)(2,1)}, bf16[8,2048]{1,0:T(8,128)(2,1)}) custom-call(bf16[256,128]{1,0:T(8,128)(2,1)S(1)} %collective-permute-done.15.refs_0_, bf16[256,128]{1,0:T(8,128)(2,1)S(1)} %collective-permute-done.16.refs_1_, ...), custom_call_target="tpu_custom_call" | custom-call | tf_op jit(solution)/shard_map/pallas_call | solution.py:552
Async XLA Ops:
  2.8 13.3 %collective-permute-start = (bf16[384,128]{1,0:T(8,128)(2,1)}, bf16[384,128]{1,0:T(8,128)(2,1)S(1)}, u32[]{:S(2)}, u32[]{:S(2)}) collective-permute-start(bf16[384,128]{1,0:T(8,128)(2,1)} %get-tuple-element.19), channel_id=1, source_target_pairs={{0,14},{1,15},{2,12},{3,13},{4,10},{5,11},{6,8},{7,9},{8,6},{9,7},... | collective-permute-start | bytes 294920 | tf_op jit(solution)/shard_map/ppermute | solution.py:490
  8.9 13.7 %collective-permute-start.1 = (bf16[384,128]{1,0:T(8,128)(2,1)}, bf16[384,128]{1,0:T(8,128)(2,1)S(1)}, u32[]{:S(2)}, u32[]{:S(2)}) collective-permute-start(bf16[384,128]{1,0:T(8,128)(2,1)} %get-tuple-element.22), channel_id=1, source_target_pairs={{0,12},{1,13},{2,14},{3,15},{4,8},{5,9},{6,10},{7,11},{8,4},{9,5},... | collective-permute-start | bytes 294920 | tf_op jit(solution)/shard_map/ppermute | solution.py:490
  9.1 15.6 %collective-permute-start.2 = (bf16[384,128]{1,0:T(8,128)(2,1)}, bf16[384,128]{1,0:T(8,128)(2,1)S(1)}, u32[]{:S(2)}, u32[]{:S(2)}) collective-permute-start(bf16[384,128]{1,0:T(8,128)(2,1)} %get-tuple-element.23), channel_id=1, source_target_pairs={{0,10},{1,11},{2,8},{3,9},{4,14},{5,15},{6,12},{7,13},{8,2},{9,3},... | collective-permute-start | bytes 294920 | tf_op jit(solution)/shard_map/ppermute | solution.py:490
  9.9 16.0 %collective-permute-start.3 = (bf16[384,128]{1,0:T(8,128)(2,1)}, bf16[384,128]{1,0:T(8,128)(2,1)S(1)}, u32[]{:S(2)}, u32[]{:S(2)}) collective-permute-start(bf16[384,128]{1,0:T(8,128)(2,1)} %get-tuple-element.24), channel_id=1, source_target_pairs={{0,8},{1,9},{2,10},{3,11},{4,12},{5,13},{6,14},{7,15},{8,0},{9,1},... | collective-permute-start | bytes 294920 | tf_op jit(solution)/shard_map/ppermute | solution.py:490
  11.9 14.0 %collective-permute-start.4 = (bf16[384,128]{1,0:T(8,128)(2,1)}, bf16[384,128]{1,0:T(8,128)(2,1)S(1)}, u32[]{:S(2)}, u32[]{:S(2)}) collective-permute-start(bf16[384,128]{1,0:T(8,128)(2,1)} %get-tuple-element.25), channel_id=1, source_target_pairs={{0,6},{1,7},{2,4},{3,5},{4,2},{5,3},{6,0},{7,1},{8,14},{9,15},{10,... | collective-permute-start | bytes 294920 | tf_op jit(solution)/shard_map/ppermute | solution.py:490
  16.1 10.7 %collective-permute-start.5 = (bf16[384,128]{1,0:T(8,128)(2,1)}, bf16[384,128]{1,0:T(8,128)(2,1)S(1)}, u32[]{:S(2)}, u32[]{:S(2)}) collective-permute-start(bf16[384,128]{1,0:T(8,128)(2,1)} %get-tuple-element.26), channel_id=1, source_target_pairs={{0,4},{1,5},{2,6},{3,7},{4,0},{5,1},{6,2},{7,3},{8,12},{9,13},{10,... | collective-permute-start | bytes 294920 | tf_op jit(solution)/shard_map/ppermute | solution.py:490
  21.0 0.9 %copy-start = (bf16[384,128]{1,0:T(8,128)(2,1)S(1)}, bf16[384,128]{1,0:T(8,128)(2,1)}, u32[]{:S(2)}) copy-start(bf16[384,128]{1,0:T(8,128)(2,1)} %get-tuple-element.18.source) | copy-start | bytes 294916
  21.9 0.9 %copy-start.1 = (bf16[384,128]{1,0:T(8,128)(2,1)S(1)}, bf16[384,128]{1,0:T(8,128)(2,1)}, u32[]{:S(2)}) copy-start(bf16[384,128]{1,0:T(8,128)(2,1)} %get-tuple-element.27) | copy-start | bytes 294916
  22.8 4.6 %collective-permute-start.6 = (bf16[384,128]{1,0:T(8,128)(2,1)S(1)}, bf16[384,128]{1,0:T(8,128)(2,1)S(1)}, u32[]{:S(2)}, u32[]{:S(2)}) collective-permute-start(bf16[384,128]{1,0:T(8,128)(2,1)S(1)} %copy-done.1), channel_id=1, source_target_pairs={{0,2},{1,3},{2,0},{3,1},{4,6},{5,7},{6,4},{7,5},{8,10},{9,11},{10,... | collective-permute-start | bytes 294920 | tf_op jit(solution)/shard_map/ppermute | solution.py:490
  24.8 2.6 %collective-permute-start.7 = (bf16[384,128]{1,0:T(8,128)(2,1)S(1)}, bf16[384,128]{1,0:T(8,128)(2,1)S(1)}, u32[]{:S(2)}, u32[]{:S(2)}) collective-permute-start(bf16[384,128]{1,0:T(8,128)(2,1)S(1)} %get-tuple-element.21.refs_0_), channel_id=1, source_target_pairs={{0,1},{1,0},{2,3},{3,2},{4,5},{5,4},{6,7},{7,6},{8,9},{9,8},{10,11... | collective-permute-start | bytes 294920 | tf_op jit(solution)/shard_map/ppermute | solution.py:490
  25.9 2.0 %collective-permute-start.8 = (bf16[384,128]{1,0:T(8,128)(2,1)S(1)}, bf16[384,128]{1,0:T(8,128)(2,1)S(1)}, u32[]{:S(2)}, u32[]{:S(2)}) collective-permute-start(bf16[384,128]{1,0:T(8,128)(2,1)S(1)} %collective-permute-done.after.refs_1_), channel_id=1, source_target_pairs={{0,1},{1,0},{2,3},{3,2},{4,5},{5,4},{6,7},{7,6},{8,9},{9,8},{10,11... | collective-permute-start | bytes 294920 | tf_op jit(solution)/shard_map/ppermute | solution.py:490
  25.9 2.1 %collective-permute-start.9 = (bf16[384,128]{1,0:T(8,128)(2,1)S(1)}, bf16[384,128]{1,0:T(8,128)(2,1)S(1)}, u32[]{:S(2)}, u32[]{:S(2)}) collective-permute-start(bf16[384,128]{1,0:T(8,128)(2,1)S(1)} %collective-permute-done.1.refs_2_), channel_id=1, source_target_pairs={{0,1},{1,0},{2,3},{3,2},{4,5},{5,4},{6,7},{7,6},{8,9},{9,8},{10,11... | collective-permute-start | bytes 294920 | tf_op jit(solution)/shard_map/ppermute | solution.py:490
  26.9 1.6 %collective-permute-start.10 = (bf16[384,128]{1,0:T(8,128)(2,1)S(1)}, bf16[384,128]{1,0:T(8,128)(2,1)S(1)}, u32[]{:S(2)}, u32[]{:S(2)}) collective-permute-start(bf16[384,128]{1,0:T(8,128)(2,1)S(1)} %collective-permute-done.2.refs_3_), channel_id=1, source_target_pairs={{0,1},{1,0},{2,3},{3,2},{4,5},{5,4},{6,7},{7,6},{8,9},{9,8},{10,11... | collective-permute-start | bytes 294920 | tf_op jit(solution)/shard_map/ppermute | solution.py:490
  27.4 1.3 %collective-permute-start.11 = (bf16[384,128]{1,0:T(8,128)(2,1)S(1)}, bf16[384,128]{1,0:T(8,128)(2,1)S(1)}, u32[]{:S(2)}, u32[]{:S(2)}) collective-permute-start(bf16[384,128]{1,0:T(8,128)(2,1)S(1)} %collective-permute-done.3.refs_4_), channel_id=1, source_target_pairs={{0,1},{1,0},{2,3},{3,2},{4,5},{5,4},{6,7},{7,6},{8,9},{9,8},{10,11... | collective-permute-start | bytes 294920 | tf_op jit(solution)/shard_map/ppermute | solution.py:490
  27.4 1.5 %collective-permute-start.12 = (bf16[384,128]{1,0:T(8,128)(2,1)S(1)}, bf16[384,128]{1,0:T(8,128)(2,1)S(1)}, u32[]{:S(2)}, u32[]{:S(2)}) collective-permute-start(bf16[384,128]{1,0:T(8,128)(2,1)S(1)} %collective-permute-done.4.refs_5_), channel_id=1, source_target_pairs={{0,1},{1,0},{2,3},{3,2},{4,5},{5,4},{6,7},{7,6},{8,9},{9,8},{10,11... | collective-permute-start | bytes 294920 | tf_op jit(solution)/shard_map/ppermute | solution.py:490
  27.9 1.3 %collective-permute-start.13 = (bf16[384,128]{1,0:T(8,128)(2,1)S(1)}, bf16[384,128]{1,0:T(8,128)(2,1)S(1)}, u32[]{:S(2)}, u32[]{:S(2)}) collective-permute-start(bf16[384,128]{1,0:T(8,128)(2,1)S(1)} %collective-permute-done.5.refs_6_), channel_id=1, source_target_pairs={{0,1},{1,0},{2,3},{3,2},{4,5},{5,4},{6,7},{7,6},{8,9},{9,8},{10,11... | collective-permute-start | bytes 294920 | tf_op jit(solution)/shard_map/ppermute | solution.py:490
  28.0 1.4 %collective-permute-start.14 = (bf16[384,128]{1,0:T(8,128)(2,1)S(1)}, bf16[384,128]{1,0:T(8,128)(2,1)S(1)}, u32[]{:S(2)}, u32[]{:S(2)}) collective-permute-start(bf16[384,128]{1,0:T(8,128)(2,1)S(1)} %collective-permute-done.6.refs_7_), channel_id=1, source_target_pairs={{0,1},{1,0},{2,3},{3,2},{4,5},{5,4},{6,7},{7,6},{8,9},{9,8},{10,11... | collective-permute-start | bytes 294920 | tf_op jit(solution)/shard_map/ppermute | solution.py:490
  32.5 6.0 %collective-permute-start.15 = (bf16[256,128]{1,0:T(8,128)(2,1)S(1)}, bf16[256,128]{1,0:T(8,128)(2,1)S(1)}, u32[]{:S(2)}, u32[]{:S(2)}) collective-permute-start(bf16[256,128]{1,0:T(8,128)(2,1)S(1)} %get-tuple-element.28), channel_id=1, source_target_pairs={{0,0},{1,5},{2,2},{3,7},{4,4},{5,1},{6,6},{7,3},{8,8},{9,13},{10,1... | collective-permute-start | bytes 196616 | tf_op jit(solution)/shard_map/ppermute | solution.py:549
  33.2 6.4 %collective-permute-start.16 = (bf16[256,128]{1,0:T(8,128)(2,1)S(1)}, bf16[256,128]{1,0:T(8,128)(2,1)S(1)}, u32[]{:S(2)}, u32[]{:S(2)}) collective-permute-start(bf16[256,128]{1,0:T(8,128)(2,1)S(1)} %get-tuple-element.29), channel_id=1, source_target_pairs={{0,2},{1,7},{2,0},{3,5},{4,6},{5,3},{6,4},{7,1},{8,10},{9,15},{10,... | collective-permute-start | bytes 196616 | tf_op jit(solution)/shard_map/ppermute | solution.py:549
  34.2 6.1 %collective-permute-start.17 = (bf16[256,128]{1,0:T(8,128)(2,1)S(1)}, bf16[256,128]{1,0:T(8,128)(2,1)S(1)}, u32[]{:S(2)}, u32[]{:S(2)}) collective-permute-start(bf16[256,128]{1,0:T(8,128)(2,1)S(1)} %get-tuple-element.30), channel_id=1, source_target_pairs={{0,12},{1,9},{2,14},{3,11},{4,8},{5,13},{6,10},{7,15},{8,4},{9,1},... | collective-permute-start | bytes 196616 | tf_op jit(solution)/shard_map/ppermute | solution.py:549
  37.4 7.4 %collective-permute-start.18 = (bf16[256,128]{1,0:T(8,128)(2,1)S(1)}, bf16[256,128]{1,0:T(8,128)(2,1)S(1)}, u32[]{:S(2)}, u32[]{:S(2)}) collective-permute-start(bf16[256,128]{1,0:T(8,128)(2,1)S(1)} %get-tuple-element.31), channel_id=1, source_target_pairs={{0,14},{1,11},{2,12},{3,9},{4,10},{5,15},{6,8},{7,13},{8,6},{9,3},... | collective-permute-start | bytes 196616 | tf_op jit(solution)/shard_map/ppermute | solution.py:549
  38.6 6.3 %collective-permute-start.19 = (bf16[256,128]{1,0:T(8,128)(2,1)S(1)}, bf16[256,128]{1,0:T(8,128)(2,1)S(1)}, u32[]{:S(2)}, u32[]{:S(2)}) collective-permute-start(bf16[256,128]{1,0:T(8,128)(2,1)S(1)} %collective-permute-done.15.refs_0_), channel_id=1, source_target_pairs={{0,1},{1,0},{2,3},{3,2},{4,5},{5,4},{6,7},{7,6},{8,9},{9,8},{10,11... | collective-permute-start | bytes 196616 | tf_op jit(solution)/shard_map/ppermute | solution.py:490
  39.6 5.2 %collective-permute-start.20 = (bf16[256,128]{1,0:T(8,128)(2,1)S(1)}, bf16[256,128]{1,0:T(8,128)(2,1)S(1)}, u32[]{:S(2)}, u32[]{:S(2)}) collective-permute-start(bf16[256,128]{1,0:T(8,128)(2,1)S(1)} %collective-permute-done.16.refs_1_), channel_id=1, source_target_pairs={{0,1},{1,0},{2,3},{3,2},{4,5},{5,4},{6,7},{7,6},{8,9},{9,8},{10,11... | collective-permute-start | bytes 196616 | tf_op jit(solution)/shard_map/ppermute | solution.py:490
  40.3 4.5 %collective-permute-start.21 = (bf16[256,128]{1,0:T(8,128)(2,1)S(1)}, bf16[256,128]{1,0:T(8,128)(2,1)S(1)}, u32[]{:S(2)}, u32[]{:S(2)}) collective-permute-start(bf16[256,128]{1,0:T(8,128)(2,1)S(1)} %collective-permute-done.17.refs_2_), channel_id=1, source_target_pairs={{0,1},{1,0},{2,3},{3,2},{4,5},{5,4},{6,7},{7,6},{8,9},{9,8},{10,11... | collective-permute-start | bytes 196616 | tf_op jit(solution)/shard_map/ppermute | solution.py:490
  44.8 1.3 %collective-permute-start.22 = (bf16[256,128]{1,0:T(8,128)(2,1)S(1)}, bf16[256,128]{1,0:T(8,128)(2,1)S(1)}, u32[]{:S(2)}, u32[]{:S(2)}) collective-permute-start(bf16[256,128]{1,0:T(8,128)(2,1)S(1)} %collective-permute-done.18.refs_3_), channel_id=1, source_target_pairs={{0,1},{1,0},{2,3},{3,2},{4,5},{5,4},{6,7},{7,6},{8,9},{9,8},{10,11... | collective-permute-start | bytes 196616 | tf_op jit(solution)/shard_map/ppermute | solution.py:490

commit v7 on v6

--- a/solution.py
+++ b/solution.py
@@ -289,8 +289,18 @@
     return copies
 
 
+def step_order(chips):
+    far, near = list(range(chips - 1, chips // 2 - 1, -1)), list(range(1, chips // 2))
+    return [0] + far[:2] + near[:2] + far[2:] + near[2:]
+
+
 def by_step(items):
-    return [items[-j % len(items)] for j in range(len(items))]
+    order = step_order(len(items))
+    return [items[order.index(j)] for j in range(len(items))]
+
+
+def in_order(items):
+    return [items[j] for j in step_order(len(items))]
 
 
 def pack_kernel(chips, *refs):
@@ -334,33 +344,44 @@
     bounds[...] = jnp.where(row == 0, held[0][0], jnp.where(row == 1, held[1][0], held[2][0]))
 
 
-def softmax_mix(query, key, value, scale, permit):
-    scores = lax.dot_general(
-        query, key, (((1,), (1,)), ((), ())), preferred_element_type=jnp.float32
-    )
-    scores = jnp.where(permit, scores * scale, -1e30)
-    peak = jnp.max(scores, axis=1, keepdims=True)
-    weights = jnp.exp(scores - peak)
-    total = jnp.sum(weights, axis=1, keepdims=True)
-    mixed = jnp.dot(weights.astype(jnp.bfloat16), value, preferred_element_type=jnp.float32)
-    return mixed / total
-
-
-def paired_mix(query, key, value, depth, permit):
-    scale = 1.0 / math.sqrt(depth)
-    lane = lax.broadcasted_iota(jnp.int32, query.shape, 1) // depth
+def mix_all(units):
+    scores = [
+        lax.dot_general(query, key, (((1,), (1,)), ((), ())), preferred_element_type=jnp.float32)
+        for query, key, value, depth, permit in units
+    ]
+    weights, totals = [], []
+    for score, (query, key, value, depth, permit) in zip(scores, units):
+        score = jnp.where(permit, score, -1e30)
+        peak = jnp.max(score, axis=1, keepdims=True)
+        weight = jnp.exp2((score - peak) * (math.log2(math.e) / math.sqrt(depth)))
+        totals.append(jnp.sum(weight, axis=1, keepdims=True))
+        weights.append(weight.astype(jnp.bfloat16))
+    return [
+        jnp.dot(weight, unit[2], preferred_element_type=jnp.float32) / total
+        for weight, total, unit in zip(weights, totals, units)
+    ]
+
+
+def pair_units(query, key, value, permit):
+    lane = lax.broadcasted_iota(jnp.int32, query.shape, 1) // HDA
     zero = jnp.zeros_like(query)
-    result = None
-    for h in range(LANES // depth):
-        one = softmax_mix(jnp.where(lane == h, query, zero), key, value, scale, permit)
-        result = one if h == 0 else jnp.where(lane == h, one, result)
+    return [
+        (jnp.where(lane == h, query, zero), key, value, HDA, permit) for h in range(LANES // HDA)
+    ]
+
+
+def pair_join(mixed):
+    lane = lax.broadcasted_iota(jnp.int32, mixed[0].shape, 1) // HDA
+    result = mixed[0]
+    for h in range(1, len(mixed)):
+        result = jnp.where(lane == h, mixed[h], result)
     return result
 
 
 def shares(chips):
-    turn = chips // 4
-    first = [j for j in range(chips) if (j // turn ^ j // (2 * turn)) % 2 == 0]
-    return [(j, j ^ turn) for j in first]
+    zero = list(range(chips - 1, 3 * chips // 4 - 1, -1)) + list(range(chips // 4 - 1, -1, -1))
+    one = list(range(3 * chips // 4 - 1, chips // 4 - 1, -1))
+    return list(zip(zero, one))
 
 
 def attend_kernel(chips, rows, parts, pairs, bounds, *refs):
@@ -411,14 +432,17 @@
 
     q_at, k_at = places(rows, rows)
     permit = k_at < video_valid
-    for h in range(parts):
-        mixed = softmax_mix(
+    units = [
+        (
             asked(h * rows),
             slab((parts + h) * rows),
             slab((2 * parts + h) * rows),
-            1.0 / math.sqrt(HDV),
+            HDV,
             permit,
         )
+        for h in range(parts)
+    ]
+    for h, mixed in enumerate(mix_all(units)):
         put(h * rows, mixed)
 
     cross = 3 * parts * rows
@@ -431,6 +455,7 @@
     q_at, k_at = places(half, rows)
     center = jnp.clip((q_at - offset) << bits, 0, video_valid - 1)
     toward_audio = (k_at < video_valid) & (jnp.abs(k_at - center) <= tv // 8)
+    units = []
     for p in range(pairs):
         at = cross + p * rows
         cross_query = asked(at)
@@ -444,10 +469,17 @@
         listen_query = split(asked(at))[1]
         at += pairs * rows
         sound_keys, sound_values = split(slab(at))
+        units += pair_units(cross_query, sound_keys, sound_values, toward_video)
+        units += pair_units(audio_query, audio_keys, audio_values, within_audio)
+        units += pair_units(listen_query, cross_keys, cross_values, toward_audio)
+    mixed = mix_all(units)
+    heads = LANES // HDA
+    for p in range(pairs):
+        seen, heard, listened = (
+            pair_join(mixed[(3 * p + i) * heads : (3 * p + i + 1) * heads]) for i in range(3)
+        )
         out = (parts + p) * rows
-        put(out, paired_mix(cross_query, sound_keys, sound_values, HDA, toward_video))
-        heard = paired_mix(audio_query, audio_keys, audio_values, HDA, within_audio)
-        listened = paired_mix(listen_query, cross_keys, cross_values, HDA, toward_audio)
+        put(out, seen)
         both = jnp.concatenate(
             [heard.reshape(-1, half, LANES), listened.reshape(-1, half, LANES)], axis=1
         )
@@ -544,7 +576,7 @@
         in_specs=[vmem] * (1 + 2 * chips),
         out_specs=[vmem] * len(share),
         compiler_params=params,
-    )(bounds, *by_step(own), *by_step(other))
+    )(bounds, *in_order(own), *in_order(other))
     back = [
         lax.ppermute(piece, "seq", [(i, i ^ 2 * pair[i % 2]) for i in range(n)])
         for piece, pair in zip(done, share)

time: 47.1 us -> 42.8 us (0.909)
  starting transfers between devices: 27.7 us -> 24.7 us
  Pallas kernels: 6.84 us -> 4.61 us
  waiting for transfers between devices: 8.59 us -> 9.55 us
    ppermute x19, starting transfers between devices: 21.7 us -> 18.7 us  [swap(): return lax.ppermute(piece, 'seq', [(i, i ^ step) for i in range(n)])]
    pallas_call x1, Pallas kernels: 3.18 us -> 0.95 us  [shards_packed(): pl.pallas_call(functools.partial(attend_kernel, chips, rows, parts, pairs...]
    ppermute x4, waiting for transfers between devices: 3.26 us -> 4.26 us  [shards_packed(): lax.ppermute(piece, 'seq', [(i, i ^ 2 * pair[i % 2]) for i in range(n)])]
  transfers between devices with their start and end apart: 23 -> 23, of which waited for: 11 -> 12; matrix products, arithmetic and copies ran while one was open for 0% -> 0% of each run, Pallas kernels for 2% -> 2%
where the time goes in v7:
time: 42.8 us; the launch traced here: 42.5 us
  starting transfers between devices  24.7 us (58%)
  waiting for transfers between devices  9.55 us (22%)
  Pallas kernels  4.61 us (11%)
  between operations  2.65 us (6%)
  local copies, waits for them, and re-layouts  1.06 us (2%)
    ppermute x19, starting transfers between devices, swap(): return lax.ppermute(piece, 'seq', [(i, i ^ step) for i in range(n)])  18.7 us
    ppermute x4, starting transfers between devices, shards_packed(): lax.ppermute(piece, 'seq', [(i, i ^ 2 * pair[i % 2]) for i in range(n)])  6 us
    ppermute x19, waiting for transfers between devices, swap(): return lax.ppermute(piece, 'seq', [(i, i ^ step) for i in range(n)])  5.3 us
    ppermute x4, waiting for transfers between devices, shards_packed(): lax.ppermute(piece, 'seq', [(i, i ^ 2 * pair[i % 2]) for i in range(n)])  4.26 us
    pallas_call x1, Pallas kernels, shards_packed(): pl.pallas_call(functools.partial(pack_kernel, chips), out_shape=[buffer((...  2.18 us
    unnamed x4, local copies, waits for them, and re-layouts  1.06 us
    pallas_call x1, Pallas kernels, shards_packed(): pl.pallas_call(functools.partial(attend_kernel, chips, rows, parts, pairs...  0.95 us
  transfers between devices with their start and end apart: 23, of which 12 were waited for; matrix products, arithmetic and copies ran while one was open for 0% of the time, Pallas kernels for 2%

profile of v7, /device:TPU:0, one launch (start us, length us, event | category | flops | bytes accessed | tf_op | source)
XLA Modules:
  0.0 42.5 jit_solution(11566817044723716823)
XLA Ops:
  0.6 2.2 %shard_map.174 = (bf16[384,128]{1,0:T(8,128)(2,1)}, bf16[384,128]{1,0:T(8,128)(2,1)}, bf16[384,128]{1,0:T(8,128)(2,1)}, bf16[384,128]{1,0:T(8,128)(2,1)}, bf16[3...) custom-call(bf16[16,4096]{1,0:T(8,128)(2,1)} %refs_0_.1, ...), custom_call_target="tpu_custom_call" | custom-call | tf_op jit(solution)/shard_map/pallas_call | solution.py:551
  2.8 6.1 %collective-permute-start = (bf16[384,128]{1,0:T(8,128)(2,1)}, bf16[384,128]{1,0:T(8,128)(2,1)S(1)}, u32[]{:S(2)}, u32[]{:S(2)}) collective-permute-start(bf16[384,128]{1,0:T(8,128)(2,1)} %get-tuple-element.19), channel_id=1, source_target_pairs={{0,14},{1,15},{2,12},{3,13},{4,10},{5,11},{6,8},{7,9},{8,6},{9,7},... | collective-permute-start | bytes 294920 | tf_op jit(solution)/shard_map/ppermute | solution.py:522
  8.9 0.2 collective-permute-start.1
  9.1 0.4 collective-permute-start.2
  9.5 0.0 collective-permute-start.3
  9.5 5.2 %collective-permute-start.4 = (bf16[384,128]{1,0:T(8,128)(2,1)}, bf16[384,128]{1,0:T(8,128)(2,1)S(1)}, u32[]{:S(2)}, u32[]{:S(2)}) collective-permute-start(bf16[384,128]{1,0:T(8,128)(2,1)} %get-tuple-element.25), channel_id=1, source_target_pairs={{0,10},{1,11},{2,8},{3,9},{4,14},{5,15},{6,12},{7,13},{8,2},{9,3},... | collective-permute-start | bytes 294920 | tf_op jit(solution)/shard_map/ppermute | solution.py:522
  16.7 0.0 collective-permute-done.after.refs_1_
  16.7 1.5 %collective-permute-start.5 = (bf16[384,128]{1,0:T(8,128)(2,1)}, bf16[384,128]{1,0:T(8,128)(2,1)S(1)}, u32[]{:S(2)}, u32[]{:S(2)}) collective-permute-start(bf16[384,128]{1,0:T(8,128)(2,1)} %get-tuple-element.26), channel_id=1, source_target_pairs={{0,8},{1,9},{2,10},{3,11},{4,12},{5,13},{6,14},{7,15},{8,0},{9,1},... | collective-permute-start | bytes 294920 | tf_op jit(solution)/shard_map/ppermute | solution.py:522
  18.2 0.0 copy-start
  18.2 0.9 %copy-done = bf16[384,128]{1,0:T(8,128)(2,1)S(1)} copy-done((bf16[384,128]{1,0:T(8,128)(2,1)S(1)}, bf16[384,128]{1,0:T(8,128)(2,1)}, u32[]{:S(2)}) %copy-start) | copy-done | bytes 98328
  19.1 0.0 copy-start.1
  19.1 0.7 %shard_map.175 = (bf16[384,128]{1,0:T(8,128)(2,1)S(1)}, s32[8,128]{1,0:T(8,128)S(1)}) custom-call(bf16[384,128]{1,0:T(8,128)(2,1)S(1)} %copy-done, s32[1]{0:T(128)S(6)} %copy.19.video_len, s32[1]{0:T(128)S(6)} %copy.20.audio_len, s32[1]{0:T(128)S(6)} %copy.21.shift, bf16[384,128]{1,0:T(8,128)(2,1)S(1)} %collective-permute-done.after.refs_1_), custom_call_target="tpu_custom_call" | custom-call | tf_op jit(solution)/shard_map/pallas_call | solution.py:562
  19.8 0.0 collective-permute-done.1.refs_2_
  19.8 0.2 copy-done.1
  20.0 3.1 %collective-permute-start.6 = (bf16[384,128]{1,0:T(8,128)(2,1)S(1)}, bf16[384,128]{1,0:T(8,128)(2,1)S(1)}, u32[]{:S(2)}, u32[]{:S(2)}) collective-permute-start(bf16[384,128]{1,0:T(8,128)(2,1)S(1)} %copy-done.1), channel_id=1, source_target_pairs={{0,6},{1,7},{2,4},{3,5},{4,2},{5,3},{6,0},{7,1},{8,14},{9,15},{10,... | collective-permute-start | bytes 294920 | tf_op jit(solution)/shard_map/ppermute | solution.py:522
  23.1 0.0 collective-permute-done.2.refs_3_
  23.1 0.0 collective-permute-start.7
  23.1 0.0 collective-permute-done.3.refs_4_
  23.1 0.5 %collective-permute-start.8 = (bf16[384,128]{1,0:T(8,128)(2,1)S(1)}, bf16[384,128]{1,0:T(8,128)(2,1)S(1)}, u32[]{:S(2)}, u32[]{:S(2)}) collective-permute-start(bf16[384,128]{1,0:T(8,128)(2,1)S(1)} %collective-permute-done.after.refs_1_), channel_id=1, source_target_pairs={{0,1},{1,0},{2,3},{3,2},{4,5},{5,4},{6,7},{7,6},{8,9},{9,8},{10,11... | collective-permute-start | bytes 294920 | tf_op jit(solution)/shard_map/ppermute | solution.py:522
  23.6 1.0 %collective-permute-done.4.refs_5_ = bf16[384,128]{1,0:T(8,128)(2,1)S(1)} collective-permute-done((bf16[384,128]{1,0:T(8,128)(2,1)}, bf16[384,128]{1,0:T(8,128)(2,1)S(1)}, u32[]{:S(2)}, u32[]{:S(2)}) %collective-permute-start.4) | collective-permute-done | bytes 98336 | tf_op jit(solution)/shard_map/ppermute | solution.py:522
  24.7 0.0 collective-permute-start.9
  24.7 1.2 %collective-permute-done.5.refs_6_ = bf16[384,128]{1,0:T(8,128)(2,1)S(1)} collective-permute-done((bf16[384,128]{1,0:T(8,128)(2,1)}, bf16[384,128]{1,0:T(8,128)(2,1)S(1)}, u32[]{:S(2)}, u32[]{:S(2)}) %collective-permute-start.5) | collective-permute-done | bytes 98336 | tf_op jit(solution)/shard_map/ppermute | solution.py:522
  25.9 0.0 collective-permute-start.10
  25.9 0.9 %collective-permute-done.6.refs_7_ = bf16[384,128]{1,0:T(8,128)(2,1)S(1)} collective-permute-done((bf16[384,128]{1,0:T(8,128)(2,1)S(1)}, bf16[384,128]{1,0:T(8,128)(2,1)S(1)}, u32[]{:S(2)}, u32[]{:S(2)}) %collective-permute-start.6) | collective-permute-done | bytes 98336 | tf_op jit(solution)/shard_map/ppermute | solution.py:522
  26.8 0.0 collective-permute-start.11
  26.8 0.0 collective-permute-done.7.refs_8_
  26.8 0.5 %collective-permute-start.12 = (bf16[384,128]{1,0:T(8,128)(2,1)S(1)}, bf16[384,128]{1,0:T(8,128)(2,1)S(1)}, u32[]{:S(2)}, u32[]{:S(2)}) collective-permute-start(bf16[384,128]{1,0:T(8,128)(2,1)S(1)} %collective-permute-done.4.refs_5_), channel_id=1, source_target_pairs={{0,1},{1,0},{2,3},{3,2},{4,5},{5,4},{6,7},{7,6},{8,9},{9,8},{10,11... | collective-permute-start | bytes 294920 | tf_op jit(solution)/shard_map/ppermute | solution.py:522
  27.3 0.0 collective-permute-done.8.refs_9_
  27.3 0.1 collective-permute-start.13
  27.4 0.0 collective-permute-done.9.refs_10_
  27.4 0.4 %collective-permute-start.14 = (bf16[384,128]{1,0:T(8,128)(2,1)S(1)}, bf16[384,128]{1,0:T(8,128)(2,1)S(1)}, u32[]{:S(2)}, u32[]{:S(2)}) collective-permute-start(bf16[384,128]{1,0:T(8,128)(2,1)S(1)} %collective-permute-done.6.refs_7_), channel_id=1, source_target_pairs={{0,1},{1,0},{2,3},{3,2},{4,5},{5,4},{6,7},{7,6},{8,9},{9,8},{10,11... | collective-permute-start | bytes 294920 | tf_op jit(solution)/shard_map/ppermute | solution.py:522
  27.8 0.0 collective-permute-done.10.refs_11_
  27.8 0.3 collective-permute-done.11.refs_12_
  28.1 0.2 collective-permute-done.12.refs_13_
  28.3 0.4 collective-permute-done.13.refs_14_
  28.6 0.2 collective-permute-done.14.refs_15_
  28.8 0.9 %shard_map.176 = (bf16[256,128]{1,0:T(8,128)(2,1)S(1)}, bf16[256,128]{1,0:T(8,128)(2,1)S(1)}, bf16[256,128]{1,0:T(8,128)(2,1)S(1)}, bf16[256,128]{1,0:T(8,128)(2,1)S(1)}) custom-call(s32[8,128]{1,0:T(8,128)S(1)} %get-tuple-element.20.bounds, bf16[384,128]{1,0:T(8,128)(2,1)S(1)} %get-tuple-element.21.refs_0_, ...), custom_call_target="tpu_custom_call" | custom-call | tf_op jit(solution)/shard_map/pallas_call | solution.py:573
  29.7 3.5 %collective-permute-start.15 = (bf16[256,128]{1,0:T(8,128)(2,1)S(1)}, bf16[256,128]{1,0:T(8,128)(2,1)S(1)}, u32[]{:S(2)}, u32[]{:S(2)}) collective-permute-start(bf16[256,128]{1,0:T(8,128)(2,1)S(1)} %get-tuple-element.28), channel_id=1, source_target_pairs={{0,14},{1,11},{2,12},{3,9},{4,10},{5,15},{6,8},{7,13},{8,6},{9,3},... | collective-permute-start | bytes 196616 | tf_op jit(solution)/shard_map/ppermute | solution.py:581
  33.2 1.4 %collective-permute-start.16 = (bf16[256,128]{1,0:T(8,128)(2,1)S(1)}, bf16[256,128]{1,0:T(8,128)(2,1)S(1)}, u32[]{:S(2)}, u32[]{:S(2)}) collective-permute-start(bf16[256,128]{1,0:T(8,128)(2,1)S(1)} %get-tuple-element.29), channel_id=1, source_target_pairs={{0,12},{1,9},{2,14},{3,11},{4,8},{5,13},{6,10},{7,15},{8,4},{9,1},... | collective-permute-start | bytes 196616 | tf_op jit(solution)/shard_map/ppermute | solution.py:581
  34.6 0.5 %collective-permute-start.17 = (bf16[256,128]{1,0:T(8,128)(2,1)S(1)}, bf16[256,128]{1,0:T(8,128)(2,1)S(1)}, u32[]{:S(2)}, u32[]{:S(2)}) collective-permute-start(bf16[256,128]{1,0:T(8,128)(2,1)S(1)} %get-tuple-element.30), channel_id=1, source_target_pairs={{0,2},{1,7},{2,0},{3,5},{4,6},{5,3},{6,4},{7,1},{8,10},{9,15},{10,... | collective-permute-start | bytes 196616 | tf_op jit(solution)/shard_map/ppermute | solution.py:581
  35.1 0.7 %collective-permute-start.18 = (bf16[256,128]{1,0:T(8,128)(2,1)S(1)}, bf16[256,128]{1,0:T(8,128)(2,1)S(1)}, u32[]{:S(2)}, u32[]{:S(2)}) collective-permute-start(bf16[256,128]{1,0:T(8,128)(2,1)S(1)} %get-tuple-element.31), channel_id=1, source_target_pairs={{0,0},{1,5},{2,2},{3,7},{4,4},{5,1},{6,6},{7,3},{8,8},{9,13},{10,1... | collective-permute-start | bytes 196616 | tf_op jit(solution)/shard_map/ppermute | solution.py:581
  35.7 1.8 %collective-permute-done.15.refs_0_ = bf16[256,128]{1,0:T(8,128)(2,1)S(1)} collective-permute-done((bf16[256,128]{1,0:T(8,128)(2,1)S(1)}, bf16[256,128]{1,0:T(8,128)(2,1)S(1)}, u32[]{:S(2)}, u32[]{:S(2)}) %collective-permute-start.15) | collective-permute-done | bytes 65568 | tf_op jit(solution)/shard_map/ppermute | solution.py:581
  37.6 0.0 collective-permute-start.19
  37.6 2.4 %collective-permute-done.16.refs_1_ = bf16[256,128]{1,0:T(8,128)(2,1)S(1)} collective-permute-done((bf16[256,128]{1,0:T(8,128)(2,1)S(1)}, bf16[256,128]{1,0:T(8,128)(2,1)S(1)}, u32[]{:S(2)}, u32[]{:S(2)}) %collective-permute-start.16) | collective-permute-done | bytes 65568 | tf_op jit(solution)/shard_map/ppermute | solution.py:581
  40.0 0.0 collective-permute-start.20
  40.0 0.0 collective-permute-done.17.refs_2_
  40.0 0.5 %collective-permute-start.21 = (bf16[256,128]{1,0:T(8,128)(2,1)S(1)}, bf16[256,128]{1,0:T(8,128)(2,1)S(1)}, u32[]{:S(2)}, u32[]{:S(2)}) collective-permute-start(bf16[256,128]{1,0:T(8,128)(2,1)S(1)} %collective-permute-done.17.refs_2_), channel_id=1, source_target_pairs={{0,1},{1,0},{2,3},{3,2},{4,5},{5,4},{6,7},{7,6},{8,9},{9,8},{10,11... | collective-permute-start | bytes 196616 | tf_op jit(solution)/shard_map/ppermute | solution.py:522
  40.5 0.0 collective-permute-done.18.refs_3_
  40.5 0.1 collective-permute-start.22
  40.6 0.0 collective-permute-done.19.refs_4_
  40.6 0.7 %collective-permute-done.20.refs_5_ = bf16[256,128]{1,0:T(8,128)(2,1)S(1)} collective-permute-done((bf16[256,128]{1,0:T(8,128)(2,1)S(1)}, bf16[256,128]{1,0:T(8,128)(2,1)S(1)}, u32[]{:S(2)}, u32[]{:S(2)}) %collective-permute-start.20) | collective-permute-done | bytes 65568 | tf_op jit(solution)/shard_map/ppermute | solution.py:522
  41.3 0.2 collective-permute-done.21.refs_6_
  41.4 0.4 collective-permute-done.22.refs_7_
  41.8 0.8 %shard_map.177 = (bf16[16,4096]{1,0:T(8,128)(2,1)}, bf16[8,2048]{1,0:T(8,128)(2,1)}, bf16[16,2048]{1,0:T(8,128)(2,1)}, bf16[8,2048]{1,0:T(8,128)(2,1)}) custom-call(bf16[256,128]{1,0:T(8,128)(2,1)S(1)} %collective-permute-done.15.refs_0_, bf16[256,128]{1,0:T(8,128)(2,1)S(1)} %collective-permute-done.16.refs_1_, ...), custom_call_target="tpu_custom_call" | custom-call | tf_op jit(solution)/shard_map/pallas_call | solution.py:584
Async XLA Ops:
  2.8 13.9 %collective-permute-start = (bf16[384,128]{1,0:T(8,128)(2,1)}, bf16[384,128]{1,0:T(8,128)(2,1)S(1)}, u32[]{:S(2)}, u32[]{:S(2)}) collective-permute-start(bf16[384,128]{1,0:T(8,128)(2,1)} %get-tuple-element.19), channel_id=1, source_target_pairs={{0,14},{1,15},{2,12},{3,13},{4,10},{5,11},{6,8},{7,9},{8,6},{9,7},... | collective-permute-start | bytes 294920 | tf_op jit(solution)/shard_map/ppermute | solution.py:522
  8.9 10.9 %collective-permute-start.1 = (bf16[384,128]{1,0:T(8,128)(2,1)}, bf16[384,128]{1,0:T(8,128)(2,1)S(1)}, u32[]{:S(2)}, u32[]{:S(2)}) collective-permute-start(bf16[384,128]{1,0:T(8,128)(2,1)} %get-tuple-element.22), channel_id=1, source_target_pairs={{0,12},{1,13},{2,14},{3,15},{4,8},{5,9},{6,10},{7,11},{8,4},{9,5},... | collective-permute-start | bytes 294920 | tf_op jit(solution)/shard_map/ppermute | solution.py:522
  9.1 14.0 %collective-permute-start.2 = (bf16[384,128]{1,0:T(8,128)(2,1)}, bf16[384,128]{1,0:T(8,128)(2,1)S(1)}, u32[]{:S(2)}, u32[]{:S(2)}) collective-permute-start(bf16[384,128]{1,0:T(8,128)(2,1)} %get-tuple-element.23), channel_id=1, source_target_pairs={{0,2},{1,3},{2,0},{3,1},{4,6},{5,7},{6,4},{7,5},{8,10},{9,11},{10,... | collective-permute-start | bytes 294920 | tf_op jit(solution)/shard_map/ppermute | solution.py:522
  9.5 13.6 %collective-permute-start.3 = (bf16[384,128]{1,0:T(8,128)(2,1)}, bf16[384,128]{1,0:T(8,128)(2,1)S(1)}, u32[]{:S(2)}, u32[]{:S(2)}) collective-permute-start(bf16[384,128]{1,0:T(8,128)(2,1)} %get-tuple-element.24), channel_id=1, source_target_pairs={{0,4},{1,5},{2,6},{3,7},{4,0},{5,1},{6,2},{7,3},{8,12},{9,13},{10,... | collective-permute-start | bytes 294920 | tf_op jit(solution)/shard_map/ppermute | solution.py:522
  9.5 15.1 %collective-permute-start.4 = (bf16[384,128]{1,0:T(8,128)(2,1)}, bf16[384,128]{1,0:T(8,128)(2,1)S(1)}, u32[]{:S(2)}, u32[]{:S(2)}) collective-permute-start(bf16[384,128]{1,0:T(8,128)(2,1)} %get-tuple-element.25), channel_id=1, source_target_pairs={{0,10},{1,11},{2,8},{3,9},{4,14},{5,15},{6,12},{7,13},{8,2},{9,3},... | collective-permute-start | bytes 294920 | tf_op jit(solution)/shard_map/ppermute | solution.py:522
  16.7 9.2 %collective-permute-start.5 = (bf16[384,128]{1,0:T(8,128)(2,1)}, bf16[384,128]{1,0:T(8,128)(2,1)S(1)}, u32[]{:S(2)}, u32[]{:S(2)}) collective-permute-start(bf16[384,128]{1,0:T(8,128)(2,1)} %get-tuple-element.26), channel_id=1, source_target_pairs={{0,8},{1,9},{2,10},{3,11},{4,12},{5,13},{6,14},{7,15},{8,0},{9,1},... | collective-permute-start | bytes 294920 | tf_op jit(solution)/shard_map/ppermute | solution.py:522
  18.2 0.9 %copy-start = (bf16[384,128]{1,0:T(8,128)(2,1)S(1)}, bf16[384,128]{1,0:T(8,128)(2,1)}, u32[]{:S(2)}) copy-start(bf16[384,128]{1,0:T(8,128)(2,1)} %get-tuple-element.18.source) | copy-start | bytes 294916
  19.1 0.9 %copy-start.1 = (bf16[384,128]{1,0:T(8,128)(2,1)S(1)}, bf16[384,128]{1,0:T(8,128)(2,1)}, u32[]{:S(2)}) copy-start(bf16[384,128]{1,0:T(8,128)(2,1)} %get-tuple-element.27) | copy-start | bytes 294916
  20.0 6.8 %collective-permute-start.6 = (bf16[384,128]{1,0:T(8,128)(2,1)S(1)}, bf16[384,128]{1,0:T(8,128)(2,1)S(1)}, u32[]{:S(2)}, u32[]{:S(2)}) collective-permute-start(bf16[384,128]{1,0:T(8,128)(2,1)S(1)} %copy-done.1), channel_id=1, source_target_pairs={{0,6},{1,7},{2,4},{3,5},{4,2},{5,3},{6,0},{7,1},{8,14},{9,15},{10,... | collective-permute-start | bytes 294920 | tf_op jit(solution)/shard_map/ppermute | solution.py:522
  23.1 3.7 %collective-permute-start.7 = (bf16[384,128]{1,0:T(8,128)(2,1)S(1)}, bf16[384,128]{1,0:T(8,128)(2,1)S(1)}, u32[]{:S(2)}, u32[]{:S(2)}) collective-permute-start(bf16[384,128]{1,0:T(8,128)(2,1)S(1)} %get-tuple-element.21.refs_0_), channel_id=1, source_target_pairs={{0,1},{1,0},{2,3},{3,2},{4,5},{5,4},{6,7},{7,6},{8,9},{9,8},{10,11... | collective-permute-start | bytes 294920 | tf_op jit(solution)/shard_map/ppermute | solution.py:522
  23.1 4.2 %collective-permute-start.8 = (bf16[384,128]{1,0:T(8,128)(2,1)S(1)}, bf16[384,128]{1,0:T(8,128)(2,1)S(1)}, u32[]{:S(2)}, u32[]{:S(2)}) collective-permute-start(bf16[384,128]{1,0:T(8,128)(2,1)S(1)} %collective-permute-done.after.refs_1_), channel_id=1, source_target_pairs={{0,1},{1,0},{2,3},{3,2},{4,5},{5,4},{6,7},{7,6},{8,9},{9,8},{10,11... | collective-permute-start | bytes 294920 | tf_op jit(solution)/shard_map/ppermute | solution.py:522
  24.7 2.7 %collective-permute-start.9 = (bf16[384,128]{1,0:T(8,128)(2,1)S(1)}, bf16[384,128]{1,0:T(8,128)(2,1)S(1)}, u32[]{:S(2)}, u32[]{:S(2)}) collective-permute-start(bf16[384,128]{1,0:T(8,128)(2,1)S(1)} %collective-permute-done.1.refs_2_), channel_id=1, source_target_pairs={{0,1},{1,0},{2,3},{3,2},{4,5},{5,4},{6,7},{7,6},{8,9},{9,8},{10,11... | collective-permute-start | bytes 294920 | tf_op jit(solution)/shard_map/ppermute | solution.py:522
  25.9 1.9 %collective-permute-start.10 = (bf16[384,128]{1,0:T(8,128)(2,1)S(1)}, bf16[384,128]{1,0:T(8,128)(2,1)S(1)}, u32[]{:S(2)}, u32[]{:S(2)}) collective-permute-start(bf16[384,128]{1,0:T(8,128)(2,1)S(1)} %collective-permute-done.2.refs_3_), channel_id=1, source_target_pairs={{0,1},{1,0},{2,3},{3,2},{4,5},{5,4},{6,7},{7,6},{8,9},{9,8},{10,11... | collective-permute-start | bytes 294920 | tf_op jit(solution)/shard_map/ppermute | solution.py:522
  26.8 1.3 %collective-permute-start.11 = (bf16[384,128]{1,0:T(8,128)(2,1)S(1)}, bf16[384,128]{1,0:T(8,128)(2,1)S(1)}, u32[]{:S(2)}, u32[]{:S(2)}) collective-permute-start(bf16[384,128]{1,0:T(8,128)(2,1)S(1)} %collective-permute-done.3.refs_4_), channel_id=1, source_target_pairs={{0,1},{1,0},{2,3},{3,2},{4,5},{5,4},{6,7},{7,6},{8,9},{9,8},{10,11... | collective-permute-start | bytes 294920 | tf_op jit(solution)/shard_map/ppermute | solution.py:522
  26.8 1.5 %collective-permute-start.12 = (bf16[384,128]{1,0:T(8,128)(2,1)S(1)}, bf16[384,128]{1,0:T(8,128)(2,1)S(1)}, u32[]{:S(2)}, u32[]{:S(2)}) collective-permute-start(bf16[384,128]{1,0:T(8,128)(2,1)S(1)} %collective-permute-done.4.refs_5_), channel_id=1, source_target_pairs={{0,1},{1,0},{2,3},{3,2},{4,5},{5,4},{6,7},{7,6},{8,9},{9,8},{10,11... | collective-permute-start | bytes 294920 | tf_op jit(solution)/shard_map/ppermute | solution.py:522
  27.3 1.3 %collective-permute-start.13 = (bf16[384,128]{1,0:T(8,128)(2,1)S(1)}, bf16[384,128]{1,0:T(8,128)(2,1)S(1)}, u32[]{:S(2)}, u32[]{:S(2)}) collective-permute-start(bf16[384,128]{1,0:T(8,128)(2,1)S(1)} %collective-permute-done.5.refs_6_), channel_id=1, source_target_pairs={{0,1},{1,0},{2,3},{3,2},{4,5},{5,4},{6,7},{7,6},{8,9},{9,8},{10,11... | collective-permute-start | bytes 294920 | tf_op jit(solution)/shard_map/ppermute | solution.py:522
  27.4 1.4 %collective-permute-start.14 = (bf16[384,128]{1,0:T(8,128)(2,1)S(1)}, bf16[384,128]{1,0:T(8,128)(2,1)S(1)}, u32[]{:S(2)}, u32[]{:S(2)}) collective-permute-start(bf16[384,128]{1,0:T(8,128)(2,1)S(1)} %collective-permute-done.6.refs_7_), channel_id=1, source_target_pairs={{0,1},{1,0},{2,3},{3,2},{4,5},{5,4},{6,7},{7,6},{8,9},{9,8},{10,11... | collective-permute-start | bytes 294920 | tf_op jit(solution)/shard_map/ppermute | solution.py:522
  29.7 7.8 %collective-permute-start.15 = (bf16[256,128]{1,0:T(8,128)(2,1)S(1)}, bf16[256,128]{1,0:T(8,128)(2,1)S(1)}, u32[]{:S(2)}, u32[]{:S(2)}) collective-permute-start(bf16[256,128]{1,0:T(8,128)(2,1)S(1)} %get-tuple-element.28), channel_id=1, source_target_pairs={{0,14},{1,11},{2,12},{3,9},{4,10},{5,15},{6,8},{7,13},{8,6},{9,3},... | collective-permute-start | bytes 196616 | tf_op jit(solution)/shard_map/ppermute | solution.py:581
  33.2 6.8 %collective-permute-start.16 = (bf16[256,128]{1,0:T(8,128)(2,1)S(1)}, bf16[256,128]{1,0:T(8,128)(2,1)S(1)}, u32[]{:S(2)}, u32[]{:S(2)}) collective-permute-start(bf16[256,128]{1,0:T(8,128)(2,1)S(1)} %get-tuple-element.29), channel_id=1, source_target_pairs={{0,12},{1,9},{2,14},{3,11},{4,8},{5,13},{6,10},{7,15},{8,4},{9,1},... | collective-permute-start | bytes 196616 | tf_op jit(solution)/shard_map/ppermute | solution.py:581
  34.6 5.4 %collective-permute-start.17 = (bf16[256,128]{1,0:T(8,128)(2,1)S(1)}, bf16[256,128]{1,0:T(8,128)(2,1)S(1)}, u32[]{:S(2)}, u32[]{:S(2)}) collective-permute-start(bf16[256,128]{1,0:T(8,128)(2,1)S(1)} %get-tuple-element.30), channel_id=1, source_target_pairs={{0,2},{1,7},{2,0},{3,5},{4,6},{5,3},{6,4},{7,1},{8,10},{9,15},{10,... | collective-permute-start | bytes 196616 | tf_op jit(solution)/shard_map/ppermute | solution.py:581
  35.1 5.4 %collective-permute-start.18 = (bf16[256,128]{1,0:T(8,128)(2,1)S(1)}, bf16[256,128]{1,0:T(8,128)(2,1)S(1)}, u32[]{:S(2)}, u32[]{:S(2)}) collective-permute-start(bf16[256,128]{1,0:T(8,128)(2,1)S(1)} %get-tuple-element.31), channel_id=1, source_target_pairs={{0,0},{1,5},{2,2},{3,7},{4,4},{5,1},{6,6},{7,3},{8,8},{9,13},{10,1... | collective-permute-start | bytes 196616 | tf_op jit(solution)/shard_map/ppermute | solution.py:581
  37.6 3.0 %collective-permute-start.19 = (bf16[256,128]{1,0:T(8,128)(2,1)S(1)}, bf16[256,128]{1,0:T(8,128)(2,1)S(1)}, u32[]{:S(2)}, u32[]{:S(2)}) collective-permute-start(bf16[256,128]{1,0:T(8,128)(2,1)S(1)} %collective-permute-done.15.refs_0_), channel_id=1, source_target_pairs={{0,1},{1,0},{2,3},{3,2},{4,5},{5,4},{6,7},{7,6},{8,9},{9,8},{10,11... | collective-permute-start | bytes 196616 | tf_op jit(solution)/shard_map/ppermute | solution.py:522
  40.0 1.3 %collective-permute-start.20 = (bf16[256,128]{1,0:T(8,128)(2,1)S(1)}, bf16[256,128]{1,0:T(8,128)(2,1)S(1)}, u32[]{:S(2)}, u32[]{:S(2)}) collective-permute-start(bf16[256,128]{1,0:T(8,128)(2,1)S(1)} %collective-permute-done.16.refs_1_), channel_id=1, source_target_pairs={{0,1},{1,0},{2,3},{3,2},{4,5},{5,4},{6,7},{7,6},{8,9},{9,8},{10,11... | collective-permute-start | bytes 196616 | tf_op jit(solution)/shard_map/ppermute | solution.py:522
  40.0 1.4 %collective-permute-start.21 = (bf16[256,128]{1,0:T(8,128)(2,1)S(1)}, bf16[256,128]{1,0:T(8,128)(2,1)S(1)}, u32[]{:S(2)}, u32[]{:S(2)}) collective-permute-start(bf16[256,128]{1,0:T(8,128)(2,1)S(1)} %collective-permute-done.17.refs_2_), channel_id=1, source_target_pairs={{0,1},{1,0},{2,3},{3,2},{4,5},{5,4},{6,7},{7,6},{8,9},{9,8},{10,11... | collective-permute-start | bytes 196616 | tf_op jit(solution)/shard_map/ppermute | solution.py:522
  40.5 1.3 %collective-permute-start.22 = (bf16[256,128]{1,0:T(8,128)(2,1)S(1)}, bf16[256,128]{1,0:T(8,128)(2,1)S(1)}, u32[]{:S(2)}, u32[]{:S(2)}) collective-permute-start(bf16[256,128]{1,0:T(8,128)(2,1)S(1)} %collective-permute-done.18.refs_3_), channel_id=1, source_target_pairs={{0,1},{1,0},{2,3},{3,2},{4,5},{5,4},{6,7},{7,6},{8,9},{9,8},{10,11... | collective-permute-start | bytes 196616 | tf_op jit(solution)/shard_map/ppermute | solution.py:522

commit v8 on v7

--- a/solution.py
+++ b/solution.py
@@ -291,7 +291,7 @@
 
 def step_order(chips):
     far, near = list(range(chips - 1, chips // 2 - 1, -1)), list(range(1, chips // 2))
-    return [0] + far[:2] + near[:2] + far[2:] + near[2:]
+    return [0] + near[:1] + far[:2] + near[1:2] + far[2:] + near[2:]
 
 
 def by_step(items):
@@ -335,13 +335,9 @@
             at += rows
 
 
-def keep_kernel(source, video_len, audio_len, shift, after, kept, bounds, *scratch):
-    held, arrived = scratch[:3], scratch[3]
-    copies = fetch((source, video_len, audio_len, shift), (kept, *held), arrived)
-    for copy in copies:
-        copy.wait()
+def bounds_kernel(video_len, audio_len, shift, after, slab, bounds, same):
     row = lax.broadcasted_iota(jnp.int32, bounds.shape, 0)
-    bounds[...] = jnp.where(row == 0, held[0][0], jnp.where(row == 1, held[1][0], held[2][0]))
+    bounds[...] = jnp.where(row == 0, video_len[0], jnp.where(row == 1, audio_len[0], shift[0]))
 
 
 def mix_all(units):
@@ -537,6 +533,7 @@
     pairs = audio_query.shape[1] // chips // LANES
     vmem = pl.BlockSpec(memory_space=pltpu.VMEM)
     hbm = pl.BlockSpec(memory_space=pltpu.HBM)
+    smem = pl.BlockSpec(memory_space=pltpu.SMEM)
     params = pltpu.CompilerParams(vmem_limit_bytes=32 * 1024 * 1024)
 
     def buffer(*shape):
@@ -550,23 +547,27 @@
     )
     packed = pl.pallas_call(
         functools.partial(pack_kernel, chips),
-        out_shape=[buffer((3 * parts + 6 * pairs) * rows, LANES)] * chips,
+        out_shape=[pltpu.VMEM(((3 * parts + 6 * pairs) * rows, LANES), jnp.bfloat16)] * chips,
         in_specs=[hbm] * 12,
         out_specs=[vmem] * chips,
         scratch_shapes=[pltpu.VMEM(source.shape, source.dtype) for source in sources]
         + [pltpu.SemaphoreType.DMA((12,))],
-        compiler_params=pltpu.CompilerParams(vmem_limit_bytes=60 * 1024 * 1024),
-    )(*sources)
+        compiler_params=params,
+    )(*[pltpu.with_memory_space_constraint(source, pltpu.HBM) for source in sources])
     packed = by_step(packed)
     moved = [swap(packed[j], n, 2 * j) for j in range(1, chips)]
-    kept, bounds = pl.pallas_call(
-        keep_kernel,
-        out_shape=(packed[0], jax.ShapeDtypeStruct((8, LANES), jnp.int32)),
-        in_specs=[hbm] * 4 + [pl.BlockSpec(memory_space=pl.ANY)],
-        out_specs=(vmem, vmem),
-        scratch_shapes=[pltpu.SMEM((1,), jnp.int32)] * 3 + [pltpu.SemaphoreType.DMA((4,))],
+    anywhere = pl.BlockSpec(memory_space=pl.ANY)
+    bounds, kept = pl.pallas_call(
+        bounds_kernel,
+        out_shape=(
+            pltpu.VMEM((8, LANES), jnp.int32),
+            pltpu.VMEM(packed[0].shape, packed[0].dtype),
+        ),
+        in_specs=[smem] * 3 + [anywhere] * 2,
+        out_specs=(vmem, anywhere),
+        input_output_aliases={4: 1},
         compiler_params=params,
-    )(packed[0], video_length, audio_length, align_offset, moved[-1])
+    )(video_length, audio_length, align_offset, moved[0], packed[0])
     own = [kept] + moved
     other = [swap(piece, n, 1) for piece in own]
     share = shares(chips)

time: 42.8 us -> 40.6 us (0.949)
  waiting for transfers between devices: 9.55 us -> 13.4 us
  starting transfers between devices: 24.7 us -> 21.3 us
  Pallas kernels: 4.61 us -> 3.04 us
  local copies, waits for them, and re-layouts: 1.06 us -> 0 us
    ppermute x19, waiting for transfers between devices: 5.3 us -> 9.8 us  [swap(): return lax.ppermute(piece, 'seq', [(i, i ^ step) for i in range(n)])]
    ppermute x19, starting transfers between devices: 18.7 us -> 15.3 us  [swap(): return lax.ppermute(piece, 'seq', [(i, i ^ step) for i in range(n)])]
    pallas_call x2, Pallas kernels: 2.89 us -> 1.31 us  [the longest x1 1.31 us: shards_packed(): pl.pallas_call(functools.partial(pack_kernel, chips), out_shape=[pltpu.VM...]
    unnamed x4 -> x0, local copies, waits for them, and re-layouts: 1.06 us -> none
    ppermute x4, waiting for transfers between devices: 4.26 us -> 3.55 us  [shards_packed(): lax.ppermute(piece, 'seq', [(i, i ^ 2 * pair[i % 2]) for i in range(n)])]
  transfers between devices with their start and end apart: 23 -> 23, of which waited for: 12 -> 12; matrix products, arithmetic and copies ran while one was open for 0% -> 0% of each run, Pallas kernels for 2% -> 0%
where the time goes in v8:
time: 40.6 us; the launch traced here: 40.4 us
  starting transfers between devices  21.3 us (52%)
  waiting for transfers between devices  13.4 us (33%)
  Pallas kernels  3.04 us (7%)
  between operations  2.66 us (7%)
    ppermute x19, starting transfers between devices, swap(): return lax.ppermute(piece, 'seq', [(i, i ^ step) for i in range(n)])  15.3 us
    ppermute x19, waiting for transfers between devices, swap(): return lax.ppermute(piece, 'seq', [(i, i ^ step) for i in range(n)])  9.8 us
    ppermute x4, starting transfers between devices, shards_packed(): lax.ppermute(piece, 'seq', [(i, i ^ 2 * pair[i % 2]) for i in range(n)])  6 us
    ppermute x4, waiting for transfers between devices, shards_packed(): lax.ppermute(piece, 'seq', [(i, i ^ 2 * pair[i % 2]) for i in range(n)])  3.55 us
    pallas_call x1, Pallas kernels, shards_packed(): pl.pallas_call(functools.partial(pack_kernel, chips), out_shape=[pltpu.VM...  1.31 us
    pallas_call x1, Pallas kernels, shards_packed(): pl.pallas_call(functools.partial(attend_kernel, chips, rows, parts, pairs...  0.95 us
  transfers between devices with their start and end apart: 23, of which 12 were waited for; matrix products, arithmetic and copies ran while one was open for 0% of the time, Pallas kernels for 0%

profile of v8, /device:TPU:0, one launch (start us, length us, event | category | flops | bytes accessed | tf_op | source)
XLA Modules:
  0.0 40.4 jit_solution(749634887200112738)
XLA Ops:
  0.6 1.3 %shard_map.174 = (bf16[384,128]{1,0:T(8,128)(2,1)S(1)}, bf16[384,128]{1,0:T(8,128)(2,1)S(1)}, bf16[384,128]{1,0:T(8,128)(2,1)S(1)}, bf16[384,128]{1,0:T(8,128)(2...) custom-call(bf16[16,4096]{1,0:T(8,128)(2,1)} %refs_0_.1, ...), custom_call_target="tpu_custom_call" | custom-call | tf_op jit(solution)/shard_map/pallas_call | solution.py:548
  1.9 3.0 %collective-permute-start = (bf16[384,128]{1,0:T(8,128)(2,1)S(1)}, bf16[384,128]{1,0:T(8,128)(2,1)S(1)}, u32[]{:S(2)}, u32[]{:S(2)}) collective-permute-start(bf16[384,128]{1,0:T(8,128)(2,1)S(1)} %get-tuple-element.18), channel_id=1, source_target_pairs={{0,2},{1,3},{2,0},{3,1},{4,6},{5,7},{6,4},{7,5},{8,10},{9,11},{10,... | collective-permute-start | bytes 294920 | tf_op jit(solution)/shard_map/ppermute | solution.py:518
  5.0 3.5 %collective-permute-start.1 = (bf16[384,128]{1,0:T(8,128)(2,1)S(1)}, bf16[384,128]{1,0:T(8,128)(2,1)S(1)}, u32[]{:S(2)}, u32[]{:S(2)}) collective-permute-start(bf16[384,128]{1,0:T(8,128)(2,1)S(1)} %get-tuple-element.22), channel_id=1, source_target_pairs={{0,14},{1,15},{2,12},{3,13},{4,10},{5,11},{6,8},{7,9},{8,6},{9,7},... | collective-permute-start | bytes 294920 | tf_op jit(solution)/shard_map/ppermute | solution.py:518
  8.5 0.1 collective-permute-start.2
  8.6 0.0 collective-permute-start.3
  8.6 5.3 %collective-permute-start.4 = (bf16[384,128]{1,0:T(8,128)(2,1)S(1)}, bf16[384,128]{1,0:T(8,128)(2,1)S(1)}, u32[]{:S(2)}, u32[]{:S(2)}) collective-permute-start(bf16[384,128]{1,0:T(8,128)(2,1)S(1)} %get-tuple-element.25), channel_id=1, source_target_pairs={{0,10},{1,11},{2,8},{3,9},{4,14},{5,15},{6,12},{7,13},{8,2},{9,3},... | collective-permute-start | bytes 294920 | tf_op jit(solution)/shard_map/ppermute | solution.py:518
  15.8 0.0 collective-permute-done.after.refs_1_
  15.8 0.1 collective-permute-start.5
  15.9 0.0 collective-permute-done.1.refs_2_
  15.9 1.0 %collective-permute-start.6 = (bf16[384,128]{1,0:T(8,128)(2,1)S(1)}, bf16[384,128]{1,0:T(8,128)(2,1)S(1)}, u32[]{:S(2)}, u32[]{:S(2)}) collective-permute-start(bf16[384,128]{1,0:T(8,128)(2,1)S(1)} %get-tuple-element.27), channel_id=1, source_target_pairs={{0,6},{1,7},{2,4},{3,5},{4,2},{5,3},{6,0},{7,1},{8,14},{9,15},{10,... | collective-permute-start | bytes 294920 | tf_op jit(solution)/shard_map/ppermute | solution.py:518
  16.9 0.0 collective-permute-done.2.refs_3_
  16.9 0.0 collective-permute-start.7
  16.9 0.0 collective-permute-done.3.refs_4_
  16.9 0.5 %collective-permute-start.8 = (bf16[384,128]{1,0:T(8,128)(2,1)S(1)}, bf16[384,128]{1,0:T(8,128)(2,1)S(1)}, u32[]{:S(2)}, u32[]{:S(2)}) collective-permute-start(bf16[384,128]{1,0:T(8,128)(2,1)S(1)} %collective-permute-done.after.refs_1_), channel_id=1, source_target_pairs={{0,1},{1,0},{2,3},{3,2},{4,5},{5,4},{6,7},{7,6},{8,9},{9,8},{10,11... | collective-permute-start | bytes 294920 | tf_op jit(solution)/shard_map/ppermute | solution.py:518
  17.4 7.3 %collective-permute-done.4.refs_5_ = bf16[384,128]{1,0:T(8,128)(2,1)S(1)} collective-permute-done((bf16[384,128]{1,0:T(8,128)(2,1)S(1)}, bf16[384,128]{1,0:T(8,128)(2,1)S(1)}, u32[]{:S(2)}, u32[]{:S(2)}) %collective-permute-start.4) | collective-permute-done | bytes 98336 | tf_op jit(solution)/shard_map/ppermute | solution.py:518
  24.7 0.0 collective-permute-start.9
  24.7 0.2 collective-permute-done.5.refs_6_
  24.9 0.3 collective-permute-start.10
  25.2 0.0 collective-permute-done.6.refs_7_
  25.2 0.2 collective-permute-start.11
  25.5 0.0 collective-permute-done.7.refs_8_
  25.5 0.3 collective-permute-start.12
  25.8 0.0 collective-permute-done.8.refs_9_
  25.8 0.2 collective-permute-start.13
  26.0 0.1 collective-permute-done.9.refs_10_
  26.0 0.2 collective-permute-start.14
  26.3 0.0 collective-permute-done.10.refs_11_
  26.3 0.3 collective-permute-done.11.refs_12_
  26.5 0.2 collective-permute-done.12.refs_13_
  26.8 0.3 collective-permute-done.13.refs_14_
  27.1 0.3 collective-permute-done.14.refs_15_
  27.3 1.0 %shard_map.176 = (bf16[256,128]{1,0:T(8,128)(2,1)S(1)}, bf16[256,128]{1,0:T(8,128)(2,1)S(1)}, bf16[256,128]{1,0:T(8,128)(2,1)S(1)}, bf16[256,128]{1,0:T(8,128)(2,1)S(1)}) custom-call(s32[8,128]{1,0:T(8,128)S(1)} %get-tuple-element.20.bounds, bf16[384,128]{1,0:T(8,128)(2,1)S(1)} %get-tuple-element.21.refs_0_, ...), custom_call_target="tpu_custom_call" | custom-call | tf_op jit(solution)/shard_map/pallas_call | solution.py:574
  28.3 3.4 %collective-permute-start.15 = (bf16[256,128]{1,0:T(8,128)(2,1)S(1)}, bf16[256,128]{1,0:T(8,128)(2,1)S(1)}, u32[]{:S(2)}, u32[]{:S(2)}) collective-permute-start(bf16[256,128]{1,0:T(8,128)(2,1)S(1)} %get-tuple-element.28), channel_id=1, source_target_pairs={{0,14},{1,11},{2,12},{3,9},{4,10},{5,15},{6,8},{7,13},{8,6},{9,3},... | collective-permute-start | bytes 196616 | tf_op jit(solution)/shard_map/ppermute | solution.py:582
  31.7 1.3 %collective-permute-start.16 = (bf16[256,128]{1,0:T(8,128)(2,1)S(1)}, bf16[256,128]{1,0:T(8,128)(2,1)S(1)}, u32[]{:S(2)}, u32[]{:S(2)}) collective-permute-start(bf16[256,128]{1,0:T(8,128)(2,1)S(1)} %get-tuple-element.29), channel_id=1, source_target_pairs={{0,12},{1,9},{2,14},{3,11},{4,8},{5,13},{6,10},{7,15},{8,4},{9,1},... | collective-permute-start | bytes 196616 | tf_op jit(solution)/shard_map/ppermute | solution.py:582
  33.1 0.6 %collective-permute-start.17 = (bf16[256,128]{1,0:T(8,128)(2,1)S(1)}, bf16[256,128]{1,0:T(8,128)(2,1)S(1)}, u32[]{:S(2)}, u32[]{:S(2)}) collective-permute-start(bf16[256,128]{1,0:T(8,128)(2,1)S(1)} %get-tuple-element.30), channel_id=1, source_target_pairs={{0,2},{1,7},{2,0},{3,5},{4,6},{5,3},{6,4},{7,1},{8,10},{9,15},{10,... | collective-permute-start | bytes 196616 | tf_op jit(solution)/shard_map/ppermute | solution.py:582
  33.6 0.7 %collective-permute-start.18 = (bf16[256,128]{1,0:T(8,128)(2,1)S(1)}, bf16[256,128]{1,0:T(8,128)(2,1)S(1)}, u32[]{:S(2)}, u32[]{:S(2)}) collective-permute-start(bf16[256,128]{1,0:T(8,128)(2,1)S(1)} %get-tuple-element.31), channel_id=1, source_target_pairs={{0,0},{1,5},{2,2},{3,7},{4,4},{5,1},{6,6},{7,3},{8,8},{9,13},{10,1... | collective-permute-start | bytes 196616 | tf_op jit(solution)/shard_map/ppermute | solution.py:582
  34.3 1.2 %collective-permute-done.15.refs_0_ = bf16[256,128]{1,0:T(8,128)(2,1)S(1)} collective-permute-done((bf16[256,128]{1,0:T(8,128)(2,1)S(1)}, bf16[256,128]{1,0:T(8,128)(2,1)S(1)}, u32[]{:S(2)}, u32[]{:S(2)}) %collective-permute-start.15) | collective-permute-done | bytes 65568 | tf_op jit(solution)/shard_map/ppermute | solution.py:582
  35.5 0.0 collective-permute-start.19
  35.5 2.4 %collective-permute-done.16.refs_1_ = bf16[256,128]{1,0:T(8,128)(2,1)S(1)} collective-permute-done((bf16[256,128]{1,0:T(8,128)(2,1)S(1)}, bf16[256,128]{1,0:T(8,128)(2,1)S(1)}, u32[]{:S(2)}, u32[]{:S(2)}) %collective-permute-start.16) | collective-permute-done | bytes 65568 | tf_op jit(solution)/shard_map/ppermute | solution.py:582
  37.9 0.0 collective-permute-start.20
  37.9 0.0 collective-permute-done.17.refs_2_
  37.9 0.5 %collective-permute-start.21 = (bf16[256,128]{1,0:T(8,128)(2,1)S(1)}, bf16[256,128]{1,0:T(8,128)(2,1)S(1)}, u32[]{:S(2)}, u32[]{:S(2)}) collective-permute-start(bf16[256,128]{1,0:T(8,128)(2,1)S(1)} %collective-permute-done.17.refs_2_), channel_id=1, source_target_pairs={{0,1},{1,0},{2,3},{3,2},{4,5},{5,4},{6,7},{7,6},{8,9},{9,8},{10,11... | collective-permute-start | bytes 196616 | tf_op jit(solution)/shard_map/ppermute | solution.py:518
  38.4 0.0 collective-permute-done.18.refs_3_
  38.4 0.1 collective-permute-start.22
  38.4 0.0 collective-permute-done.19.refs_4_
  38.4 0.7 %collective-permute-done.20.refs_5_ = bf16[256,128]{1,0:T(8,128)(2,1)S(1)} collective-permute-done((bf16[256,128]{1,0:T(8,128)(2,1)S(1)}, bf16[256,128]{1,0:T(8,128)(2,1)S(1)}, u32[]{:S(2)}, u32[]{:S(2)}) %collective-permute-start.20) | collective-permute-done | bytes 65568 | tf_op jit(solution)/shard_map/ppermute | solution.py:518
  39.1 0.2 collective-permute-done.21.refs_6_
  39.3 0.4 collective-permute-done.22.refs_7_
  39.6 0.8 %shard_map.177 = (bf16[16,4096]{1,0:T(8,128)(2,1)}, bf16[8,2048]{1,0:T(8,128)(2,1)}, bf16[16,2048]{1,0:T(8,128)(2,1)}, bf16[8,2048]{1,0:T(8,128)(2,1)}) custom-call(bf16[256,128]{1,0:T(8,128)(2,1)S(1)} %collective-permute-done.15.refs_0_, bf16[256,128]{1,0:T(8,128)(2,1)S(1)} %collective-permute-done.16.refs_1_, ...), custom_call_target="tpu_custom_call" | custom-call | tf_op jit(solution)/shard_map/pallas_call | solution.py:585
  (1 shorter events, 0.0 us)
Async XLA Ops:
  1.9 13.9 %collective-permute-start = (bf16[384,128]{1,0:T(8,128)(2,1)S(1)}, bf16[384,128]{1,0:T(8,128)(2,1)S(1)}, u32[]{:S(2)}, u32[]{:S(2)}) collective-permute-start(bf16[384,128]{1,0:T(8,128)(2,1)S(1)} %get-tuple-element.18), channel_id=1, source_target_pairs={{0,2},{1,3},{2,0},{3,1},{4,6},{5,7},{6,4},{7,5},{8,10},{9,11},{10,... | collective-permute-start | bytes 294920 | tf_op jit(solution)/shard_map/ppermute | solution.py:518
  5.0 10.9 %collective-permute-start.1 = (bf16[384,128]{1,0:T(8,128)(2,1)S(1)}, bf16[384,128]{1,0:T(8,128)(2,1)S(1)}, u32[]{:S(2)}, u32[]{:S(2)}) collective-permute-start(bf16[384,128]{1,0:T(8,128)(2,1)S(1)} %get-tuple-element.22), channel_id=1, source_target_pairs={{0,14},{1,15},{2,12},{3,13},{4,10},{5,11},{6,8},{7,9},{8,6},{9,7},... | collective-permute-start | bytes 294920 | tf_op jit(solution)/shard_map/ppermute | solution.py:518
  8.5 8.4 %collective-permute-start.2 = (bf16[384,128]{1,0:T(8,128)(2,1)S(1)}, bf16[384,128]{1,0:T(8,128)(2,1)S(1)}, u32[]{:S(2)}, u32[]{:S(2)}) collective-permute-start(bf16[384,128]{1,0:T(8,128)(2,1)S(1)} %get-tuple-element.23), channel_id=1, source_target_pairs={{0,12},{1,13},{2,14},{3,15},{4,8},{5,9},{6,10},{7,11},{8,4},{9,5},... | collective-permute-start | bytes 294920 | tf_op jit(solution)/shard_map/ppermute | solution.py:518
  8.6 8.3 %collective-permute-start.3 = (bf16[384,128]{1,0:T(8,128)(2,1)S(1)}, bf16[384,128]{1,0:T(8,128)(2,1)S(1)}, u32[]{:S(2)}, u32[]{:S(2)}) collective-permute-start(bf16[384,128]{1,0:T(8,128)(2,1)S(1)} %get-tuple-element.24), channel_id=1, source_target_pairs={{0,4},{1,5},{2,6},{3,7},{4,0},{5,1},{6,2},{7,3},{8,12},{9,13},{10,... | collective-permute-start | bytes 294920 | tf_op jit(solution)/shard_map/ppermute | solution.py:518
  8.6 16.1 %collective-permute-start.4 = (bf16[384,128]{1,0:T(8,128)(2,1)S(1)}, bf16[384,128]{1,0:T(8,128)(2,1)S(1)}, u32[]{:S(2)}, u32[]{:S(2)}) collective-permute-start(bf16[384,128]{1,0:T(8,128)(2,1)S(1)} %get-tuple-element.25), channel_id=1, source_target_pairs={{0,10},{1,11},{2,8},{3,9},{4,14},{5,15},{6,12},{7,13},{8,2},{9,3},... | collective-permute-start | bytes 294920 | tf_op jit(solution)/shard_map/ppermute | solution.py:518
  15.8 9.1 %collective-permute-start.5 = (bf16[384,128]{1,0:T(8,128)(2,1)S(1)}, bf16[384,128]{1,0:T(8,128)(2,1)S(1)}, u32[]{:S(2)}, u32[]{:S(2)}) collective-permute-start(bf16[384,128]{1,0:T(8,128)(2,1)S(1)} %get-tuple-element.26), channel_id=1, source_target_pairs={{0,8},{1,9},{2,10},{3,11},{4,12},{5,13},{6,14},{7,15},{8,0},{9,1},... | collective-permute-start | bytes 294920 | tf_op jit(solution)/shard_map/ppermute | solution.py:518
  15.9 9.3 %collective-permute-start.6 = (bf16[384,128]{1,0:T(8,128)(2,1)S(1)}, bf16[384,128]{1,0:T(8,128)(2,1)S(1)}, u32[]{:S(2)}, u32[]{:S(2)}) collective-permute-start(bf16[384,128]{1,0:T(8,128)(2,1)S(1)} %get-tuple-element.27), channel_id=1, source_target_pairs={{0,6},{1,7},{2,4},{3,5},{4,2},{5,3},{6,0},{7,1},{8,14},{9,15},{10,... | collective-permute-start | bytes 294920 | tf_op jit(solution)/shard_map/ppermute | solution.py:518
  16.9 8.5 %collective-permute-start.7 = (bf16[384,128]{1,0:T(8,128)(2,1)S(1)}, bf16[384,128]{1,0:T(8,128)(2,1)S(1)}, u32[]{:S(2)}, u32[]{:S(2)}) collective-permute-start(bf16[384,128]{1,0:T(8,128)(2,1)S(1)} %get-tuple-element.21.refs_0_), channel_id=1, source_target_pairs={{0,1},{1,0},{2,3},{3,2},{4,5},{5,4},{6,7},{7,6},{8,9},{9,8},{10,11... | collective-permute-start | bytes 294920 | tf_op jit(solution)/shard_map/ppermute | solution.py:518
  16.9 8.8 %collective-permute-start.8 = (bf16[384,128]{1,0:T(8,128)(2,1)S(1)}, bf16[384,128]{1,0:T(8,128)(2,1)S(1)}, u32[]{:S(2)}, u32[]{:S(2)}) collective-permute-start(bf16[384,128]{1,0:T(8,128)(2,1)S(1)} %collective-permute-done.after.refs_1_), channel_id=1, source_target_pairs={{0,1},{1,0},{2,3},{3,2},{4,5},{5,4},{6,7},{7,6},{8,9},{9,8},{10,11... | collective-permute-start | bytes 294920 | tf_op jit(solution)/shard_map/ppermute | solution.py:518
  24.7 1.3 %collective-permute-start.9 = (bf16[384,128]{1,0:T(8,128)(2,1)S(1)}, bf16[384,128]{1,0:T(8,128)(2,1)S(1)}, u32[]{:S(2)}, u32[]{:S(2)}) collective-permute-start(bf16[384,128]{1,0:T(8,128)(2,1)S(1)} %collective-permute-done.1.refs_2_), channel_id=1, source_target_pairs={{0,1},{1,0},{2,3},{3,2},{4,5},{5,4},{6,7},{7,6},{8,9},{9,8},{10,11... | collective-permute-start | bytes 294920 | tf_op jit(solution)/shard_map/ppermute | solution.py:518
  24.9 1.3 %collective-permute-start.10 = (bf16[384,128]{1,0:T(8,128)(2,1)S(1)}, bf16[384,128]{1,0:T(8,128)(2,1)S(1)}, u32[]{:S(2)}, u32[]{:S(2)}) collective-permute-start(bf16[384,128]{1,0:T(8,128)(2,1)S(1)} %collective-permute-done.2.refs_3_), channel_id=1, source_target_pairs={{0,1},{1,0},{2,3},{3,2},{4,5},{5,4},{6,7},{7,6},{8,9},{9,8},{10,11... | collective-permute-start | bytes 294920 | tf_op jit(solution)/shard_map/ppermute | solution.py:518
  25.2 1.3 %collective-permute-start.11 = (bf16[384,128]{1,0:T(8,128)(2,1)S(1)}, bf16[384,128]{1,0:T(8,128)(2,1)S(1)}, u32[]{:S(2)}, u32[]{:S(2)}) collective-permute-start(bf16[384,128]{1,0:T(8,128)(2,1)S(1)} %collective-permute-done.3.refs_4_), channel_id=1, source_target_pairs={{0,1},{1,0},{2,3},{3,2},{4,5},{5,4},{6,7},{7,6},{8,9},{9,8},{10,11... | collective-permute-start | bytes 294920 | tf_op jit(solution)/shard_map/ppermute | solution.py:518
  25.5 1.3 %collective-permute-start.12 = (bf16[384,128]{1,0:T(8,128)(2,1)S(1)}, bf16[384,128]{1,0:T(8,128)(2,1)S(1)}, u32[]{:S(2)}, u32[]{:S(2)}) collective-permute-start(bf16[384,128]{1,0:T(8,128)(2,1)S(1)} %collective-permute-done.4.refs_5_), channel_id=1, source_target_pairs={{0,1},{1,0},{2,3},{3,2},{4,5},{5,4},{6,7},{7,6},{8,9},{9,8},{10,11... | collective-permute-start | bytes 294920 | tf_op jit(solution)/shard_map/ppermute | solution.py:518
  25.8 1.3 %collective-permute-start.13 = (bf16[384,128]{1,0:T(8,128)(2,1)S(1)}, bf16[384,128]{1,0:T(8,128)(2,1)S(1)}, u32[]{:S(2)}, u32[]{:S(2)}) collective-permute-start(bf16[384,128]{1,0:T(8,128)(2,1)S(1)} %collective-permute-done.5.refs_6_), channel_id=1, source_target_pairs={{0,1},{1,0},{2,3},{3,2},{4,5},{5,4},{6,7},{7,6},{8,9},{9,8},{10,11... | collective-permute-start | bytes 294920 | tf_op jit(solution)/shard_map/ppermute | solution.py:518
  26.0 1.3 %collective-permute-start.14 = (bf16[384,128]{1,0:T(8,128)(2,1)S(1)}, bf16[384,128]{1,0:T(8,128)(2,1)S(1)}, u32[]{:S(2)}, u32[]{:S(2)}) collective-permute-start(bf16[384,128]{1,0:T(8,128)(2,1)S(1)} %collective-permute-done.6.refs_7_), channel_id=1, source_target_pairs={{0,1},{1,0},{2,3},{3,2},{4,5},{5,4},{6,7},{7,6},{8,9},{9,8},{10,11... | collective-permute-start | bytes 294920 | tf_op jit(solution)/shard_map/ppermute | solution.py:518
  28.3 7.2 %collective-permute-start.15 = (bf16[256,128]{1,0:T(8,128)(2,1)S(1)}, bf16[256,128]{1,0:T(8,128)(2,1)S(1)}, u32[]{:S(2)}, u32[]{:S(2)}) collective-permute-start(bf16[256,128]{1,0:T(8,128)(2,1)S(1)} %get-tuple-element.28), channel_id=1, source_target_pairs={{0,14},{1,11},{2,12},{3,9},{4,10},{5,15},{6,8},{7,13},{8,6},{9,3},... | collective-permute-start | bytes 196616 | tf_op jit(solution)/shard_map/ppermute | solution.py:582
  31.7 6.1 %collective-permute-start.16 = (bf16[256,128]{1,0:T(8,128)(2,1)S(1)}, bf16[256,128]{1,0:T(8,128)(2,1)S(1)}, u32[]{:S(2)}, u32[]{:S(2)}) collective-permute-start(bf16[256,128]{1,0:T(8,128)(2,1)S(1)} %get-tuple-element.29), channel_id=1, source_target_pairs={{0,12},{1,9},{2,14},{3,11},{4,8},{5,13},{6,10},{7,15},{8,4},{9,1},... | collective-permute-start | bytes 196616 | tf_op jit(solution)/shard_map/ppermute | solution.py:582
  33.1 4.8 %collective-permute-start.17 = (bf16[256,128]{1,0:T(8,128)(2,1)S(1)}, bf16[256,128]{1,0:T(8,128)(2,1)S(1)}, u32[]{:S(2)}, u32[]{:S(2)}) collective-permute-start(bf16[256,128]{1,0:T(8,128)(2,1)S(1)} %get-tuple-element.30), channel_id=1, source_target_pairs={{0,2},{1,7},{2,0},{3,5},{4,6},{5,3},{6,4},{7,1},{8,10},{9,15},{10,... | collective-permute-start | bytes 196616 | tf_op jit(solution)/shard_map/ppermute | solution.py:582
  33.6 4.7 %collective-permute-start.18 = (bf16[256,128]{1,0:T(8,128)(2,1)S(1)}, bf16[256,128]{1,0:T(8,128)(2,1)S(1)}, u32[]{:S(2)}, u32[]{:S(2)}) collective-permute-start(bf16[256,128]{1,0:T(8,128)(2,1)S(1)} %get-tuple-element.31), channel_id=1, source_target_pairs={{0,0},{1,5},{2,2},{3,7},{4,4},{5,1},{6,6},{7,3},{8,8},{9,13},{10,1... | collective-permute-start | bytes 196616 | tf_op jit(solution)/shard_map/ppermute | solution.py:582
  35.5 3.0 %collective-permute-start.19 = (bf16[256,128]{1,0:T(8,128)(2,1)S(1)}, bf16[256,128]{1,0:T(8,128)(2,1)S(1)}, u32[]{:S(2)}, u32[]{:S(2)}) collective-permute-start(bf16[256,128]{1,0:T(8,128)(2,1)S(1)} %collective-permute-done.15.refs_0_), channel_id=1, source_target_pairs={{0,1},{1,0},{2,3},{3,2},{4,5},{5,4},{6,7},{7,6},{8,9},{9,8},{10,11... | collective-permute-start | bytes 196616 | tf_op jit(solution)/shard_map/ppermute | solution.py:518
  37.9 1.3 %collective-permute-start.20 = (bf16[256,128]{1,0:T(8,128)(2,1)S(1)}, bf16[256,128]{1,0:T(8,128)(2,1)S(1)}, u32[]{:S(2)}, u32[]{:S(2)}) collective-permute-start(bf16[256,128]{1,0:T(8,128)(2,1)S(1)} %collective-permute-done.16.refs_1_), channel_id=1, source_target_pairs={{0,1},{1,0},{2,3},{3,2},{4,5},{5,4},{6,7},{7,6},{8,9},{9,8},{10,11... | collective-permute-start | bytes 196616 | tf_op jit(solution)/shard_map/ppermute | solution.py:518
  37.9 1.4 %collective-permute-start.21 = (bf16[256,128]{1,0:T(8,128)(2,1)S(1)}, bf16[256,128]{1,0:T(8,128)(2,1)S(1)}, u32[]{:S(2)}, u32[]{:S(2)}) collective-permute-start(bf16[256,128]{1,0:T(8,128)(2,1)S(1)} %collective-permute-done.17.refs_2_), channel_id=1, source_target_pairs={{0,1},{1,0},{2,3},{3,2},{4,5},{5,4},{6,7},{7,6},{8,9},{9,8},{10,11... | collective-permute-start | bytes 196616 | tf_op jit(solution)/shard_map/ppermute | solution.py:518
  38.4 1.3 %collective-permute-start.22 = (bf16[256,128]{1,0:T(8,128)(2,1)S(1)}, bf16[256,128]{1,0:T(8,128)(2,1)S(1)}, u32[]{:S(2)}, u32[]{:S(2)}) collective-permute-start(bf16[256,128]{1,0:T(8,128)(2,1)S(1)} %collective-permute-done.18.refs_3_), channel_id=1, source_target_pairs={{0,1},{1,0},{2,3},{3,2},{4,5},{5,4},{6,7},{7,6},{8,9},{9,8},{10,11... | collective-permute-start | bytes 196616 | tf_op jit(solution)/shard_map/ppermute | solution.py:518

commit v9 on v8

--- a/solution.py
+++ b/solution.py
@@ -291,7 +291,7 @@
 
 def step_order(chips):
     far, near = list(range(chips - 1, chips // 2 - 1, -1)), list(range(1, chips // 2))
-    return [0] + near[:1] + far[:2] + near[1:2] + far[2:] + near[2:]
+    return [0] + far[:1] + near[:1] + far[1:2] + near[1:2] + far[2:] + near[2:]
 
 
 def by_step(items):
@@ -375,9 +375,10 @@
 
 
 def shares(chips):
-    zero = list(range(chips - 1, 3 * chips // 4 - 1, -1)) + list(range(chips // 4 - 1, -1, -1))
-    one = list(range(3 * chips // 4 - 1, chips // 4 - 1, -1))
-    return list(zip(zero, one))
+    quarter = chips // 4
+    far = list(zip(range(chips - 1, 3 * quarter - 1, -1), range(3 * quarter - 1, 2 * quarter - 1, -1)))
+    near = list(zip(range(quarter - 1, -1, -1), range(2 * quarter - 1, quarter - 1, -1)))
+    return [pair for both in zip(far, near) for pair in both]
 
 
 def attend_kernel(chips, rows, parts, pairs, bounds, *refs):
@@ -567,7 +568,7 @@
         out_specs=(vmem, anywhere),
         input_output_aliases={4: 1},
         compiler_params=params,
-    )(video_length, audio_length, align_offset, moved[0], packed[0])
+    )(video_length, audio_length, align_offset, moved[-1], packed[0])
     own = [kept] + moved
     other = [swap(piece, n, 1) for piece in own]
     share = shares(chips)

time: 40.6 us -> 40.6 us (level)
    ppermute x4, waiting for transfers between devices: 3.55 us -> 4.08 us  [shards_packed(): lax.ppermute(piece, 'seq', [(i, i ^ 2 * pair[i % 2]) for i in range(n)])]
    ppermute x19, waiting for transfers between devices: 9.8 us -> 9.3 us  [swap(): return lax.ppermute(piece, 'seq', [(i, i ^ step) for i in range(n)])]
where the time goes in v9:
time: 40.6 us; the launch traced here: 40.4 us
  starting transfers between devices  21.3 us (52%)
  waiting for transfers between devices  13.4 us (33%)
  Pallas kernels  3.04 us (7%)
  between operations  2.64 us (7%)
    ppermute x19, starting transfers between devices, swap(): return lax.ppermute(piece, 'seq', [(i, i ^ step) for i in range(n)])  15.3 us
    ppermute x19, waiting for transfers between devices, swap(): return lax.ppermute(piece, 'seq', [(i, i ^ step) for i in range(n)])  9.3 us
    ppermute x4, starting transfers between devices, shards_packed(): lax.ppermute(piece, 'seq', [(i, i ^ 2 * pair[i % 2]) for i in range(n)])  6 us
    ppermute x4, waiting for transfers between devices, shards_packed(): lax.ppermute(piece, 'seq', [(i, i ^ 2 * pair[i % 2]) for i in range(n)])  4.08 us
    pallas_call x1, Pallas kernels, shards_packed(): pl.pallas_call(functools.partial(pack_kernel, chips), out_shape=[pltpu.VM...  1.31 us
    pallas_call x1, Pallas kernels, shards_packed(): pl.pallas_call(functools.partial(attend_kernel, chips, rows, parts, pairs...  0.95 us
  transfers between devices with their start and end apart: 23, of which 12 were waited for; matrix products, arithmetic and copies ran while one was open for 0% of the time, Pallas kernels for 0%

profile of v9, /device:TPU:0, one launch (start us, length us, event | category | flops | bytes accessed | tf_op | source)
XLA Modules:
  0.0 40.4 jit_solution(15210583982562713304)
XLA Ops:
  0.6 1.3 %shard_map.174 = (bf16[384,128]{1,0:T(8,128)(2,1)S(1)}, bf16[384,128]{1,0:T(8,128)(2,1)S(1)}, bf16[384,128]{1,0:T(8,128)(2,1)S(1)}, bf16[384,128]{1,0:T(8,128)(2...) custom-call(bf16[16,4096]{1,0:T(8,128)(2,1)} %refs_0_.1, ...), custom_call_target="tpu_custom_call" | custom-call | tf_op jit(solution)/shard_map/pallas_call | solution.py:549
  1.9 6.1 %collective-permute-start = (bf16[384,128]{1,0:T(8,128)(2,1)S(1)}, bf16[384,128]{1,0:T(8,128)(2,1)S(1)}, u32[]{:S(2)}, u32[]{:S(2)}) collective-permute-start(bf16[384,128]{1,0:T(8,128)(2,1)S(1)} %get-tuple-element.18), channel_id=1, source_target_pairs={{0,14},{1,15},{2,12},{3,13},{4,10},{5,11},{6,8},{7,9},{8,6},{9,7},... | collective-permute-start | bytes 294920 | tf_op jit(solution)/shard_map/ppermute | solution.py:519
  8.0 0.5 %collective-permute-start.1 = (bf16[384,128]{1,0:T(8,128)(2,1)S(1)}, bf16[384,128]{1,0:T(8,128)(2,1)S(1)}, u32[]{:S(2)}, u32[]{:S(2)}) collective-permute-start(bf16[384,128]{1,0:T(8,128)(2,1)S(1)} %get-tuple-element.22), channel_id=1, source_target_pairs={{0,2},{1,3},{2,0},{3,1},{4,6},{5,7},{6,4},{7,5},{8,10},{9,11},{10,... | collective-permute-start | bytes 294920 | tf_op jit(solution)/shard_map/ppermute | solution.py:519
  8.5 0.1 collective-permute-start.2
  8.7 0.0 collective-permute-start.3
  8.7 5.2 %collective-permute-start.4 = (bf16[384,128]{1,0:T(8,128)(2,1)S(1)}, bf16[384,128]{1,0:T(8,128)(2,1)S(1)}, u32[]{:S(2)}, u32[]{:S(2)}) collective-permute-start(bf16[384,128]{1,0:T(8,128)(2,1)S(1)} %get-tuple-element.25), channel_id=1, source_target_pairs={{0,10},{1,11},{2,8},{3,9},{4,14},{5,15},{6,12},{7,13},{8,2},{9,3},... | collective-permute-start | bytes 294920 | tf_op jit(solution)/shard_map/ppermute | solution.py:519
  15.8 0.0 collective-permute-done.after.refs_1_
  15.8 0.7 %collective-permute-start.5 = (bf16[384,128]{1,0:T(8,128)(2,1)S(1)}, bf16[384,128]{1,0:T(8,128)(2,1)S(1)}, u32[]{:S(2)}, u32[]{:S(2)}) collective-permute-start(bf16[384,128]{1,0:T(8,128)(2,1)S(1)} %get-tuple-element.26), channel_id=1, source_target_pairs={{0,8},{1,9},{2,10},{3,11},{4,12},{5,13},{6,14},{7,15},{8,0},{9,1},... | collective-permute-start | bytes 294920 | tf_op jit(solution)/shard_map/ppermute | solution.py:519
  16.6 0.0 collective-permute-done.1.refs_2_
  16.6 0.6 %collective-permute-start.6 = (bf16[384,128]{1,0:T(8,128)(2,1)S(1)}, bf16[384,128]{1,0:T(8,128)(2,1)S(1)}, u32[]{:S(2)}, u32[]{:S(2)}) collective-permute-start(bf16[384,128]{1,0:T(8,128)(2,1)S(1)} %get-tuple-element.27), channel_id=1, source_target_pairs={{0,6},{1,7},{2,4},{3,5},{4,2},{5,3},{6,0},{7,1},{8,14},{9,15},{10,... | collective-permute-start | bytes 294920 | tf_op jit(solution)/shard_map/ppermute | solution.py:519
  17.1 0.0 collective-permute-done.2.refs_3_
  17.1 0.0 collective-permute-start.7
  17.1 0.0 collective-permute-done.3.refs_4_
  17.1 0.5 %collective-permute-start.8 = (bf16[384,128]{1,0:T(8,128)(2,1)S(1)}, bf16[384,128]{1,0:T(8,128)(2,1)S(1)}, u32[]{:S(2)}, u32[]{:S(2)}) collective-permute-start(bf16[384,128]{1,0:T(8,128)(2,1)S(1)} %collective-permute-done.after.refs_1_), channel_id=1, source_target_pairs={{0,1},{1,0},{2,3},{3,2},{4,5},{5,4},{6,7},{7,6},{8,9},{9,8},{10,11... | collective-permute-start | bytes 294920 | tf_op jit(solution)/shard_map/ppermute | solution.py:519
  17.7 5.7 %collective-permute-done.4.refs_5_ = bf16[384,128]{1,0:T(8,128)(2,1)S(1)} collective-permute-done((bf16[384,128]{1,0:T(8,128)(2,1)S(1)}, bf16[384,128]{1,0:T(8,128)(2,1)S(1)}, u32[]{:S(2)}, u32[]{:S(2)}) %collective-permute-start.4) | collective-permute-done | bytes 98336 | tf_op jit(solution)/shard_map/ppermute | solution.py:519
  23.4 0.0 collective-permute-start.9
  23.4 1.5 %collective-permute-done.5.refs_6_ = bf16[384,128]{1,0:T(8,128)(2,1)S(1)} collective-permute-done((bf16[384,128]{1,0:T(8,128)(2,1)S(1)}, bf16[384,128]{1,0:T(8,128)(2,1)S(1)}, u32[]{:S(2)}, u32[]{:S(2)}) %collective-permute-start.5) | collective-permute-done | bytes 98336 | tf_op jit(solution)/shard_map/ppermute | solution.py:519
  24.8 0.0 collective-permute-start.10
  24.8 0.0 collective-permute-done.6.refs_7_
  24.8 0.5 %collective-permute-start.11 = (bf16[384,128]{1,0:T(8,128)(2,1)S(1)}, bf16[384,128]{1,0:T(8,128)(2,1)S(1)}, u32[]{:S(2)}, u32[]{:S(2)}) collective-permute-start(bf16[384,128]{1,0:T(8,128)(2,1)S(1)} %collective-permute-done.3.refs_4_), channel_id=1, source_target_pairs={{0,1},{1,0},{2,3},{3,2},{4,5},{5,4},{6,7},{7,6},{8,9},{9,8},{10,11... | collective-permute-start | bytes 294920 | tf_op jit(solution)/shard_map/ppermute | solution.py:519
  25.3 0.0 collective-permute-done.7.refs_8_
  25.3 0.1 collective-permute-start.12
  25.4 0.0 collective-permute-done.8.refs_9_
  25.4 0.4 %collective-permute-start.13 = (bf16[384,128]{1,0:T(8,128)(2,1)S(1)}, bf16[384,128]{1,0:T(8,128)(2,1)S(1)}, u32[]{:S(2)}, u32[]{:S(2)}) collective-permute-start(bf16[384,128]{1,0:T(8,128)(2,1)S(1)} %collective-permute-done.5.refs_6_), channel_id=1, source_target_pairs={{0,1},{1,0},{2,3},{3,2},{4,5},{5,4},{6,7},{7,6},{8,9},{9,8},{10,11... | collective-permute-start | bytes 294920 | tf_op jit(solution)/shard_map/ppermute | solution.py:519
  25.8 0.0 collective-permute-done.9.refs_10_
  25.8 0.1 collective-permute-start.14
  25.9 0.2 collective-permute-done.10.refs_11_
  26.1 0.2 collective-permute-done.11.refs_12_
  26.3 0.4 collective-permute-done.12.refs_13_
  26.6 0.2 collective-permute-done.13.refs_14_
  26.8 0.4 collective-permute-done.14.refs_15_
  27.1 1.0 %shard_map.176 = (bf16[256,128]{1,0:T(8,128)(2,1)S(1)}, bf16[256,128]{1,0:T(8,128)(2,1)S(1)}, bf16[256,128]{1,0:T(8,128)(2,1)S(1)}, bf16[256,128]{1,0:T(8,128)(2,1)S(1)}) custom-call(s32[8,128]{1,0:T(8,128)S(1)} %get-tuple-element.20.bounds, bf16[384,128]{1,0:T(8,128)(2,1)S(1)} %get-tuple-element.21.refs_0_, ...), custom_call_target="tpu_custom_call" | custom-call | tf_op jit(solution)/shard_map/pallas_call | solution.py:575
  28.1 2.6 %collective-permute-start.15 = (bf16[256,128]{1,0:T(8,128)(2,1)S(1)}, bf16[256,128]{1,0:T(8,128)(2,1)S(1)}, u32[]{:S(2)}, u32[]{:S(2)}) collective-permute-start(bf16[256,128]{1,0:T(8,128)(2,1)S(1)} %get-tuple-element.28), channel_id=1, source_target_pairs={{0,14},{1,11},{2,12},{3,9},{4,10},{5,15},{6,8},{7,13},{8,6},{9,3},... | collective-permute-start | bytes 196616 | tf_op jit(solution)/shard_map/ppermute | solution.py:583
  30.7 1.3 %collective-permute-start.16 = (bf16[256,128]{1,0:T(8,128)(2,1)S(1)}, bf16[256,128]{1,0:T(8,128)(2,1)S(1)}, u32[]{:S(2)}, u32[]{:S(2)}) collective-permute-start(bf16[256,128]{1,0:T(8,128)(2,1)S(1)} %get-tuple-element.29), channel_id=1, source_target_pairs={{0,2},{1,7},{2,0},{3,5},{4,6},{5,3},{6,4},{7,1},{8,10},{9,15},{10,... | collective-permute-start | bytes 196616 | tf_op jit(solution)/shard_map/ppermute | solution.py:583
  32.1 1.4 %collective-permute-start.17 = (bf16[256,128]{1,0:T(8,128)(2,1)S(1)}, bf16[256,128]{1,0:T(8,128)(2,1)S(1)}, u32[]{:S(2)}, u32[]{:S(2)}) collective-permute-start(bf16[256,128]{1,0:T(8,128)(2,1)S(1)} %get-tuple-element.30), channel_id=1, source_target_pairs={{0,12},{1,9},{2,14},{3,11},{4,8},{5,13},{6,10},{7,15},{8,4},{9,1},... | collective-permute-start | bytes 196616 | tf_op jit(solution)/shard_map/ppermute | solution.py:583
  33.5 0.7 %collective-permute-start.18 = (bf16[256,128]{1,0:T(8,128)(2,1)S(1)}, bf16[256,128]{1,0:T(8,128)(2,1)S(1)}, u32[]{:S(2)}, u32[]{:S(2)}) collective-permute-start(bf16[256,128]{1,0:T(8,128)(2,1)S(1)} %get-tuple-element.31), channel_id=1, source_target_pairs={{0,0},{1,5},{2,2},{3,7},{4,4},{5,1},{6,6},{7,3},{8,8},{9,13},{10,1... | collective-permute-start | bytes 196616 | tf_op jit(solution)/shard_map/ppermute | solution.py:583
  34.1 1.2 %collective-permute-done.15.refs_0_ = bf16[256,128]{1,0:T(8,128)(2,1)S(1)} collective-permute-done((bf16[256,128]{1,0:T(8,128)(2,1)S(1)}, bf16[256,128]{1,0:T(8,128)(2,1)S(1)}, u32[]{:S(2)}, u32[]{:S(2)}) %collective-permute-start.15) | collective-permute-done | bytes 65568 | tf_op jit(solution)/shard_map/ppermute | solution.py:583
  35.3 0.0 collective-permute-start.19
  35.3 0.5 %collective-permute-done.16.refs_1_ = bf16[256,128]{1,0:T(8,128)(2,1)S(1)} collective-permute-done((bf16[256,128]{1,0:T(8,128)(2,1)S(1)}, bf16[256,128]{1,0:T(8,128)(2,1)S(1)}, u32[]{:S(2)}, u32[]{:S(2)}) %collective-permute-start.16) | collective-permute-done | bytes 65568 | tf_op jit(solution)/shard_map/ppermute | solution.py:583
  35.8 0.0 collective-permute-start.20
  35.8 2.4 %collective-permute-done.17.refs_2_ = bf16[256,128]{1,0:T(8,128)(2,1)S(1)} collective-permute-done((bf16[256,128]{1,0:T(8,128)(2,1)S(1)}, bf16[256,128]{1,0:T(8,128)(2,1)S(1)}, u32[]{:S(2)}, u32[]{:S(2)}) %collective-permute-start.17) | collective-permute-done | bytes 65568 | tf_op jit(solution)/shard_map/ppermute | solution.py:583
  38.2 0.0 collective-permute-start.21
  38.2 0.0 collective-permute-done.18.refs_3_
  38.2 0.5 %collective-permute-start.22 = (bf16[256,128]{1,0:T(8,128)(2,1)S(1)}, bf16[256,128]{1,0:T(8,128)(2,1)S(1)}, u32[]{:S(2)}, u32[]{:S(2)}) collective-permute-start(bf16[256,128]{1,0:T(8,128)(2,1)S(1)} %collective-permute-done.18.refs_3_), channel_id=1, source_target_pairs={{0,1},{1,0},{2,3},{3,2},{4,5},{5,4},{6,7},{7,6},{8,9},{9,8},{10,11... | collective-permute-start | bytes 196616 | tf_op jit(solution)/shard_map/ppermute | solution.py:519
  38.7 0.0 collective-permute-done.19.refs_4_
  38.7 0.0 collective-permute-done.20.refs_5_
  38.7 0.7 %collective-permute-done.21.refs_6_ = bf16[256,128]{1,0:T(8,128)(2,1)S(1)} collective-permute-done((bf16[256,128]{1,0:T(8,128)(2,1)S(1)}, bf16[256,128]{1,0:T(8,128)(2,1)S(1)}, u32[]{:S(2)}, u32[]{:S(2)}) %collective-permute-start.21) | collective-permute-done | bytes 65568 | tf_op jit(solution)/shard_map/ppermute | solution.py:519
  39.5 0.2 collective-permute-done.22.refs_7_
  39.6 0.8 %shard_map.177 = (bf16[16,4096]{1,0:T(8,128)(2,1)}, bf16[8,2048]{1,0:T(8,128)(2,1)}, bf16[16,2048]{1,0:T(8,128)(2,1)}, bf16[8,2048]{1,0:T(8,128)(2,1)}) custom-call(bf16[256,128]{1,0:T(8,128)(2,1)S(1)} %collective-permute-done.15.refs_0_, bf16[256,128]{1,0:T(8,128)(2,1)S(1)} %collective-permute-done.16.refs_1_, ...), custom_call_target="tpu_custom_call" | custom-call | tf_op jit(solution)/shard_map/pallas_call | solution.py:586
  (1 shorter events, 0.0 us)
Async XLA Ops:
  1.9 13.9 %collective-permute-start = (bf16[384,128]{1,0:T(8,128)(2,1)S(1)}, bf16[384,128]{1,0:T(8,128)(2,1)S(1)}, u32[]{:S(2)}, u32[]{:S(2)}) collective-permute-start(bf16[384,128]{1,0:T(8,128)(2,1)S(1)} %get-tuple-element.18), channel_id=1, source_target_pairs={{0,14},{1,15},{2,12},{3,13},{4,10},{5,11},{6,8},{7,9},{8,6},{9,7},... | collective-permute-start | bytes 294920 | tf_op jit(solution)/shard_map/ppermute | solution.py:519
  8.0 8.5 %collective-permute-start.1 = (bf16[384,128]{1,0:T(8,128)(2,1)S(1)}, bf16[384,128]{1,0:T(8,128)(2,1)S(1)}, u32[]{:S(2)}, u32[]{:S(2)}) collective-permute-start(bf16[384,128]{1,0:T(8,128)(2,1)S(1)} %get-tuple-element.22), channel_id=1, source_target_pairs={{0,2},{1,3},{2,0},{3,1},{4,6},{5,7},{6,4},{7,5},{8,10},{9,11},{10,... | collective-permute-start | bytes 294920 | tf_op jit(solution)/shard_map/ppermute | solution.py:519
  8.5 8.6 %collective-permute-start.2 = (bf16[384,128]{1,0:T(8,128)(2,1)S(1)}, bf16[384,128]{1,0:T(8,128)(2,1)S(1)}, u32[]{:S(2)}, u32[]{:S(2)}) collective-permute-start(bf16[384,128]{1,0:T(8,128)(2,1)S(1)} %get-tuple-element.23), channel_id=1, source_target_pairs={{0,12},{1,13},{2,14},{3,15},{4,8},{5,9},{6,10},{7,11},{8,4},{9,5},... | collective-permute-start | bytes 294920 | tf_op jit(solution)/shard_map/ppermute | solution.py:519
  8.7 8.5 %collective-permute-start.3 = (bf16[384,128]{1,0:T(8,128)(2,1)S(1)}, bf16[384,128]{1,0:T(8,128)(2,1)S(1)}, u32[]{:S(2)}, u32[]{:S(2)}) collective-permute-start(bf16[384,128]{1,0:T(8,128)(2,1)S(1)} %get-tuple-element.24), channel_id=1, source_target_pairs={{0,4},{1,5},{2,6},{3,7},{4,0},{5,1},{6,2},{7,3},{8,12},{9,13},{10,... | collective-permute-start | bytes 294920 | tf_op jit(solution)/shard_map/ppermute | solution.py:519
  8.7 14.7 %collective-permute-start.4 = (bf16[384,128]{1,0:T(8,128)(2,1)S(1)}, bf16[384,128]{1,0:T(8,128)(2,1)S(1)}, u32[]{:S(2)}, u32[]{:S(2)}) collective-permute-start(bf16[384,128]{1,0:T(8,128)(2,1)S(1)} %get-tuple-element.25), channel_id=1, source_target_pairs={{0,10},{1,11},{2,8},{3,9},{4,14},{5,15},{6,12},{7,13},{8,2},{9,3},... | collective-permute-start | bytes 294920 | tf_op jit(solution)/shard_map/ppermute | solution.py:519
  15.8 9.0 %collective-permute-start.5 = (bf16[384,128]{1,0:T(8,128)(2,1)S(1)}, bf16[384,128]{1,0:T(8,128)(2,1)S(1)}, u32[]{:S(2)}, u32[]{:S(2)}) collective-permute-start(bf16[384,128]{1,0:T(8,128)(2,1)S(1)} %get-tuple-element.26), channel_id=1, source_target_pairs={{0,8},{1,9},{2,10},{3,11},{4,12},{5,13},{6,14},{7,15},{8,0},{9,1},... | collective-permute-start | bytes 294920 | tf_op jit(solution)/shard_map/ppermute | solution.py:519
  16.6 8.2 %collective-permute-start.6 = (bf16[384,128]{1,0:T(8,128)(2,1)S(1)}, bf16[384,128]{1,0:T(8,128)(2,1)S(1)}, u32[]{:S(2)}, u32[]{:S(2)}) collective-permute-start(bf16[384,128]{1,0:T(8,128)(2,1)S(1)} %get-tuple-element.27), channel_id=1, source_target_pairs={{0,6},{1,7},{2,4},{3,5},{4,2},{5,3},{6,0},{7,1},{8,14},{9,15},{10,... | collective-permute-start | bytes 294920 | tf_op jit(solution)/shard_map/ppermute | solution.py:519
  17.1 8.2 %collective-permute-start.7 = (bf16[384,128]{1,0:T(8,128)(2,1)S(1)}, bf16[384,128]{1,0:T(8,128)(2,1)S(1)}, u32[]{:S(2)}, u32[]{:S(2)}) collective-permute-start(bf16[384,128]{1,0:T(8,128)(2,1)S(1)} %get-tuple-element.21.refs_0_), channel_id=1, source_target_pairs={{0,1},{1,0},{2,3},{3,2},{4,5},{5,4},{6,7},{7,6},{8,9},{9,8},{10,11... | collective-permute-start | bytes 294920 | tf_op jit(solution)/shard_map/ppermute | solution.py:519
  17.1 8.3 %collective-permute-start.8 = (bf16[384,128]{1,0:T(8,128)(2,1)S(1)}, bf16[384,128]{1,0:T(8,128)(2,1)S(1)}, u32[]{:S(2)}, u32[]{:S(2)}) collective-permute-start(bf16[384,128]{1,0:T(8,128)(2,1)S(1)} %collective-permute-done.after.refs_1_), channel_id=1, source_target_pairs={{0,1},{1,0},{2,3},{3,2},{4,5},{5,4},{6,7},{7,6},{8,9},{9,8},{10,11... | collective-permute-start | bytes 294920 | tf_op jit(solution)/shard_map/ppermute | solution.py:519
  23.4 2.5 %collective-permute-start.9 = (bf16[384,128]{1,0:T(8,128)(2,1)S(1)}, bf16[384,128]{1,0:T(8,128)(2,1)S(1)}, u32[]{:S(2)}, u32[]{:S(2)}) collective-permute-start(bf16[384,128]{1,0:T(8,128)(2,1)S(1)} %collective-permute-done.1.refs_2_), channel_id=1, source_target_pairs={{0,1},{1,0},{2,3},{3,2},{4,5},{5,4},{6,7},{7,6},{8,9},{9,8},{10,11... | collective-permute-start | bytes 294920 | tf_op jit(solution)/shard_map/ppermute | solution.py:519
  24.8 1.3 %collective-permute-start.10 = (bf16[384,128]{1,0:T(8,128)(2,1)S(1)}, bf16[384,128]{1,0:T(8,128)(2,1)S(1)}, u32[]{:S(2)}, u32[]{:S(2)}) collective-permute-start(bf16[384,128]{1,0:T(8,128)(2,1)S(1)} %collective-permute-done.2.refs_3_), channel_id=1, source_target_pairs={{0,1},{1,0},{2,3},{3,2},{4,5},{5,4},{6,7},{7,6},{8,9},{9,8},{10,11... | collective-permute-start | bytes 294920 | tf_op jit(solution)/shard_map/ppermute | solution.py:519
  24.8 1.5 %collective-permute-start.11 = (bf16[384,128]{1,0:T(8,128)(2,1)S(1)}, bf16[384,128]{1,0:T(8,128)(2,1)S(1)}, u32[]{:S(2)}, u32[]{:S(2)}) collective-permute-start(bf16[384,128]{1,0:T(8,128)(2,1)S(1)} %collective-permute-done.3.refs_4_), channel_id=1, source_target_pairs={{0,1},{1,0},{2,3},{3,2},{4,5},{5,4},{6,7},{7,6},{8,9},{9,8},{10,11... | collective-permute-start | bytes 294920 | tf_op jit(solution)/shard_map/ppermute | solution.py:519
  25.3 1.3 %collective-permute-start.12 = (bf16[384,128]{1,0:T(8,128)(2,1)S(1)}, bf16[384,128]{1,0:T(8,128)(2,1)S(1)}, u32[]{:S(2)}, u32[]{:S(2)}) collective-permute-start(bf16[384,128]{1,0:T(8,128)(2,1)S(1)} %collective-permute-done.4.refs_5_), channel_id=1, source_target_pairs={{0,1},{1,0},{2,3},{3,2},{4,5},{5,4},{6,7},{7,6},{8,9},{9,8},{10,11... | collective-permute-start | bytes 294920 | tf_op jit(solution)/shard_map/ppermute | solution.py:519
  25.4 1.4 %collective-permute-start.13 = (bf16[384,128]{1,0:T(8,128)(2,1)S(1)}, bf16[384,128]{1,0:T(8,128)(2,1)S(1)}, u32[]{:S(2)}, u32[]{:S(2)}) collective-permute-start(bf16[384,128]{1,0:T(8,128)(2,1)S(1)} %collective-permute-done.5.refs_6_), channel_id=1, source_target_pairs={{0,1},{1,0},{2,3},{3,2},{4,5},{5,4},{6,7},{7,6},{8,9},{9,8},{10,11... | collective-permute-start | bytes 294920 | tf_op jit(solution)/shard_map/ppermute | solution.py:519
  25.8 1.3 %collective-permute-start.14 = (bf16[384,128]{1,0:T(8,128)(2,1)S(1)}, bf16[384,128]{1,0:T(8,128)(2,1)S(1)}, u32[]{:S(2)}, u32[]{:S(2)}) collective-permute-start(bf16[384,128]{1,0:T(8,128)(2,1)S(1)} %collective-permute-done.6.refs_7_), channel_id=1, source_target_pairs={{0,1},{1,0},{2,3},{3,2},{4,5},{5,4},{6,7},{7,6},{8,9},{9,8},{10,11... | collective-permute-start | bytes 294920 | tf_op jit(solution)/shard_map/ppermute | solution.py:519
  28.1 7.2 %collective-permute-start.15 = (bf16[256,128]{1,0:T(8,128)(2,1)S(1)}, bf16[256,128]{1,0:T(8,128)(2,1)S(1)}, u32[]{:S(2)}, u32[]{:S(2)}) collective-permute-start(bf16[256,128]{1,0:T(8,128)(2,1)S(1)} %get-tuple-element.28), channel_id=1, source_target_pairs={{0,14},{1,11},{2,12},{3,9},{4,10},{5,15},{6,8},{7,13},{8,6},{9,3},... | collective-permute-start | bytes 196616 | tf_op jit(solution)/shard_map/ppermute | solution.py:583
  30.7 5.1 %collective-permute-start.16 = (bf16[256,128]{1,0:T(8,128)(2,1)S(1)}, bf16[256,128]{1,0:T(8,128)(2,1)S(1)}, u32[]{:S(2)}, u32[]{:S(2)}) collective-permute-start(bf16[256,128]{1,0:T(8,128)(2,1)S(1)} %get-tuple-element.29), channel_id=1, source_target_pairs={{0,2},{1,7},{2,0},{3,5},{4,6},{5,3},{6,4},{7,1},{8,10},{9,15},{10,... | collective-permute-start | bytes 196616 | tf_op jit(solution)/shard_map/ppermute | solution.py:583
  32.1 6.2 %collective-permute-start.17 = (bf16[256,128]{1,0:T(8,128)(2,1)S(1)}, bf16[256,128]{1,0:T(8,128)(2,1)S(1)}, u32[]{:S(2)}, u32[]{:S(2)}) collective-permute-start(bf16[256,128]{1,0:T(8,128)(2,1)S(1)} %get-tuple-element.30), channel_id=1, source_target_pairs={{0,12},{1,9},{2,14},{3,11},{4,8},{5,13},{6,10},{7,15},{8,4},{9,1},... | collective-permute-start | bytes 196616 | tf_op jit(solution)/shard_map/ppermute | solution.py:583
  33.5 4.8 %collective-permute-start.18 = (bf16[256,128]{1,0:T(8,128)(2,1)S(1)}, bf16[256,128]{1,0:T(8,128)(2,1)S(1)}, u32[]{:S(2)}, u32[]{:S(2)}) collective-permute-start(bf16[256,128]{1,0:T(8,128)(2,1)S(1)} %get-tuple-element.31), channel_id=1, source_target_pairs={{0,0},{1,5},{2,2},{3,7},{4,4},{5,1},{6,6},{7,3},{8,8},{9,13},{10,1... | collective-permute-start | bytes 196616 | tf_op jit(solution)/shard_map/ppermute | solution.py:583
  35.3 3.4 %collective-permute-start.19 = (bf16[256,128]{1,0:T(8,128)(2,1)S(1)}, bf16[256,128]{1,0:T(8,128)(2,1)S(1)}, u32[]{:S(2)}, u32[]{:S(2)}) collective-permute-start(bf16[256,128]{1,0:T(8,128)(2,1)S(1)} %collective-permute-done.15.refs_0_), channel_id=1, source_target_pairs={{0,1},{1,0},{2,3},{3,2},{4,5},{5,4},{6,7},{7,6},{8,9},{9,8},{10,11... | collective-permute-start | bytes 196616 | tf_op jit(solution)/shard_map/ppermute | solution.py:519
  35.8 2.9 %collective-permute-start.20 = (bf16[256,128]{1,0:T(8,128)(2,1)S(1)}, bf16[256,128]{1,0:T(8,128)(2,1)S(1)}, u32[]{:S(2)}, u32[]{:S(2)}) collective-permute-start(bf16[256,128]{1,0:T(8,128)(2,1)S(1)} %collective-permute-done.16.refs_1_), channel_id=1, source_target_pairs={{0,1},{1,0},{2,3},{3,2},{4,5},{5,4},{6,7},{7,6},{8,9},{9,8},{10,11... | collective-permute-start | bytes 196616 | tf_op jit(solution)/shard_map/ppermute | solution.py:519
  38.2 1.3 %collective-permute-start.21 = (bf16[256,128]{1,0:T(8,128)(2,1)S(1)}, bf16[256,128]{1,0:T(8,128)(2,1)S(1)}, u32[]{:S(2)}, u32[]{:S(2)}) collective-permute-start(bf16[256,128]{1,0:T(8,128)(2,1)S(1)} %collective-permute-done.17.refs_2_), channel_id=1, source_target_pairs={{0,1},{1,0},{2,3},{3,2},{4,5},{5,4},{6,7},{7,6},{8,9},{9,8},{10,11... | collective-permute-start | bytes 196616 | tf_op jit(solution)/shard_map/ppermute | solution.py:519
  38.2 1.4 %collective-permute-start.22 = (bf16[256,128]{1,0:T(8,128)(2,1)S(1)}, bf16[256,128]{1,0:T(8,128)(2,1)S(1)}, u32[]{:S(2)}, u32[]{:S(2)}) collective-permute-start(bf16[256,128]{1,0:T(8,128)(2,1)S(1)} %collective-permute-done.18.refs_3_), channel_id=1, source_target_pairs={{0,1},{1,0},{2,3},{3,2},{4,5},{5,4},{6,7},{7,6},{8,9},{9,8},{10,11... | collective-permute-start | bytes 196616 | tf_op jit(solution)/shard_map/ppermute | solution.py:519

commit v10 on v9

--- a/solution.py
+++ b/solution.py
@@ -378,7 +378,7 @@
     quarter = chips // 4
     far = list(zip(range(chips - 1, 3 * quarter - 1, -1), range(3 * quarter - 1, 2 * quarter - 1, -1)))
     near = list(zip(range(quarter - 1, -1, -1), range(2 * quarter - 1, quarter - 1, -1)))
-    return [pair for both in zip(far, near) for pair in both]
+    return far + near
 
 
 def attend_kernel(chips, rows, parts, pairs, bounds, *refs):

time: 40.6 us -> 40.1 us (0.988)
  waiting for transfers between devices: 13.4 us -> 12.7 us
    ppermute x4, waiting for transfers between devices: 4.08 us -> 3.35 us  [shards_packed(): lax.ppermute(piece, 'seq', [(i, i ^ 2 * pair[i % 2]) for i in range(n)])]
  transfers between devices with their start and end apart: 23 -> 23, of which waited for: 12 -> 13; matrix products, arithmetic and copies ran while one was open for 0% -> 0% of each run, Pallas kernels for 0% -> 0%
where the time goes in v10:
time: 40.1 us; the launch traced here: 39.9 us
  starting transfers between devices  21.5 us (54%)
  waiting for transfers between devices  12.7 us (32%)
  Pallas kernels  3.04 us (8%)
  between operations  2.64 us (7%)
    ppermute x19, starting transfers between devices, swap(): return lax.ppermute(piece, 'seq', [(i, i ^ step) for i in range(n)])  15.5 us
    ppermute x19, waiting for transfers between devices, swap(): return lax.ppermute(piece, 'seq', [(i, i ^ step) for i in range(n)])  9.3 us
    ppermute x4, starting transfers between devices, shards_packed(): lax.ppermute(piece, 'seq', [(i, i ^ 2 * pair[i % 2]) for i in range(n)])  6 us
    ppermute x4, waiting for transfers between devices, shards_packed(): lax.ppermute(piece, 'seq', [(i, i ^ 2 * pair[i % 2]) for i in range(n)])  3.35 us
    pallas_call x1, Pallas kernels, shards_packed(): pl.pallas_call(functools.partial(pack_kernel, chips), out_shape=[pltpu.VM...  1.31 us
    pallas_call x1, Pallas kernels, shards_packed(): pl.pallas_call(functools.partial(attend_kernel, chips, rows, parts, pairs...  0.95 us
  transfers between devices with their start and end apart: 23, of which 13 were waited for; matrix products, arithmetic and copies ran while one was open for 0% of the time, Pallas kernels for 0%

profile of v10, /device:TPU:0, one launch (start us, length us, event | category | flops | bytes accessed | tf_op | source)
XLA Modules:
  0.0 39.9 jit_solution(16889853645193778038)
XLA Ops:
  0.6 1.3 %shard_map.174 = (bf16[384,128]{1,0:T(8,128)(2,1)S(1)}, bf16[384,128]{1,0:T(8,128)(2,1)S(1)}, bf16[384,128]{1,0:T(8,128)(2,1)S(1)}, bf16[384,128]{1,0:T(8,128)(2...) custom-call(bf16[16,4096]{1,0:T(8,128)(2,1)} %refs_0_.1, ...), custom_call_target="tpu_custom_call" | custom-call | tf_op jit(solution)/shard_map/pallas_call | solution.py:549
  1.9 6.1 %collective-permute-start = (bf16[384,128]{1,0:T(8,128)(2,1)S(1)}, bf16[384,128]{1,0:T(8,128)(2,1)S(1)}, u32[]{:S(2)}, u32[]{:S(2)}) collective-permute-start(bf16[384,128]{1,0:T(8,128)(2,1)S(1)} %get-tuple-element.18), channel_id=1, source_target_pairs={{0,14},{1,15},{2,12},{3,13},{4,10},{5,11},{6,8},{7,9},{8,6},{9,7},... | collective-permute-start | bytes 294920 | tf_op jit(solution)/shard_map/ppermute | solution.py:519
  8.0 0.5 %collective-permute-start.1 = (bf16[384,128]{1,0:T(8,128)(2,1)S(1)}, bf16[384,128]{1,0:T(8,128)(2,1)S(1)}, u32[]{:S(2)}, u32[]{:S(2)}) collective-permute-start(bf16[384,128]{1,0:T(8,128)(2,1)S(1)} %get-tuple-element.22), channel_id=1, source_target_pairs={{0,2},{1,3},{2,0},{3,1},{4,6},{5,7},{6,4},{7,5},{8,10},{9,11},{10,... | collective-permute-start | bytes 294920 | tf_op jit(solution)/shard_map/ppermute | solution.py:519
  8.5 0.1 collective-permute-start.2
  8.7 0.0 collective-permute-start.3
  8.7 5.2 %collective-permute-start.4 = (bf16[384,128]{1,0:T(8,128)(2,1)S(1)}, bf16[384,128]{1,0:T(8,128)(2,1)S(1)}, u32[]{:S(2)}, u32[]{:S(2)}) collective-permute-start(bf16[384,128]{1,0:T(8,128)(2,1)S(1)} %get-tuple-element.25), channel_id=1, source_target_pairs={{0,10},{1,11},{2,8},{3,9},{4,14},{5,15},{6,12},{7,13},{8,2},{9,3},... | collective-permute-start | bytes 294920 | tf_op jit(solution)/shard_map/ppermute | solution.py:519
  15.8 0.0 collective-permute-done.after.refs_1_
  15.8 0.7 %collective-permute-start.5 = (bf16[384,128]{1,0:T(8,128)(2,1)S(1)}, bf16[384,128]{1,0:T(8,128)(2,1)S(1)}, u32[]{:S(2)}, u32[]{:S(2)}) collective-permute-start(bf16[384,128]{1,0:T(8,128)(2,1)S(1)} %get-tuple-element.26), channel_id=1, source_target_pairs={{0,8},{1,9},{2,10},{3,11},{4,12},{5,13},{6,14},{7,15},{8,0},{9,1},... | collective-permute-start | bytes 294920 | tf_op jit(solution)/shard_map/ppermute | solution.py:519
  16.6 0.0 collective-permute-done.1.refs_2_
  16.6 0.6 %collective-permute-start.6 = (bf16[384,128]{1,0:T(8,128)(2,1)S(1)}, bf16[384,128]{1,0:T(8,128)(2,1)S(1)}, u32[]{:S(2)}, u32[]{:S(2)}) collective-permute-start(bf16[384,128]{1,0:T(8,128)(2,1)S(1)} %get-tuple-element.27), channel_id=1, source_target_pairs={{0,6},{1,7},{2,4},{3,5},{4,2},{5,3},{6,0},{7,1},{8,14},{9,15},{10,... | collective-permute-start | bytes 294920 | tf_op jit(solution)/shard_map/ppermute | solution.py:519
  17.1 0.0 collective-permute-done.2.refs_3_
  17.1 0.0 collective-permute-start.7
  17.1 0.0 collective-permute-done.3.refs_4_
  17.1 0.5 %collective-permute-start.8 = (bf16[384,128]{1,0:T(8,128)(2,1)S(1)}, bf16[384,128]{1,0:T(8,128)(2,1)S(1)}, u32[]{:S(2)}, u32[]{:S(2)}) collective-permute-start(bf16[384,128]{1,0:T(8,128)(2,1)S(1)} %collective-permute-done.after.refs_1_), channel_id=1, source_target_pairs={{0,1},{1,0},{2,3},{3,2},{4,5},{5,4},{6,7},{7,6},{8,9},{9,8},{10,11... | collective-permute-start | bytes 294920 | tf_op jit(solution)/shard_map/ppermute | solution.py:519
  17.7 5.7 %collective-permute-done.4.refs_5_ = bf16[384,128]{1,0:T(8,128)(2,1)S(1)} collective-permute-done((bf16[384,128]{1,0:T(8,128)(2,1)S(1)}, bf16[384,128]{1,0:T(8,128)(2,1)S(1)}, u32[]{:S(2)}, u32[]{:S(2)}) %collective-permute-start.4) | collective-permute-done | bytes 98336 | tf_op jit(solution)/shard_map/ppermute | solution.py:519
  23.4 0.0 collective-permute-start.9
  23.4 1.5 %collective-permute-done.5.refs_6_ = bf16[384,128]{1,0:T(8,128)(2,1)S(1)} collective-permute-done((bf16[384,128]{1,0:T(8,128)(2,1)S(1)}, bf16[384,128]{1,0:T(8,128)(2,1)S(1)}, u32[]{:S(2)}, u32[]{:S(2)}) %collective-permute-start.5) | collective-permute-done | bytes 98336 | tf_op jit(solution)/shard_map/ppermute | solution.py:519
  24.8 0.0 collective-permute-start.10
  24.8 0.0 collective-permute-done.6.refs_7_
  24.8 0.5 %collective-permute-start.11 = (bf16[384,128]{1,0:T(8,128)(2,1)S(1)}, bf16[384,128]{1,0:T(8,128)(2,1)S(1)}, u32[]{:S(2)}, u32[]{:S(2)}) collective-permute-start(bf16[384,128]{1,0:T(8,128)(2,1)S(1)} %collective-permute-done.3.refs_4_), channel_id=1, source_target_pairs={{0,1},{1,0},{2,3},{3,2},{4,5},{5,4},{6,7},{7,6},{8,9},{9,8},{10,11... | collective-permute-start | bytes 294920 | tf_op jit(solution)/shard_map/ppermute | solution.py:519
  25.3 0.0 collective-permute-done.7.refs_8_
  25.3 0.1 collective-permute-start.12
  25.4 0.0 collective-permute-done.8.refs_9_
  25.4 0.4 %collective-permute-start.13 = (bf16[384,128]{1,0:T(8,128)(2,1)S(1)}, bf16[384,128]{1,0:T(8,128)(2,1)S(1)}, u32[]{:S(2)}, u32[]{:S(2)}) collective-permute-start(bf16[384,128]{1,0:T(8,128)(2,1)S(1)} %collective-permute-done.5.refs_6_), channel_id=1, source_target_pairs={{0,1},{1,0},{2,3},{3,2},{4,5},{5,4},{6,7},{7,6},{8,9},{9,8},{10,11... | collective-permute-start | bytes 294920 | tf_op jit(solution)/shard_map/ppermute | solution.py:519
  25.8 0.0 collective-permute-done.9.refs_10_
  25.8 0.1 collective-permute-start.14
  25.9 0.2 collective-permute-done.10.refs_11_
  26.1 0.2 collective-permute-done.11.refs_12_
  26.3 0.4 collective-permute-done.12.refs_13_
  26.6 0.2 collective-permute-done.13.refs_14_
  26.8 0.4 collective-permute-done.14.refs_15_
  27.1 1.0 %shard_map.176 = (bf16[256,128]{1,0:T(8,128)(2,1)S(1)}, bf16[256,128]{1,0:T(8,128)(2,1)S(1)}, bf16[256,128]{1,0:T(8,128)(2,1)S(1)}, bf16[256,128]{1,0:T(8,128)(2,1)S(1)}) custom-call(s32[8,128]{1,0:T(8,128)S(1)} %get-tuple-element.20.bounds, bf16[384,128]{1,0:T(8,128)(2,1)S(1)} %get-tuple-element.21.refs_0_, ...), custom_call_target="tpu_custom_call" | custom-call | tf_op jit(solution)/shard_map/pallas_call | solution.py:575
  28.1 2.6 %collective-permute-start.15 = (bf16[256,128]{1,0:T(8,128)(2,1)S(1)}, bf16[256,128]{1,0:T(8,128)(2,1)S(1)}, u32[]{:S(2)}, u32[]{:S(2)}) collective-permute-start(bf16[256,128]{1,0:T(8,128)(2,1)S(1)} %get-tuple-element.28), channel_id=1, source_target_pairs={{0,14},{1,11},{2,12},{3,9},{4,10},{5,15},{6,8},{7,13},{8,6},{9,3},... | collective-permute-start | bytes 196616 | tf_op jit(solution)/shard_map/ppermute | solution.py:583
  30.7 2.7 %collective-permute-start.16 = (bf16[256,128]{1,0:T(8,128)(2,1)S(1)}, bf16[256,128]{1,0:T(8,128)(2,1)S(1)}, u32[]{:S(2)}, u32[]{:S(2)}) collective-permute-start(bf16[256,128]{1,0:T(8,128)(2,1)S(1)} %get-tuple-element.29), channel_id=1, source_target_pairs={{0,12},{1,9},{2,14},{3,11},{4,8},{5,13},{6,10},{7,15},{8,4},{9,1},... | collective-permute-start | bytes 196616 | tf_op jit(solution)/shard_map/ppermute | solution.py:583
  33.4 0.1 collective-permute-start.17
  33.5 0.7 %collective-permute-start.18 = (bf16[256,128]{1,0:T(8,128)(2,1)S(1)}, bf16[256,128]{1,0:T(8,128)(2,1)S(1)}, u32[]{:S(2)}, u32[]{:S(2)}) collective-permute-start(bf16[256,128]{1,0:T(8,128)(2,1)S(1)} %get-tuple-element.31), channel_id=1, source_target_pairs={{0,0},{1,5},{2,2},{3,7},{4,4},{5,1},{6,6},{7,3},{8,8},{9,13},{10,1... | collective-permute-start | bytes 196616 | tf_op jit(solution)/shard_map/ppermute | solution.py:583
  34.1 1.5 %collective-permute-done.15.refs_0_ = bf16[256,128]{1,0:T(8,128)(2,1)S(1)} collective-permute-done((bf16[256,128]{1,0:T(8,128)(2,1)S(1)}, bf16[256,128]{1,0:T(8,128)(2,1)S(1)}, u32[]{:S(2)}, u32[]{:S(2)}) %collective-permute-start.15) | collective-permute-done | bytes 65568 | tf_op jit(solution)/shard_map/ppermute | solution.py:583
  35.6 0.2 collective-permute-start.19
  35.8 1.2 %collective-permute-done.16.refs_1_ = bf16[256,128]{1,0:T(8,128)(2,1)S(1)} collective-permute-done((bf16[256,128]{1,0:T(8,128)(2,1)S(1)}, bf16[256,128]{1,0:T(8,128)(2,1)S(1)}, u32[]{:S(2)}, u32[]{:S(2)}) %collective-permute-start.16) | collective-permute-done | bytes 65568 | tf_op jit(solution)/shard_map/ppermute | solution.py:583
  37.0 0.0 collective-permute-start.20
  37.0 0.7 %collective-permute-done.17.refs_2_ = bf16[256,128]{1,0:T(8,128)(2,1)S(1)} collective-permute-done((bf16[256,128]{1,0:T(8,128)(2,1)S(1)}, bf16[256,128]{1,0:T(8,128)(2,1)S(1)}, u32[]{:S(2)}, u32[]{:S(2)}) %collective-permute-start.17) | collective-permute-done | bytes 65568 | tf_op jit(solution)/shard_map/ppermute | solution.py:583
  37.7 0.1 collective-permute-start.21
  37.7 0.0 collective-permute-done.18.refs_3_
  37.8 0.4 %collective-permute-start.22 = (bf16[256,128]{1,0:T(8,128)(2,1)S(1)}, bf16[256,128]{1,0:T(8,128)(2,1)S(1)}, u32[]{:S(2)}, u32[]{:S(2)}) collective-permute-start(bf16[256,128]{1,0:T(8,128)(2,1)S(1)} %collective-permute-done.18.refs_3_), channel_id=1, source_target_pairs={{0,1},{1,0},{2,3},{3,2},{4,5},{5,4},{6,7},{7,6},{8,9},{9,8},{10,11... | collective-permute-start | bytes 196616 | tf_op jit(solution)/shard_map/ppermute | solution.py:519
  38.2 0.0 collective-permute-done.19.refs_4_
  38.2 0.1 collective-permute-done.20.refs_5_
  38.2 0.7 %collective-permute-done.21.refs_6_ = bf16[256,128]{1,0:T(8,128)(2,1)S(1)} collective-permute-done((bf16[256,128]{1,0:T(8,128)(2,1)S(1)}, bf16[256,128]{1,0:T(8,128)(2,1)S(1)}, u32[]{:S(2)}, u32[]{:S(2)}) %collective-permute-start.21) | collective-permute-done | bytes 65568 | tf_op jit(solution)/shard_map/ppermute | solution.py:519
  38.9 0.2 collective-permute-done.22.refs_7_
  39.1 0.8 %shard_map.177 = (bf16[16,4096]{1,0:T(8,128)(2,1)}, bf16[8,2048]{1,0:T(8,128)(2,1)}, bf16[16,2048]{1,0:T(8,128)(2,1)}, bf16[8,2048]{1,0:T(8,128)(2,1)}) custom-call(bf16[256,128]{1,0:T(8,128)(2,1)S(1)} %collective-permute-done.15.refs_0_, bf16[256,128]{1,0:T(8,128)(2,1)S(1)} %collective-permute-done.16.refs_1_, ...), custom_call_target="tpu_custom_call" | custom-call | tf_op jit(solution)/shard_map/pallas_call | solution.py:586
  (1 shorter events, 0.0 us)
Async XLA Ops:
  1.9 13.9 %collective-permute-start = (bf16[384,128]{1,0:T(8,128)(2,1)S(1)}, bf16[384,128]{1,0:T(8,128)(2,1)S(1)}, u32[]{:S(2)}, u32[]{:S(2)}) collective-permute-start(bf16[384,128]{1,0:T(8,128)(2,1)S(1)} %get-tuple-element.18), channel_id=1, source_target_pairs={{0,14},{1,15},{2,12},{3,13},{4,10},{5,11},{6,8},{7,9},{8,6},{9,7},... | collective-permute-start | bytes 294920 | tf_op jit(solution)/shard_map/ppermute | solution.py:519
  8.0 8.5 %collective-permute-start.1 = (bf16[384,128]{1,0:T(8,128)(2,1)S(1)}, bf16[384,128]{1,0:T(8,128)(2,1)S(1)}, u32[]{:S(2)}, u32[]{:S(2)}) collective-permute-start(bf16[384,128]{1,0:T(8,128)(2,1)S(1)} %get-tuple-element.22), channel_id=1, source_target_pairs={{0,2},{1,3},{2,0},{3,1},{4,6},{5,7},{6,4},{7,5},{8,10},{9,11},{10,... | collective-permute-start | bytes 294920 | tf_op jit(solution)/shard_map/ppermute | solution.py:519
  8.5 8.6 %collective-permute-start.2 = (bf16[384,128]{1,0:T(8,128)(2,1)S(1)}, bf16[384,128]{1,0:T(8,128)(2,1)S(1)}, u32[]{:S(2)}, u32[]{:S(2)}) collective-permute-start(bf16[384,128]{1,0:T(8,128)(2,1)S(1)} %get-tuple-element.23), channel_id=1, source_target_pairs={{0,12},{1,13},{2,14},{3,15},{4,8},{5,9},{6,10},{7,11},{8,4},{9,5},... | collective-permute-start | bytes 294920 | tf_op jit(solution)/shard_map/ppermute | solution.py:519
  8.7 8.5 %collective-permute-start.3 = (bf16[384,128]{1,0:T(8,128)(2,1)S(1)}, bf16[384,128]{1,0:T(8,128)(2,1)S(1)}, u32[]{:S(2)}, u32[]{:S(2)}) collective-permute-start(bf16[384,128]{1,0:T(8,128)(2,1)S(1)} %get-tuple-element.24), channel_id=1, source_target_pairs={{0,4},{1,5},{2,6},{3,7},{4,0},{5,1},{6,2},{7,3},{8,12},{9,13},{10,... | collective-permute-start | bytes 294920 | tf_op jit(solution)/shard_map/ppermute | solution.py:519
  8.7 14.7 %collective-permute-start.4 = (bf16[384,128]{1,0:T(8,128)(2,1)S(1)}, bf16[384,128]{1,0:T(8,128)(2,1)S(1)}, u32[]{:S(2)}, u32[]{:S(2)}) collective-permute-start(bf16[384,128]{1,0:T(8,128)(2,1)S(1)} %get-tuple-element.25), channel_id=1, source_target_pairs={{0,10},{1,11},{2,8},{3,9},{4,14},{5,15},{6,12},{7,13},{8,2},{9,3},... | collective-permute-start | bytes 294920 | tf_op jit(solution)/shard_map/ppermute | solution.py:519
  15.8 9.0 %collective-permute-start.5 = (bf16[384,128]{1,0:T(8,128)(2,1)S(1)}, bf16[384,128]{1,0:T(8,128)(2,1)S(1)}, u32[]{:S(2)}, u32[]{:S(2)}) collective-permute-start(bf16[384,128]{1,0:T(8,128)(2,1)S(1)} %get-tuple-element.26), channel_id=1, source_target_pairs={{0,8},{1,9},{2,10},{3,11},{4,12},{5,13},{6,14},{7,15},{8,0},{9,1},... | collective-permute-start | bytes 294920 | tf_op jit(solution)/shard_map/ppermute | solution.py:519
  16.6 8.2 %collective-permute-start.6 = (bf16[384,128]{1,0:T(8,128)(2,1)S(1)}, bf16[384,128]{1,0:T(8,128)(2,1)S(1)}, u32[]{:S(2)}, u32[]{:S(2)}) collective-permute-start(bf16[384,128]{1,0:T(8,128)(2,1)S(1)} %get-tuple-element.27), channel_id=1, source_target_pairs={{0,6},{1,7},{2,4},{3,5},{4,2},{5,3},{6,0},{7,1},{8,14},{9,15},{10,... | collective-permute-start | bytes 294920 | tf_op jit(solution)/shard_map/ppermute | solution.py:519
  17.1 8.2 %collective-permute-start.7 = (bf16[384,128]{1,0:T(8,128)(2,1)S(1)}, bf16[384,128]{1,0:T(8,128)(2,1)S(1)}, u32[]{:S(2)}, u32[]{:S(2)}) collective-permute-start(bf16[384,128]{1,0:T(8,128)(2,1)S(1)} %get-tuple-element.21.refs_0_), channel_id=1, source_target_pairs={{0,1},{1,0},{2,3},{3,2},{4,5},{5,4},{6,7},{7,6},{8,9},{9,8},{10,11... | collective-permute-start | bytes 294920 | tf_op jit(solution)/shard_map/ppermute | solution.py:519
  17.1 8.3 %collective-permute-start.8 = (bf16[384,128]{1,0:T(8,128)(2,1)S(1)}, bf16[384,128]{1,0:T(8,128)(2,1)S(1)}, u32[]{:S(2)}, u32[]{:S(2)}) collective-permute-start(bf16[384,128]{1,0:T(8,128)(2,1)S(1)} %collective-permute-done.after.refs_1_), channel_id=1, source_target_pairs={{0,1},{1,0},{2,3},{3,2},{4,5},{5,4},{6,7},{7,6},{8,9},{9,8},{10,11... | collective-permute-start | bytes 294920 | tf_op jit(solution)/shard_map/ppermute | solution.py:519
  23.4 2.5 %collective-permute-start.9 = (bf16[384,128]{1,0:T(8,128)(2,1)S(1)}, bf16[384,128]{1,0:T(8,128)(2,1)S(1)}, u32[]{:S(2)}, u32[]{:S(2)}) collective-permute-start(bf16[384,128]{1,0:T(8,128)(2,1)S(1)} %collective-permute-done.1.refs_2_), channel_id=1, source_target_pairs={{0,1},{1,0},{2,3},{3,2},{4,5},{5,4},{6,7},{7,6},{8,9},{9,8},{10,11... | collective-permute-start | bytes 294920 | tf_op jit(solution)/shard_map/ppermute | solution.py:519
  24.8 1.3 %collective-permute-start.10 = (bf16[384,128]{1,0:T(8,128)(2,1)S(1)}, bf16[384,128]{1,0:T(8,128)(2,1)S(1)}, u32[]{:S(2)}, u32[]{:S(2)}) collective-permute-start(bf16[384,128]{1,0:T(8,128)(2,1)S(1)} %collective-permute-done.2.refs_3_), channel_id=1, source_target_pairs={{0,1},{1,0},{2,3},{3,2},{4,5},{5,4},{6,7},{7,6},{8,9},{9,8},{10,11... | collective-permute-start | bytes 294920 | tf_op jit(solution)/shard_map/ppermute | solution.py:519
  24.8 1.5 %collective-permute-start.11 = (bf16[384,128]{1,0:T(8,128)(2,1)S(1)}, bf16[384,128]{1,0:T(8,128)(2,1)S(1)}, u32[]{:S(2)}, u32[]{:S(2)}) collective-permute-start(bf16[384,128]{1,0:T(8,128)(2,1)S(1)} %collective-permute-done.3.refs_4_), channel_id=1, source_target_pairs={{0,1},{1,0},{2,3},{3,2},{4,5},{5,4},{6,7},{7,6},{8,9},{9,8},{10,11... | collective-permute-start | bytes 294920 | tf_op jit(solution)/shard_map/ppermute | solution.py:519
  25.3 1.3 %collective-permute-start.12 = (bf16[384,128]{1,0:T(8,128)(2,1)S(1)}, bf16[384,128]{1,0:T(8,128)(2,1)S(1)}, u32[]{:S(2)}, u32[]{:S(2)}) collective-permute-start(bf16[384,128]{1,0:T(8,128)(2,1)S(1)} %collective-permute-done.4.refs_5_), channel_id=1, source_target_pairs={{0,1},{1,0},{2,3},{3,2},{4,5},{5,4},{6,7},{7,6},{8,9},{9,8},{10,11... | collective-permute-start | bytes 294920 | tf_op jit(solution)/shard_map/ppermute | solution.py:519
  25.4 1.4 %collective-permute-start.13 = (bf16[384,128]{1,0:T(8,128)(2,1)S(1)}, bf16[384,128]{1,0:T(8,128)(2,1)S(1)}, u32[]{:S(2)}, u32[]{:S(2)}) collective-permute-start(bf16[384,128]{1,0:T(8,128)(2,1)S(1)} %collective-permute-done.5.refs_6_), channel_id=1, source_target_pairs={{0,1},{1,0},{2,3},{3,2},{4,5},{5,4},{6,7},{7,6},{8,9},{9,8},{10,11... | collective-permute-start | bytes 294920 | tf_op jit(solution)/shard_map/ppermute | solution.py:519
  25.8 1.3 %collective-permute-start.14 = (bf16[384,128]{1,0:T(8,128)(2,1)S(1)}, bf16[384,128]{1,0:T(8,128)(2,1)S(1)}, u32[]{:S(2)}, u32[]{:S(2)}) collective-permute-start(bf16[384,128]{1,0:T(8,128)(2,1)S(1)} %collective-permute-done.6.refs_7_), channel_id=1, source_target_pairs={{0,1},{1,0},{2,3},{3,2},{4,5},{5,4},{6,7},{7,6},{8,9},{9,8},{10,11... | collective-permute-start | bytes 294920 | tf_op jit(solution)/shard_map/ppermute | solution.py:519
  28.1 7.5 %collective-permute-start.15 = (bf16[256,128]{1,0:T(8,128)(2,1)S(1)}, bf16[256,128]{1,0:T(8,128)(2,1)S(1)}, u32[]{:S(2)}, u32[]{:S(2)}) collective-permute-start(bf16[256,128]{1,0:T(8,128)(2,1)S(1)} %get-tuple-element.28), channel_id=1, source_target_pairs={{0,14},{1,11},{2,12},{3,9},{4,10},{5,15},{6,8},{7,13},{8,6},{9,3},... | collective-permute-start | bytes 196616 | tf_op jit(solution)/shard_map/ppermute | solution.py:583
  30.7 6.3 %collective-permute-start.16 = (bf16[256,128]{1,0:T(8,128)(2,1)S(1)}, bf16[256,128]{1,0:T(8,128)(2,1)S(1)}, u32[]{:S(2)}, u32[]{:S(2)}) collective-permute-start(bf16[256,128]{1,0:T(8,128)(2,1)S(1)} %get-tuple-element.29), channel_id=1, source_target_pairs={{0,12},{1,9},{2,14},{3,11},{4,8},{5,13},{6,10},{7,15},{8,4},{9,1},... | collective-permute-start | bytes 196616 | tf_op jit(solution)/shard_map/ppermute | solution.py:583
  33.4 4.3 %collective-permute-start.17 = (bf16[256,128]{1,0:T(8,128)(2,1)S(1)}, bf16[256,128]{1,0:T(8,128)(2,1)S(1)}, u32[]{:S(2)}, u32[]{:S(2)}) collective-permute-start(bf16[256,128]{1,0:T(8,128)(2,1)S(1)} %get-tuple-element.30), channel_id=1, source_target_pairs={{0,2},{1,7},{2,0},{3,5},{4,6},{5,3},{6,4},{7,1},{8,10},{9,15},{10,... | collective-permute-start | bytes 196616 | tf_op jit(solution)/shard_map/ppermute | solution.py:583
  33.5 4.3 %collective-permute-start.18 = (bf16[256,128]{1,0:T(8,128)(2,1)S(1)}, bf16[256,128]{1,0:T(8,128)(2,1)S(1)}, u32[]{:S(2)}, u32[]{:S(2)}) collective-permute-start(bf16[256,128]{1,0:T(8,128)(2,1)S(1)} %get-tuple-element.31), channel_id=1, source_target_pairs={{0,0},{1,5},{2,2},{3,7},{4,4},{5,1},{6,6},{7,3},{8,8},{9,13},{10,1... | collective-permute-start | bytes 196616 | tf_op jit(solution)/shard_map/ppermute | solution.py:583
  35.6 2.6 %collective-permute-start.19 = (bf16[256,128]{1,0:T(8,128)(2,1)S(1)}, bf16[256,128]{1,0:T(8,128)(2,1)S(1)}, u32[]{:S(2)}, u32[]{:S(2)}) collective-permute-start(bf16[256,128]{1,0:T(8,128)(2,1)S(1)} %collective-permute-done.15.refs_0_), channel_id=1, source_target_pairs={{0,1},{1,0},{2,3},{3,2},{4,5},{5,4},{6,7},{7,6},{8,9},{9,8},{10,11... | collective-permute-start | bytes 196616 | tf_op jit(solution)/shard_map/ppermute | solution.py:519
  37.0 1.3 %collective-permute-start.20 = (bf16[256,128]{1,0:T(8,128)(2,1)S(1)}, bf16[256,128]{1,0:T(8,128)(2,1)S(1)}, u32[]{:S(2)}, u32[]{:S(2)}) collective-permute-start(bf16[256,128]{1,0:T(8,128)(2,1)S(1)} %collective-permute-done.16.refs_1_), channel_id=1, source_target_pairs={{0,1},{1,0},{2,3},{3,2},{4,5},{5,4},{6,7},{7,6},{8,9},{9,8},{10,11... | collective-permute-start | bytes 196616 | tf_op jit(solution)/shard_map/ppermute | solution.py:519
  37.7 1.3 %collective-permute-start.21 = (bf16[256,128]{1,0:T(8,128)(2,1)S(1)}, bf16[256,128]{1,0:T(8,128)(2,1)S(1)}, u32[]{:S(2)}, u32[]{:S(2)}) collective-permute-start(bf16[256,128]{1,0:T(8,128)(2,1)S(1)} %collective-permute-done.17.refs_2_), channel_id=1, source_target_pairs={{0,1},{1,0},{2,3},{3,2},{4,5},{5,4},{6,7},{7,6},{8,9},{9,8},{10,11... | collective-permute-start | bytes 196616 | tf_op jit(solution)/shard_map/ppermute | solution.py:519
  37.8 1.3 %collective-permute-start.22 = (bf16[256,128]{1,0:T(8,128)(2,1)S(1)}, bf16[256,128]{1,0:T(8,128)(2,1)S(1)}, u32[]{:S(2)}, u32[]{:S(2)}) collective-permute-start(bf16[256,128]{1,0:T(8,128)(2,1)S(1)} %collective-permute-done.18.refs_3_), channel_id=1, source_target_pairs={{0,1},{1,0},{2,3},{3,2},{4,5},{5,4},{6,7},{7,6},{8,9},{9,8},{10,11... | collective-permute-start | bytes 196616 | tf_op jit(solution)/shard_map/ppermute | solution.py:519

commit v11 on v10

--- a/solution.py
+++ b/solution.py
@@ -376,7 +376,7 @@
 
 def shares(chips):
     quarter = chips // 4
-    far = list(zip(range(chips - 1, 3 * quarter - 1, -1), range(3 * quarter - 1, 2 * quarter - 1, -1)))
+    far = [(chips - 1 - 2 * i - i % 2, chips - 2 - 2 * i + i % 2) for i in range(quarter)]
     near = list(zip(range(quarter - 1, -1, -1), range(2 * quarter - 1, quarter - 1, -1)))
     return far + near
 

time: 40.1 us -> 40.7 us (1.015)
  waiting for transfers between devices: 12.7 us -> 13.6 us
    ppermute x4, starting transfers between devices: 6 us -> 4.6 us  [shards_packed(): lax.ppermute(piece, 'seq', [(i, i ^ 2 * pair[i % 2]) for i in range(n)])]
    ppermute x19, starting transfers between devices: 15.5 us -> 16.6 us  [swap(): return lax.ppermute(piece, 'seq', [(i, i ^ step) for i in range(n)])]
    ppermute x4, waiting for transfers between devices: 3.35 us -> 4.33 us  [shards_packed(): lax.ppermute(piece, 'seq', [(i, i ^ 2 * pair[i % 2]) for i in range(n)])]
  transfers between devices with their start and end apart: 23 -> 23, of which waited for: 13 -> 12; matrix products, arithmetic and copies ran while one was open for 0% -> 0% of each run, Pallas kernels for 0% -> 0%
where the time goes in v11:
time: 40.7 us; the launch traced here: 40.5 us
  starting transfers between devices  21.2 us (52%)
  waiting for transfers between devices  13.6 us (33%)
  Pallas kernels  3.04 us (7%)
  between operations  2.64 us (6%)
    ppermute x19, starting transfers between devices, swap(): return lax.ppermute(piece, 'seq', [(i, i ^ step) for i in range(n)])  16.6 us
    ppermute x19, waiting for transfers between devices, swap(): return lax.ppermute(piece, 'seq', [(i, i ^ step) for i in range(n)])  9.3 us
    ppermute x4, starting transfers between devices, shards_packed(): lax.ppermute(piece, 'seq', [(i, i ^ 2 * pair[i % 2]) for i in range(n)])  4.6 us
    ppermute x4, waiting for transfers between devices, shards_packed(): lax.ppermute(piece, 'seq', [(i, i ^ 2 * pair[i % 2]) for i in range(n)])  4.33 us
    pallas_call x1, Pallas kernels, shards_packed(): pl.pallas_call(functools.partial(pack_kernel, chips), out_shape=[pltpu.VM...  1.31 us
    pallas_call x1, Pallas kernels, shards_packed(): pl.pallas_call(functools.partial(attend_kernel, chips, rows, parts, pairs...  0.95 us
  transfers between devices with their start and end apart: 23, of which 12 were waited for; matrix products, arithmetic and copies ran while one was open for 0% of the time, Pallas kernels for 0%

profile of v11, /device:TPU:0, one launch (start us, length us, event | category | flops | bytes accessed | tf_op | source)
XLA Modules:
  0.0 40.5 jit_solution(7442984012001921138)
XLA Ops:
  0.6 1.3 %shard_map.174 = (bf16[384,128]{1,0:T(8,128)(2,1)S(1)}, bf16[384,128]{1,0:T(8,128)(2,1)S(1)}, bf16[384,128]{1,0:T(8,128)(2,1)S(1)}, bf16[384,128]{1,0:T(8,128)(2...) custom-call(bf16[16,4096]{1,0:T(8,128)(2,1)} %refs_0_.1, ...), custom_call_target="tpu_custom_call" | custom-call | tf_op jit(solution)/shard_map/pallas_call | solution.py:549
  1.9 6.1 %collective-permute-start = (bf16[384,128]{1,0:T(8,128)(2,1)S(1)}, bf16[384,128]{1,0:T(8,128)(2,1)S(1)}, u32[]{:S(2)}, u32[]{:S(2)}) collective-permute-start(bf16[384,128]{1,0:T(8,128)(2,1)S(1)} %get-tuple-element.18), channel_id=1, source_target_pairs={{0,14},{1,15},{2,12},{3,13},{4,10},{5,11},{6,8},{7,9},{8,6},{9,7},... | collective-permute-start | bytes 294920 | tf_op jit(solution)/shard_map/ppermute | solution.py:519
  8.0 0.5 %collective-permute-start.1 = (bf16[384,128]{1,0:T(8,128)(2,1)S(1)}, bf16[384,128]{1,0:T(8,128)(2,1)S(1)}, u32[]{:S(2)}, u32[]{:S(2)}) collective-permute-start(bf16[384,128]{1,0:T(8,128)(2,1)S(1)} %get-tuple-element.22), channel_id=1, source_target_pairs={{0,2},{1,3},{2,0},{3,1},{4,6},{5,7},{6,4},{7,5},{8,10},{9,11},{10,... | collective-permute-start | bytes 294920 | tf_op jit(solution)/shard_map/ppermute | solution.py:519
  8.5 0.1 collective-permute-start.2
  8.7 0.0 collective-permute-start.3
  8.7 5.2 %collective-permute-start.4 = (bf16[384,128]{1,0:T(8,128)(2,1)S(1)}, bf16[384,128]{1,0:T(8,128)(2,1)S(1)}, u32[]{:S(2)}, u32[]{:S(2)}) collective-permute-start(bf16[384,128]{1,0:T(8,128)(2,1)S(1)} %get-tuple-element.25), channel_id=1, source_target_pairs={{0,10},{1,11},{2,8},{3,9},{4,14},{5,15},{6,12},{7,13},{8,2},{9,3},... | collective-permute-start | bytes 294920 | tf_op jit(solution)/shard_map/ppermute | solution.py:519
  15.8 0.0 collective-permute-done.after.refs_1_
  15.8 0.7 %collective-permute-start.5 = (bf16[384,128]{1,0:T(8,128)(2,1)S(1)}, bf16[384,128]{1,0:T(8,128)(2,1)S(1)}, u32[]{:S(2)}, u32[]{:S(2)}) collective-permute-start(bf16[384,128]{1,0:T(8,128)(2,1)S(1)} %get-tuple-element.26), channel_id=1, source_target_pairs={{0,8},{1,9},{2,10},{3,11},{4,12},{5,13},{6,14},{7,15},{8,0},{9,1},... | collective-permute-start | bytes 294920 | tf_op jit(solution)/shard_map/ppermute | solution.py:519
  16.6 0.0 collective-permute-done.1.refs_2_
  16.6 0.6 %collective-permute-start.6 = (bf16[384,128]{1,0:T(8,128)(2,1)S(1)}, bf16[384,128]{1,0:T(8,128)(2,1)S(1)}, u32[]{:S(2)}, u32[]{:S(2)}) collective-permute-start(bf16[384,128]{1,0:T(8,128)(2,1)S(1)} %get-tuple-element.27), channel_id=1, source_target_pairs={{0,6},{1,7},{2,4},{3,5},{4,2},{5,3},{6,0},{7,1},{8,14},{9,15},{10,... | collective-permute-start | bytes 294920 | tf_op jit(solution)/shard_map/ppermute | solution.py:519
  17.1 0.0 collective-permute-done.2.refs_3_
  17.1 0.0 collective-permute-start.7
  17.1 0.0 collective-permute-done.3.refs_4_
  17.1 0.5 %collective-permute-start.8 = (bf16[384,128]{1,0:T(8,128)(2,1)S(1)}, bf16[384,128]{1,0:T(8,128)(2,1)S(1)}, u32[]{:S(2)}, u32[]{:S(2)}) collective-permute-start(bf16[384,128]{1,0:T(8,128)(2,1)S(1)} %collective-permute-done.after.refs_1_), channel_id=1, source_target_pairs={{0,1},{1,0},{2,3},{3,2},{4,5},{5,4},{6,7},{7,6},{8,9},{9,8},{10,11... | collective-permute-start | bytes 294920 | tf_op jit(solution)/shard_map/ppermute | solution.py:519
  17.7 5.7 %collective-permute-done.4.refs_5_ = bf16[384,128]{1,0:T(8,128)(2,1)S(1)} collective-permute-done((bf16[384,128]{1,0:T(8,128)(2,1)S(1)}, bf16[384,128]{1,0:T(8,128)(2,1)S(1)}, u32[]{:S(2)}, u32[]{:S(2)}) %collective-permute-start.4) | collective-permute-done | bytes 98336 | tf_op jit(solution)/shard_map/ppermute | solution.py:519
  23.4 0.0 collective-permute-start.9
  23.4 1.5 %collective-permute-done.5.refs_6_ = bf16[384,128]{1,0:T(8,128)(2,1)S(1)} collective-permute-done((bf16[384,128]{1,0:T(8,128)(2,1)S(1)}, bf16[384,128]{1,0:T(8,128)(2,1)S(1)}, u32[]{:S(2)}, u32[]{:S(2)}) %collective-permute-start.5) | collective-permute-done | bytes 98336 | tf_op jit(solution)/shard_map/ppermute | solution.py:519
  24.8 0.0 collective-permute-start.10
  24.8 0.0 collective-permute-done.6.refs_7_
  24.8 0.5 %collective-permute-start.11 = (bf16[384,128]{1,0:T(8,128)(2,1)S(1)}, bf16[384,128]{1,0:T(8,128)(2,1)S(1)}, u32[]{:S(2)}, u32[]{:S(2)}) collective-permute-start(bf16[384,128]{1,0:T(8,128)(2,1)S(1)} %collective-permute-done.3.refs_4_), channel_id=1, source_target_pairs={{0,1},{1,0},{2,3},{3,2},{4,5},{5,4},{6,7},{7,6},{8,9},{9,8},{10,11... | collective-permute-start | bytes 294920 | tf_op jit(solution)/shard_map/ppermute | solution.py:519
  25.3 0.0 collective-permute-done.7.refs_8_
  25.3 0.1 collective-permute-start.12
  25.4 0.0 collective-permute-done.8.refs_9_
  25.4 0.4 %collective-permute-start.13 = (bf16[384,128]{1,0:T(8,128)(2,1)S(1)}, bf16[384,128]{1,0:T(8,128)(2,1)S(1)}, u32[]{:S(2)}, u32[]{:S(2)}) collective-permute-start(bf16[384,128]{1,0:T(8,128)(2,1)S(1)} %collective-permute-done.5.refs_6_), channel_id=1, source_target_pairs={{0,1},{1,0},{2,3},{3,2},{4,5},{5,4},{6,7},{7,6},{8,9},{9,8},{10,11... | collective-permute-start | bytes 294920 | tf_op jit(solution)/shard_map/ppermute | solution.py:519
  25.8 0.0 collective-permute-done.9.refs_10_
  25.8 0.1 collective-permute-start.14
  25.9 0.2 collective-permute-done.10.refs_11_
  26.1 0.2 collective-permute-done.11.refs_12_
  26.3 0.4 collective-permute-done.12.refs_13_
  26.6 0.2 collective-permute-done.13.refs_14_
  26.8 0.4 collective-permute-done.14.refs_15_
  27.1 1.0 %shard_map.176 = (bf16[256,128]{1,0:T(8,128)(2,1)S(1)}, bf16[256,128]{1,0:T(8,128)(2,1)S(1)}, bf16[256,128]{1,0:T(8,128)(2,1)S(1)}, bf16[256,128]{1,0:T(8,128)(2,1)S(1)}) custom-call(s32[8,128]{1,0:T(8,128)S(1)} %get-tuple-element.20.bounds, bf16[384,128]{1,0:T(8,128)(2,1)S(1)} %get-tuple-element.21.refs_0_, ...), custom_call_target="tpu_custom_call" | custom-call | tf_op jit(solution)/shard_map/pallas_call | solution.py:575
  28.1 2.6 %collective-permute-start.15 = (bf16[256,128]{1,0:T(8,128)(2,1)S(1)}, bf16[256,128]{1,0:T(8,128)(2,1)S(1)}, u32[]{:S(2)}, u32[]{:S(2)}) collective-permute-start(bf16[256,128]{1,0:T(8,128)(2,1)S(1)} %get-tuple-element.28), channel_id=1, source_target_pairs={{0,14},{1,13},{2,12},{3,15},{4,10},{5,9},{6,8},{7,11},{8,6},{9,5},... | collective-permute-start | bytes 196616 | tf_op jit(solution)/shard_map/ppermute | solution.py:583
  30.7 0.0 collective-permute-start.16
  30.7 1.3 %collective-permute-start.17 = (bf16[256,128]{1,0:T(8,128)(2,1)S(1)}, bf16[256,128]{1,0:T(8,128)(2,1)S(1)}, u32[]{:S(2)}, u32[]{:S(2)}) collective-permute-start(bf16[256,128]{1,0:T(8,128)(2,1)S(1)} %get-tuple-element.30), channel_id=1, source_target_pairs={{0,2},{1,7},{2,0},{3,5},{4,6},{5,3},{6,4},{7,1},{8,10},{9,15},{10,... | collective-permute-start | bytes 196616 | tf_op jit(solution)/shard_map/ppermute | solution.py:583
  32.1 0.7 %collective-permute-start.18 = (bf16[256,128]{1,0:T(8,128)(2,1)S(1)}, bf16[256,128]{1,0:T(8,128)(2,1)S(1)}, u32[]{:S(2)}, u32[]{:S(2)}) collective-permute-start(bf16[256,128]{1,0:T(8,128)(2,1)S(1)} %get-tuple-element.31), channel_id=1, source_target_pairs={{0,0},{1,5},{2,2},{3,7},{4,4},{5,1},{6,6},{7,3},{8,8},{9,13},{10,1... | collective-permute-start | bytes 196616 | tf_op jit(solution)/shard_map/ppermute | solution.py:583
  32.7 3.3 %collective-permute-done.15.refs_0_ = bf16[256,128]{1,0:T(8,128)(2,1)S(1)} collective-permute-done((bf16[256,128]{1,0:T(8,128)(2,1)S(1)}, bf16[256,128]{1,0:T(8,128)(2,1)S(1)}, u32[]{:S(2)}, u32[]{:S(2)}) %collective-permute-start.15) | collective-permute-done | bytes 65568 | tf_op jit(solution)/shard_map/ppermute | solution.py:583
  36.0 0.0 collective-permute-start.19
  36.0 1.1 %collective-permute-done.16.refs_1_ = bf16[256,128]{1,0:T(8,128)(2,1)S(1)} collective-permute-done((bf16[256,128]{1,0:T(8,128)(2,1)S(1)}, bf16[256,128]{1,0:T(8,128)(2,1)S(1)}, u32[]{:S(2)}, u32[]{:S(2)}) %collective-permute-start.16) | collective-permute-done | bytes 65568 | tf_op jit(solution)/shard_map/ppermute | solution.py:583
  37.1 1.3 %collective-permute-start.20 = (bf16[256,128]{1,0:T(8,128)(2,1)S(1)}, bf16[256,128]{1,0:T(8,128)(2,1)S(1)}, u32[]{:S(2)}, u32[]{:S(2)}) collective-permute-start(bf16[256,128]{1,0:T(8,128)(2,1)S(1)} %collective-permute-done.16.refs_1_), channel_id=1, source_target_pairs={{0,1},{1,0},{2,3},{3,2},{4,5},{5,4},{6,7},{7,6},{8,9},{9,8},{10,11... | collective-permute-start | bytes 196616 | tf_op jit(solution)/shard_map/ppermute | solution.py:519
  38.3 0.0 collective-permute-done.17.refs_2_
  38.3 0.0 collective-permute-start.21
  38.3 0.0 collective-permute-done.18.refs_3_
  38.3 0.5 %collective-permute-start.22 = (bf16[256,128]{1,0:T(8,128)(2,1)S(1)}, bf16[256,128]{1,0:T(8,128)(2,1)S(1)}, u32[]{:S(2)}, u32[]{:S(2)}) collective-permute-start(bf16[256,128]{1,0:T(8,128)(2,1)S(1)} %collective-permute-done.18.refs_3_), channel_id=1, source_target_pairs={{0,1},{1,0},{2,3},{3,2},{4,5},{5,4},{6,7},{7,6},{8,9},{9,8},{10,11... | collective-permute-start | bytes 196616 | tf_op jit(solution)/shard_map/ppermute | solution.py:519
  38.8 0.0 collective-permute-done.19.refs_4_
  38.8 0.4 collective-permute-done.20.refs_5_
  39.2 0.4 collective-permute-done.21.refs_6_
  39.6 0.2 collective-permute-done.22.refs_7_
  39.7 0.8 %shard_map.177 = (bf16[16,4096]{1,0:T(8,128)(2,1)}, bf16[8,2048]{1,0:T(8,128)(2,1)}, bf16[16,2048]{1,0:T(8,128)(2,1)}, bf16[8,2048]{1,0:T(8,128)(2,1)}) custom-call(bf16[256,128]{1,0:T(8,128)(2,1)S(1)} %collective-permute-done.15.refs_0_, bf16[256,128]{1,0:T(8,128)(2,1)S(1)} %collective-permute-done.16.refs_1_, ...), custom_call_target="tpu_custom_call" | custom-call | tf_op jit(solution)/shard_map/pallas_call | solution.py:586
  (1 shorter events, 0.0 us)
Async XLA Ops:
  1.9 13.9 %collective-permute-start = (bf16[384,128]{1,0:T(8,128)(2,1)S(1)}, bf16[384,128]{1,0:T(8,128)(2,1)S(1)}, u32[]{:S(2)}, u32[]{:S(2)}) collective-permute-start(bf16[384,128]{1,0:T(8,128)(2,1)S(1)} %get-tuple-element.18), channel_id=1, source_target_pairs={{0,14},{1,15},{2,12},{3,13},{4,10},{5,11},{6,8},{7,9},{8,6},{9,7},... | collective-permute-start | bytes 294920 | tf_op jit(solution)/shard_map/ppermute | solution.py:519
  8.0 8.5 %collective-permute-start.1 = (bf16[384,128]{1,0:T(8,128)(2,1)S(1)}, bf16[384,128]{1,0:T(8,128)(2,1)S(1)}, u32[]{:S(2)}, u32[]{:S(2)}) collective-permute-start(bf16[384,128]{1,0:T(8,128)(2,1)S(1)} %get-tuple-element.22), channel_id=1, source_target_pairs={{0,2},{1,3},{2,0},{3,1},{4,6},{5,7},{6,4},{7,5},{8,10},{9,11},{10,... | collective-permute-start | bytes 294920 | tf_op jit(solution)/shard_map/ppermute | solution.py:519
  8.5 8.6 %collective-permute-start.2 = (bf16[384,128]{1,0:T(8,128)(2,1)S(1)}, bf16[384,128]{1,0:T(8,128)(2,1)S(1)}, u32[]{:S(2)}, u32[]{:S(2)}) collective-permute-start(bf16[384,128]{1,0:T(8,128)(2,1)S(1)} %get-tuple-element.23), channel_id=1, source_target_pairs={{0,12},{1,13},{2,14},{3,15},{4,8},{5,9},{6,10},{7,11},{8,4},{9,5},... | collective-permute-start | bytes 294920 | tf_op jit(solution)/shard_map/ppermute | solution.py:519
  8.7 8.5 %collective-permute-start.3 = (bf16[384,128]{1,0:T(8,128)(2,1)S(1)}, bf16[384,128]{1,0:T(8,128)(2,1)S(1)}, u32[]{:S(2)}, u32[]{:S(2)}) collective-permute-start(bf16[384,128]{1,0:T(8,128)(2,1)S(1)} %get-tuple-element.24), channel_id=1, source_target_pairs={{0,4},{1,5},{2,6},{3,7},{4,0},{5,1},{6,2},{7,3},{8,12},{9,13},{10,... | collective-permute-start | bytes 294920 | tf_op jit(solution)/shard_map/ppermute | solution.py:519
  8.7 14.7 %collective-permute-start.4 = (bf16[384,128]{1,0:T(8,128)(2,1)S(1)}, bf16[384,128]{1,0:T(8,128)(2,1)S(1)}, u32[]{:S(2)}, u32[]{:S(2)}) collective-permute-start(bf16[384,128]{1,0:T(8,128)(2,1)S(1)} %get-tuple-element.25), channel_id=1, source_target_pairs={{0,10},{1,11},{2,8},{3,9},{4,14},{5,15},{6,12},{7,13},{8,2},{9,3},... | collective-permute-start | bytes 294920 | tf_op jit(solution)/shard_map/ppermute | solution.py:519
  15.8 9.0 %collective-permute-start.5 = (bf16[384,128]{1,0:T(8,128)(2,1)S(1)}, bf16[384,128]{1,0:T(8,128)(2,1)S(1)}, u32[]{:S(2)}, u32[]{:S(2)}) collective-permute-start(bf16[384,128]{1,0:T(8,128)(2,1)S(1)} %get-tuple-element.26), channel_id=1, source_target_pairs={{0,8},{1,9},{2,10},{3,11},{4,12},{5,13},{6,14},{7,15},{8,0},{9,1},... | collective-permute-start | bytes 294920 | tf_op jit(solution)/shard_map/ppermute | solution.py:519
  16.6 8.2 %collective-permute-start.6 = (bf16[384,128]{1,0:T(8,128)(2,1)S(1)}, bf16[384,128]{1,0:T(8,128)(2,1)S(1)}, u32[]{:S(2)}, u32[]{:S(2)}) collective-permute-start(bf16[384,128]{1,0:T(8,128)(2,1)S(1)} %get-tuple-element.27), channel_id=1, source_target_pairs={{0,6},{1,7},{2,4},{3,5},{4,2},{5,3},{6,0},{7,1},{8,14},{9,15},{10,... | collective-permute-start | bytes 294920 | tf_op jit(solution)/shard_map/ppermute | solution.py:519
  17.1 8.2 %collective-permute-start.7 = (bf16[384,128]{1,0:T(8,128)(2,1)S(1)}, bf16[384,128]{1,0:T(8,128)(2,1)S(1)}, u32[]{:S(2)}, u32[]{:S(2)}) collective-permute-start(bf16[384,128]{1,0:T(8,128)(2,1)S(1)} %get-tuple-element.21.refs_0_), channel_id=1, source_target_pairs={{0,1},{1,0},{2,3},{3,2},{4,5},{5,4},{6,7},{7,6},{8,9},{9,8},{10,11... | collective-permute-start | bytes 294920 | tf_op jit(solution)/shard_map/ppermute | solution.py:519
  17.1 8.3 %collective-permute-start.8 = (bf16[384,128]{1,0:T(8,128)(2,1)S(1)}, bf16[384,128]{1,0:T(8,128)(2,1)S(1)}, u32[]{:S(2)}, u32[]{:S(2)}) collective-permute-start(bf16[384,128]{1,0:T(8,128)(2,1)S(1)} %collective-permute-done.after.refs_1_), channel_id=1, source_target_pairs={{0,1},{1,0},{2,3},{3,2},{4,5},{5,4},{6,7},{7,6},{8,9},{9,8},{10,11... | collective-permute-start | bytes 294920 | tf_op jit(solution)/shard_map/ppermute | solution.py:519
  23.4 2.5 %collective-permute-start.9 = (bf16[384,128]{1,0:T(8,128)(2,1)S(1)}, bf16[384,128]{1,0:T(8,128)(2,1)S(1)}, u32[]{:S(2)}, u32[]{:S(2)}) collective-permute-start(bf16[384,128]{1,0:T(8,128)(2,1)S(1)} %collective-permute-done.1.refs_2_), channel_id=1, source_target_pairs={{0,1},{1,0},{2,3},{3,2},{4,5},{5,4},{6,7},{7,6},{8,9},{9,8},{10,11... | collective-permute-start | bytes 294920 | tf_op jit(solution)/shard_map/ppermute | solution.py:519
  24.8 1.3 %collective-permute-start.10 = (bf16[384,128]{1,0:T(8,128)(2,1)S(1)}, bf16[384,128]{1,0:T(8,128)(2,1)S(1)}, u32[]{:S(2)}, u32[]{:S(2)}) collective-permute-start(bf16[384,128]{1,0:T(8,128)(2,1)S(1)} %collective-permute-done.2.refs_3_), channel_id=1, source_target_pairs={{0,1},{1,0},{2,3},{3,2},{4,5},{5,4},{6,7},{7,6},{8,9},{9,8},{10,11... | collective-permute-start | bytes 294920 | tf_op jit(solution)/shard_map/ppermute | solution.py:519
  24.8 1.5 %collective-permute-start.11 = (bf16[384,128]{1,0:T(8,128)(2,1)S(1)}, bf16[384,128]{1,0:T(8,128)(2,1)S(1)}, u32[]{:S(2)}, u32[]{:S(2)}) collective-permute-start(bf16[384,128]{1,0:T(8,128)(2,1)S(1)} %collective-permute-done.3.refs_4_), channel_id=1, source_target_pairs={{0,1},{1,0},{2,3},{3,2},{4,5},{5,4},{6,7},{7,6},{8,9},{9,8},{10,11... | collective-permute-start | bytes 294920 | tf_op jit(solution)/shard_map/ppermute | solution.py:519
  25.3 1.3 %collective-permute-start.12 = (bf16[384,128]{1,0:T(8,128)(2,1)S(1)}, bf16[384,128]{1,0:T(8,128)(2,1)S(1)}, u32[]{:S(2)}, u32[]{:S(2)}) collective-permute-start(bf16[384,128]{1,0:T(8,128)(2,1)S(1)} %collective-permute-done.4.refs_5_), channel_id=1, source_target_pairs={{0,1},{1,0},{2,3},{3,2},{4,5},{5,4},{6,7},{7,6},{8,9},{9,8},{10,11... | collective-permute-start | bytes 294920 | tf_op jit(solution)/shard_map/ppermute | solution.py:519
  25.4 1.4 %collective-permute-start.13 = (bf16[384,128]{1,0:T(8,128)(2,1)S(1)}, bf16[384,128]{1,0:T(8,128)(2,1)S(1)}, u32[]{:S(2)}, u32[]{:S(2)}) collective-permute-start(bf16[384,128]{1,0:T(8,128)(2,1)S(1)} %collective-permute-done.5.refs_6_), channel_id=1, source_target_pairs={{0,1},{1,0},{2,3},{3,2},{4,5},{5,4},{6,7},{7,6},{8,9},{9,8},{10,11... | collective-permute-start | bytes 294920 | tf_op jit(solution)/shard_map/ppermute | solution.py:519
  25.8 1.3 %collective-permute-start.14 = (bf16[384,128]{1,0:T(8,128)(2,1)S(1)}, bf16[384,128]{1,0:T(8,128)(2,1)S(1)}, u32[]{:S(2)}, u32[]{:S(2)}) collective-permute-start(bf16[384,128]{1,0:T(8,128)(2,1)S(1)} %collective-permute-done.6.refs_7_), channel_id=1, source_target_pairs={{0,1},{1,0},{2,3},{3,2},{4,5},{5,4},{6,7},{7,6},{8,9},{9,8},{10,11... | collective-permute-start | bytes 294920 | tf_op jit(solution)/shard_map/ppermute | solution.py:519
  28.1 7.9 %collective-permute-start.15 = (bf16[256,128]{1,0:T(8,128)(2,1)S(1)}, bf16[256,128]{1,0:T(8,128)(2,1)S(1)}, u32[]{:S(2)}, u32[]{:S(2)}) collective-permute-start(bf16[256,128]{1,0:T(8,128)(2,1)S(1)} %get-tuple-element.28), channel_id=1, source_target_pairs={{0,14},{1,13},{2,12},{3,15},{4,10},{5,9},{6,8},{7,11},{8,6},{9,5},... | collective-permute-start | bytes 196616 | tf_op jit(solution)/shard_map/ppermute | solution.py:583
  30.7 6.3 %collective-permute-start.16 = (bf16[256,128]{1,0:T(8,128)(2,1)S(1)}, bf16[256,128]{1,0:T(8,128)(2,1)S(1)}, u32[]{:S(2)}, u32[]{:S(2)}) collective-permute-start(bf16[256,128]{1,0:T(8,128)(2,1)S(1)} %get-tuple-element.29), channel_id=1, source_target_pairs={{0,8},{1,11},{2,10},{3,9},{4,12},{5,15},{6,14},{7,13},{8,0},{9,3},... | collective-permute-start | bytes 196616 | tf_op jit(solution)/shard_map/ppermute | solution.py:583
  30.7 7.6 %collective-permute-start.17 = (bf16[256,128]{1,0:T(8,128)(2,1)S(1)}, bf16[256,128]{1,0:T(8,128)(2,1)S(1)}, u32[]{:S(2)}, u32[]{:S(2)}) collective-permute-start(bf16[256,128]{1,0:T(8,128)(2,1)S(1)} %get-tuple-element.30), channel_id=1, source_target_pairs={{0,2},{1,7},{2,0},{3,5},{4,6},{5,3},{6,4},{7,1},{8,10},{9,15},{10,... | collective-permute-start | bytes 196616 | tf_op jit(solution)/shard_map/ppermute | solution.py:583
  32.1 6.3 %collective-permute-start.18 = (bf16[256,128]{1,0:T(8,128)(2,1)S(1)}, bf16[256,128]{1,0:T(8,128)(2,1)S(1)}, u32[]{:S(2)}, u32[]{:S(2)}) collective-permute-start(bf16[256,128]{1,0:T(8,128)(2,1)S(1)} %get-tuple-element.31), channel_id=1, source_target_pairs={{0,0},{1,5},{2,2},{3,7},{4,4},{5,1},{6,6},{7,3},{8,8},{9,13},{10,1... | collective-permute-start | bytes 196616 | tf_op jit(solution)/shard_map/ppermute | solution.py:583
  36.0 2.9 %collective-permute-start.19 = (bf16[256,128]{1,0:T(8,128)(2,1)S(1)}, bf16[256,128]{1,0:T(8,128)(2,1)S(1)}, u32[]{:S(2)}, u32[]{:S(2)}) collective-permute-start(bf16[256,128]{1,0:T(8,128)(2,1)S(1)} %collective-permute-done.15.refs_0_), channel_id=1, source_target_pairs={{0,1},{1,0},{2,3},{3,2},{4,5},{5,4},{6,7},{7,6},{8,9},{9,8},{10,11... | collective-permute-start | bytes 196616 | tf_op jit(solution)/shard_map/ppermute | solution.py:519
  37.1 2.2 %collective-permute-start.20 = (bf16[256,128]{1,0:T(8,128)(2,1)S(1)}, bf16[256,128]{1,0:T(8,128)(2,1)S(1)}, u32[]{:S(2)}, u32[]{:S(2)}) collective-permute-start(bf16[256,128]{1,0:T(8,128)(2,1)S(1)} %collective-permute-done.16.refs_1_), channel_id=1, source_target_pairs={{0,1},{1,0},{2,3},{3,2},{4,5},{5,4},{6,7},{7,6},{8,9},{9,8},{10,11... | collective-permute-start | bytes 196616 | tf_op jit(solution)/shard_map/ppermute | solution.py:519
  38.3 1.3 %collective-permute-start.21 = (bf16[256,128]{1,0:T(8,128)(2,1)S(1)}, bf16[256,128]{1,0:T(8,128)(2,1)S(1)}, u32[]{:S(2)}, u32[]{:S(2)}) collective-permute-start(bf16[256,128]{1,0:T(8,128)(2,1)S(1)} %collective-permute-done.17.refs_2_), channel_id=1, source_target_pairs={{0,1},{1,0},{2,3},{3,2},{4,5},{5,4},{6,7},{7,6},{8,9},{9,8},{10,11... | collective-permute-start | bytes 196616 | tf_op jit(solution)/shard_map/ppermute | solution.py:519
  38.3 1.4 %collective-permute-start.22 = (bf16[256,128]{1,0:T(8,128)(2,1)S(1)}, bf16[256,128]{1,0:T(8,128)(2,1)S(1)}, u32[]{:S(2)}, u32[]{:S(2)}) collective-permute-start(bf16[256,128]{1,0:T(8,128)(2,1)S(1)} %collective-permute-done.18.refs_3_), channel_id=1, source_target_pairs={{0,1},{1,0},{2,3},{3,2},{4,5},{5,4},{6,7},{7,6},{8,9},{9,8},{10,11... | collective-permute-start | bytes 196616 | tf_op jit(solution)/shard_map/ppermute | solution.py:519

commit v12 on v11

--- a/solution.py
+++ b/solution.py
@@ -376,15 +376,14 @@
 
 def shares(chips):
     quarter = chips // 4
-    far = [(chips - 1 - 2 * i - i % 2, chips - 2 - 2 * i + i % 2) for i in range(quarter)]
-    near = list(zip(range(quarter - 1, -1, -1), range(2 * quarter - 1, quarter - 1, -1)))
-    return far + near
+    return [(chips - 1 - i, 3 * quarter - 1 - i) for i in range(quarter)]
 
 
 def attend_kernel(chips, rows, parts, pairs, bounds, *refs):
     own, other = by_step(refs[:chips]), by_step(refs[chips : 2 * chips])
-    done = refs[2 * chips :]
     share = shares(chips)
+    side = chips // 2
+    done, near_done = refs[2 * chips : 2 * chips + len(share)], refs[2 * chips + len(share) :]
     every = [ref for both in zip(own, other) for ref in both]
     half = rows // 2
     tv, ta = 2 * chips * rows, 2 * chips * half
@@ -397,7 +396,7 @@
         return jnp.concatenate([ref[at : at + rows, :] for ref in every], axis=0)
 
     def asked(at):
-        pieces = []
+        pieces = [own[j][at : at + rows, :] for j in range(side)]
         for zero, one in share:
             for c in range(2):
                 low = (own, other)[c][zero][at : at + rows, :]
@@ -414,18 +413,22 @@
     def places(q_step, k_step):
         shape = (chips * q_step, 2 * chips * k_step)
         k_at = lax.broadcasted_iota(jnp.int32, shape, 1) ^ (me * k_step)
-        starts = []
+        within = lax.broadcasted_iota(jnp.int32, (q_step, 1), 0)
+        starts = [within + (me ^ (2 * j)) * q_step for j in range(side)]
         for zero, one in share:
             chip = home ^ jnp.where(core == 0, 2 * zero, 2 * one)
-            starts.append(lax.broadcasted_iota(jnp.int32, (2 * q_step, 1), 0) + chip * q_step)
+            starts += [within + (chip + c) * q_step for c in range(2)]
         return jnp.concatenate(starts, axis=0), k_at
 
     def put(at, mixed):
-        count = done[0].shape[0] // 2
-        for u in range(len(share)):
-            for c in range(2):
-                piece = mixed[(2 * u + c) * rows : (2 * u + c + 1) * rows]
-                done[u][c * count + at : c * count + at + rows, :] = piece.astype(jnp.bfloat16)
+        count = near_done[0].shape[0]
+        for i in range(chips):
+            piece = mixed[i * rows : (i + 1) * rows].astype(jnp.bfloat16)
+            if i < side:
+                near_done[i][at : at + rows, :] = piece
+            else:
+                u, c = divmod(i - side, 2)
+                done[u][c * count + at : c * count + at + rows, :] = piece
 
     q_at, k_at = places(rows, rows)
     permit = k_at < video_valid
@@ -485,34 +488,38 @@
 
 def unpack_kernel(chips, *refs):
     share = shares(chips)
-    back, other = refs[: len(share)], refs[len(share) : 2 * len(share)]
-    video_mixed, audio_mixed, video_cross, audio_cross = refs[2 * len(share) :]
+    count, side = len(share), chips // 2
+    back, other, near = refs[:count], refs[count : 2 * count], refs[2 * count : 2 * count + side]
+    video_mixed, audio_mixed, video_cross, audio_cross = refs[2 * count + side :]
     rows = video_mixed.shape[0]
     half = audio_mixed.shape[0]
     parts = video_mixed.shape[1] // chips // LANES
     pairs = audio_mixed.shape[1] // chips // LANES
     me = lax.axis_index("seq")
     core, home = me % 2, me // 2
+
+    def place(ref, base, chip):
+        for h in range(parts):
+            at = pl.multiple_of((chip * parts + h) * LANES, LANES)
+            video_mixed[:, pl.ds(at, LANES)] = ref[pl.ds(base + h * rows, rows), :]
+        for p in range(pairs):
+            at = pl.multiple_of((chip * pairs + p) * LANES, LANES)
+            out = (parts + p) * rows
+            video_cross[:, pl.ds(at, LANES)] = ref[pl.ds(base + out, rows), :]
+            both = ref[pl.ds(base + out + pairs * rows, rows), :]
+            audio_mixed[:, pl.ds(at, LANES)] = both[:half, :]
+            audio_cross[:, pl.ds(at, LANES)] = both[half:, :]
+
+    for j in range(side):
+        place(near[j], 0, home ^ j)
     for u, (zero, one) in enumerate(share):
-        for ref, chip in (
-            (back[u], home ^ jnp.where(core == 0, zero, one)),
-            (other[u], home ^ jnp.where(core == 0, one, zero)),
-        ):
-            base = pl.multiple_of(core * (ref.shape[0] // 2), 16)
-
-            def piece(at):
-                return ref[pl.ds(base + at, rows), :]
-
-            for h in range(parts):
-                at = pl.multiple_of((chip * parts + h) * LANES, LANES)
-                video_mixed[:, pl.ds(at, LANES)] = piece(h * rows)
-            for p in range(pairs):
-                at = pl.multiple_of((chip * pairs + p) * LANES, LANES)
-                out = (parts + p) * rows
-                video_cross[:, pl.ds(at, LANES)] = piece(out)
-                both = piece(out + pairs * rows)
-                audio_mixed[:, pl.ds(at, LANES)] = both[:half, :]
-                audio_cross[:, pl.ds(at, LANES)] = both[half:, :]
+        base = pl.multiple_of(core * near[0].shape[0], 16)
+        place(back[u], base, home ^ jnp.where(core == 0, zero, one))
+        place(other[u], base, home ^ jnp.where(core == 0, one, zero))
+
+
+def tie_kernel(*refs):
+    pass
 
 
 def swap(piece, n, step):
@@ -572,17 +579,29 @@
     own = [kept] + moved
     other = [swap(piece, n, 1) for piece in own]
     share = shares(chips)
-    done = pl.pallas_call(
+    side = chips // 2
+    out_rows = (parts + 2 * pairs) * rows
+    results = pl.pallas_call(
         functools.partial(attend_kernel, chips, rows, parts, pairs),
-        out_shape=[buffer(2 * (parts + 2 * pairs) * rows, LANES)] * len(share),
+        out_shape=[buffer(2 * out_rows, LANES)] * len(share) + [buffer(out_rows, LANES)] * side,
         in_specs=[vmem] * (1 + 2 * chips),
-        out_specs=[vmem] * len(share),
+        out_specs=[vmem] * (len(share) + side),
         compiler_params=params,
     )(bounds, *in_order(own), *in_order(other))
     back = [
         lax.ppermute(piece, "seq", [(i, i ^ 2 * pair[i % 2]) for i in range(n)])
-        for piece, pair in zip(done, share)
+        for piece, pair in zip(results, share)
     ]
+    near = list(results[len(share) :])
+    near = near[:1] + [swap(near[j], n, 2 * j) for j in range(1, side)]
+    back = pl.pallas_call(
+        tie_kernel,
+        out_shape=[buffer(*piece.shape) for piece in back],
+        in_specs=[anywhere] * (len(share) + side - 1),
+        out_specs=[anywhere] * len(share),
+        input_output_aliases={u: u for u in range(len(share))},
+        compiler_params=params,
+    )(*back, *near[1:])
     return pl.pallas_call(
         functools.partial(unpack_kernel, chips),
         out_shape=(
@@ -591,10 +610,10 @@
             buffer(*cross_video_query.shape),
             buffer(*cross_audio_query.shape),
         ),
-        in_specs=[vmem] * (2 * len(share)),
+        in_specs=[vmem] * (2 * len(share) + side),
         out_specs=(vmem,) * 4,
         compiler_params=params,
-    )(*back, *[swap(piece, n, 1) for piece in back])
+    )(*back, *[swap(piece, n, 1) for piece in back], *near)
 
 
 def shards(*arrays):

time: 40.7 us -> 41.6 us (1.022)
  starting transfers between devices: 21.2 us -> 24.2 us
  waiting for transfers between devices: 13.6 us -> 11.5 us
    ppermute x4 -> x2, waiting for transfers between devices: 4.33 us -> 0.01 us  [shards_packed(): lax.ppermute(piece, 'seq', [(i, i ^ 2 * pair[i % 2]) for i in range(n)])]
    ppermute x19 -> x20, starting transfers between devices: 16.6 us -> 18.9 us  [swap(): return lax.ppermute(piece, 'seq', [(i, i ^ step) for i in range(n)])]
    ppermute x19 -> x20, waiting for transfers between devices: 9.3 us -> 11.5 us  [swap(): return lax.ppermute(piece, 'seq', [(i, i ^ step) for i in range(n)])]
    ppermute x4 -> x2, starting transfers between devices: 4.6 us -> 5.3 us  [shards_packed(): lax.ppermute(piece, 'seq', [(i, i ^ 2 * pair[i % 2]) for i in range(n)])]
  transfers between devices with their start and end apart: 23 -> 22, of which waited for: 12 -> 12; matrix products, arithmetic and copies ran while one was open for 0% -> 0% of each run, Pallas kernels for 0% -> 0%
where the time goes in v12:
time: 41.6 us; the launch traced here: 41.4 us
  starting transfers between devices  24.2 us (58%)
  waiting for transfers between devices  11.5 us (28%)
  Pallas kernels  3.05 us (7%)
  between operations  2.64 us (6%)
    ppermute x20, starting transfers between devices, swap(): return lax.ppermute(piece, 'seq', [(i, i ^ step) for i in range(n)])  18.9 us
    ppermute x20, waiting for transfers between devices, swap(): return lax.ppermute(piece, 'seq', [(i, i ^ step) for i in range(n)])  11.5 us
    ppermute x2, starting transfers between devices, shards_packed(): lax.ppermute(piece, 'seq', [(i, i ^ 2 * pair[i % 2]) for i in range(n)])  5.3 us
    pallas_call x1, Pallas kernels, shards_packed(): pl.pallas_call(functools.partial(pack_kernel, chips), out_shape=[pltpu.VM...  1.31 us
    pallas_call x1, Pallas kernels, shards_packed(): pl.pallas_call(functools.partial(attend_kernel, chips, rows, parts, pairs...  0.95 us
  transfers between devices with their start and end apart: 22, of which 12 were waited for; matrix products, arithmetic and copies ran while one was open for 0% of the time, Pallas kernels for 0%

profile of v12, /device:TPU:0, one launch (start us, length us, event | category | flops | bytes accessed | tf_op | source)
XLA Modules:
  0.0 41.4 jit_solution(14869725396686970033)
XLA Ops:
  0.6 1.3 %shard_map.174 = (bf16[384,128]{1,0:T(8,128)(2,1)S(1)}, bf16[384,128]{1,0:T(8,128)(2,1)S(1)}, bf16[384,128]{1,0:T(8,128)(2,1)S(1)}, bf16[384,128]{1,0:T(8,128)(2...) custom-call(bf16[16,4096]{1,0:T(8,128)(2,1)} %refs_0_.1, ...), custom_call_target="tpu_custom_call" | custom-call | tf_op jit(solution)/shard_map/pallas_call | solution.py:556
  1.9 6.1 %collective-permute-start = (bf16[384,128]{1,0:T(8,128)(2,1)S(1)}, bf16[384,128]{1,0:T(8,128)(2,1)S(1)}, u32[]{:S(2)}, u32[]{:S(2)}) collective-permute-start(bf16[384,128]{1,0:T(8,128)(2,1)S(1)} %get-tuple-element.22), channel_id=1, source_target_pairs={{0,14},{1,15},{2,12},{3,13},{4,10},{5,11},{6,8},{7,9},{8,6},{9,7},... | collective-permute-start | bytes 294920 | tf_op jit(solution)/shard_map/ppermute | solution.py:526
  8.0 0.5 %collective-permute-start.1 = (bf16[384,128]{1,0:T(8,128)(2,1)S(1)}, bf16[384,128]{1,0:T(8,128)(2,1)S(1)}, u32[]{:S(2)}, u32[]{:S(2)}) collective-permute-start(bf16[384,128]{1,0:T(8,128)(2,1)S(1)} %get-tuple-element.26), channel_id=1, source_target_pairs={{0,2},{1,3},{2,0},{3,1},{4,6},{5,7},{6,4},{7,5},{8,10},{9,11},{10,... | collective-permute-start | bytes 294920 | tf_op jit(solution)/shard_map/ppermute | solution.py:526
  8.5 0.1 collective-permute-start.2
  8.7 0.0 collective-permute-start.3
  8.7 5.2 %collective-permute-start.4 = (bf16[384,128]{1,0:T(8,128)(2,1)S(1)}, bf16[384,128]{1,0:T(8,128)(2,1)S(1)}, u32[]{:S(2)}, u32[]{:S(2)}) collective-permute-start(bf16[384,128]{1,0:T(8,128)(2,1)S(1)} %get-tuple-element.29), channel_id=1, source_target_pairs={{0,10},{1,11},{2,8},{3,9},{4,14},{5,15},{6,12},{7,13},{8,2},{9,3},... | collective-permute-start | bytes 294920 | tf_op jit(solution)/shard_map/ppermute | solution.py:526
  15.8 0.0 collective-permute-done.after.refs_1_
  15.8 0.7 %collective-permute-start.5 = (bf16[384,128]{1,0:T(8,128)(2,1)S(1)}, bf16[384,128]{1,0:T(8,128)(2,1)S(1)}, u32[]{:S(2)}, u32[]{:S(2)}) collective-permute-start(bf16[384,128]{1,0:T(8,128)(2,1)S(1)} %get-tuple-element.30), channel_id=1, source_target_pairs={{0,8},{1,9},{2,10},{3,11},{4,12},{5,13},{6,14},{7,15},{8,0},{9,1},... | collective-permute-start | bytes 294920 | tf_op jit(solution)/shard_map/ppermute | solution.py:526
  16.6 0.0 collective-permute-done.1.refs_2_
  16.6 0.6 %collective-permute-start.6 = (bf16[384,128]{1,0:T(8,128)(2,1)S(1)}, bf16[384,128]{1,0:T(8,128)(2,1)S(1)}, u32[]{:S(2)}, u32[]{:S(2)}) collective-permute-start(bf16[384,128]{1,0:T(8,128)(2,1)S(1)} %get-tuple-element.31), channel_id=1, source_target_pairs={{0,6},{1,7},{2,4},{3,5},{4,2},{5,3},{6,0},{7,1},{8,14},{9,15},{10,... | collective-permute-start | bytes 294920 | tf_op jit(solution)/shard_map/ppermute | solution.py:526
  17.1 0.0 collective-permute-done.2.refs_3_
  17.1 0.0 collective-permute-start.7
  17.1 0.0 collective-permute-done.3.refs_4_
  17.1 0.5 %collective-permute-start.8 = (bf16[384,128]{1,0:T(8,128)(2,1)S(1)}, bf16[384,128]{1,0:T(8,128)(2,1)S(1)}, u32[]{:S(2)}, u32[]{:S(2)}) collective-permute-start(bf16[384,128]{1,0:T(8,128)(2,1)S(1)} %collective-permute-done.after.refs_1_), channel_id=1, source_target_pairs={{0,1},{1,0},{2,3},{3,2},{4,5},{5,4},{6,7},{7,6},{8,9},{9,8},{10,11... | collective-permute-start | bytes 294920 | tf_op jit(solution)/shard_map/ppermute | solution.py:526
  17.7 5.7 %collective-permute-done.4.refs_5_ = bf16[384,128]{1,0:T(8,128)(2,1)S(1)} collective-permute-done((bf16[384,128]{1,0:T(8,128)(2,1)S(1)}, bf16[384,128]{1,0:T(8,128)(2,1)S(1)}, u32[]{:S(2)}, u32[]{:S(2)}) %collective-permute-start.4) | collective-permute-done | bytes 98336 | tf_op jit(solution)/shard_map/ppermute | solution.py:526
  23.4 0.0 collective-permute-start.9
  23.4 1.5 %collective-permute-done.5.refs_6_ = bf16[384,128]{1,0:T(8,128)(2,1)S(1)} collective-permute-done((bf16[384,128]{1,0:T(8,128)(2,1)S(1)}, bf16[384,128]{1,0:T(8,128)(2,1)S(1)}, u32[]{:S(2)}, u32[]{:S(2)}) %collective-permute-start.5) | collective-permute-done | bytes 98336 | tf_op jit(solution)/shard_map/ppermute | solution.py:526
  24.8 0.0 collective-permute-start.10
  24.8 0.0 collective-permute-done.6.refs_7_
  24.8 0.5 %collective-permute-start.11 = (bf16[384,128]{1,0:T(8,128)(2,1)S(1)}, bf16[384,128]{1,0:T(8,128)(2,1)S(1)}, u32[]{:S(2)}, u32[]{:S(2)}) collective-permute-start(bf16[384,128]{1,0:T(8,128)(2,1)S(1)} %collective-permute-done.3.refs_4_), channel_id=1, source_target_pairs={{0,1},{1,0},{2,3},{3,2},{4,5},{5,4},{6,7},{7,6},{8,9},{9,8},{10,11... | collective-permute-start | bytes 294920 | tf_op jit(solution)/shard_map/ppermute | solution.py:526
  25.3 0.0 collective-permute-done.7.refs_8_
  25.3 0.1 collective-permute-start.12
  25.4 0.0 collective-permute-done.8.refs_9_
  25.4 0.4 %collective-permute-start.13 = (bf16[384,128]{1,0:T(8,128)(2,1)S(1)}, bf16[384,128]{1,0:T(8,128)(2,1)S(1)}, u32[]{:S(2)}, u32[]{:S(2)}) collective-permute-start(bf16[384,128]{1,0:T(8,128)(2,1)S(1)} %collective-permute-done.5.refs_6_), channel_id=1, source_target_pairs={{0,1},{1,0},{2,3},{3,2},{4,5},{5,4},{6,7},{7,6},{8,9},{9,8},{10,11... | collective-permute-start | bytes 294920 | tf_op jit(solution)/shard_map/ppermute | solution.py:526
  25.8 0.0 collective-permute-done.9.refs_10_
  25.8 0.1 collective-permute-start.14
  25.9 0.2 collective-permute-done.10.refs_11_
  26.1 0.2 collective-permute-done.11.refs_12_
  26.3 0.4 collective-permute-done.12.refs_13_
  26.6 0.2 collective-permute-done.13.refs_14_
  26.8 0.4 collective-permute-done.14.refs_15_
  27.1 0.9 %shard_map.176 = (bf16[256,128]{1,0:T(8,128)(2,1)S(1)}, bf16[256,128]{1,0:T(8,128)(2,1)S(1)}, bf16[128,128]{1,0:T(8,128)(2,1)S(1)}, bf16[128,128]{1,0:T(8,128)(2...) custom-call(s32[8,128]{1,0:T(8,128)S(1)} %get-tuple-element.24.bounds, ...), custom_call_target="tpu_custom_call" | custom-call | tf_op jit(solution)/shard_map/pallas_call | solution.py:584
  28.1 2.6 %collective-permute-start.15 = (bf16[256,128]{1,0:T(8,128)(2,1)S(1)}, bf16[256,128]{1,0:T(8,128)(2,1)S(1)}, u32[]{:S(2)}, u32[]{:S(2)}) collective-permute-start(bf16[256,128]{1,0:T(8,128)(2,1)S(1)} %get-tuple-element.32), channel_id=1, source_target_pairs={{0,14},{1,11},{2,12},{3,9},{4,10},{5,15},{6,8},{7,13},{8,6},{9,3},... | collective-permute-start | bytes 196616 | tf_op jit(solution)/shard_map/ppermute | solution.py:592
  30.7 2.7 %collective-permute-start.16 = (bf16[256,128]{1,0:T(8,128)(2,1)S(1)}, bf16[256,128]{1,0:T(8,128)(2,1)S(1)}, u32[]{:S(2)}, u32[]{:S(2)}) collective-permute-start(bf16[256,128]{1,0:T(8,128)(2,1)S(1)} %get-tuple-element.33), channel_id=1, source_target_pairs={{0,12},{1,9},{2,14},{3,11},{4,8},{5,13},{6,10},{7,15},{8,4},{9,1},... | collective-permute-start | bytes 196616 | tf_op jit(solution)/shard_map/ppermute | solution.py:592
  33.4 0.1 collective-permute-start.17
  33.5 0.0 collective-permute-start.18
  33.5 3.4 %collective-permute-start.19 = (bf16[128,128]{1,0:T(8,128)(2,1)S(1)}, bf16[128,128]{1,0:T(8,128)(2,1)S(1)}, u32[]{:S(2)}, u32[]{:S(2)}) collective-permute-start(bf16[128,128]{1,0:T(8,128)(2,1)S(1)} %get-tuple-element.36), channel_id=1, source_target_pairs={{0,6},{1,7},{2,4},{3,5},{4,2},{5,3},{6,0},{7,1},{8,14},{9,15},{10,... | collective-permute-start | bytes 98312 | tf_op jit(solution)/shard_map/ppermute | solution.py:526
  36.9 0.4 %collective-permute-done.17.refs_2_.refs_5_ = bf16[128,128]{1,0:T(8,128)(2,1)S(1)} collective-permute-done((bf16[128,128]{1,0:T(8,128)(2,1)S(1)}, bf16[128,128]{1,0:T(8,128)(2,1)S(1)}, u32[]{:S(2)}, u32[]{:S(2)}) %collective-permute-start.17) | collective-permute-done | bytes 32800 | tf_op jit(solution)/shard_map/ppermute | solution.py:526
  37.3 0.4 %collective-permute-done.18.refs_3_.refs_6_ = bf16[128,128]{1,0:T(8,128)(2,1)S(1)} collective-permute-done((bf16[128,128]{1,0:T(8,128)(2,1)S(1)}, bf16[128,128]{1,0:T(8,128)(2,1)S(1)}, u32[]{:S(2)}, u32[]{:S(2)}) %collective-permute-start.18) | collective-permute-done | bytes 32800 | tf_op jit(solution)/shard_map/ppermute | solution.py:526
  37.7 1.4 %collective-permute-done.19.refs_4_.refs_7_ = bf16[128,128]{1,0:T(8,128)(2,1)S(1)} collective-permute-done((bf16[128,128]{1,0:T(8,128)(2,1)S(1)}, bf16[128,128]{1,0:T(8,128)(2,1)S(1)}, u32[]{:S(2)}, u32[]{:S(2)}) %collective-permute-start.19) | collective-permute-done | bytes 32800 | tf_op jit(solution)/shard_map/ppermute | solution.py:526
  39.1 0.0 collective-permute-done.15.refs_0_
  39.1 0.0 collective-permute-done.16.refs_1_
  39.1 0.1 collective-permute-start.20
  39.2 0.5 %collective-permute-start.21 = (bf16[256,128]{1,0:T(8,128)(2,1)S(1)}, bf16[256,128]{1,0:T(8,128)(2,1)S(1)}, u32[]{:S(2)}, u32[]{:S(2)}) collective-permute-start(bf16[256,128]{1,0:T(8,128)(2,1)S(1)} %get-tuple-element.38.refs_1_), channel_id=1, source_target_pairs={{0,1},{1,0},{2,3},{3,2},{4,5},{5,4},{6,7},{7,6},{8,9},{9,8},{10,11... | collective-permute-start | bytes 196616 | tf_op jit(solution)/shard_map/ppermute | solution.py:526
  39.7 0.7 %collective-permute-done.20.refs_2_ = bf16[256,128]{1,0:T(8,128)(2,1)S(1)} collective-permute-done((bf16[256,128]{1,0:T(8,128)(2,1)S(1)}, bf16[256,128]{1,0:T(8,128)(2,1)S(1)}, u32[]{:S(2)}, u32[]{:S(2)}) %collective-permute-start.20) | collective-permute-done | bytes 65568 | tf_op jit(solution)/shard_map/ppermute | solution.py:526
  40.5 0.2 collective-permute-done.21.refs_3_
  40.6 0.8 %shard_map.178 = (bf16[16,4096]{1,0:T(8,128)(2,1)}, bf16[8,2048]{1,0:T(8,128)(2,1)}, bf16[16,2048]{1,0:T(8,128)(2,1)}, bf16[8,2048]{1,0:T(8,128)(2,1)}) custom-call(bf16[256,128]{1,0:T(8,128)(2,1)S(1)} %get-tuple-element.37.refs_0_, bf16[256,128]{1,0:T(8,128)(2,1)S(1)} %get-tuple-element.38.refs_1_, bf16[256,128]{1,0:T(8,128)(2,1)S(1)} %collective-permute-done.20.refs_2_, ...), custom_call_target="tpu_custom_call" | custom-call | tf_op jit(solution)/shard_map/pallas_call | solution.py:605
  (2 shorter events, 0.0 us)
Async XLA Ops:
  1.9 13.9 %collective-permute-start = (bf16[384,128]{1,0:T(8,128)(2,1)S(1)}, bf16[384,128]{1,0:T(8,128)(2,1)S(1)}, u32[]{:S(2)}, u32[]{:S(2)}) collective-permute-start(bf16[384,128]{1,0:T(8,128)(2,1)S(1)} %get-tuple-element.22), channel_id=1, source_target_pairs={{0,14},{1,15},{2,12},{3,13},{4,10},{5,11},{6,8},{7,9},{8,6},{9,7},... | collective-permute-start | bytes 294920 | tf_op jit(solution)/shard_map/ppermute | solution.py:526
  8.0 8.5 %collective-permute-start.1 = (bf16[384,128]{1,0:T(8,128)(2,1)S(1)}, bf16[384,128]{1,0:T(8,128)(2,1)S(1)}, u32[]{:S(2)}, u32[]{:S(2)}) collective-permute-start(bf16[384,128]{1,0:T(8,128)(2,1)S(1)} %get-tuple-element.26), channel_id=1, source_target_pairs={{0,2},{1,3},{2,0},{3,1},{4,6},{5,7},{6,4},{7,5},{8,10},{9,11},{10,... | collective-permute-start | bytes 294920 | tf_op jit(solution)/shard_map/ppermute | solution.py:526
  8.5 8.6 %collective-permute-start.2 = (bf16[384,128]{1,0:T(8,128)(2,1)S(1)}, bf16[384,128]{1,0:T(8,128)(2,1)S(1)}, u32[]{:S(2)}, u32[]{:S(2)}) collective-permute-start(bf16[384,128]{1,0:T(8,128)(2,1)S(1)} %get-tuple-element.27), channel_id=1, source_target_pairs={{0,12},{1,13},{2,14},{3,15},{4,8},{5,9},{6,10},{7,11},{8,4},{9,5},... | collective-permute-start | bytes 294920 | tf_op jit(solution)/shard_map/ppermute | solution.py:526
  8.7 8.5 %collective-permute-start.3 = (bf16[384,128]{1,0:T(8,128)(2,1)S(1)}, bf16[384,128]{1,0:T(8,128)(2,1)S(1)}, u32[]{:S(2)}, u32[]{:S(2)}) collective-permute-start(bf16[384,128]{1,0:T(8,128)(2,1)S(1)} %get-tuple-element.28), channel_id=1, source_target_pairs={{0,4},{1,5},{2,6},{3,7},{4,0},{5,1},{6,2},{7,3},{8,12},{9,13},{10,... | collective-permute-start | bytes 294920 | tf_op jit(solution)/shard_map/ppermute | solution.py:526
  8.7 14.7 %collective-permute-start.4 = (bf16[384,128]{1,0:T(8,128)(2,1)S(1)}, bf16[384,128]{1,0:T(8,128)(2,1)S(1)}, u32[]{:S(2)}, u32[]{:S(2)}) collective-permute-start(bf16[384,128]{1,0:T(8,128)(2,1)S(1)} %get-tuple-element.29), channel_id=1, source_target_pairs={{0,10},{1,11},{2,8},{3,9},{4,14},{5,15},{6,12},{7,13},{8,2},{9,3},... | collective-permute-start | bytes 294920 | tf_op jit(solution)/shard_map/ppermute | solution.py:526
  15.8 9.0 %collective-permute-start.5 = (bf16[384,128]{1,0:T(8,128)(2,1)S(1)}, bf16[384,128]{1,0:T(8,128)(2,1)S(1)}, u32[]{:S(2)}, u32[]{:S(2)}) collective-permute-start(bf16[384,128]{1,0:T(8,128)(2,1)S(1)} %get-tuple-element.30), channel_id=1, source_target_pairs={{0,8},{1,9},{2,10},{3,11},{4,12},{5,13},{6,14},{7,15},{8,0},{9,1},... | collective-permute-start | bytes 294920 | tf_op jit(solution)/shard_map/ppermute | solution.py:526
  16.6 8.2 %collective-permute-start.6 = (bf16[384,128]{1,0:T(8,128)(2,1)S(1)}, bf16[384,128]{1,0:T(8,128)(2,1)S(1)}, u32[]{:S(2)}, u32[]{:S(2)}) collective-permute-start(bf16[384,128]{1,0:T(8,128)(2,1)S(1)} %get-tuple-element.31), channel_id=1, source_target_pairs={{0,6},{1,7},{2,4},{3,5},{4,2},{5,3},{6,0},{7,1},{8,14},{9,15},{10,... | collective-permute-start | bytes 294920 | tf_op jit(solution)/shard_map/ppermute | solution.py:526
  17.1 8.2 %collective-permute-start.7 = (bf16[384,128]{1,0:T(8,128)(2,1)S(1)}, bf16[384,128]{1,0:T(8,128)(2,1)S(1)}, u32[]{:S(2)}, u32[]{:S(2)}) collective-permute-start(bf16[384,128]{1,0:T(8,128)(2,1)S(1)} %get-tuple-element.25.refs_0_), channel_id=1, source_target_pairs={{0,1},{1,0},{2,3},{3,2},{4,5},{5,4},{6,7},{7,6},{8,9},{9,8},{10,11... | collective-permute-start | bytes 294920 | tf_op jit(solution)/shard_map/ppermute | solution.py:526
  17.1 8.3 %collective-permute-start.8 = (bf16[384,128]{1,0:T(8,128)(2,1)S(1)}, bf16[384,128]{1,0:T(8,128)(2,1)S(1)}, u32[]{:S(2)}, u32[]{:S(2)}) collective-permute-start(bf16[384,128]{1,0:T(8,128)(2,1)S(1)} %collective-permute-done.after.refs_1_), channel_id=1, source_target_pairs={{0,1},{1,0},{2,3},{3,2},{4,5},{5,4},{6,7},{7,6},{8,9},{9,8},{10,11... | collective-permute-start | bytes 294920 | tf_op jit(solution)/shard_map/ppermute | solution.py:526
  23.4 2.5 %collective-permute-start.9 = (bf16[384,128]{1,0:T(8,128)(2,1)S(1)}, bf16[384,128]{1,0:T(8,128)(2,1)S(1)}, u32[]{:S(2)}, u32[]{:S(2)}) collective-permute-start(bf16[384,128]{1,0:T(8,128)(2,1)S(1)} %collective-permute-done.1.refs_2_), channel_id=1, source_target_pairs={{0,1},{1,0},{2,3},{3,2},{4,5},{5,4},{6,7},{7,6},{8,9},{9,8},{10,11... | collective-permute-start | bytes 294920 | tf_op jit(solution)/shard_map/ppermute | solution.py:526
  24.8 1.3 %collective-permute-start.10 = (bf16[384,128]{1,0:T(8,128)(2,1)S(1)}, bf16[384,128]{1,0:T(8,128)(2,1)S(1)}, u32[]{:S(2)}, u32[]{:S(2)}) collective-permute-start(bf16[384,128]{1,0:T(8,128)(2,1)S(1)} %collective-permute-done.2.refs_3_), channel_id=1, source_target_pairs={{0,1},{1,0},{2,3},{3,2},{4,5},{5,4},{6,7},{7,6},{8,9},{9,8},{10,11... | collective-permute-start | bytes 294920 | tf_op jit(solution)/shard_map/ppermute | solution.py:526
  24.8 1.5 %collective-permute-start.11 = (bf16[384,128]{1,0:T(8,128)(2,1)S(1)}, bf16[384,128]{1,0:T(8,128)(2,1)S(1)}, u32[]{:S(2)}, u32[]{:S(2)}) collective-permute-start(bf16[384,128]{1,0:T(8,128)(2,1)S(1)} %collective-permute-done.3.refs_4_), channel_id=1, source_target_pairs={{0,1},{1,0},{2,3},{3,2},{4,5},{5,4},{6,7},{7,6},{8,9},{9,8},{10,11... | collective-permute-start | bytes 294920 | tf_op jit(solution)/shard_map/ppermute | solution.py:526
  25.3 1.3 %collective-permute-start.12 = (bf16[384,128]{1,0:T(8,128)(2,1)S(1)}, bf16[384,128]{1,0:T(8,128)(2,1)S(1)}, u32[]{:S(2)}, u32[]{:S(2)}) collective-permute-start(bf16[384,128]{1,0:T(8,128)(2,1)S(1)} %collective-permute-done.4.refs_5_), channel_id=1, source_target_pairs={{0,1},{1,0},{2,3},{3,2},{4,5},{5,4},{6,7},{7,6},{8,9},{9,8},{10,11... | collective-permute-start | bytes 294920 | tf_op jit(solution)/shard_map/ppermute | solution.py:526
  25.4 1.4 %collective-permute-start.13 = (bf16[384,128]{1,0:T(8,128)(2,1)S(1)}, bf16[384,128]{1,0:T(8,128)(2,1)S(1)}, u32[]{:S(2)}, u32[]{:S(2)}) collective-permute-start(bf16[384,128]{1,0:T(8,128)(2,1)S(1)} %collective-permute-done.5.refs_6_), channel_id=1, source_target_pairs={{0,1},{1,0},{2,3},{3,2},{4,5},{5,4},{6,7},{7,6},{8,9},{9,8},{10,11... | collective-permute-start | bytes 294920 | tf_op jit(solution)/shard_map/ppermute | solution.py:526
  25.8 1.3 %collective-permute-start.14 = (bf16[384,128]{1,0:T(8,128)(2,1)S(1)}, bf16[384,128]{1,0:T(8,128)(2,1)S(1)}, u32[]{:S(2)}, u32[]{:S(2)}) collective-permute-start(bf16[384,128]{1,0:T(8,128)(2,1)S(1)} %collective-permute-done.6.refs_7_), channel_id=1, source_target_pairs={{0,1},{1,0},{2,3},{3,2},{4,5},{5,4},{6,7},{7,6},{8,9},{9,8},{10,11... | collective-permute-start | bytes 294920 | tf_op jit(solution)/shard_map/ppermute | solution.py:526
  28.1 11.0 %collective-permute-start.15 = (bf16[256,128]{1,0:T(8,128)(2,1)S(1)}, bf16[256,128]{1,0:T(8,128)(2,1)S(1)}, u32[]{:S(2)}, u32[]{:S(2)}) collective-permute-start(bf16[256,128]{1,0:T(8,128)(2,1)S(1)} %get-tuple-element.32), channel_id=1, source_target_pairs={{0,14},{1,11},{2,12},{3,9},{4,10},{5,15},{6,8},{7,13},{8,6},{9,3},... | collective-permute-start | bytes 196616 | tf_op jit(solution)/shard_map/ppermute | solution.py:592
  30.7 8.4 %collective-permute-start.16 = (bf16[256,128]{1,0:T(8,128)(2,1)S(1)}, bf16[256,128]{1,0:T(8,128)(2,1)S(1)}, u32[]{:S(2)}, u32[]{:S(2)}) collective-permute-start(bf16[256,128]{1,0:T(8,128)(2,1)S(1)} %get-tuple-element.33), channel_id=1, source_target_pairs={{0,12},{1,9},{2,14},{3,11},{4,8},{5,13},{6,10},{7,15},{8,4},{9,1},... | collective-permute-start | bytes 196616 | tf_op jit(solution)/shard_map/ppermute | solution.py:592
  33.4 3.9 %collective-permute-start.17 = (bf16[128,128]{1,0:T(8,128)(2,1)S(1)}, bf16[128,128]{1,0:T(8,128)(2,1)S(1)}, u32[]{:S(2)}, u32[]{:S(2)}) collective-permute-start(bf16[128,128]{1,0:T(8,128)(2,1)S(1)} %get-tuple-element.34), channel_id=1, source_target_pairs={{0,2},{1,3},{2,0},{3,1},{4,6},{5,7},{6,4},{7,5},{8,10},{9,11},{10,... | collective-permute-start | bytes 98312 | tf_op jit(solution)/shard_map/ppermute | solution.py:526
  33.5 4.3 %collective-permute-start.18 = (bf16[128,128]{1,0:T(8,128)(2,1)S(1)}, bf16[128,128]{1,0:T(8,128)(2,1)S(1)}, u32[]{:S(2)}, u32[]{:S(2)}) collective-permute-start(bf16[128,128]{1,0:T(8,128)(2,1)S(1)} %get-tuple-element.35), channel_id=1, source_target_pairs={{0,4},{1,5},{2,6},{3,7},{4,0},{5,1},{6,2},{7,3},{8,12},{9,13},{10,... | collective-permute-start | bytes 98312 | tf_op jit(solution)/shard_map/ppermute | solution.py:526
  33.5 5.7 %collective-permute-start.19 = (bf16[128,128]{1,0:T(8,128)(2,1)S(1)}, bf16[128,128]{1,0:T(8,128)(2,1)S(1)}, u32[]{:S(2)}, u32[]{:S(2)}) collective-permute-start(bf16[128,128]{1,0:T(8,128)(2,1)S(1)} %get-tuple-element.36), channel_id=1, source_target_pairs={{0,6},{1,7},{2,4},{3,5},{4,2},{5,3},{6,0},{7,1},{8,14},{9,15},{10,... | collective-permute-start | bytes 98312 | tf_op jit(solution)/shard_map/ppermute | solution.py:526
  39.1 1.3 %collective-permute-start.20 = (bf16[256,128]{1,0:T(8,128)(2,1)S(1)}, bf16[256,128]{1,0:T(8,128)(2,1)S(1)}, u32[]{:S(2)}, u32[]{:S(2)}) collective-permute-start(bf16[256,128]{1,0:T(8,128)(2,1)S(1)} %get-tuple-element.37.refs_0_), channel_id=1, source_target_pairs={{0,1},{1,0},{2,3},{3,2},{4,5},{5,4},{6,7},{7,6},{8,9},{9,8},{10,11... | collective-permute-start | bytes 196616 | tf_op jit(solution)/shard_map/ppermute | solution.py:526
  39.2 1.4 %collective-permute-start.21 = (bf16[256,128]{1,0:T(8,128)(2,1)S(1)}, bf16[256,128]{1,0:T(8,128)(2,1)S(1)}, u32[]{:S(2)}, u32[]{:S(2)}) collective-permute-start(bf16[256,128]{1,0:T(8,128)(2,1)S(1)} %get-tuple-element.38.refs_1_), channel_id=1, source_target_pairs={{0,1},{1,0},{2,3},{3,2},{4,5},{5,4},{6,7},{7,6},{8,9},{9,8},{10,11... | collective-permute-start | bytes 196616 | tf_op jit(solution)/shard_map/ppermute | solution.py:526

commit v13 on v10

--- a/solution.py
+++ b/solution.py
@@ -335,9 +335,17 @@
             at += rows
 
 
-def bounds_kernel(video_len, audio_len, shift, after, slab, bounds, same):
+def gather_kernel(video_len, audio_len, shift, *refs):
+    slabs, bounds, merged = refs[:-2], refs[-2], refs[-1]
     row = lax.broadcasted_iota(jnp.int32, bounds.shape, 0)
     bounds[...] = jnp.where(row == 0, video_len[0], jnp.where(row == 1, audio_len[0], shift[0]))
+    for i, slab in enumerate(slabs):
+        merged[i] = slab[...]
+
+
+def merge_kernel(*refs):
+    for i, slab in enumerate(refs[:-1]):
+        refs[-1][i] = slab[...]
 
 
 def mix_all(units):
@@ -382,8 +390,8 @@
 
 
 def attend_kernel(chips, rows, parts, pairs, bounds, *refs):
-    own, other = by_step(refs[:chips]), by_step(refs[chips : 2 * chips])
-    done = refs[2 * chips :]
+    own, early, late, done = by_step(refs[:chips]), refs[chips], refs[chips + 1], refs[chips + 2 :]
+    other = by_step([ref.at[i] for ref in (early, late) for i in range(ref.shape[0])])
     share = shares(chips)
     every = [ref for both in zip(own, other) for ref in both]
     half = rows // 2
@@ -557,28 +565,34 @@
     )(*[pltpu.with_memory_space_constraint(source, pltpu.HBM) for source in sources])
     packed = by_step(packed)
     moved = [swap(packed[j], n, 2 * j) for j in range(1, chips)]
-    anywhere = pl.BlockSpec(memory_space=pl.ANY)
-    bounds, kept = pl.pallas_call(
-        bounds_kernel,
+    own = in_order(packed[:1] + moved)
+    early = chips // 2
+    slab = packed[0].shape
+    bounds, first = pl.pallas_call(
+        gather_kernel,
         out_shape=(
             pltpu.VMEM((8, LANES), jnp.int32),
-            pltpu.VMEM(packed[0].shape, packed[0].dtype),
-        ),
-        in_specs=[smem] * 3 + [anywhere] * 2,
-        out_specs=(vmem, anywhere),
-        input_output_aliases={4: 1},
+            pltpu.VMEM((early,) + slab, jnp.bfloat16),
+        ),
+        in_specs=[smem] * 3 + [vmem] * early,
+        out_specs=(vmem, vmem),
         compiler_params=params,
-    )(video_length, audio_length, align_offset, moved[-1], packed[0])
-    own = [kept] + moved
-    other = [swap(piece, n, 1) for piece in own]
+    )(video_length, audio_length, align_offset, *own[:early])
+    second = pl.pallas_call(
+        merge_kernel,
+        out_shape=pltpu.VMEM((chips - early,) + slab, jnp.bfloat16),
+        in_specs=[vmem] * (chips - early),
+        out_specs=vmem,
+        compiler_params=params,
+    )(*own[early:])
     share = shares(chips)
     done = pl.pallas_call(
         functools.partial(attend_kernel, chips, rows, parts, pairs),
         out_shape=[buffer(2 * (parts + 2 * pairs) * rows, LANES)] * len(share),
-        in_specs=[vmem] * (1 + 2 * chips),
+        in_specs=[vmem] * (3 + chips),
         out_specs=[vmem] * len(share),
         compiler_params=params,
-    )(bounds, *in_order(own), *in_order(other))
+    )(bounds, *own, swap(first, n, 1), swap(second, n, 1))
     back = [
         lax.ppermute(piece, "seq", [(i, i ^ 2 * pair[i % 2]) for i in range(n)])
         for piece, pair in zip(done, share)

time: 40.1 us -> 40 us (level)
  waiting for transfers between devices: 12.7 us -> 11.6 us
  starting transfers between devices: 21.5 us -> 22.5 us
    ppermute x19 -> x13, waiting for transfers between devices: 9.3 us -> 8.27 us  [swap(): return lax.ppermute(piece, 'seq', [(i, i ^ step) for i in range(n)])]
    ppermute x19 -> x13, starting transfers between devices: 15.5 us -> 16.2 us  [swap(): return lax.ppermute(piece, 'seq', [(i, i ^ step) for i in range(n)])]
  transfers between devices with their start and end apart: 23 -> 17, of which waited for: 13 -> 8; matrix products, arithmetic and copies ran while one was open for 0% -> 0% of each run, Pallas kernels for 0% -> 0%
where the time goes in v13:
time: 40 us; the launch traced here: 39.8 us
  starting transfers between devices  22.5 us (56%)
  waiting for transfers between devices  11.6 us (29%)
  Pallas kernels  3.08 us (8%)
  between operations  2.67 us (7%)
    ppermute x13, starting transfers between devices, swap(): return lax.ppermute(piece, 'seq', [(i, i ^ step) for i in range(n)])  16.2 us
    ppermute x13, waiting for transfers between devices, swap(): return lax.ppermute(piece, 'seq', [(i, i ^ step) for i in range(n)])  8.27 us
    ppermute x4, starting transfers between devices, shards_packed(): lax.ppermute(piece, 'seq', [(i, i ^ 2 * pair[i % 2]) for i in range(n)])  6.29 us
    ppermute x4, waiting for transfers between devices, shards_packed(): lax.ppermute(piece, 'seq', [(i, i ^ 2 * pair[i % 2]) for i in range(n)])  3.29 us
    pallas_call x1, Pallas kernels, shards_packed(): pl.pallas_call(functools.partial(pack_kernel, chips), out_shape=[pltpu.VM...  1.31 us
    pallas_call x1, Pallas kernels, shards_packed(): pl.pallas_call(functools.partial(attend_kernel, chips, rows, parts, pairs...  0.95 us
  transfers between devices with their start and end apart: 17, of which 8 were waited for; matrix products, arithmetic and copies ran while one was open for 0% of the time, Pallas kernels for 0%

profile of v13, /device:TPU:0, one launch (start us, length us, event | category | flops | bytes accessed | tf_op | source)
XLA Modules:
  0.0 39.8 jit_solution(1723871969501997918)
XLA Ops:
  0.6 1.3 %shard_map.174 = (bf16[384,128]{1,0:T(8,128)(2,1)S(1)}, bf16[384,128]{1,0:T(8,128)(2,1)S(1)}, bf16[384,128]{1,0:T(8,128)(2,1)S(1)}, bf16[384,128]{1,0:T(8,128)(2...) custom-call(bf16[16,4096]{1,0:T(8,128)(2,1)} %refs_0_.1, ...), custom_call_target="tpu_custom_call" | custom-call | tf_op jit(solution)/shard_map/pallas_call | solution.py:557
  1.9 6.1 %collective-permute-start = (bf16[384,128]{1,0:T(8,128)(2,1)S(1)}, bf16[384,128]{1,0:T(8,128)(2,1)S(1)}, u32[]{:S(2)}, u32[]{:S(2)}) collective-permute-start(bf16[384,128]{1,0:T(8,128)(2,1)S(1)} %get-tuple-element.19), channel_id=1, source_target_pairs={{0,14},{1,15},{2,12},{3,13},{4,10},{5,11},{6,8},{7,9},{8,6},{9,7},... | collective-permute-start | bytes 294920 | tf_op jit(solution)/shard_map/ppermute | solution.py:527
  8.0 0.5 %collective-permute-start.1 = (bf16[384,128]{1,0:T(8,128)(2,1)S(1)}, bf16[384,128]{1,0:T(8,128)(2,1)S(1)}, u32[]{:S(2)}, u32[]{:S(2)}) collective-permute-start(bf16[384,128]{1,0:T(8,128)(2,1)S(1)} %get-tuple-element.20), channel_id=1, source_target_pairs={{0,2},{1,3},{2,0},{3,1},{4,6},{5,7},{6,4},{7,5},{8,10},{9,11},{10,... | collective-permute-start | bytes 294920 | tf_op jit(solution)/shard_map/ppermute | solution.py:527
  8.5 0.1 collective-permute-start.2
  8.7 0.0 collective-permute-start.3
  8.7 5.2 %collective-permute-start.4 = (bf16[384,128]{1,0:T(8,128)(2,1)S(1)}, bf16[384,128]{1,0:T(8,128)(2,1)S(1)}, u32[]{:S(2)}, u32[]{:S(2)}) collective-permute-start(bf16[384,128]{1,0:T(8,128)(2,1)S(1)} %get-tuple-element.24), channel_id=1, source_target_pairs={{0,10},{1,11},{2,8},{3,9},{4,14},{5,15},{6,12},{7,13},{8,2},{9,3},... | collective-permute-start | bytes 294920 | tf_op jit(solution)/shard_map/ppermute | solution.py:527
  13.9 0.0 collective-permute-done.refs_1_
  13.9 2.7 %collective-permute-start.5 = (bf16[384,128]{1,0:T(8,128)(2,1)S(1)}, bf16[384,128]{1,0:T(8,128)(2,1)S(1)}, u32[]{:S(2)}, u32[]{:S(2)}) collective-permute-start(bf16[384,128]{1,0:T(8,128)(2,1)S(1)} %get-tuple-element.25), channel_id=1, source_target_pairs={{0,8},{1,9},{2,10},{3,11},{4,12},{5,13},{6,14},{7,15},{8,0},{9,1},... | collective-permute-start | bytes 294920 | tf_op jit(solution)/shard_map/ppermute | solution.py:527
  16.6 0.0 collective-permute-done.1.refs_2_
  16.6 0.5 %collective-permute-start.6 = (bf16[384,128]{1,0:T(8,128)(2,1)S(1)}, bf16[384,128]{1,0:T(8,128)(2,1)S(1)}, u32[]{:S(2)}, u32[]{:S(2)}) collective-permute-start(bf16[384,128]{1,0:T(8,128)(2,1)S(1)} %get-tuple-element.26), channel_id=1, source_target_pairs={{0,6},{1,7},{2,4},{3,5},{4,2},{5,3},{6,0},{7,1},{8,14},{9,15},{10,... | collective-permute-start | bytes 294920 | tf_op jit(solution)/shard_map/ppermute | solution.py:527
  19.0 0.0 collective-permute-done.2.refs_3_
  19.1 0.1 collective-permute-start.7
  19.1 0.0 collective-permute-done.3.refs_0_.refs_4_
  19.2 4.2 %collective-permute-done.4.refs_1_.refs_5_ = bf16[384,128]{1,0:T(8,128)(2,1)S(1)} collective-permute-done((bf16[384,128]{1,0:T(8,128)(2,1)S(1)}, bf16[384,128]{1,0:T(8,128)(2,1)S(1)}, u32[]{:S(2)}, u32[]{:S(2)}) %collective-permute-start.4) | collective-permute-done | bytes 98336 | tf_op jit(solution)/shard_map/ppermute | solution.py:527
  23.4 1.5 %collective-permute-done.5.refs_2_.refs_6_ = bf16[384,128]{1,0:T(8,128)(2,1)S(1)} collective-permute-done((bf16[384,128]{1,0:T(8,128)(2,1)S(1)}, bf16[384,128]{1,0:T(8,128)(2,1)S(1)}, u32[]{:S(2)}, u32[]{:S(2)}) %collective-permute-start.5) | collective-permute-done | bytes 98336 | tf_op jit(solution)/shard_map/ppermute | solution.py:527
  24.8 0.0 collective-permute-done.6.refs_3_.refs_7_
  24.8 0.1 collective-permute-start.8
  24.9 0.0 collective-permute-done.7.refs_8_
  24.9 1.7 %collective-permute-done.8.refs_9_ = bf16[4,384,128]{2,1,0:T(8,128)(2,1)S(1)} collective-permute-done((bf16[4,384,128]{2,1,0:T(8,128)(2,1)S(1)}, bf16[4,384,128]{2,1,0:T(8,128)(2,1)S(1)}, u32[]{:S(2)}, u32[]{:S(2)}) %collective-permute-start.8) | collective-permute-done | bytes 393248 | tf_op jit(solution)/shard_map/ppermute | solution.py:527
  26.6 0.9 %shard_map.177 = (bf16[256,128]{1,0:T(8,128)(2,1)S(1)}, bf16[256,128]{1,0:T(8,128)(2,1)S(1)}, bf16[256,128]{1,0:T(8,128)(2,1)S(1)}, bf16[256,128]{1,0:T(8,128)(2,1)S(1)}) custom-call(s32[8,128]{1,0:T(8,128)S(1)} %get-tuple-element.22.bounds, bf16[384,128]{1,0:T(8,128)(2,1)S(1)} %get-tuple-element.18.refs_0_, ...), custom_call_target="tpu_custom_call" | custom-call | tf_op jit(solution)/shard_map/pallas_call | solution.py:589
  27.6 2.5 %collective-permute-start.9 = (bf16[256,128]{1,0:T(8,128)(2,1)S(1)}, bf16[256,128]{1,0:T(8,128)(2,1)S(1)}, u32[]{:S(2)}, u32[]{:S(2)}) collective-permute-start(bf16[256,128]{1,0:T(8,128)(2,1)S(1)} %get-tuple-element.28), channel_id=1, source_target_pairs={{0,14},{1,11},{2,12},{3,9},{4,10},{5,15},{6,8},{7,13},{8,6},{9,3},... | collective-permute-start | bytes 196616 | tf_op jit(solution)/shard_map/ppermute | solution.py:597
  30.1 3.2 %collective-permute-start.10 = (bf16[256,128]{1,0:T(8,128)(2,1)S(1)}, bf16[256,128]{1,0:T(8,128)(2,1)S(1)}, u32[]{:S(2)}, u32[]{:S(2)}) collective-permute-start(bf16[256,128]{1,0:T(8,128)(2,1)S(1)} %get-tuple-element.29), channel_id=1, source_target_pairs={{0,12},{1,9},{2,14},{3,11},{4,8},{5,13},{6,10},{7,15},{8,4},{9,1},... | collective-permute-start | bytes 196616 | tf_op jit(solution)/shard_map/ppermute | solution.py:597
  33.2 0.0 collective-permute-start.11
  33.2 0.7 %collective-permute-start.12 = (bf16[256,128]{1,0:T(8,128)(2,1)S(1)}, bf16[256,128]{1,0:T(8,128)(2,1)S(1)}, u32[]{:S(2)}, u32[]{:S(2)}) collective-permute-start(bf16[256,128]{1,0:T(8,128)(2,1)S(1)} %get-tuple-element.31), channel_id=1, source_target_pairs={{0,0},{1,5},{2,2},{3,7},{4,4},{5,1},{6,6},{7,3},{8,8},{9,13},{10,1... | collective-permute-start | bytes 196616 | tf_op jit(solution)/shard_map/ppermute | solution.py:597
  33.9 1.2 %collective-permute-done.9.refs_0_ = bf16[256,128]{1,0:T(8,128)(2,1)S(1)} collective-permute-done((bf16[256,128]{1,0:T(8,128)(2,1)S(1)}, bf16[256,128]{1,0:T(8,128)(2,1)S(1)}, u32[]{:S(2)}, u32[]{:S(2)}) %collective-permute-start.9) | collective-permute-done | bytes 65568 | tf_op jit(solution)/shard_map/ppermute | solution.py:597
  35.1 0.3 collective-permute-start.13
  35.4 1.0 %collective-permute-done.10.refs_1_ = bf16[256,128]{1,0:T(8,128)(2,1)S(1)} collective-permute-done((bf16[256,128]{1,0:T(8,128)(2,1)S(1)}, bf16[256,128]{1,0:T(8,128)(2,1)S(1)}, u32[]{:S(2)}, u32[]{:S(2)}) %collective-permute-start.10) | collective-permute-done | bytes 65568 | tf_op jit(solution)/shard_map/ppermute | solution.py:597
  36.5 0.1 collective-permute-start.14
  36.5 1.1 %collective-permute-done.11.refs_2_ = bf16[256,128]{1,0:T(8,128)(2,1)S(1)} collective-permute-done((bf16[256,128]{1,0:T(8,128)(2,1)S(1)}, bf16[256,128]{1,0:T(8,128)(2,1)S(1)}, u32[]{:S(2)}, u32[]{:S(2)}) %collective-permute-start.11) | collective-permute-done | bytes 65568 | tf_op jit(solution)/shard_map/ppermute | solution.py:597
  37.6 0.0 collective-permute-start.15
  37.6 0.0 collective-permute-done.12.refs_3_
  37.6 0.5 %collective-permute-start.16 = (bf16[256,128]{1,0:T(8,128)(2,1)S(1)}, bf16[256,128]{1,0:T(8,128)(2,1)S(1)}, u32[]{:S(2)}, u32[]{:S(2)}) collective-permute-start(bf16[256,128]{1,0:T(8,128)(2,1)S(1)} %collective-permute-done.12.refs_3_), channel_id=1, source_target_pairs={{0,1},{1,0},{2,3},{3,2},{4,5},{5,4},{6,7},{7,6},{8,9},{9,8},{10,11... | collective-permute-start | bytes 196616 | tf_op jit(solution)/shard_map/ppermute | solution.py:527
  38.1 0.0 collective-permute-done.13.refs_4_
  38.1 0.0 collective-permute-done.14.refs_5_
  38.1 0.7 %collective-permute-done.15.refs_6_ = bf16[256,128]{1,0:T(8,128)(2,1)S(1)} collective-permute-done((bf16[256,128]{1,0:T(8,128)(2,1)S(1)}, bf16[256,128]{1,0:T(8,128)(2,1)S(1)}, u32[]{:S(2)}, u32[]{:S(2)}) %collective-permute-start.15) | collective-permute-done | bytes 65568 | tf_op jit(solution)/shard_map/ppermute | solution.py:527
  38.8 0.2 collective-permute-done.16.refs_7_
  39.0 0.8 %shard_map.178 = (bf16[16,4096]{1,0:T(8,128)(2,1)}, bf16[8,2048]{1,0:T(8,128)(2,1)}, bf16[16,2048]{1,0:T(8,128)(2,1)}, bf16[8,2048]{1,0:T(8,128)(2,1)}) custom-call(bf16[256,128]{1,0:T(8,128)(2,1)S(1)} %collective-permute-done.9.refs_0_, bf16[256,128]{1,0:T(8,128)(2,1)S(1)} %collective-permute-done.10.refs_1_, ...), custom_call_target="tpu_custom_call" | custom-call | tf_op jit(solution)/shard_map/pallas_call | solution.py:600
  (2 shorter events, 0.1 us)
Async XLA Ops:
  1.9 11.9 %collective-permute-start = (bf16[384,128]{1,0:T(8,128)(2,1)S(1)}, bf16[384,128]{1,0:T(8,128)(2,1)S(1)}, u32[]{:S(2)}, u32[]{:S(2)}) collective-permute-start(bf16[384,128]{1,0:T(8,128)(2,1)S(1)} %get-tuple-element.19), channel_id=1, source_target_pairs={{0,14},{1,15},{2,12},{3,13},{4,10},{5,11},{6,8},{7,9},{8,6},{9,7},... | collective-permute-start | bytes 294920 | tf_op jit(solution)/shard_map/ppermute | solution.py:527
  8.0 8.5 %collective-permute-start.1 = (bf16[384,128]{1,0:T(8,128)(2,1)S(1)}, bf16[384,128]{1,0:T(8,128)(2,1)S(1)}, u32[]{:S(2)}, u32[]{:S(2)}) collective-permute-start(bf16[384,128]{1,0:T(8,128)(2,1)S(1)} %get-tuple-element.20), channel_id=1, source_target_pairs={{0,2},{1,3},{2,0},{3,1},{4,6},{5,7},{6,4},{7,5},{8,10},{9,11},{10,... | collective-permute-start | bytes 294920 | tf_op jit(solution)/shard_map/ppermute | solution.py:527
  8.5 10.5 %collective-permute-start.2 = (bf16[384,128]{1,0:T(8,128)(2,1)S(1)}, bf16[384,128]{1,0:T(8,128)(2,1)S(1)}, u32[]{:S(2)}, u32[]{:S(2)}) collective-permute-start(bf16[384,128]{1,0:T(8,128)(2,1)S(1)} %get-tuple-element.21), channel_id=1, source_target_pairs={{0,12},{1,13},{2,14},{3,15},{4,8},{5,9},{6,10},{7,11},{8,4},{9,5},... | collective-permute-start | bytes 294920 | tf_op jit(solution)/shard_map/ppermute | solution.py:527
  8.7 10.5 %collective-permute-start.3 = (bf16[384,128]{1,0:T(8,128)(2,1)S(1)}, bf16[384,128]{1,0:T(8,128)(2,1)S(1)}, u32[]{:S(2)}, u32[]{:S(2)}) collective-permute-start(bf16[384,128]{1,0:T(8,128)(2,1)S(1)} %get-tuple-element.23), channel_id=1, source_target_pairs={{0,4},{1,5},{2,6},{3,7},{4,0},{5,1},{6,2},{7,3},{8,12},{9,13},{10,... | collective-permute-start | bytes 294920 | tf_op jit(solution)/shard_map/ppermute | solution.py:527
  8.7 14.7 %collective-permute-start.4 = (bf16[384,128]{1,0:T(8,128)(2,1)S(1)}, bf16[384,128]{1,0:T(8,128)(2,1)S(1)}, u32[]{:S(2)}, u32[]{:S(2)}) collective-permute-start(bf16[384,128]{1,0:T(8,128)(2,1)S(1)} %get-tuple-element.24), channel_id=1, source_target_pairs={{0,10},{1,11},{2,8},{3,9},{4,14},{5,15},{6,12},{7,13},{8,2},{9,3},... | collective-permute-start | bytes 294920 | tf_op jit(solution)/shard_map/ppermute | solution.py:527
  13.9 10.9 %collective-permute-start.5 = (bf16[384,128]{1,0:T(8,128)(2,1)S(1)}, bf16[384,128]{1,0:T(8,128)(2,1)S(1)}, u32[]{:S(2)}, u32[]{:S(2)}) collective-permute-start(bf16[384,128]{1,0:T(8,128)(2,1)S(1)} %get-tuple-element.25), channel_id=1, source_target_pairs={{0,8},{1,9},{2,10},{3,11},{4,12},{5,13},{6,14},{7,15},{8,0},{9,1},... | collective-permute-start | bytes 294920 | tf_op jit(solution)/shard_map/ppermute | solution.py:527
  16.6 8.3 %collective-permute-start.6 = (bf16[384,128]{1,0:T(8,128)(2,1)S(1)}, bf16[384,128]{1,0:T(8,128)(2,1)S(1)}, u32[]{:S(2)}, u32[]{:S(2)}) collective-permute-start(bf16[384,128]{1,0:T(8,128)(2,1)S(1)} %get-tuple-element.26), channel_id=1, source_target_pairs={{0,6},{1,7},{2,4},{3,5},{4,2},{5,3},{6,0},{7,1},{8,14},{9,15},{10,... | collective-permute-start | bytes 294920 | tf_op jit(solution)/shard_map/ppermute | solution.py:527
  19.1 5.9 %collective-permute-start.7 = (bf16[4,384,128]{2,1,0:T(8,128)(2,1)S(1)}, bf16[4,384,128]{2,1,0:T(8,128)(2,1)S(1)}, u32[]{:S(2)}, u32[]{:S(2)}) collective-permute-start(bf16[4,384,128]{2,1,0:T(8,128)(2,1)S(1)} %get-tuple-element.27), channel_id=1, source_target_pairs={{0,1},{1,0},{2,3},{3,2},{4,5},{5,4},{6,7},{7,6},{8,9},{9,8},{10,11... | collective-permute-start | bytes 1179656 | tf_op jit(solution)/shard_map/ppermute | solution.py:527
  24.8 1.8 %collective-permute-start.8 = (bf16[4,384,128]{2,1,0:T(8,128)(2,1)S(1)}, bf16[4,384,128]{2,1,0:T(8,128)(2,1)S(1)}, u32[]{:S(2)}, u32[]{:S(2)}) collective-permute-start(bf16[4,384,128]{2,1,0:T(8,128)(2,1)S(1)} %shard_map.176), channel_id=1, source_target_pairs={{0,1},{1,0},{2,3},{3,2},{4,5},{5,4},{6,7},{7,6},{8,9},{9,8},{10,11... | collective-permute-start | bytes 1179656 | tf_op jit(solution)/shard_map/ppermute | solution.py:527
  27.6 7.5 %collective-permute-start.9 = (bf16[256,128]{1,0:T(8,128)(2,1)S(1)}, bf16[256,128]{1,0:T(8,128)(2,1)S(1)}, u32[]{:S(2)}, u32[]{:S(2)}) collective-permute-start(bf16[256,128]{1,0:T(8,128)(2,1)S(1)} %get-tuple-element.28), channel_id=1, source_target_pairs={{0,14},{1,11},{2,12},{3,9},{4,10},{5,15},{6,8},{7,13},{8,6},{9,3},... | collective-permute-start | bytes 196616 | tf_op jit(solution)/shard_map/ppermute | solution.py:597
  30.1 6.4 %collective-permute-start.10 = (bf16[256,128]{1,0:T(8,128)(2,1)S(1)}, bf16[256,128]{1,0:T(8,128)(2,1)S(1)}, u32[]{:S(2)}, u32[]{:S(2)}) collective-permute-start(bf16[256,128]{1,0:T(8,128)(2,1)S(1)} %get-tuple-element.29), channel_id=1, source_target_pairs={{0,12},{1,9},{2,14},{3,11},{4,8},{5,13},{6,10},{7,15},{8,4},{9,1},... | collective-permute-start | bytes 196616 | tf_op jit(solution)/shard_map/ppermute | solution.py:597
  33.2 4.4 %collective-permute-start.11 = (bf16[256,128]{1,0:T(8,128)(2,1)S(1)}, bf16[256,128]{1,0:T(8,128)(2,1)S(1)}, u32[]{:S(2)}, u32[]{:S(2)}) collective-permute-start(bf16[256,128]{1,0:T(8,128)(2,1)S(1)} %get-tuple-element.30), channel_id=1, source_target_pairs={{0,2},{1,7},{2,0},{3,5},{4,6},{5,3},{6,4},{7,1},{8,10},{9,15},{10,... | collective-permute-start | bytes 196616 | tf_op jit(solution)/shard_map/ppermute | solution.py:597
  33.2 4.4 %collective-permute-start.12 = (bf16[256,128]{1,0:T(8,128)(2,1)S(1)}, bf16[256,128]{1,0:T(8,128)(2,1)S(1)}, u32[]{:S(2)}, u32[]{:S(2)}) collective-permute-start(bf16[256,128]{1,0:T(8,128)(2,1)S(1)} %get-tuple-element.31), channel_id=1, source_target_pairs={{0,0},{1,5},{2,2},{3,7},{4,4},{5,1},{6,6},{7,3},{8,8},{9,13},{10,1... | collective-permute-start | bytes 196616 | tf_op jit(solution)/shard_map/ppermute | solution.py:597
  35.1 3.0 %collective-permute-start.13 = (bf16[256,128]{1,0:T(8,128)(2,1)S(1)}, bf16[256,128]{1,0:T(8,128)(2,1)S(1)}, u32[]{:S(2)}, u32[]{:S(2)}) collective-permute-start(bf16[256,128]{1,0:T(8,128)(2,1)S(1)} %collective-permute-done.9.refs_0_), channel_id=1, source_target_pairs={{0,1},{1,0},{2,3},{3,2},{4,5},{5,4},{6,7},{7,6},{8,9},{9,8},{10,11... | collective-permute-start | bytes 196616 | tf_op jit(solution)/shard_map/ppermute | solution.py:527
  36.5 1.7 %collective-permute-start.14 = (bf16[256,128]{1,0:T(8,128)(2,1)S(1)}, bf16[256,128]{1,0:T(8,128)(2,1)S(1)}, u32[]{:S(2)}, u32[]{:S(2)}) collective-permute-start(bf16[256,128]{1,0:T(8,128)(2,1)S(1)} %collective-permute-done.10.refs_1_), channel_id=1, source_target_pairs={{0,1},{1,0},{2,3},{3,2},{4,5},{5,4},{6,7},{7,6},{8,9},{9,8},{10,11... | collective-permute-start | bytes 196616 | tf_op jit(solution)/shard_map/ppermute | solution.py:527
  37.6 1.3 %collective-permute-start.15 = (bf16[256,128]{1,0:T(8,128)(2,1)S(1)}, bf16[256,128]{1,0:T(8,128)(2,1)S(1)}, u32[]{:S(2)}, u32[]{:S(2)}) collective-permute-start(bf16[256,128]{1,0:T(8,128)(2,1)S(1)} %collective-permute-done.11.refs_2_), channel_id=1, source_target_pairs={{0,1},{1,0},{2,3},{3,2},{4,5},{5,4},{6,7},{7,6},{8,9},{9,8},{10,11... | collective-permute-start | bytes 196616 | tf_op jit(solution)/shard_map/ppermute | solution.py:527
  37.6 1.4 %collective-permute-start.16 = (bf16[256,128]{1,0:T(8,128)(2,1)S(1)}, bf16[256,128]{1,0:T(8,128)(2,1)S(1)}, u32[]{:S(2)}, u32[]{:S(2)}) collective-permute-start(bf16[256,128]{1,0:T(8,128)(2,1)S(1)} %collective-permute-done.12.refs_3_), channel_id=1, source_target_pairs={{0,1},{1,0},{2,3},{3,2},{4,5},{5,4},{6,7},{7,6},{8,9},{9,8},{10,11... | collective-permute-start | bytes 196616 | tf_op jit(solution)/shard_map/ppermute | solution.py:527

commit v14 on v13

--- a/solution.py
+++ b/solution.py
@@ -291,7 +291,7 @@
 
 def step_order(chips):
     far, near = list(range(chips - 1, chips // 2 - 1, -1)), list(range(1, chips // 2))
-    return [0] + far[:1] + near[:1] + far[1:2] + near[1:2] + far[2:] + near[2:]
+    return [0] + far[:1] + near[:1] + far[1:2] + near[1:] + far[2:]
 
 
 def by_step(items):

time: 40 us -> 39 us (0.975)
  waiting for transfers between devices: 11.6 us -> 10.4 us
    ppermute x13, waiting for transfers between devices: 8.27 us -> 7.7 us  [swap(): return lax.ppermute(piece, 'seq', [(i, i ^ step) for i in range(n)])]
    ppermute x4, waiting for transfers between devices: 3.29 us -> 2.74 us  [shards_packed(): lax.ppermute(piece, 'seq', [(i, i ^ 2 * pair[i % 2]) for i in range(n)])]
    ppermute x13, starting transfers between devices: 16.2 us -> 16.6 us  [swap(): return lax.ppermute(piece, 'seq', [(i, i ^ step) for i in range(n)])]
where the time goes in v14:
time: 39 us; the launch traced here: 38.8 us
  starting transfers between devices  22.6 us (58%)
  waiting for transfers between devices  10.4 us (27%)
  Pallas kernels  3.08 us (8%)
  between operations  2.68 us (7%)
    ppermute x13, starting transfers between devices, swap(): return lax.ppermute(piece, 'seq', [(i, i ^ step) for i in range(n)])  16.6 us
    ppermute x13, waiting for transfers between devices, swap(): return lax.ppermute(piece, 'seq', [(i, i ^ step) for i in range(n)])  7.7 us
    ppermute x4, starting transfers between devices, shards_packed(): lax.ppermute(piece, 'seq', [(i, i ^ 2 * pair[i % 2]) for i in range(n)])  6 us
    ppermute x4, waiting for transfers between devices, shards_packed(): lax.ppermute(piece, 'seq', [(i, i ^ 2 * pair[i % 2]) for i in range(n)])  2.74 us
    pallas_call x1, Pallas kernels, shards_packed(): pl.pallas_call(functools.partial(pack_kernel, chips), out_shape=[pltpu.VM...  1.31 us
    pallas_call x1, Pallas kernels, shards_packed(): pl.pallas_call(functools.partial(attend_kernel, chips, rows, parts, pairs...  0.95 us
  transfers between devices with their start and end apart: 17, of which 8 were waited for; matrix products, arithmetic and copies ran while one was open for 0% of the time, Pallas kernels for 0%

profile of v14, /device:TPU:0, one launch (start us, length us, event | category | flops | bytes accessed | tf_op | source)
XLA Modules:
  0.0 38.8 jit_solution(8825365197692113876)
XLA Ops:
  0.6 1.3 %shard_map.174 = (bf16[384,128]{1,0:T(8,128)(2,1)S(1)}, bf16[384,128]{1,0:T(8,128)(2,1)S(1)}, bf16[384,128]{1,0:T(8,128)(2,1)S(1)}, bf16[384,128]{1,0:T(8,128)(2...) custom-call(bf16[16,4096]{1,0:T(8,128)(2,1)} %refs_0_.1, ...), custom_call_target="tpu_custom_call" | custom-call | tf_op jit(solution)/shard_map/pallas_call | solution.py:557
  1.9 6.1 %collective-permute-start = (bf16[384,128]{1,0:T(8,128)(2,1)S(1)}, bf16[384,128]{1,0:T(8,128)(2,1)S(1)}, u32[]{:S(2)}, u32[]{:S(2)}) collective-permute-start(bf16[384,128]{1,0:T(8,128)(2,1)S(1)} %get-tuple-element.19), channel_id=1, source_target_pairs={{0,14},{1,15},{2,12},{3,13},{4,10},{5,11},{6,8},{7,9},{8,6},{9,7},... | collective-permute-start | bytes 294920 | tf_op jit(solution)/shard_map/ppermute | solution.py:527
  8.0 0.5 %collective-permute-start.1 = (bf16[384,128]{1,0:T(8,128)(2,1)S(1)}, bf16[384,128]{1,0:T(8,128)(2,1)S(1)}, u32[]{:S(2)}, u32[]{:S(2)}) collective-permute-start(bf16[384,128]{1,0:T(8,128)(2,1)S(1)} %get-tuple-element.20), channel_id=1, source_target_pairs={{0,2},{1,3},{2,0},{3,1},{4,6},{5,7},{6,4},{7,5},{8,10},{9,11},{10,... | collective-permute-start | bytes 294920 | tf_op jit(solution)/shard_map/ppermute | solution.py:527
  8.5 0.1 collective-permute-start.2
  8.7 0.0 collective-permute-start.3
  8.7 3.1 %collective-permute-start.4 = (bf16[384,128]{1,0:T(8,128)(2,1)S(1)}, bf16[384,128]{1,0:T(8,128)(2,1)S(1)}, u32[]{:S(2)}, u32[]{:S(2)}) collective-permute-start(bf16[384,128]{1,0:T(8,128)(2,1)S(1)} %get-tuple-element.24), channel_id=1, source_target_pairs={{0,6},{1,7},{2,4},{3,5},{4,2},{5,3},{6,0},{7,1},{8,14},{9,15},{10,... | collective-permute-start | bytes 294920 | tf_op jit(solution)/shard_map/ppermute | solution.py:527
  11.7 0.0 collective-permute-done.refs_1_
  11.7 6.1 %collective-permute-start.5 = (bf16[384,128]{1,0:T(8,128)(2,1)S(1)}, bf16[384,128]{1,0:T(8,128)(2,1)S(1)}, u32[]{:S(2)}, u32[]{:S(2)}) collective-permute-start(bf16[384,128]{1,0:T(8,128)(2,1)S(1)} %get-tuple-element.25), channel_id=1, source_target_pairs={{0,10},{1,11},{2,8},{3,9},{4,14},{5,15},{6,12},{7,13},{8,2},{9,3},... | collective-permute-start | bytes 294920 | tf_op jit(solution)/shard_map/ppermute | solution.py:527
  17.8 0.0 collective-permute-done.1.refs_2_
  17.8 0.0 collective-permute-start.6
  19.8 0.0 collective-permute-done.2.refs_3_
  19.8 0.1 collective-permute-start.7
  19.9 0.0 collective-permute-done.3.refs_0_.refs_4_
  19.9 0.0 collective-permute-done.4.refs_1_.refs_5_
  19.9 4.2 %collective-permute-done.5.refs_2_.refs_6_ = bf16[384,128]{1,0:T(8,128)(2,1)S(1)} collective-permute-done((bf16[384,128]{1,0:T(8,128)(2,1)S(1)}, bf16[384,128]{1,0:T(8,128)(2,1)S(1)}, u32[]{:S(2)}, u32[]{:S(2)}) %collective-permute-start.5) | collective-permute-done | bytes 98336 | tf_op jit(solution)/shard_map/ppermute | solution.py:527
  24.1 0.6 %collective-permute-done.6.refs_3_.refs_7_ = bf16[384,128]{1,0:T(8,128)(2,1)S(1)} collective-permute-done((bf16[384,128]{1,0:T(8,128)(2,1)S(1)}, bf16[384,128]{1,0:T(8,128)(2,1)S(1)}, u32[]{:S(2)}, u32[]{:S(2)}) %collective-permute-start.6) | collective-permute-done | bytes 98336 | tf_op jit(solution)/shard_map/ppermute | solution.py:527
  24.7 0.1 collective-permute-start.8
  24.8 0.0 collective-permute-done.7.refs_8_
  24.8 1.7 %collective-permute-done.8.refs_9_ = bf16[4,384,128]{2,1,0:T(8,128)(2,1)S(1)} collective-permute-done((bf16[4,384,128]{2,1,0:T(8,128)(2,1)S(1)}, bf16[4,384,128]{2,1,0:T(8,128)(2,1)S(1)}, u32[]{:S(2)}, u32[]{:S(2)}) %collective-permute-start.8) | collective-permute-done | bytes 393248 | tf_op jit(solution)/shard_map/ppermute | solution.py:527
  26.5 0.9 %shard_map.177 = (bf16[256,128]{1,0:T(8,128)(2,1)S(1)}, bf16[256,128]{1,0:T(8,128)(2,1)S(1)}, bf16[256,128]{1,0:T(8,128)(2,1)S(1)}, bf16[256,128]{1,0:T(8,128)(2,1)S(1)}) custom-call(s32[8,128]{1,0:T(8,128)S(1)} %get-tuple-element.22.bounds, bf16[384,128]{1,0:T(8,128)(2,1)S(1)} %get-tuple-element.18.refs_0_, ...), custom_call_target="tpu_custom_call" | custom-call | tf_op jit(solution)/shard_map/pallas_call | solution.py:589
  27.5 2.6 %collective-permute-start.9 = (bf16[256,128]{1,0:T(8,128)(2,1)S(1)}, bf16[256,128]{1,0:T(8,128)(2,1)S(1)}, u32[]{:S(2)}, u32[]{:S(2)}) collective-permute-start(bf16[256,128]{1,0:T(8,128)(2,1)S(1)} %get-tuple-element.28), channel_id=1, source_target_pairs={{0,14},{1,11},{2,12},{3,9},{4,10},{5,15},{6,8},{7,13},{8,6},{9,3},... | collective-permute-start | bytes 196616 | tf_op jit(solution)/shard_map/ppermute | solution.py:597
  30.0 1.7 %collective-permute-start.10 = (bf16[256,128]{1,0:T(8,128)(2,1)S(1)}, bf16[256,128]{1,0:T(8,128)(2,1)S(1)}, u32[]{:S(2)}, u32[]{:S(2)}) collective-permute-start(bf16[256,128]{1,0:T(8,128)(2,1)S(1)} %get-tuple-element.29), channel_id=1, source_target_pairs={{0,12},{1,9},{2,14},{3,11},{4,8},{5,13},{6,10},{7,15},{8,4},{9,1},... | collective-permute-start | bytes 196616 | tf_op jit(solution)/shard_map/ppermute | solution.py:597
  31.8 1.0 %collective-permute-start.11 = (bf16[256,128]{1,0:T(8,128)(2,1)S(1)}, bf16[256,128]{1,0:T(8,128)(2,1)S(1)}, u32[]{:S(2)}, u32[]{:S(2)}) collective-permute-start(bf16[256,128]{1,0:T(8,128)(2,1)S(1)} %get-tuple-element.30), channel_id=1, source_target_pairs={{0,2},{1,7},{2,0},{3,5},{4,6},{5,3},{6,4},{7,1},{8,10},{9,15},{10,... | collective-permute-start | bytes 196616 | tf_op jit(solution)/shard_map/ppermute | solution.py:597
  32.8 0.7 %collective-permute-start.12 = (bf16[256,128]{1,0:T(8,128)(2,1)S(1)}, bf16[256,128]{1,0:T(8,128)(2,1)S(1)}, u32[]{:S(2)}, u32[]{:S(2)}) collective-permute-start(bf16[256,128]{1,0:T(8,128)(2,1)S(1)} %get-tuple-element.31), channel_id=1, source_target_pairs={{0,0},{1,5},{2,2},{3,7},{4,4},{5,1},{6,6},{7,3},{8,8},{9,13},{10,1... | collective-permute-start | bytes 196616 | tf_op jit(solution)/shard_map/ppermute | solution.py:597
  33.5 1.4 %collective-permute-done.9.refs_0_ = bf16[256,128]{1,0:T(8,128)(2,1)S(1)} collective-permute-done((bf16[256,128]{1,0:T(8,128)(2,1)S(1)}, bf16[256,128]{1,0:T(8,128)(2,1)S(1)}, u32[]{:S(2)}, u32[]{:S(2)}) %collective-permute-start.9) | collective-permute-done | bytes 65568 | tf_op jit(solution)/shard_map/ppermute | solution.py:597
  34.9 0.0 collective-permute-start.13
  34.9 1.4 %collective-permute-done.10.refs_1_ = bf16[256,128]{1,0:T(8,128)(2,1)S(1)} collective-permute-done((bf16[256,128]{1,0:T(8,128)(2,1)S(1)}, bf16[256,128]{1,0:T(8,128)(2,1)S(1)}, u32[]{:S(2)}, u32[]{:S(2)}) %collective-permute-start.10) | collective-permute-done | bytes 65568 | tf_op jit(solution)/shard_map/ppermute | solution.py:597
  36.2 0.0 collective-permute-start.14
  36.2 0.0 collective-permute-done.11.refs_2_
  36.2 0.5 %collective-permute-start.15 = (bf16[256,128]{1,0:T(8,128)(2,1)S(1)}, bf16[256,128]{1,0:T(8,128)(2,1)S(1)}, u32[]{:S(2)}, u32[]{:S(2)}) collective-permute-start(bf16[256,128]{1,0:T(8,128)(2,1)S(1)} %collective-permute-done.11.refs_2_), channel_id=1, source_target_pairs={{0,1},{1,0},{2,3},{3,2},{4,5},{5,4},{6,7},{7,6},{8,9},{9,8},{10,11... | collective-permute-start | bytes 196616 | tf_op jit(solution)/shard_map/ppermute | solution.py:527
  36.8 0.0 collective-permute-done.12.refs_3_
  36.8 0.1 collective-permute-start.16
  36.8 0.0 collective-permute-done.13.refs_4_
  36.8 0.7 %collective-permute-done.14.refs_5_ = bf16[256,128]{1,0:T(8,128)(2,1)S(1)} collective-permute-done((bf16[256,128]{1,0:T(8,128)(2,1)S(1)}, bf16[256,128]{1,0:T(8,128)(2,1)S(1)}, u32[]{:S(2)}, u32[]{:S(2)}) %collective-permute-start.14) | collective-permute-done | bytes 65568 | tf_op jit(solution)/shard_map/ppermute | solution.py:527
  37.5 0.2 collective-permute-done.15.refs_6_
  37.7 0.4 collective-permute-done.16.refs_7_
  38.0 0.8 %shard_map.178 = (bf16[16,4096]{1,0:T(8,128)(2,1)}, bf16[8,2048]{1,0:T(8,128)(2,1)}, bf16[16,2048]{1,0:T(8,128)(2,1)}, bf16[8,2048]{1,0:T(8,128)(2,1)}) custom-call(bf16[256,128]{1,0:T(8,128)(2,1)S(1)} %collective-permute-done.9.refs_0_, bf16[256,128]{1,0:T(8,128)(2,1)S(1)} %collective-permute-done.10.refs_1_, ...), custom_call_target="tpu_custom_call" | custom-call | tf_op jit(solution)/shard_map/pallas_call | solution.py:600
  (2 shorter events, 0.1 us)
Async XLA Ops:
  1.9 9.8 %collective-permute-start = (bf16[384,128]{1,0:T(8,128)(2,1)S(1)}, bf16[384,128]{1,0:T(8,128)(2,1)S(1)}, u32[]{:S(2)}, u32[]{:S(2)}) collective-permute-start(bf16[384,128]{1,0:T(8,128)(2,1)S(1)} %get-tuple-element.19), channel_id=1, source_target_pairs={{0,14},{1,15},{2,12},{3,13},{4,10},{5,11},{6,8},{7,9},{8,6},{9,7},... | collective-permute-start | bytes 294920 | tf_op jit(solution)/shard_map/ppermute | solution.py:527
  8.0 9.8 %collective-permute-start.1 = (bf16[384,128]{1,0:T(8,128)(2,1)S(1)}, bf16[384,128]{1,0:T(8,128)(2,1)S(1)}, u32[]{:S(2)}, u32[]{:S(2)}) collective-permute-start(bf16[384,128]{1,0:T(8,128)(2,1)S(1)} %get-tuple-element.20), channel_id=1, source_target_pairs={{0,2},{1,3},{2,0},{3,1},{4,6},{5,7},{6,4},{7,5},{8,10},{9,11},{10,... | collective-permute-start | bytes 294920 | tf_op jit(solution)/shard_map/ppermute | solution.py:527
  8.5 11.2 %collective-permute-start.2 = (bf16[384,128]{1,0:T(8,128)(2,1)S(1)}, bf16[384,128]{1,0:T(8,128)(2,1)S(1)}, u32[]{:S(2)}, u32[]{:S(2)}) collective-permute-start(bf16[384,128]{1,0:T(8,128)(2,1)S(1)} %get-tuple-element.21), channel_id=1, source_target_pairs={{0,12},{1,13},{2,14},{3,15},{4,8},{5,9},{6,10},{7,11},{8,4},{9,5},... | collective-permute-start | bytes 294920 | tf_op jit(solution)/shard_map/ppermute | solution.py:527
  8.7 11.2 %collective-permute-start.3 = (bf16[384,128]{1,0:T(8,128)(2,1)S(1)}, bf16[384,128]{1,0:T(8,128)(2,1)S(1)}, u32[]{:S(2)}, u32[]{:S(2)}) collective-permute-start(bf16[384,128]{1,0:T(8,128)(2,1)S(1)} %get-tuple-element.23), channel_id=1, source_target_pairs={{0,4},{1,5},{2,6},{3,7},{4,0},{5,1},{6,2},{7,3},{8,12},{9,13},{10,... | collective-permute-start | bytes 294920 | tf_op jit(solution)/shard_map/ppermute | solution.py:527
  8.7 11.2 %collective-permute-start.4 = (bf16[384,128]{1,0:T(8,128)(2,1)S(1)}, bf16[384,128]{1,0:T(8,128)(2,1)S(1)}, u32[]{:S(2)}, u32[]{:S(2)}) collective-permute-start(bf16[384,128]{1,0:T(8,128)(2,1)S(1)} %get-tuple-element.24), channel_id=1, source_target_pairs={{0,6},{1,7},{2,4},{3,5},{4,2},{5,3},{6,0},{7,1},{8,14},{9,15},{10,... | collective-permute-start | bytes 294920 | tf_op jit(solution)/shard_map/ppermute | solution.py:527
  11.7 12.3 %collective-permute-start.5 = (bf16[384,128]{1,0:T(8,128)(2,1)S(1)}, bf16[384,128]{1,0:T(8,128)(2,1)S(1)}, u32[]{:S(2)}, u32[]{:S(2)}) collective-permute-start(bf16[384,128]{1,0:T(8,128)(2,1)S(1)} %get-tuple-element.25), channel_id=1, source_target_pairs={{0,10},{1,11},{2,8},{3,9},{4,14},{5,15},{6,12},{7,13},{8,2},{9,3},... | collective-permute-start | bytes 294920 | tf_op jit(solution)/shard_map/ppermute | solution.py:527
  17.8 6.9 %collective-permute-start.6 = (bf16[384,128]{1,0:T(8,128)(2,1)S(1)}, bf16[384,128]{1,0:T(8,128)(2,1)S(1)}, u32[]{:S(2)}, u32[]{:S(2)}) collective-permute-start(bf16[384,128]{1,0:T(8,128)(2,1)S(1)} %get-tuple-element.26), channel_id=1, source_target_pairs={{0,8},{1,9},{2,10},{3,11},{4,12},{5,13},{6,14},{7,15},{8,0},{9,1},... | collective-permute-start | bytes 294920 | tf_op jit(solution)/shard_map/ppermute | solution.py:527
  19.8 5.0 %collective-permute-start.7 = (bf16[4,384,128]{2,1,0:T(8,128)(2,1)S(1)}, bf16[4,384,128]{2,1,0:T(8,128)(2,1)S(1)}, u32[]{:S(2)}, u32[]{:S(2)}) collective-permute-start(bf16[4,384,128]{2,1,0:T(8,128)(2,1)S(1)} %get-tuple-element.27), channel_id=1, source_target_pairs={{0,1},{1,0},{2,3},{3,2},{4,5},{5,4},{6,7},{7,6},{8,9},{9,8},{10,11... | collective-permute-start | bytes 1179656 | tf_op jit(solution)/shard_map/ppermute | solution.py:527
  24.7 1.8 %collective-permute-start.8 = (bf16[4,384,128]{2,1,0:T(8,128)(2,1)S(1)}, bf16[4,384,128]{2,1,0:T(8,128)(2,1)S(1)}, u32[]{:S(2)}, u32[]{:S(2)}) collective-permute-start(bf16[4,384,128]{2,1,0:T(8,128)(2,1)S(1)} %shard_map.176), channel_id=1, source_target_pairs={{0,1},{1,0},{2,3},{3,2},{4,5},{5,4},{6,7},{7,6},{8,9},{9,8},{10,11... | collective-permute-start | bytes 1179656 | tf_op jit(solution)/shard_map/ppermute | solution.py:527
  27.5 7.4 %collective-permute-start.9 = (bf16[256,128]{1,0:T(8,128)(2,1)S(1)}, bf16[256,128]{1,0:T(8,128)(2,1)S(1)}, u32[]{:S(2)}, u32[]{:S(2)}) collective-permute-start(bf16[256,128]{1,0:T(8,128)(2,1)S(1)} %get-tuple-element.28), channel_id=1, source_target_pairs={{0,14},{1,11},{2,12},{3,9},{4,10},{5,15},{6,8},{7,13},{8,6},{9,3},... | collective-permute-start | bytes 196616 | tf_op jit(solution)/shard_map/ppermute | solution.py:597
  30.0 6.2 %collective-permute-start.10 = (bf16[256,128]{1,0:T(8,128)(2,1)S(1)}, bf16[256,128]{1,0:T(8,128)(2,1)S(1)}, u32[]{:S(2)}, u32[]{:S(2)}) collective-permute-start(bf16[256,128]{1,0:T(8,128)(2,1)S(1)} %get-tuple-element.29), channel_id=1, source_target_pairs={{0,12},{1,9},{2,14},{3,11},{4,8},{5,13},{6,10},{7,15},{8,4},{9,1},... | collective-permute-start | bytes 196616 | tf_op jit(solution)/shard_map/ppermute | solution.py:597
  31.8 4.5 %collective-permute-start.11 = (bf16[256,128]{1,0:T(8,128)(2,1)S(1)}, bf16[256,128]{1,0:T(8,128)(2,1)S(1)}, u32[]{:S(2)}, u32[]{:S(2)}) collective-permute-start(bf16[256,128]{1,0:T(8,128)(2,1)S(1)} %get-tuple-element.30), channel_id=1, source_target_pairs={{0,2},{1,7},{2,0},{3,5},{4,6},{5,3},{6,4},{7,1},{8,10},{9,15},{10,... | collective-permute-start | bytes 196616 | tf_op jit(solution)/shard_map/ppermute | solution.py:597
  32.8 3.9 %collective-permute-start.12 = (bf16[256,128]{1,0:T(8,128)(2,1)S(1)}, bf16[256,128]{1,0:T(8,128)(2,1)S(1)}, u32[]{:S(2)}, u32[]{:S(2)}) collective-permute-start(bf16[256,128]{1,0:T(8,128)(2,1)S(1)} %get-tuple-element.31), channel_id=1, source_target_pairs={{0,0},{1,5},{2,2},{3,7},{4,4},{5,1},{6,6},{7,3},{8,8},{9,13},{10,1... | collective-permute-start | bytes 196616 | tf_op jit(solution)/shard_map/ppermute | solution.py:597
  34.9 2.0 %collective-permute-start.13 = (bf16[256,128]{1,0:T(8,128)(2,1)S(1)}, bf16[256,128]{1,0:T(8,128)(2,1)S(1)}, u32[]{:S(2)}, u32[]{:S(2)}) collective-permute-start(bf16[256,128]{1,0:T(8,128)(2,1)S(1)} %collective-permute-done.9.refs_0_), channel_id=1, source_target_pairs={{0,1},{1,0},{2,3},{3,2},{4,5},{5,4},{6,7},{7,6},{8,9},{9,8},{10,11... | collective-permute-start | bytes 196616 | tf_op jit(solution)/shard_map/ppermute | solution.py:527
  36.2 1.3 %collective-permute-start.14 = (bf16[256,128]{1,0:T(8,128)(2,1)S(1)}, bf16[256,128]{1,0:T(8,128)(2,1)S(1)}, u32[]{:S(2)}, u32[]{:S(2)}) collective-permute-start(bf16[256,128]{1,0:T(8,128)(2,1)S(1)} %collective-permute-done.10.refs_1_), channel_id=1, source_target_pairs={{0,1},{1,0},{2,3},{3,2},{4,5},{5,4},{6,7},{7,6},{8,9},{9,8},{10,11... | collective-permute-start | bytes 196616 | tf_op jit(solution)/shard_map/ppermute | solution.py:527
  36.2 1.4 %collective-permute-start.15 = (bf16[256,128]{1,0:T(8,128)(2,1)S(1)}, bf16[256,128]{1,0:T(8,128)(2,1)S(1)}, u32[]{:S(2)}, u32[]{:S(2)}) collective-permute-start(bf16[256,128]{1,0:T(8,128)(2,1)S(1)} %collective-permute-done.11.refs_2_), channel_id=1, source_target_pairs={{0,1},{1,0},{2,3},{3,2},{4,5},{5,4},{6,7},{7,6},{8,9},{9,8},{10,11... | collective-permute-start | bytes 196616 | tf_op jit(solution)/shard_map/ppermute | solution.py:527
  36.8 1.3 %collective-permute-start.16 = (bf16[256,128]{1,0:T(8,128)(2,1)S(1)}, bf16[256,128]{1,0:T(8,128)(2,1)S(1)}, u32[]{:S(2)}, u32[]{:S(2)}) collective-permute-start(bf16[256,128]{1,0:T(8,128)(2,1)S(1)} %collective-permute-done.12.refs_3_), channel_id=1, source_target_pairs={{0,1},{1,0},{2,3},{3,2},{4,5},{5,4},{6,7},{7,6},{8,9},{9,8},{10,11... | collective-permute-start | bytes 196616 | tf_op jit(solution)/shard_map/ppermute | solution.py:527

commit v15 on v14

--- a/solution.py
+++ b/solution.py
@@ -390,8 +390,8 @@
 
 
 def attend_kernel(chips, rows, parts, pairs, bounds, *refs):
-    own, early, late, done = by_step(refs[:chips]), refs[chips], refs[chips + 1], refs[chips + 2 :]
-    other = by_step([ref.at[i] for ref in (early, late) for i in range(ref.shape[0])])
+    own, merged, done = by_step(refs[:chips]), refs[chips : 3 * chips // 2], refs[3 * chips // 2 :]
+    other = by_step([ref.at[i] for ref in merged for i in range(ref.shape[0])])
     share = shares(chips)
     every = [ref for both in zip(own, other) for ref in both]
     half = rows // 2
@@ -491,10 +491,17 @@
         put(out + pairs * rows, both.reshape(-1, LANES))
 
 
+def hand_kernel(*refs):
+    core = lax.axis_index("seq") % 2
+    for u, ref in enumerate(refs[:-1]):
+        count = refs[-1].shape[1]
+        refs[-1][u] = ref[pl.ds(pl.multiple_of((1 - core) * count, 16), count), :]
+
+
 def unpack_kernel(chips, *refs):
     share = shares(chips)
-    back, other = refs[: len(share)], refs[len(share) : 2 * len(share)]
-    video_mixed, audio_mixed, video_cross, audio_cross = refs[2 * len(share) :]
+    back, handed = refs[: len(share)], refs[len(share)]
+    video_mixed, audio_mixed, video_cross, audio_cross = refs[len(share) + 1 :]
     rows = video_mixed.shape[0]
     half = audio_mixed.shape[0]
     parts = video_mixed.shape[1] // chips // LANES
@@ -502,11 +509,11 @@
     me = lax.axis_index("seq")
     core, home = me % 2, me // 2
     for u, (zero, one) in enumerate(share):
-        for ref, chip in (
-            (back[u], home ^ jnp.where(core == 0, zero, one)),
-            (other[u], home ^ jnp.where(core == 0, one, zero)),
+        for ref, base, chip in (
+            (back[u], core * handed.shape[1], home ^ jnp.where(core == 0, zero, one)),
+            (handed.at[u], 0, home ^ jnp.where(core == 0, one, zero)),
         ):
-            base = pl.multiple_of(core * (ref.shape[0] // 2), 16)
+            base = pl.multiple_of(base, 16)
 
             def piece(at):
                 return ref[pl.ds(base + at, rows), :]
@@ -566,37 +573,43 @@
     packed = by_step(packed)
     moved = [swap(packed[j], n, 2 * j) for j in range(1, chips)]
     own = in_order(packed[:1] + moved)
-    early = chips // 2
-    slab = packed[0].shape
+    joint = pltpu.VMEM((2,) + packed[0].shape, jnp.bfloat16)
     bounds, first = pl.pallas_call(
         gather_kernel,
-        out_shape=(
-            pltpu.VMEM((8, LANES), jnp.int32),
-            pltpu.VMEM((early,) + slab, jnp.bfloat16),
-        ),
-        in_specs=[smem] * 3 + [vmem] * early,
+        out_shape=(pltpu.VMEM((8, LANES), jnp.int32), joint),
+        in_specs=[smem] * 3 + [vmem] * 2,
         out_specs=(vmem, vmem),
         compiler_params=params,
-    )(video_length, audio_length, align_offset, *own[:early])
-    second = pl.pallas_call(
-        merge_kernel,
-        out_shape=pltpu.VMEM((chips - early,) + slab, jnp.bfloat16),
-        in_specs=[vmem] * (chips - early),
-        out_specs=vmem,
-        compiler_params=params,
-    )(*own[early:])
+    )(video_length, audio_length, align_offset, *own[:2])
+    merged = [first] + [
+        pl.pallas_call(
+            merge_kernel,
+            out_shape=joint,
+            in_specs=[vmem] * 2,
+            out_specs=vmem,
+            compiler_params=params,
+        )(*own[i : i + 2])
+        for i in range(2, chips, 2)
+    ]
     share = shares(chips)
     done = pl.pallas_call(
         functools.partial(attend_kernel, chips, rows, parts, pairs),
         out_shape=[buffer(2 * (parts + 2 * pairs) * rows, LANES)] * len(share),
-        in_specs=[vmem] * (3 + chips),
+        in_specs=[vmem] * (1 + chips + len(merged)),
         out_specs=[vmem] * len(share),
         compiler_params=params,
-    )(bounds, *own, swap(first, n, 1), swap(second, n, 1))
+    )(bounds, *own, *[swap(piece, n, 1) for piece in merged])
     back = [
         lax.ppermute(piece, "seq", [(i, i ^ 2 * pair[i % 2]) for i in range(n)])
         for piece, pair in zip(done, share)
     ]
+    handed = pl.pallas_call(
+        hand_kernel,
+        out_shape=pltpu.VMEM((len(share), done[0].shape[0] // 2, LANES), jnp.bfloat16),
+        in_specs=[vmem] * len(share),
+        out_specs=vmem,
+        compiler_params=params,
+    )(*back)
     return pl.pallas_call(
         functools.partial(unpack_kernel, chips),
         out_shape=(
@@ -605,10 +618,10 @@
             buffer(*cross_video_query.shape),
             buffer(*cross_audio_query.shape),
         ),
-        in_specs=[vmem] * (2 * len(share)),
+        in_specs=[vmem] * (len(share) + 1),
         out_specs=(vmem,) * 4,
         compiler_params=params,
-    )(*back, *[swap(piece, n, 1) for piece in back])
+    )(*back, swap(handed, n, 1))
 
 
 def shards(*arrays):

time: 39 us -> 38.4 us (0.985)
  waiting for transfers between devices: 10.4 us -> 9.28 us
  starting transfers between devices: 22.6 us -> 23.2 us
    ppermute x13 -> x12, waiting for transfers between devices: 7.7 us -> 6.54 us  [swap(): return lax.ppermute(piece, 'seq', [(i, i ^ step) for i in range(n)])]
    ppermute x13 -> x12, starting transfers between devices: 16.6 us -> 17.2 us  [swap(): return lax.ppermute(piece, 'seq', [(i, i ^ step) for i in range(n)])]
  transfers between devices with their start and end apart: 17 -> 16, of which waited for: 8 -> 6; matrix products, arithmetic and copies ran while one was open for 0% -> 0% of each run, Pallas kernels for 0% -> 0%
where the time goes in v15:
time: 38.4 us; the launch traced here: 38.2 us
  starting transfers between devices  23.2 us (60%)
  waiting for transfers between devices  9.28 us (24%)
  Pallas kernels  3.08 us (8%)
  between operations  2.7 us (7%)
    ppermute x12, starting transfers between devices, swap(): return lax.ppermute(piece, 'seq', [(i, i ^ step) for i in range(n)])  17.2 us
    ppermute x12, waiting for transfers between devices, swap(): return lax.ppermute(piece, 'seq', [(i, i ^ step) for i in range(n)])  6.54 us
    ppermute x4, starting transfers between devices, shards_packed(): lax.ppermute(piece, 'seq', [(i, i ^ 2 * pair[i % 2]) for i in range(n)])  6 us
    ppermute x4, waiting for transfers between devices, shards_packed(): lax.ppermute(piece, 'seq', [(i, i ^ 2 * pair[i % 2]) for i in range(n)])  2.75 us
    pallas_call x1, Pallas kernels, shards_packed(): pl.pallas_call(functools.partial(pack_kernel, chips), out_shape=[pltpu.VM...  1.31 us
    pallas_call x1, Pallas kernels, shards_packed(): pl.pallas_call(functools.partial(attend_kernel, chips, rows, parts, pairs...  0.95 us
  transfers between devices with their start and end apart: 16, of which 6 were waited for; matrix products, arithmetic and copies ran while one was open for 0% of the time, Pallas kernels for 0%

profile of v15, /device:TPU:0, one launch (start us, length us, event | category | flops | bytes accessed | tf_op | source)
XLA Modules:
  0.0 38.2 jit_solution(10958514772543736390)
XLA Ops:
  0.6 1.3 %shard_map.174 = (bf16[384,128]{1,0:T(8,128)(2,1)S(1)}, bf16[384,128]{1,0:T(8,128)(2,1)S(1)}, bf16[384,128]{1,0:T(8,128)(2,1)S(1)}, bf16[384,128]{1,0:T(8,128)(2...) custom-call(bf16[16,4096]{1,0:T(8,128)(2,1)} %refs_0_.1, ...), custom_call_target="tpu_custom_call" | custom-call | tf_op jit(solution)/shard_map/pallas_call | solution.py:564
  1.9 6.1 %collective-permute-start = (bf16[384,128]{1,0:T(8,128)(2,1)S(1)}, bf16[384,128]{1,0:T(8,128)(2,1)S(1)}, u32[]{:S(2)}, u32[]{:S(2)}) collective-permute-start(bf16[384,128]{1,0:T(8,128)(2,1)S(1)} %get-tuple-element.19), channel_id=1, source_target_pairs={{0,14},{1,15},{2,12},{3,13},{4,10},{5,11},{6,8},{7,9},{8,6},{9,7},... | collective-permute-start | bytes 294920 | tf_op jit(solution)/shard_map/ppermute | solution.py:534
  8.0 0.5 %collective-permute-start.1 = (bf16[384,128]{1,0:T(8,128)(2,1)S(1)}, bf16[384,128]{1,0:T(8,128)(2,1)S(1)}, u32[]{:S(2)}, u32[]{:S(2)}) collective-permute-start(bf16[384,128]{1,0:T(8,128)(2,1)S(1)} %get-tuple-element.21), channel_id=1, source_target_pairs={{0,2},{1,3},{2,0},{3,1},{4,6},{5,7},{6,4},{7,5},{8,10},{9,11},{10,... | collective-permute-start | bytes 294920 | tf_op jit(solution)/shard_map/ppermute | solution.py:534
  8.5 0.1 collective-permute-start.2
  8.7 0.0 collective-permute-start.3
  8.7 3.1 %collective-permute-start.4 = (bf16[384,128]{1,0:T(8,128)(2,1)S(1)}, bf16[384,128]{1,0:T(8,128)(2,1)S(1)}, u32[]{:S(2)}, u32[]{:S(2)}) collective-permute-start(bf16[384,128]{1,0:T(8,128)(2,1)S(1)} %get-tuple-element.24), channel_id=1, source_target_pairs={{0,6},{1,7},{2,4},{3,5},{4,2},{5,3},{6,0},{7,1},{8,14},{9,15},{10,... | collective-permute-start | bytes 294920 | tf_op jit(solution)/shard_map/ppermute | solution.py:534
  11.7 0.0 collective-permute-done.refs_1_
  11.7 6.1 %collective-permute-start.5 = (bf16[384,128]{1,0:T(8,128)(2,1)S(1)}, bf16[384,128]{1,0:T(8,128)(2,1)S(1)}, u32[]{:S(2)}, u32[]{:S(2)}) collective-permute-start(bf16[384,128]{1,0:T(8,128)(2,1)S(1)} %get-tuple-element.25), channel_id=1, source_target_pairs={{0,10},{1,11},{2,8},{3,9},{4,14},{5,15},{6,12},{7,13},{8,2},{9,3},... | collective-permute-start | bytes 294920 | tf_op jit(solution)/shard_map/ppermute | solution.py:534
  17.8 0.0 collective-permute-done.1.refs_0_.refs_2_
  17.8 0.0 collective-permute-start.6
  19.8 0.0 collective-permute-done.2.refs_1_.refs_3_
  19.8 0.1 collective-permute-start.7
  19.9 0.0 collective-permute-done.3.refs_0_.refs_4_
  19.9 0.6 %collective-permute-start.8 = (bf16[2,384,128]{2,1,0:T(8,128)(2,1)S(1)}, bf16[2,384,128]{2,1,0:T(8,128)(2,1)S(1)}, u32[]{:S(2)}, u32[]{:S(2)}) collective-permute-start(bf16[2,384,128]{2,1,0:T(8,128)(2,1)S(1)} %shard_map.176), channel_id=1, source_target_pairs={{0,1},{1,0},{2,3},{3,2},{4,5},{5,4},{6,7},{7,6},{8,9},{9,8},{10,11... | collective-permute-start | bytes 589832 | tf_op jit(solution)/shard_map/ppermute | solution.py:534
  20.5 0.0 collective-permute-done.4.refs_1_.refs_5_
  20.5 0.1 collective-permute-start.9
  20.6 3.5 %collective-permute-done.5.refs_0_.refs_6_ = bf16[384,128]{1,0:T(8,128)(2,1)S(1)} collective-permute-done((bf16[384,128]{1,0:T(8,128)(2,1)S(1)}, bf16[384,128]{1,0:T(8,128)(2,1)S(1)}, u32[]{:S(2)}, u32[]{:S(2)}) %collective-permute-start.5) | collective-permute-done | bytes 98336 | tf_op jit(solution)/shard_map/ppermute | solution.py:534
  24.1 0.6 %collective-permute-done.6.refs_1_.refs_7_ = bf16[384,128]{1,0:T(8,128)(2,1)S(1)} collective-permute-done((bf16[384,128]{1,0:T(8,128)(2,1)S(1)}, bf16[384,128]{1,0:T(8,128)(2,1)S(1)}, u32[]{:S(2)}, u32[]{:S(2)}) %collective-permute-start.6) | collective-permute-done | bytes 98336 | tf_op jit(solution)/shard_map/ppermute | solution.py:534
  24.7 0.1 collective-permute-start.10
  24.8 0.0 collective-permute-done.7.refs_8_
  24.8 0.0 collective-permute-done.8.refs_9_
  24.8 0.0 collective-permute-done.9.refs_10_
  24.8 1.4 %collective-permute-done.10.refs_11_ = bf16[2,384,128]{2,1,0:T(8,128)(2,1)S(1)} collective-permute-done((bf16[2,384,128]{2,1,0:T(8,128)(2,1)S(1)}, bf16[2,384,128]{2,1,0:T(8,128)(2,1)S(1)}, u32[]{:S(2)}, u32[]{:S(2)}) %collective-permute-start.10) | collective-permute-done | bytes 196640 | tf_op jit(solution)/shard_map/ppermute | solution.py:534
  26.2 0.9 %shard_map.179 = (bf16[256,128]{1,0:T(8,128)(2,1)S(1)}, bf16[256,128]{1,0:T(8,128)(2,1)S(1)}, bf16[256,128]{1,0:T(8,128)(2,1)S(1)}, bf16[256,128]{1,0:T(8,128)(2,1)S(1)}) custom-call(s32[8,128]{1,0:T(8,128)S(1)} %get-tuple-element.20.bounds, bf16[384,128]{1,0:T(8,128)(2,1)S(1)} %get-tuple-element.18.refs_0_, ...), custom_call_target="tpu_custom_call" | custom-call | tf_op jit(solution)/shard_map/pallas_call | solution.py:595
  27.2 2.6 %collective-permute-start.11 = (bf16[256,128]{1,0:T(8,128)(2,1)S(1)}, bf16[256,128]{1,0:T(8,128)(2,1)S(1)}, u32[]{:S(2)}, u32[]{:S(2)}) collective-permute-start(bf16[256,128]{1,0:T(8,128)(2,1)S(1)} %get-tuple-element.28), channel_id=1, source_target_pairs={{0,14},{1,11},{2,12},{3,9},{4,10},{5,15},{6,8},{7,13},{8,6},{9,3},... | collective-permute-start | bytes 196616 | tf_op jit(solution)/shard_map/ppermute | solution.py:603
  29.8 1.7 %collective-permute-start.12 = (bf16[256,128]{1,0:T(8,128)(2,1)S(1)}, bf16[256,128]{1,0:T(8,128)(2,1)S(1)}, u32[]{:S(2)}, u32[]{:S(2)}) collective-permute-start(bf16[256,128]{1,0:T(8,128)(2,1)S(1)} %get-tuple-element.29), channel_id=1, source_target_pairs={{0,12},{1,9},{2,14},{3,11},{4,8},{5,13},{6,10},{7,15},{8,4},{9,1},... | collective-permute-start | bytes 196616 | tf_op jit(solution)/shard_map/ppermute | solution.py:603
  31.5 1.0 %collective-permute-start.13 = (bf16[256,128]{1,0:T(8,128)(2,1)S(1)}, bf16[256,128]{1,0:T(8,128)(2,1)S(1)}, u32[]{:S(2)}, u32[]{:S(2)}) collective-permute-start(bf16[256,128]{1,0:T(8,128)(2,1)S(1)} %get-tuple-element.30), channel_id=1, source_target_pairs={{0,2},{1,7},{2,0},{3,5},{4,6},{5,3},{6,4},{7,1},{8,10},{9,15},{10,... | collective-permute-start | bytes 196616 | tf_op jit(solution)/shard_map/ppermute | solution.py:603
  32.5 0.7 %collective-permute-start.14 = (bf16[256,128]{1,0:T(8,128)(2,1)S(1)}, bf16[256,128]{1,0:T(8,128)(2,1)S(1)}, u32[]{:S(2)}, u32[]{:S(2)}) collective-permute-start(bf16[256,128]{1,0:T(8,128)(2,1)S(1)} %get-tuple-element.31), channel_id=1, source_target_pairs={{0,0},{1,5},{2,2},{3,7},{4,4},{5,1},{6,6},{7,3},{8,8},{9,13},{10,1... | collective-permute-start | bytes 196616 | tf_op jit(solution)/shard_map/ppermute | solution.py:603
  33.2 1.4 %collective-permute-done.11.refs_0_ = bf16[256,128]{1,0:T(8,128)(2,1)S(1)} collective-permute-done((bf16[256,128]{1,0:T(8,128)(2,1)S(1)}, bf16[256,128]{1,0:T(8,128)(2,1)S(1)}, u32[]{:S(2)}, u32[]{:S(2)}) %collective-permute-start.11) | collective-permute-done | bytes 65568 | tf_op jit(solution)/shard_map/ppermute | solution.py:603
  34.6 1.4 %collective-permute-done.12.refs_1_ = bf16[256,128]{1,0:T(8,128)(2,1)S(1)} collective-permute-done((bf16[256,128]{1,0:T(8,128)(2,1)S(1)}, bf16[256,128]{1,0:T(8,128)(2,1)S(1)}, u32[]{:S(2)}, u32[]{:S(2)}) %collective-permute-start.12) | collective-permute-done | bytes 65568 | tf_op jit(solution)/shard_map/ppermute | solution.py:603
  35.9 0.0 collective-permute-done.13.refs_2_
  35.9 0.0 collective-permute-done.14.refs_3_
  36.0 0.5 %collective-permute-start.15 = (bf16[4,128,128]{2,1,0:T(8,128)(2,1)S(1)}, bf16[4,128,128]{2,1,0:T(8,128)(2,1)S(1)}, u32[]{:S(2)}, u32[]{:S(2)}) collective-permute-start(bf16[4,128,128]{2,1,0:T(8,128)(2,1)S(1)} %shard_map.180), channel_id=1, source_target_pairs={{0,1},{1,0},{2,3},{3,2},{4,5},{5,4},{6,7},{7,6},{8,9},{9,8},{10,11... | collective-permute-start | bytes 393224 | tf_op jit(solution)/shard_map/ppermute | solution.py:534
  36.5 1.0 %collective-permute-done.15.refs_4_ = bf16[4,128,128]{2,1,0:T(8,128)(2,1)S(1)} collective-permute-done((bf16[4,128,128]{2,1,0:T(8,128)(2,1)S(1)}, bf16[4,128,128]{2,1,0:T(8,128)(2,1)S(1)}, u32[]{:S(2)}, u32[]{:S(2)}) %collective-permute-start.15) | collective-permute-done | bytes 131104 | tf_op jit(solution)/shard_map/ppermute | solution.py:534
  37.5 0.8 %shard_map.181 = (bf16[16,4096]{1,0:T(8,128)(2,1)}, bf16[8,2048]{1,0:T(8,128)(2,1)}, bf16[16,2048]{1,0:T(8,128)(2,1)}, bf16[8,2048]{1,0:T(8,128)(2,1)}) custom-call(bf16[256,128]{1,0:T(8,128)(2,1)S(1)} %collective-permute-done.11.refs_0_, bf16[256,128]{1,0:T(8,128)(2,1)S(1)} %collective-permute-done.12.refs_1_, ...), custom_call_target="tpu_custom_call" | custom-call | tf_op jit(solution)/shard_map/pallas_call | solution.py:613
  (5 shorter events, 0.1 us)
Async XLA Ops:
  1.9 9.8 %collective-permute-start = (bf16[384,128]{1,0:T(8,128)(2,1)S(1)}, bf16[384,128]{1,0:T(8,128)(2,1)S(1)}, u32[]{:S(2)}, u32[]{:S(2)}) collective-permute-start(bf16[384,128]{1,0:T(8,128)(2,1)S(1)} %get-tuple-element.19), channel_id=1, source_target_pairs={{0,14},{1,15},{2,12},{3,13},{4,10},{5,11},{6,8},{7,9},{8,6},{9,7},... | collective-permute-start | bytes 294920 | tf_op jit(solution)/shard_map/ppermute | solution.py:534
  8.0 9.8 %collective-permute-start.1 = (bf16[384,128]{1,0:T(8,128)(2,1)S(1)}, bf16[384,128]{1,0:T(8,128)(2,1)S(1)}, u32[]{:S(2)}, u32[]{:S(2)}) collective-permute-start(bf16[384,128]{1,0:T(8,128)(2,1)S(1)} %get-tuple-element.21), channel_id=1, source_target_pairs={{0,2},{1,3},{2,0},{3,1},{4,6},{5,7},{6,4},{7,5},{8,10},{9,11},{10,... | collective-permute-start | bytes 294920 | tf_op jit(solution)/shard_map/ppermute | solution.py:534
  8.5 11.3 %collective-permute-start.2 = (bf16[384,128]{1,0:T(8,128)(2,1)S(1)}, bf16[384,128]{1,0:T(8,128)(2,1)S(1)}, u32[]{:S(2)}, u32[]{:S(2)}) collective-permute-start(bf16[384,128]{1,0:T(8,128)(2,1)S(1)} %get-tuple-element.22), channel_id=1, source_target_pairs={{0,12},{1,13},{2,14},{3,15},{4,8},{5,9},{6,10},{7,11},{8,4},{9,5},... | collective-permute-start | bytes 294920 | tf_op jit(solution)/shard_map/ppermute | solution.py:534
  8.7 11.2 %collective-permute-start.3 = (bf16[384,128]{1,0:T(8,128)(2,1)S(1)}, bf16[384,128]{1,0:T(8,128)(2,1)S(1)}, u32[]{:S(2)}, u32[]{:S(2)}) collective-permute-start(bf16[384,128]{1,0:T(8,128)(2,1)S(1)} %get-tuple-element.23), channel_id=1, source_target_pairs={{0,4},{1,5},{2,6},{3,7},{4,0},{5,1},{6,2},{7,3},{8,12},{9,13},{10,... | collective-permute-start | bytes 294920 | tf_op jit(solution)/shard_map/ppermute | solution.py:534
  8.7 11.8 %collective-permute-start.4 = (bf16[384,128]{1,0:T(8,128)(2,1)S(1)}, bf16[384,128]{1,0:T(8,128)(2,1)S(1)}, u32[]{:S(2)}, u32[]{:S(2)}) collective-permute-start(bf16[384,128]{1,0:T(8,128)(2,1)S(1)} %get-tuple-element.24), channel_id=1, source_target_pairs={{0,6},{1,7},{2,4},{3,5},{4,2},{5,3},{6,0},{7,1},{8,14},{9,15},{10,... | collective-permute-start | bytes 294920 | tf_op jit(solution)/shard_map/ppermute | solution.py:534
  11.7 12.3 %collective-permute-start.5 = (bf16[384,128]{1,0:T(8,128)(2,1)S(1)}, bf16[384,128]{1,0:T(8,128)(2,1)S(1)}, u32[]{:S(2)}, u32[]{:S(2)}) collective-permute-start(bf16[384,128]{1,0:T(8,128)(2,1)S(1)} %get-tuple-element.25), channel_id=1, source_target_pairs={{0,10},{1,11},{2,8},{3,9},{4,14},{5,15},{6,12},{7,13},{8,2},{9,3},... | collective-permute-start | bytes 294920 | tf_op jit(solution)/shard_map/ppermute | solution.py:534
  17.8 6.9 %collective-permute-start.6 = (bf16[384,128]{1,0:T(8,128)(2,1)S(1)}, bf16[384,128]{1,0:T(8,128)(2,1)S(1)}, u32[]{:S(2)}, u32[]{:S(2)}) collective-permute-start(bf16[384,128]{1,0:T(8,128)(2,1)S(1)} %get-tuple-element.26), channel_id=1, source_target_pairs={{0,8},{1,9},{2,10},{3,11},{4,12},{5,13},{6,14},{7,15},{8,0},{9,1},... | collective-permute-start | bytes 294920 | tf_op jit(solution)/shard_map/ppermute | solution.py:534
  19.8 5.0 %collective-permute-start.7 = (bf16[2,384,128]{2,1,0:T(8,128)(2,1)S(1)}, bf16[2,384,128]{2,1,0:T(8,128)(2,1)S(1)}, u32[]{:S(2)}, u32[]{:S(2)}) collective-permute-start(bf16[2,384,128]{2,1,0:T(8,128)(2,1)S(1)} %get-tuple-element.27), channel_id=1, source_target_pairs={{0,1},{1,0},{2,3},{3,2},{4,5},{5,4},{6,7},{7,6},{8,9},{9,8},{10,11... | collective-permute-start | bytes 589832 | tf_op jit(solution)/shard_map/ppermute | solution.py:534
  19.9 4.9 %collective-permute-start.8 = (bf16[2,384,128]{2,1,0:T(8,128)(2,1)S(1)}, bf16[2,384,128]{2,1,0:T(8,128)(2,1)S(1)}, u32[]{:S(2)}, u32[]{:S(2)}) collective-permute-start(bf16[2,384,128]{2,1,0:T(8,128)(2,1)S(1)} %shard_map.176), channel_id=1, source_target_pairs={{0,1},{1,0},{2,3},{3,2},{4,5},{5,4},{6,7},{7,6},{8,9},{9,8},{10,11... | collective-permute-start | bytes 589832 | tf_op jit(solution)/shard_map/ppermute | solution.py:534
  20.5 4.3 %collective-permute-start.9 = (bf16[2,384,128]{2,1,0:T(8,128)(2,1)S(1)}, bf16[2,384,128]{2,1,0:T(8,128)(2,1)S(1)}, u32[]{:S(2)}, u32[]{:S(2)}) collective-permute-start(bf16[2,384,128]{2,1,0:T(8,128)(2,1)S(1)} %shard_map.177), channel_id=1, source_target_pairs={{0,1},{1,0},{2,3},{3,2},{4,5},{5,4},{6,7},{7,6},{8,9},{9,8},{10,11... | collective-permute-start | bytes 589832 | tf_op jit(solution)/shard_map/ppermute | solution.py:534
  24.7 1.5 %collective-permute-start.10 = (bf16[2,384,128]{2,1,0:T(8,128)(2,1)S(1)}, bf16[2,384,128]{2,1,0:T(8,128)(2,1)S(1)}, u32[]{:S(2)}, u32[]{:S(2)}) collective-permute-start(bf16[2,384,128]{2,1,0:T(8,128)(2,1)S(1)} %shard_map.178), channel_id=1, source_target_pairs={{0,1},{1,0},{2,3},{3,2},{4,5},{5,4},{6,7},{7,6},{8,9},{9,8},{10,11... | collective-permute-start | bytes 589832 | tf_op jit(solution)/shard_map/ppermute | solution.py:534
  27.2 7.4 %collective-permute-start.11 = (bf16[256,128]{1,0:T(8,128)(2,1)S(1)}, bf16[256,128]{1,0:T(8,128)(2,1)S(1)}, u32[]{:S(2)}, u32[]{:S(2)}) collective-permute-start(bf16[256,128]{1,0:T(8,128)(2,1)S(1)} %get-tuple-element.28), channel_id=1, source_target_pairs={{0,14},{1,11},{2,12},{3,9},{4,10},{5,15},{6,8},{7,13},{8,6},{9,3},... | collective-permute-start | bytes 196616 | tf_op jit(solution)/shard_map/ppermute | solution.py:603
  29.8 6.2 %collective-permute-start.12 = (bf16[256,128]{1,0:T(8,128)(2,1)S(1)}, bf16[256,128]{1,0:T(8,128)(2,1)S(1)}, u32[]{:S(2)}, u32[]{:S(2)}) collective-permute-start(bf16[256,128]{1,0:T(8,128)(2,1)S(1)} %get-tuple-element.29), channel_id=1, source_target_pairs={{0,12},{1,9},{2,14},{3,11},{4,8},{5,13},{6,10},{7,15},{8,4},{9,1},... | collective-permute-start | bytes 196616 | tf_op jit(solution)/shard_map/ppermute | solution.py:603
  31.5 4.5 %collective-permute-start.13 = (bf16[256,128]{1,0:T(8,128)(2,1)S(1)}, bf16[256,128]{1,0:T(8,128)(2,1)S(1)}, u32[]{:S(2)}, u32[]{:S(2)}) collective-permute-start(bf16[256,128]{1,0:T(8,128)(2,1)S(1)} %get-tuple-element.30), channel_id=1, source_target_pairs={{0,2},{1,7},{2,0},{3,5},{4,6},{5,3},{6,4},{7,1},{8,10},{9,15},{10,... | collective-permute-start | bytes 196616 | tf_op jit(solution)/shard_map/ppermute | solution.py:603
  32.5 3.4 %collective-permute-start.14 = (bf16[256,128]{1,0:T(8,128)(2,1)S(1)}, bf16[256,128]{1,0:T(8,128)(2,1)S(1)}, u32[]{:S(2)}, u32[]{:S(2)}) collective-permute-start(bf16[256,128]{1,0:T(8,128)(2,1)S(1)} %get-tuple-element.31), channel_id=1, source_target_pairs={{0,0},{1,5},{2,2},{3,7},{4,4},{5,1},{6,6},{7,3},{8,8},{9,13},{10,1... | collective-permute-start | bytes 196616 | tf_op jit(solution)/shard_map/ppermute | solution.py:603
  36.0 1.5 %collective-permute-start.15 = (bf16[4,128,128]{2,1,0:T(8,128)(2,1)S(1)}, bf16[4,128,128]{2,1,0:T(8,128)(2,1)S(1)}, u32[]{:S(2)}, u32[]{:S(2)}) collective-permute-start(bf16[4,128,128]{2,1,0:T(8,128)(2,1)S(1)} %shard_map.180), channel_id=1, source_target_pairs={{0,1},{1,0},{2,3},{3,2},{4,5},{5,4},{6,7},{7,6},{8,9},{9,8},{10,11... | collective-permute-start | bytes 393224 | tf_op jit(solution)/shard_map/ppermute | solution.py:534

commit v16 on v15

--- a/solution.py
+++ b/solution.py
@@ -303,9 +303,8 @@
     return [items[j] for j in step_order(len(items))]
 
 
-def pack_kernel(chips, *refs):
-    sources, refs = refs[:12], refs[12:]
-    packed, held, arrived = by_step(refs[:chips]), refs[chips : chips + 12], refs[chips + 12]
+def pack_kernel(chips, steps, *refs):
+    sources, packed, held, arrived = refs[:12], refs[13:-13], refs[-13:-1], refs[-1]
     copies = fetch(sources, held, arrived)
     chip = lax.axis_index("seq") // 2
     video, cross, audio = held[0:3], held[3:6], held[6:12]
@@ -320,18 +319,18 @@
     for i, ref in enumerate(video + cross):
         copies[i].wait()
         for part in range(ref.shape[1] // chips // LANES):
-            for j in range(chips):
-                packed[j][at : at + rows, :] = group(ref, j, part)
+            for slab, j in zip(packed, steps):
+                slab[at : at + rows, :] = group(ref, j, part)
             at += rows
     for i in range(0, 6, 2):
         copies[6 + i].wait()
         copies[7 + i].wait()
         for part in range(audio[i].shape[1] // chips // LANES):
-            for j in range(chips):
+            for slab, j in zip(packed, steps):
                 pair = jnp.concatenate(
                     [group(audio[i], j, part), group(audio[i + 1], j, part)], axis=0
                 )
-                packed[j][at : at + rows, :] = pair
+                slab[at : at + rows, :] = pair
             at += rows
 
 
@@ -561,16 +560,24 @@
         audio_query, audio_keys, audio_values,
         cross_audio_query, cross_audio_keys, cross_audio_values,
     )
-    packed = pl.pallas_call(
-        functools.partial(pack_kernel, chips),
-        out_shape=[pltpu.VMEM(((3 * parts + 6 * pairs) * rows, LANES), jnp.bfloat16)] * chips,
-        in_specs=[hbm] * 12,
-        out_specs=[vmem] * chips,
-        scratch_shapes=[pltpu.VMEM(source.shape, source.dtype) for source in sources]
-        + [pltpu.SemaphoreType.DMA((12,))],
-        compiler_params=params,
-    )(*[pltpu.with_memory_space_constraint(source, pltpu.HBM) for source in sources])
-    packed = by_step(packed)
+    sources = [pltpu.with_memory_space_constraint(source, pltpu.HBM) for source in sources]
+    slab = pltpu.VMEM(((3 * parts + 6 * pairs) * rows, LANES), jnp.bfloat16)
+
+    def pack(steps, after):
+        return pl.pallas_call(
+            functools.partial(pack_kernel, chips, steps),
+            out_shape=[slab] * len(steps),
+            in_specs=[hbm] * 12 + [pl.BlockSpec(memory_space=pl.ANY)],
+            out_specs=[vmem] * len(steps),
+            scratch_shapes=[pltpu.VMEM(source.shape, source.dtype) for source in sources]
+            + [pltpu.SemaphoreType.DMA((12,))],
+            compiler_params=params,
+        )(*sources, after)
+
+    order = step_order(chips)
+    (ahead,) = pack(order[1:2], sources[0])
+    rest = pack(order[:1] + order[2:], ahead)
+    packed = by_step([rest[0], ahead, *rest[1:]])
     moved = [swap(packed[j], n, 2 * j) for j in range(1, chips)]
     own = in_order(packed[:1] + moved)
     joint = pltpu.VMEM((2,) + packed[0].shape, jnp.bfloat16)

time: 38.4 us -> 39.1 us (1.018)
  starting transfers between devices: 23.2 us -> 20.5 us
  waiting for transfers between devices: 9.28 us -> 11.4 us
  Pallas kernels: 3.08 us -> 4.28 us
    ppermute x12, starting transfers between devices: 17.2 us -> 14.5 us  [swap(): return lax.ppermute(piece, 'seq', [(i, i ^ step) for i in range(n)])]
    ppermute x12, waiting for transfers between devices: 6.54 us -> 8.32 us  [swap(): return lax.ppermute(piece, 'seq', [(i, i ^ step) for i in range(n)])]
    pallas_call x1 -> x2, Pallas kernels: 1.31 us -> 2.51 us  [pack(): pl.pallas_call(functools.partial(pack_kernel, chips, steps), out_shape=[s...]
  transfers between devices with their start and end apart: 16 -> 16, of which waited for: 6 -> 7; matrix products, arithmetic and copies ran while one was open for 0% -> 0% of each run, Pallas kernels for 0% -> 3%
where the time goes in v16:
time: 39.1 us; the launch traced here: 38.9 us
  starting transfers between devices  20.5 us (52%)
  waiting for transfers between devices  11.4 us (29%)
  Pallas kernels  4.28 us (11%)
  between operations  2.71 us (7%)
    ppermute x12, starting transfers between devices, swap(): return lax.ppermute(piece, 'seq', [(i, i ^ step) for i in range(n)])  14.5 us
    ppermute x12, waiting for transfers between devices, swap(): return lax.ppermute(piece, 'seq', [(i, i ^ step) for i in range(n)])  8.32 us
    ppermute x4, starting transfers between devices, shards_packed(): lax.ppermute(piece, 'seq', [(i, i ^ 2 * pair[i % 2]) for i in range(n)])  6 us
    ppermute x4, waiting for transfers between devices, shards_packed(): lax.ppermute(piece, 'seq', [(i, i ^ 2 * pair[i % 2]) for i in range(n)])  3.08 us
    pallas_call x2, Pallas kernels, pack(): pl.pallas_call(functools.partial(pack_kernel, chips, steps), out_shape=[s...  2.51 us
    pallas_call x1, Pallas kernels, shards_packed(): pl.pallas_call(functools.partial(attend_kernel, chips, rows, parts, pairs...  0.95 us
  transfers between devices with their start and end apart: 16, of which 7 were waited for; matrix products, arithmetic and copies ran while one was open for 0% of the time, Pallas kernels for 3%

profile of v16, /device:TPU:0, one launch (start us, length us, event | category | flops | bytes accessed | tf_op | source)
XLA Modules:
  0.0 38.9 jit_solution(2730172943799389439)
XLA Ops:
  0.6 1.2 %shard_map.174.refs_12_ = bf16[384,128]{1,0:T(8,128)(2,1)S(1)} custom-call(bf16[16,4096]{1,0:T(8,128)(2,1)} %refs_0_.3, bf16[16,4096]{1,0:T(8,128)(2,1)} %refs_1_.3, bf16[16,4096]{1,0:T(8,128)(2,1)} %refs_2_.3, bf16[16,2048]{1,0:T(8,128)(2,1)} %refs_3_.3, bf16[16,2048]{1,0:T(8,128)(2,1)} %refs_4_.3, bf16[16,2048]{1,0:T(8,128)(2,1)} %refs_5_.3, ...), custom_call_target="tpu_custom_call" | custom-call | tf_op jit(solution)/shard_map/pallas_call | solution.py:567
  1.9 6.1 %collective-permute-start = (bf16[384,128]{1,0:T(8,128)(2,1)S(1)}, bf16[384,128]{1,0:T(8,128)(2,1)S(1)}, u32[]{:S(2)}, u32[]{:S(2)}) collective-permute-start(bf16[384,128]{1,0:T(8,128)(2,1)S(1)} %shard_map.174.refs_12_), channel_id=1, source_target_pairs={{0,14},{1,15},{2,12},{3,13},{4,10},{5,11},{6,8},{7,9},{8,6},{9,7},... | collective-permute-start | bytes 294920 | tf_op jit(solution)/shard_map/ppermute | solution.py:533
  7.9 1.3 %shard_map.175 = (bf16[384,128]{1,0:T(8,128)(2,1)S(1)}, bf16[384,128]{1,0:T(8,128)(2,1)S(1)}, bf16[384,128]{1,0:T(8,128)(2,1)S(1)}, bf16[384,128]{1,0:T(8,128)(2...) custom-call(bf16[16,4096]{1,0:T(8,128)(2,1)} %refs_0_.3, ...), custom_call_target="tpu_custom_call" | custom-call | tf_op jit(solution)/shard_map/pallas_call | solution.py:567
  9.2 0.6 %collective-permute-start.1 = (bf16[384,128]{1,0:T(8,128)(2,1)S(1)}, bf16[384,128]{1,0:T(8,128)(2,1)S(1)}, u32[]{:S(2)}, u32[]{:S(2)}) collective-permute-start(bf16[384,128]{1,0:T(8,128)(2,1)S(1)} %get-tuple-element.19), channel_id=1, source_target_pairs={{0,2},{1,3},{2,0},{3,1},{4,6},{5,7},{6,4},{7,5},{8,10},{9,11},{10,... | collective-permute-start | bytes 294920 | tf_op jit(solution)/shard_map/ppermute | solution.py:533
  9.8 0.1 collective-permute-start.2
  9.9 0.0 collective-permute-start.3
  9.9 3.1 %collective-permute-start.4 = (bf16[384,128]{1,0:T(8,128)(2,1)S(1)}, bf16[384,128]{1,0:T(8,128)(2,1)S(1)}, u32[]{:S(2)}, u32[]{:S(2)}) collective-permute-start(bf16[384,128]{1,0:T(8,128)(2,1)S(1)} %get-tuple-element.22), channel_id=1, source_target_pairs={{0,6},{1,7},{2,4},{3,5},{4,2},{5,3},{6,0},{7,1},{8,14},{9,15},{10,... | collective-permute-start | bytes 294920 | tf_op jit(solution)/shard_map/ppermute | solution.py:533
  13.0 0.0 collective-permute-done.refs_1_
  13.0 3.9 %collective-permute-start.5 = (bf16[384,128]{1,0:T(8,128)(2,1)S(1)}, bf16[384,128]{1,0:T(8,128)(2,1)S(1)}, u32[]{:S(2)}, u32[]{:S(2)}) collective-permute-start(bf16[384,128]{1,0:T(8,128)(2,1)S(1)} %get-tuple-element.23), channel_id=1, source_target_pairs={{0,10},{1,11},{2,8},{3,9},{4,14},{5,15},{6,12},{7,13},{8,2},{9,3},... | collective-permute-start | bytes 294920 | tf_op jit(solution)/shard_map/ppermute | solution.py:533
  16.9 0.0 collective-permute-done.1.refs_0_.refs_2_
  16.9 0.0 collective-permute-start.6
  18.9 0.0 collective-permute-done.2.refs_1_.refs_3_
  18.9 0.1 collective-permute-start.7
  19.0 0.7 %collective-permute-done.3.refs_0_.refs_4_ = bf16[384,128]{1,0:T(8,128)(2,1)S(1)} collective-permute-done((bf16[384,128]{1,0:T(8,128)(2,1)S(1)}, bf16[384,128]{1,0:T(8,128)(2,1)S(1)}, u32[]{:S(2)}, u32[]{:S(2)}) %collective-permute-start.3) | collective-permute-done | bytes 98336 | tf_op jit(solution)/shard_map/ppermute | solution.py:533
  19.7 0.0 collective-permute-start.8
  19.7 3.0 %collective-permute-done.4.refs_1_.refs_5_ = bf16[384,128]{1,0:T(8,128)(2,1)S(1)} collective-permute-done((bf16[384,128]{1,0:T(8,128)(2,1)S(1)}, bf16[384,128]{1,0:T(8,128)(2,1)S(1)}, u32[]{:S(2)}, u32[]{:S(2)}) %collective-permute-start.4) | collective-permute-done | bytes 98336 | tf_op jit(solution)/shard_map/ppermute | solution.py:533
  22.7 0.1 collective-permute-start.9
  22.8 0.0 collective-permute-done.5.refs_0_.refs_6_
  22.8 2.2 %collective-permute-done.6.refs_1_.refs_7_ = bf16[384,128]{1,0:T(8,128)(2,1)S(1)} collective-permute-done((bf16[384,128]{1,0:T(8,128)(2,1)S(1)}, bf16[384,128]{1,0:T(8,128)(2,1)S(1)}, u32[]{:S(2)}, u32[]{:S(2)}) %collective-permute-start.6) | collective-permute-done | bytes 98336 | tf_op jit(solution)/shard_map/ppermute | solution.py:533
  25.0 0.1 collective-permute-start.10
  25.1 0.0 collective-permute-done.7.refs_8_
  25.1 0.0 collective-permute-done.8.refs_9_
  25.1 0.0 collective-permute-done.9.refs_10_
  25.1 1.4 %collective-permute-done.10.refs_11_ = bf16[2,384,128]{2,1,0:T(8,128)(2,1)S(1)} collective-permute-done((bf16[2,384,128]{2,1,0:T(8,128)(2,1)S(1)}, bf16[2,384,128]{2,1,0:T(8,128)(2,1)S(1)}, u32[]{:S(2)}, u32[]{:S(2)}) %collective-permute-start.10) | collective-permute-done | bytes 196640 | tf_op jit(solution)/shard_map/ppermute | solution.py:533
  26.5 1.0 %shard_map.180 = (bf16[256,128]{1,0:T(8,128)(2,1)S(1)}, bf16[256,128]{1,0:T(8,128)(2,1)S(1)}, bf16[256,128]{1,0:T(8,128)(2,1)S(1)}, bf16[256,128]{1,0:T(8,128)(2,1)S(1)}) custom-call(s32[8,128]{1,0:T(8,128)S(1)} %get-tuple-element.18.bounds, bf16[384,128]{1,0:T(8,128)(2,1)S(1)} %get-tuple-element.17.refs_0_, ...), custom_call_target="tpu_custom_call" | custom-call | tf_op jit(solution)/shard_map/pallas_call | solution.py:602
  27.5 2.9 %collective-permute-start.11 = (bf16[256,128]{1,0:T(8,128)(2,1)S(1)}, bf16[256,128]{1,0:T(8,128)(2,1)S(1)}, u32[]{:S(2)}, u32[]{:S(2)}) collective-permute-start(bf16[256,128]{1,0:T(8,128)(2,1)S(1)} %get-tuple-element.26), channel_id=1, source_target_pairs={{0,14},{1,11},{2,12},{3,9},{4,10},{5,15},{6,8},{7,13},{8,6},{9,3},... | collective-permute-start | bytes 196616 | tf_op jit(solution)/shard_map/ppermute | solution.py:610
  30.4 1.5 %collective-permute-start.12 = (bf16[256,128]{1,0:T(8,128)(2,1)S(1)}, bf16[256,128]{1,0:T(8,128)(2,1)S(1)}, u32[]{:S(2)}, u32[]{:S(2)}) collective-permute-start(bf16[256,128]{1,0:T(8,128)(2,1)S(1)} %get-tuple-element.27), channel_id=1, source_target_pairs={{0,12},{1,9},{2,14},{3,11},{4,8},{5,13},{6,10},{7,15},{8,4},{9,1},... | collective-permute-start | bytes 196616 | tf_op jit(solution)/shard_map/ppermute | solution.py:610
  31.9 1.0 %collective-permute-start.13 = (bf16[256,128]{1,0:T(8,128)(2,1)S(1)}, bf16[256,128]{1,0:T(8,128)(2,1)S(1)}, u32[]{:S(2)}, u32[]{:S(2)}) collective-permute-start(bf16[256,128]{1,0:T(8,128)(2,1)S(1)} %get-tuple-element.28), channel_id=1, source_target_pairs={{0,2},{1,7},{2,0},{3,5},{4,6},{5,3},{6,4},{7,1},{8,10},{9,15},{10,... | collective-permute-start | bytes 196616 | tf_op jit(solution)/shard_map/ppermute | solution.py:610
  32.8 0.7 %collective-permute-start.14 = (bf16[256,128]{1,0:T(8,128)(2,1)S(1)}, bf16[256,128]{1,0:T(8,128)(2,1)S(1)}, u32[]{:S(2)}, u32[]{:S(2)}) collective-permute-start(bf16[256,128]{1,0:T(8,128)(2,1)S(1)} %get-tuple-element.29), channel_id=1, source_target_pairs={{0,0},{1,5},{2,2},{3,7},{4,4},{5,1},{6,6},{7,3},{8,8},{9,13},{10,1... | collective-permute-start | bytes 196616 | tf_op jit(solution)/shard_map/ppermute | solution.py:610
  33.5 1.6 %collective-permute-done.11.refs_0_ = bf16[256,128]{1,0:T(8,128)(2,1)S(1)} collective-permute-done((bf16[256,128]{1,0:T(8,128)(2,1)S(1)}, bf16[256,128]{1,0:T(8,128)(2,1)S(1)}, u32[]{:S(2)}, u32[]{:S(2)}) %collective-permute-start.11) | collective-permute-done | bytes 65568 | tf_op jit(solution)/shard_map/ppermute | solution.py:610
  35.1 1.4 %collective-permute-done.12.refs_1_ = bf16[256,128]{1,0:T(8,128)(2,1)S(1)} collective-permute-done((bf16[256,128]{1,0:T(8,128)(2,1)S(1)}, bf16[256,128]{1,0:T(8,128)(2,1)S(1)}, u32[]{:S(2)}, u32[]{:S(2)}) %collective-permute-start.12) | collective-permute-done | bytes 65568 | tf_op jit(solution)/shard_map/ppermute | solution.py:610
  36.6 0.0 collective-permute-done.13.refs_2_
  36.6 0.0 collective-permute-done.14.refs_3_
  36.6 0.5 %collective-permute-start.15 = (bf16[4,128,128]{2,1,0:T(8,128)(2,1)S(1)}, bf16[4,128,128]{2,1,0:T(8,128)(2,1)S(1)}, u32[]{:S(2)}, u32[]{:S(2)}) collective-permute-start(bf16[4,128,128]{2,1,0:T(8,128)(2,1)S(1)} %shard_map.181), channel_id=1, source_target_pairs={{0,1},{1,0},{2,3},{3,2},{4,5},{5,4},{6,7},{7,6},{8,9},{9,8},{10,11... | collective-permute-start | bytes 393224 | tf_op jit(solution)/shard_map/ppermute | solution.py:533
  37.1 1.0 %collective-permute-done.15.refs_4_ = bf16[4,128,128]{2,1,0:T(8,128)(2,1)S(1)} collective-permute-done((bf16[4,128,128]{2,1,0:T(8,128)(2,1)S(1)}, bf16[4,128,128]{2,1,0:T(8,128)(2,1)S(1)}, u32[]{:S(2)}, u32[]{:S(2)}) %collective-permute-start.15) | collective-permute-done | bytes 131104 | tf_op jit(solution)/shard_map/ppermute | solution.py:533
  38.1 0.8 %shard_map.182 = (bf16[16,4096]{1,0:T(8,128)(2,1)}, bf16[8,2048]{1,0:T(8,128)(2,1)}, bf16[16,2048]{1,0:T(8,128)(2,1)}, bf16[8,2048]{1,0:T(8,128)(2,1)}) custom-call(bf16[256,128]{1,0:T(8,128)(2,1)S(1)} %collective-permute-done.11.refs_0_, bf16[256,128]{1,0:T(8,128)(2,1)S(1)} %collective-permute-done.12.refs_1_, ...), custom_call_target="tpu_custom_call" | custom-call | tf_op jit(solution)/shard_map/pallas_call | solution.py:620
  (5 shorter events, 0.1 us)
Async XLA Ops:
  1.9 11.1 %collective-permute-start = (bf16[384,128]{1,0:T(8,128)(2,1)S(1)}, bf16[384,128]{1,0:T(8,128)(2,1)S(1)}, u32[]{:S(2)}, u32[]{:S(2)}) collective-permute-start(bf16[384,128]{1,0:T(8,128)(2,1)S(1)} %shard_map.174.refs_12_), channel_id=1, source_target_pairs={{0,14},{1,15},{2,12},{3,13},{4,10},{5,11},{6,8},{7,9},{8,6},{9,7},... | collective-permute-start | bytes 294920 | tf_op jit(solution)/shard_map/ppermute | solution.py:533
  9.2 7.7 %collective-permute-start.1 = (bf16[384,128]{1,0:T(8,128)(2,1)S(1)}, bf16[384,128]{1,0:T(8,128)(2,1)S(1)}, u32[]{:S(2)}, u32[]{:S(2)}) collective-permute-start(bf16[384,128]{1,0:T(8,128)(2,1)S(1)} %get-tuple-element.19), channel_id=1, source_target_pairs={{0,2},{1,3},{2,0},{3,1},{4,6},{5,7},{6,4},{7,5},{8,10},{9,11},{10,... | collective-permute-start | bytes 294920 | tf_op jit(solution)/shard_map/ppermute | solution.py:533
  9.8 9.1 %collective-permute-start.2 = (bf16[384,128]{1,0:T(8,128)(2,1)S(1)}, bf16[384,128]{1,0:T(8,128)(2,1)S(1)}, u32[]{:S(2)}, u32[]{:S(2)}) collective-permute-start(bf16[384,128]{1,0:T(8,128)(2,1)S(1)} %get-tuple-element.20), channel_id=1, source_target_pairs={{0,12},{1,13},{2,14},{3,15},{4,8},{5,9},{6,10},{7,11},{8,4},{9,5},... | collective-permute-start | bytes 294920 | tf_op jit(solution)/shard_map/ppermute | solution.py:533
  9.9 9.8 %collective-permute-start.3 = (bf16[384,128]{1,0:T(8,128)(2,1)S(1)}, bf16[384,128]{1,0:T(8,128)(2,1)S(1)}, u32[]{:S(2)}, u32[]{:S(2)}) collective-permute-start(bf16[384,128]{1,0:T(8,128)(2,1)S(1)} %get-tuple-element.21), channel_id=1, source_target_pairs={{0,4},{1,5},{2,6},{3,7},{4,0},{5,1},{6,2},{7,3},{8,12},{9,13},{10,... | collective-permute-start | bytes 294920 | tf_op jit(solution)/shard_map/ppermute | solution.py:533
  9.9 12.8 %collective-permute-start.4 = (bf16[384,128]{1,0:T(8,128)(2,1)S(1)}, bf16[384,128]{1,0:T(8,128)(2,1)S(1)}, u32[]{:S(2)}, u32[]{:S(2)}) collective-permute-start(bf16[384,128]{1,0:T(8,128)(2,1)S(1)} %get-tuple-element.22), channel_id=1, source_target_pairs={{0,6},{1,7},{2,4},{3,5},{4,2},{5,3},{6,0},{7,1},{8,14},{9,15},{10,... | collective-permute-start | bytes 294920 | tf_op jit(solution)/shard_map/ppermute | solution.py:533
  13.0 9.8 %collective-permute-start.5 = (bf16[384,128]{1,0:T(8,128)(2,1)S(1)}, bf16[384,128]{1,0:T(8,128)(2,1)S(1)}, u32[]{:S(2)}, u32[]{:S(2)}) collective-permute-start(bf16[384,128]{1,0:T(8,128)(2,1)S(1)} %get-tuple-element.23), channel_id=1, source_target_pairs={{0,10},{1,11},{2,8},{3,9},{4,14},{5,15},{6,12},{7,13},{8,2},{9,3},... | collective-permute-start | bytes 294920 | tf_op jit(solution)/shard_map/ppermute | solution.py:533
  16.9 8.1 %collective-permute-start.6 = (bf16[384,128]{1,0:T(8,128)(2,1)S(1)}, bf16[384,128]{1,0:T(8,128)(2,1)S(1)}, u32[]{:S(2)}, u32[]{:S(2)}) collective-permute-start(bf16[384,128]{1,0:T(8,128)(2,1)S(1)} %get-tuple-element.24), channel_id=1, source_target_pairs={{0,8},{1,9},{2,10},{3,11},{4,12},{5,13},{6,14},{7,15},{8,0},{9,1},... | collective-permute-start | bytes 294920 | tf_op jit(solution)/shard_map/ppermute | solution.py:533
  18.9 6.2 %collective-permute-start.7 = (bf16[2,384,128]{2,1,0:T(8,128)(2,1)S(1)}, bf16[2,384,128]{2,1,0:T(8,128)(2,1)S(1)}, u32[]{:S(2)}, u32[]{:S(2)}) collective-permute-start(bf16[2,384,128]{2,1,0:T(8,128)(2,1)S(1)} %get-tuple-element.25), channel_id=1, source_target_pairs={{0,1},{1,0},{2,3},{3,2},{4,5},{5,4},{6,7},{7,6},{8,9},{9,8},{10,11... | collective-permute-start | bytes 589832 | tf_op jit(solution)/shard_map/ppermute | solution.py:533
  19.7 5.5 %collective-permute-start.8 = (bf16[2,384,128]{2,1,0:T(8,128)(2,1)S(1)}, bf16[2,384,128]{2,1,0:T(8,128)(2,1)S(1)}, u32[]{:S(2)}, u32[]{:S(2)}) collective-permute-start(bf16[2,384,128]{2,1,0:T(8,128)(2,1)S(1)} %shard_map.177), channel_id=1, source_target_pairs={{0,1},{1,0},{2,3},{3,2},{4,5},{5,4},{6,7},{7,6},{8,9},{9,8},{10,11... | collective-permute-start | bytes 589832 | tf_op jit(solution)/shard_map/ppermute | solution.py:533
  22.7 2.4 %collective-permute-start.9 = (bf16[2,384,128]{2,1,0:T(8,128)(2,1)S(1)}, bf16[2,384,128]{2,1,0:T(8,128)(2,1)S(1)}, u32[]{:S(2)}, u32[]{:S(2)}) collective-permute-start(bf16[2,384,128]{2,1,0:T(8,128)(2,1)S(1)} %shard_map.178), channel_id=1, source_target_pairs={{0,1},{1,0},{2,3},{3,2},{4,5},{5,4},{6,7},{7,6},{8,9},{9,8},{10,11... | collective-permute-start | bytes 589832 | tf_op jit(solution)/shard_map/ppermute | solution.py:533
  25.0 1.5 %collective-permute-start.10 = (bf16[2,384,128]{2,1,0:T(8,128)(2,1)S(1)}, bf16[2,384,128]{2,1,0:T(8,128)(2,1)S(1)}, u32[]{:S(2)}, u32[]{:S(2)}) collective-permute-start(bf16[2,384,128]{2,1,0:T(8,128)(2,1)S(1)} %shard_map.179), channel_id=1, source_target_pairs={{0,1},{1,0},{2,3},{3,2},{4,5},{5,4},{6,7},{7,6},{8,9},{9,8},{10,11... | collective-permute-start | bytes 589832 | tf_op jit(solution)/shard_map/ppermute | solution.py:533
  27.5 7.6 %collective-permute-start.11 = (bf16[256,128]{1,0:T(8,128)(2,1)S(1)}, bf16[256,128]{1,0:T(8,128)(2,1)S(1)}, u32[]{:S(2)}, u32[]{:S(2)}) collective-permute-start(bf16[256,128]{1,0:T(8,128)(2,1)S(1)} %get-tuple-element.26), channel_id=1, source_target_pairs={{0,14},{1,11},{2,12},{3,9},{4,10},{5,15},{6,8},{7,13},{8,6},{9,3},... | collective-permute-start | bytes 196616 | tf_op jit(solution)/shard_map/ppermute | solution.py:610
  30.4 6.2 %collective-permute-start.12 = (bf16[256,128]{1,0:T(8,128)(2,1)S(1)}, bf16[256,128]{1,0:T(8,128)(2,1)S(1)}, u32[]{:S(2)}, u32[]{:S(2)}) collective-permute-start(bf16[256,128]{1,0:T(8,128)(2,1)S(1)} %get-tuple-element.27), channel_id=1, source_target_pairs={{0,12},{1,9},{2,14},{3,11},{4,8},{5,13},{6,10},{7,15},{8,4},{9,1},... | collective-permute-start | bytes 196616 | tf_op jit(solution)/shard_map/ppermute | solution.py:610
  31.9 4.7 %collective-permute-start.13 = (bf16[256,128]{1,0:T(8,128)(2,1)S(1)}, bf16[256,128]{1,0:T(8,128)(2,1)S(1)}, u32[]{:S(2)}, u32[]{:S(2)}) collective-permute-start(bf16[256,128]{1,0:T(8,128)(2,1)S(1)} %get-tuple-element.28), channel_id=1, source_target_pairs={{0,2},{1,7},{2,0},{3,5},{4,6},{5,3},{6,4},{7,1},{8,10},{9,15},{10,... | collective-permute-start | bytes 196616 | tf_op jit(solution)/shard_map/ppermute | solution.py:610
  32.8 3.7 %collective-permute-start.14 = (bf16[256,128]{1,0:T(8,128)(2,1)S(1)}, bf16[256,128]{1,0:T(8,128)(2,1)S(1)}, u32[]{:S(2)}, u32[]{:S(2)}) collective-permute-start(bf16[256,128]{1,0:T(8,128)(2,1)S(1)} %get-tuple-element.29), channel_id=1, source_target_pairs={{0,0},{1,5},{2,2},{3,7},{4,4},{5,1},{6,6},{7,3},{8,8},{9,13},{10,1... | collective-permute-start | bytes 196616 | tf_op jit(solution)/shard_map/ppermute | solution.py:610
  36.6 1.5 %collective-permute-start.15 = (bf16[4,128,128]{2,1,0:T(8,128)(2,1)S(1)}, bf16[4,128,128]{2,1,0:T(8,128)(2,1)S(1)}, u32[]{:S(2)}, u32[]{:S(2)}) collective-permute-start(bf16[4,128,128]{2,1,0:T(8,128)(2,1)S(1)} %shard_map.181), channel_id=1, source_target_pairs={{0,1},{1,0},{2,3},{3,2},{4,5},{5,4},{6,7},{7,6},{8,9},{9,8},{10,11... | collective-permute-start | bytes 393224 | tf_op jit(solution)/shard_map/ppermute | solution.py:533

commit v17 on v15

--- a/solution.py
+++ b/solution.py
@@ -291,7 +291,7 @@
 
 def step_order(chips):
     far, near = list(range(chips - 1, chips // 2 - 1, -1)), list(range(1, chips // 2))
-    return [0] + far[:1] + near[:1] + far[1:2] + near[1:] + far[2:]
+    return [0] + far[:2] + near + far[2:]
 
 
 def by_step(items):

time: 38.4 us -> 38.3 us (level)
  waiting for transfers between devices: 9.28 us -> 7.91 us
  starting transfers between devices: 23.2 us -> 24.4 us
    ppermute x12, starting transfers between devices: 17.2 us -> 18.4 us  [swap(): return lax.ppermute(piece, 'seq', [(i, i ^ step) for i in range(n)])]
    ppermute x12, waiting for transfers between devices: 6.54 us -> 5.32 us  [swap(): return lax.ppermute(piece, 'seq', [(i, i ^ step) for i in range(n)])]
where the time goes in v17:
time: 38.3 us; the launch traced here: 38.1 us
  starting transfers between devices  24.4 us (64%)
  waiting for transfers between devices  7.91 us (21%)
  Pallas kernels  3.08 us (8%)
  between operations  2.7 us (7%)
    ppermute x12, starting transfers between devices, swap(): return lax.ppermute(piece, 'seq', [(i, i ^ step) for i in range(n)])  18.4 us
    ppermute x4, starting transfers between devices, shards_packed(): lax.ppermute(piece, 'seq', [(i, i ^ 2 * pair[i % 2]) for i in range(n)])  6 us
    ppermute x12, waiting for transfers between devices, swap(): return lax.ppermute(piece, 'seq', [(i, i ^ step) for i in range(n)])  5.32 us
    ppermute x4, waiting for transfers between devices, shards_packed(): lax.ppermute(piece, 'seq', [(i, i ^ 2 * pair[i % 2]) for i in range(n)])  2.59 us
    pallas_call x1, Pallas kernels, shards_packed(): pl.pallas_call(functools.partial(pack_kernel, chips), out_shape=[pltpu.VM...  1.31 us
    pallas_call x1, Pallas kernels, shards_packed(): pl.pallas_call(functools.partial(attend_kernel, chips, rows, parts, pairs...  0.95 us
  transfers between devices with their start and end apart: 16, of which 6 were waited for; matrix products, arithmetic and copies ran while one was open for 0% of the time, Pallas kernels for 0%

profile of v17, /device:TPU:0, one launch (start us, length us, event | category | flops | bytes accessed | tf_op | source)
XLA Modules:
  0.0 38.1 jit_solution(11036847312247160187)
XLA Ops:
  0.6 1.3 %shard_map.174 = (bf16[384,128]{1,0:T(8,128)(2,1)S(1)}, bf16[384,128]{1,0:T(8,128)(2,1)S(1)}, bf16[384,128]{1,0:T(8,128)(2,1)S(1)}, bf16[384,128]{1,0:T(8,128)(2...) custom-call(bf16[16,4096]{1,0:T(8,128)(2,1)} %refs_0_.1, ...), custom_call_target="tpu_custom_call" | custom-call | tf_op jit(solution)/shard_map/pallas_call | solution.py:564
  1.9 6.1 %collective-permute-start = (bf16[384,128]{1,0:T(8,128)(2,1)S(1)}, bf16[384,128]{1,0:T(8,128)(2,1)S(1)}, u32[]{:S(2)}, u32[]{:S(2)}) collective-permute-start(bf16[384,128]{1,0:T(8,128)(2,1)S(1)} %get-tuple-element.19), channel_id=1, source_target_pairs={{0,14},{1,15},{2,12},{3,13},{4,10},{5,11},{6,8},{7,9},{8,6},{9,7},... | collective-permute-start | bytes 294920 | tf_op jit(solution)/shard_map/ppermute | solution.py:534
  8.0 0.2 collective-permute-start.1
  8.2 0.4 %collective-permute-start.2 = (bf16[384,128]{1,0:T(8,128)(2,1)S(1)}, bf16[384,128]{1,0:T(8,128)(2,1)S(1)}, u32[]{:S(2)}, u32[]{:S(2)}) collective-permute-start(bf16[384,128]{1,0:T(8,128)(2,1)S(1)} %get-tuple-element.22), channel_id=1, source_target_pairs={{0,2},{1,3},{2,0},{3,1},{4,6},{5,7},{6,4},{7,5},{8,10},{9,11},{10,... | collective-permute-start | bytes 294920 | tf_op jit(solution)/shard_map/ppermute | solution.py:534
  8.7 0.0 collective-permute-start.3
  8.7 3.1 %collective-permute-start.4 = (bf16[384,128]{1,0:T(8,128)(2,1)S(1)}, bf16[384,128]{1,0:T(8,128)(2,1)S(1)}, u32[]{:S(2)}, u32[]{:S(2)}) collective-permute-start(bf16[384,128]{1,0:T(8,128)(2,1)S(1)} %get-tuple-element.24), channel_id=1, source_target_pairs={{0,6},{1,7},{2,4},{3,5},{4,2},{5,3},{6,0},{7,1},{8,14},{9,15},{10,... | collective-permute-start | bytes 294920 | tf_op jit(solution)/shard_map/ppermute | solution.py:534
  11.7 0.0 collective-permute-done.refs_1_
  11.7 6.0 %collective-permute-start.5 = (bf16[384,128]{1,0:T(8,128)(2,1)S(1)}, bf16[384,128]{1,0:T(8,128)(2,1)S(1)}, u32[]{:S(2)}, u32[]{:S(2)}) collective-permute-start(bf16[384,128]{1,0:T(8,128)(2,1)S(1)} %get-tuple-element.25), channel_id=1, source_target_pairs={{0,10},{1,11},{2,8},{3,9},{4,14},{5,15},{6,12},{7,13},{8,2},{9,3},... | collective-permute-start | bytes 294920 | tf_op jit(solution)/shard_map/ppermute | solution.py:534
  17.8 0.0 collective-permute-done.1.refs_0_.refs_2_
  17.8 1.3 %collective-permute-start.6 = (bf16[384,128]{1,0:T(8,128)(2,1)S(1)}, bf16[384,128]{1,0:T(8,128)(2,1)S(1)}, u32[]{:S(2)}, u32[]{:S(2)}) collective-permute-start(bf16[384,128]{1,0:T(8,128)(2,1)S(1)} %get-tuple-element.26), channel_id=1, source_target_pairs={{0,8},{1,9},{2,10},{3,11},{4,12},{5,13},{6,14},{7,15},{8,0},{9,1},... | collective-permute-start | bytes 294920 | tf_op jit(solution)/shard_map/ppermute | solution.py:534
  21.0 0.0 collective-permute-done.2.refs_1_.refs_3_
  21.0 0.1 collective-permute-start.7
  21.1 0.0 collective-permute-done.3.refs_0_.refs_4_
  21.1 0.6 %collective-permute-start.8 = (bf16[2,384,128]{2,1,0:T(8,128)(2,1)S(1)}, bf16[2,384,128]{2,1,0:T(8,128)(2,1)S(1)}, u32[]{:S(2)}, u32[]{:S(2)}) collective-permute-start(bf16[2,384,128]{2,1,0:T(8,128)(2,1)S(1)} %shard_map.176), channel_id=1, source_target_pairs={{0,1},{1,0},{2,3},{3,2},{4,5},{5,4},{6,7},{7,6},{8,9},{9,8},{10,11... | collective-permute-start | bytes 589832 | tf_op jit(solution)/shard_map/ppermute | solution.py:534
  21.7 0.0 collective-permute-done.4.refs_1_.refs_5_
  21.7 0.1 collective-permute-start.9
  21.8 1.9 %collective-permute-done.5.refs_0_.refs_6_ = bf16[384,128]{1,0:T(8,128)(2,1)S(1)} collective-permute-done((bf16[384,128]{1,0:T(8,128)(2,1)S(1)}, bf16[384,128]{1,0:T(8,128)(2,1)S(1)}, u32[]{:S(2)}, u32[]{:S(2)}) %collective-permute-start.5) | collective-permute-done | bytes 98336 | tf_op jit(solution)/shard_map/ppermute | solution.py:534
  23.7 1.0 %collective-permute-done.6.refs_1_.refs_7_ = bf16[384,128]{1,0:T(8,128)(2,1)S(1)} collective-permute-done((bf16[384,128]{1,0:T(8,128)(2,1)S(1)}, bf16[384,128]{1,0:T(8,128)(2,1)S(1)}, u32[]{:S(2)}, u32[]{:S(2)}) %collective-permute-start.6) | collective-permute-done | bytes 98336 | tf_op jit(solution)/shard_map/ppermute | solution.py:534
  24.7 0.1 collective-permute-start.10
  24.8 0.0 collective-permute-done.7.refs_8_
  24.8 0.0 collective-permute-done.8.refs_9_
  24.8 0.0 collective-permute-done.9.refs_10_
  24.8 1.4 %collective-permute-done.10.refs_11_ = bf16[2,384,128]{2,1,0:T(8,128)(2,1)S(1)} collective-permute-done((bf16[2,384,128]{2,1,0:T(8,128)(2,1)S(1)}, bf16[2,384,128]{2,1,0:T(8,128)(2,1)S(1)}, u32[]{:S(2)}, u32[]{:S(2)}) %collective-permute-start.10) | collective-permute-done | bytes 196640 | tf_op jit(solution)/shard_map/ppermute | solution.py:534
  26.2 0.9 %shard_map.179 = (bf16[256,128]{1,0:T(8,128)(2,1)S(1)}, bf16[256,128]{1,0:T(8,128)(2,1)S(1)}, bf16[256,128]{1,0:T(8,128)(2,1)S(1)}, bf16[256,128]{1,0:T(8,128)(2,1)S(1)}) custom-call(s32[8,128]{1,0:T(8,128)S(1)} %get-tuple-element.20.bounds, bf16[384,128]{1,0:T(8,128)(2,1)S(1)} %get-tuple-element.18.refs_0_, ...), custom_call_target="tpu_custom_call" | custom-call | tf_op jit(solution)/shard_map/pallas_call | solution.py:595
  27.2 2.5 %collective-permute-start.11 = (bf16[256,128]{1,0:T(8,128)(2,1)S(1)}, bf16[256,128]{1,0:T(8,128)(2,1)S(1)}, u32[]{:S(2)}, u32[]{:S(2)}) collective-permute-start(bf16[256,128]{1,0:T(8,128)(2,1)S(1)} %get-tuple-element.28), channel_id=1, source_target_pairs={{0,14},{1,11},{2,12},{3,9},{4,10},{5,15},{6,8},{7,13},{8,6},{9,3},... | collective-permute-start | bytes 196616 | tf_op jit(solution)/shard_map/ppermute | solution.py:603
  29.7 1.5 %collective-permute-start.12 = (bf16[256,128]{1,0:T(8,128)(2,1)S(1)}, bf16[256,128]{1,0:T(8,128)(2,1)S(1)}, u32[]{:S(2)}, u32[]{:S(2)}) collective-permute-start(bf16[256,128]{1,0:T(8,128)(2,1)S(1)} %get-tuple-element.29), channel_id=1, source_target_pairs={{0,12},{1,9},{2,14},{3,11},{4,8},{5,13},{6,10},{7,15},{8,4},{9,1},... | collective-permute-start | bytes 196616 | tf_op jit(solution)/shard_map/ppermute | solution.py:603
  31.1 1.4 %collective-permute-start.13 = (bf16[256,128]{1,0:T(8,128)(2,1)S(1)}, bf16[256,128]{1,0:T(8,128)(2,1)S(1)}, u32[]{:S(2)}, u32[]{:S(2)}) collective-permute-start(bf16[256,128]{1,0:T(8,128)(2,1)S(1)} %get-tuple-element.30), channel_id=1, source_target_pairs={{0,2},{1,7},{2,0},{3,5},{4,6},{5,3},{6,4},{7,1},{8,10},{9,15},{10,... | collective-permute-start | bytes 196616 | tf_op jit(solution)/shard_map/ppermute | solution.py:603
  32.5 0.7 %collective-permute-start.14 = (bf16[256,128]{1,0:T(8,128)(2,1)S(1)}, bf16[256,128]{1,0:T(8,128)(2,1)S(1)}, u32[]{:S(2)}, u32[]{:S(2)}) collective-permute-start(bf16[256,128]{1,0:T(8,128)(2,1)S(1)} %get-tuple-element.31), channel_id=1, source_target_pairs={{0,0},{1,5},{2,2},{3,7},{4,4},{5,1},{6,6},{7,3},{8,8},{9,13},{10,1... | collective-permute-start | bytes 196616 | tf_op jit(solution)/shard_map/ppermute | solution.py:603
  33.2 1.4 %collective-permute-done.11.refs_0_ = bf16[256,128]{1,0:T(8,128)(2,1)S(1)} collective-permute-done((bf16[256,128]{1,0:T(8,128)(2,1)S(1)}, bf16[256,128]{1,0:T(8,128)(2,1)S(1)}, u32[]{:S(2)}, u32[]{:S(2)}) %collective-permute-start.11) | collective-permute-done | bytes 65568 | tf_op jit(solution)/shard_map/ppermute | solution.py:603
  34.6 1.2 %collective-permute-done.12.refs_1_ = bf16[256,128]{1,0:T(8,128)(2,1)S(1)} collective-permute-done((bf16[256,128]{1,0:T(8,128)(2,1)S(1)}, bf16[256,128]{1,0:T(8,128)(2,1)S(1)}, u32[]{:S(2)}, u32[]{:S(2)}) %collective-permute-start.12) | collective-permute-done | bytes 65568 | tf_op jit(solution)/shard_map/ppermute | solution.py:603
  35.8 0.0 collective-permute-done.13.refs_2_
  35.8 0.0 collective-permute-done.14.refs_3_
  35.8 0.5 %collective-permute-start.15 = (bf16[4,128,128]{2,1,0:T(8,128)(2,1)S(1)}, bf16[4,128,128]{2,1,0:T(8,128)(2,1)S(1)}, u32[]{:S(2)}, u32[]{:S(2)}) collective-permute-start(bf16[4,128,128]{2,1,0:T(8,128)(2,1)S(1)} %shard_map.180), channel_id=1, source_target_pairs={{0,1},{1,0},{2,3},{3,2},{4,5},{5,4},{6,7},{7,6},{8,9},{9,8},{10,11... | collective-permute-start | bytes 393224 | tf_op jit(solution)/shard_map/ppermute | solution.py:534
  36.3 1.0 %collective-permute-done.15.refs_4_ = bf16[4,128,128]{2,1,0:T(8,128)(2,1)S(1)} collective-permute-done((bf16[4,128,128]{2,1,0:T(8,128)(2,1)S(1)}, bf16[4,128,128]{2,1,0:T(8,128)(2,1)S(1)}, u32[]{:S(2)}, u32[]{:S(2)}) %collective-permute-start.15) | collective-permute-done | bytes 131104 | tf_op jit(solution)/shard_map/ppermute | solution.py:534
  37.3 0.8 %shard_map.181 = (bf16[16,4096]{1,0:T(8,128)(2,1)}, bf16[8,2048]{1,0:T(8,128)(2,1)}, bf16[16,2048]{1,0:T(8,128)(2,1)}, bf16[8,2048]{1,0:T(8,128)(2,1)}) custom-call(bf16[256,128]{1,0:T(8,128)(2,1)S(1)} %collective-permute-done.11.refs_0_, bf16[256,128]{1,0:T(8,128)(2,1)S(1)} %collective-permute-done.12.refs_1_, ...), custom_call_target="tpu_custom_call" | custom-call | tf_op jit(solution)/shard_map/pallas_call | solution.py:613
  (5 shorter events, 0.1 us)
Async XLA Ops:
  1.9 9.8 %collective-permute-start = (bf16[384,128]{1,0:T(8,128)(2,1)S(1)}, bf16[384,128]{1,0:T(8,128)(2,1)S(1)}, u32[]{:S(2)}, u32[]{:S(2)}) collective-permute-start(bf16[384,128]{1,0:T(8,128)(2,1)S(1)} %get-tuple-element.19), channel_id=1, source_target_pairs={{0,14},{1,15},{2,12},{3,13},{4,10},{5,11},{6,8},{7,9},{8,6},{9,7},... | collective-permute-start | bytes 294920 | tf_op jit(solution)/shard_map/ppermute | solution.py:534
  8.0 9.7 %collective-permute-start.1 = (bf16[384,128]{1,0:T(8,128)(2,1)S(1)}, bf16[384,128]{1,0:T(8,128)(2,1)S(1)}, u32[]{:S(2)}, u32[]{:S(2)}) collective-permute-start(bf16[384,128]{1,0:T(8,128)(2,1)S(1)} %get-tuple-element.21), channel_id=1, source_target_pairs={{0,12},{1,13},{2,14},{3,15},{4,8},{5,9},{6,10},{7,11},{8,4},{9,5},... | collective-permute-start | bytes 294920 | tf_op jit(solution)/shard_map/ppermute | solution.py:534
  8.2 12.8 %collective-permute-start.2 = (bf16[384,128]{1,0:T(8,128)(2,1)S(1)}, bf16[384,128]{1,0:T(8,128)(2,1)S(1)}, u32[]{:S(2)}, u32[]{:S(2)}) collective-permute-start(bf16[384,128]{1,0:T(8,128)(2,1)S(1)} %get-tuple-element.22), channel_id=1, source_target_pairs={{0,2},{1,3},{2,0},{3,1},{4,6},{5,7},{6,4},{7,5},{8,10},{9,11},{10,... | collective-permute-start | bytes 294920 | tf_op jit(solution)/shard_map/ppermute | solution.py:534
  8.7 12.5 %collective-permute-start.3 = (bf16[384,128]{1,0:T(8,128)(2,1)S(1)}, bf16[384,128]{1,0:T(8,128)(2,1)S(1)}, u32[]{:S(2)}, u32[]{:S(2)}) collective-permute-start(bf16[384,128]{1,0:T(8,128)(2,1)S(1)} %get-tuple-element.23), channel_id=1, source_target_pairs={{0,4},{1,5},{2,6},{3,7},{4,0},{5,1},{6,2},{7,3},{8,12},{9,13},{10,... | collective-permute-start | bytes 294920 | tf_op jit(solution)/shard_map/ppermute | solution.py:534
  8.7 13.0 %collective-permute-start.4 = (bf16[384,128]{1,0:T(8,128)(2,1)S(1)}, bf16[384,128]{1,0:T(8,128)(2,1)S(1)}, u32[]{:S(2)}, u32[]{:S(2)}) collective-permute-start(bf16[384,128]{1,0:T(8,128)(2,1)S(1)} %get-tuple-element.24), channel_id=1, source_target_pairs={{0,6},{1,7},{2,4},{3,5},{4,2},{5,3},{6,0},{7,1},{8,14},{9,15},{10,... | collective-permute-start | bytes 294920 | tf_op jit(solution)/shard_map/ppermute | solution.py:534
  11.7 12.0 %collective-permute-start.5 = (bf16[384,128]{1,0:T(8,128)(2,1)S(1)}, bf16[384,128]{1,0:T(8,128)(2,1)S(1)}, u32[]{:S(2)}, u32[]{:S(2)}) collective-permute-start(bf16[384,128]{1,0:T(8,128)(2,1)S(1)} %get-tuple-element.25), channel_id=1, source_target_pairs={{0,10},{1,11},{2,8},{3,9},{4,14},{5,15},{6,12},{7,13},{8,2},{9,3},... | collective-permute-start | bytes 294920 | tf_op jit(solution)/shard_map/ppermute | solution.py:534
  17.8 7.0 %collective-permute-start.6 = (bf16[384,128]{1,0:T(8,128)(2,1)S(1)}, bf16[384,128]{1,0:T(8,128)(2,1)S(1)}, u32[]{:S(2)}, u32[]{:S(2)}) collective-permute-start(bf16[384,128]{1,0:T(8,128)(2,1)S(1)} %get-tuple-element.26), channel_id=1, source_target_pairs={{0,8},{1,9},{2,10},{3,11},{4,12},{5,13},{6,14},{7,15},{8,0},{9,1},... | collective-permute-start | bytes 294920 | tf_op jit(solution)/shard_map/ppermute | solution.py:534
  21.0 3.8 %collective-permute-start.7 = (bf16[2,384,128]{2,1,0:T(8,128)(2,1)S(1)}, bf16[2,384,128]{2,1,0:T(8,128)(2,1)S(1)}, u32[]{:S(2)}, u32[]{:S(2)}) collective-permute-start(bf16[2,384,128]{2,1,0:T(8,128)(2,1)S(1)} %get-tuple-element.27), channel_id=1, source_target_pairs={{0,1},{1,0},{2,3},{3,2},{4,5},{5,4},{6,7},{7,6},{8,9},{9,8},{10,11... | collective-permute-start | bytes 589832 | tf_op jit(solution)/shard_map/ppermute | solution.py:534
  21.1 3.7 %collective-permute-start.8 = (bf16[2,384,128]{2,1,0:T(8,128)(2,1)S(1)}, bf16[2,384,128]{2,1,0:T(8,128)(2,1)S(1)}, u32[]{:S(2)}, u32[]{:S(2)}) collective-permute-start(bf16[2,384,128]{2,1,0:T(8,128)(2,1)S(1)} %shard_map.176), channel_id=1, source_target_pairs={{0,1},{1,0},{2,3},{3,2},{4,5},{5,4},{6,7},{7,6},{8,9},{9,8},{10,11... | collective-permute-start | bytes 589832 | tf_op jit(solution)/shard_map/ppermute | solution.py:534
  21.7 3.1 %collective-permute-start.9 = (bf16[2,384,128]{2,1,0:T(8,128)(2,1)S(1)}, bf16[2,384,128]{2,1,0:T(8,128)(2,1)S(1)}, u32[]{:S(2)}, u32[]{:S(2)}) collective-permute-start(bf16[2,384,128]{2,1,0:T(8,128)(2,1)S(1)} %shard_map.177), channel_id=1, source_target_pairs={{0,1},{1,0},{2,3},{3,2},{4,5},{5,4},{6,7},{7,6},{8,9},{9,8},{10,11... | collective-permute-start | bytes 589832 | tf_op jit(solution)/shard_map/ppermute | solution.py:534
  24.7 1.5 %collective-permute-start.10 = (bf16[2,384,128]{2,1,0:T(8,128)(2,1)S(1)}, bf16[2,384,128]{2,1,0:T(8,128)(2,1)S(1)}, u32[]{:S(2)}, u32[]{:S(2)}) collective-permute-start(bf16[2,384,128]{2,1,0:T(8,128)(2,1)S(1)} %shard_map.178), channel_id=1, source_target_pairs={{0,1},{1,0},{2,3},{3,2},{4,5},{5,4},{6,7},{7,6},{8,9},{9,8},{10,11... | collective-permute-start | bytes 589832 | tf_op jit(solution)/shard_map/ppermute | solution.py:534
  27.2 7.4 %collective-permute-start.11 = (bf16[256,128]{1,0:T(8,128)(2,1)S(1)}, bf16[256,128]{1,0:T(8,128)(2,1)S(1)}, u32[]{:S(2)}, u32[]{:S(2)}) collective-permute-start(bf16[256,128]{1,0:T(8,128)(2,1)S(1)} %get-tuple-element.28), channel_id=1, source_target_pairs={{0,14},{1,11},{2,12},{3,9},{4,10},{5,15},{6,8},{7,13},{8,6},{9,3},... | collective-permute-start | bytes 196616 | tf_op jit(solution)/shard_map/ppermute | solution.py:603
  29.7 6.1 %collective-permute-start.12 = (bf16[256,128]{1,0:T(8,128)(2,1)S(1)}, bf16[256,128]{1,0:T(8,128)(2,1)S(1)}, u32[]{:S(2)}, u32[]{:S(2)}) collective-permute-start(bf16[256,128]{1,0:T(8,128)(2,1)S(1)} %get-tuple-element.29), channel_id=1, source_target_pairs={{0,12},{1,9},{2,14},{3,11},{4,8},{5,13},{6,10},{7,15},{8,4},{9,1},... | collective-permute-start | bytes 196616 | tf_op jit(solution)/shard_map/ppermute | solution.py:603
  31.1 4.6 %collective-permute-start.13 = (bf16[256,128]{1,0:T(8,128)(2,1)S(1)}, bf16[256,128]{1,0:T(8,128)(2,1)S(1)}, u32[]{:S(2)}, u32[]{:S(2)}) collective-permute-start(bf16[256,128]{1,0:T(8,128)(2,1)S(1)} %get-tuple-element.30), channel_id=1, source_target_pairs={{0,2},{1,7},{2,0},{3,5},{4,6},{5,3},{6,4},{7,1},{8,10},{9,15},{10,... | collective-permute-start | bytes 196616 | tf_op jit(solution)/shard_map/ppermute | solution.py:603
  32.5 3.3 %collective-permute-start.14 = (bf16[256,128]{1,0:T(8,128)(2,1)S(1)}, bf16[256,128]{1,0:T(8,128)(2,1)S(1)}, u32[]{:S(2)}, u32[]{:S(2)}) collective-permute-start(bf16[256,128]{1,0:T(8,128)(2,1)S(1)} %get-tuple-element.31), channel_id=1, source_target_pairs={{0,0},{1,5},{2,2},{3,7},{4,4},{5,1},{6,6},{7,3},{8,8},{9,13},{10,1... | collective-permute-start | bytes 196616 | tf_op jit(solution)/shard_map/ppermute | solution.py:603
  35.8 1.5 %collective-permute-start.15 = (bf16[4,128,128]{2,1,0:T(8,128)(2,1)S(1)}, bf16[4,128,128]{2,1,0:T(8,128)(2,1)S(1)}, u32[]{:S(2)}, u32[]{:S(2)}) collective-permute-start(bf16[4,128,128]{2,1,0:T(8,128)(2,1)S(1)} %shard_map.180), channel_id=1, source_target_pairs={{0,1},{1,0},{2,3},{3,2},{4,5},{5,4},{6,7},{7,6},{8,9},{9,8},{10,11... | collective-permute-start | bytes 393224 | tf_op jit(solution)/shard_map/ppermute | solution.py:534

commit v18 on v17

--- a/solution.py
+++ b/solution.py
@@ -447,8 +447,6 @@
         )
         for h in range(parts)
     ]
-    for h, mixed in enumerate(mix_all(units)):
-        put(h * rows, mixed)
 
     cross = 3 * parts * rows
     audio = cross + 3 * pairs * rows
@@ -460,7 +458,6 @@
     q_at, k_at = places(half, rows)
     center = jnp.clip((q_at - offset) << bits, 0, video_valid - 1)
     toward_audio = (k_at < video_valid) & (jnp.abs(k_at - center) <= tv // 8)
-    units = []
     for p in range(pairs):
         at = cross + p * rows
         cross_query = asked(at)
@@ -478,6 +475,9 @@
         units += pair_units(audio_query, audio_keys, audio_values, within_audio)
         units += pair_units(listen_query, cross_keys, cross_values, toward_audio)
     mixed = mix_all(units)
+    for h in range(parts):
+        put(h * rows, mixed[h])
+    mixed = mixed[parts:]
     heads = LANES // HDA
     for p in range(pairs):
         seen, heard, listened = (

time: 38.3 us -> 38.1 us (level)
  no operation moved by 1% of the time
where the time goes in v18:
time: 38.1 us; the launch traced here: 37.9 us
  starting transfers between devices  24.4 us (64%)
  waiting for transfers between devices  7.9 us (21%)
  Pallas kernels  2.91 us (8%)
  between operations  2.7 us (7%)
    ppermute x12, starting transfers between devices, swap(): return lax.ppermute(piece, 'seq', [(i, i ^ step) for i in range(n)])  18.4 us
    ppermute x4, starting transfers between devices, shards_packed(): lax.ppermute(piece, 'seq', [(i, i ^ 2 * pair[i % 2]) for i in range(n)])  6 us
    ppermute x12, waiting for transfers between devices, swap(): return lax.ppermute(piece, 'seq', [(i, i ^ step) for i in range(n)])  5.32 us
    ppermute x4, waiting for transfers between devices, shards_packed(): lax.ppermute(piece, 'seq', [(i, i ^ 2 * pair[i % 2]) for i in range(n)])  2.59 us
    pallas_call x1, Pallas kernels, shards_packed(): pl.pallas_call(functools.partial(pack_kernel, chips), out_shape=[pltpu.VM...  1.31 us
    pallas_call x1, Pallas kernels, shards_packed(): pl.pallas_call(functools.partial(attend_kernel, chips, rows, parts, pairs...  0.79 us
  transfers between devices with their start and end apart: 16, of which 6 were waited for; matrix products, arithmetic and copies ran while one was open for 0% of the time, Pallas kernels for 0%

profile of v18, /device:TPU:0, one launch (start us, length us, event | category | flops | bytes accessed | tf_op | source)
XLA Modules:
  0.0 37.9 jit_solution(9162097174132485136)
XLA Ops:
  0.6 1.3 %shard_map.174 = (bf16[384,128]{1,0:T(8,128)(2,1)S(1)}, bf16[384,128]{1,0:T(8,128)(2,1)S(1)}, bf16[384,128]{1,0:T(8,128)(2,1)S(1)}, bf16[384,128]{1,0:T(8,128)(2...) custom-call(bf16[16,4096]{1,0:T(8,128)(2,1)} %refs_0_.1, ...), custom_call_target="tpu_custom_call" | custom-call | tf_op jit(solution)/shard_map/pallas_call | solution.py:564
  1.9 6.1 %collective-permute-start = (bf16[384,128]{1,0:T(8,128)(2,1)S(1)}, bf16[384,128]{1,0:T(8,128)(2,1)S(1)}, u32[]{:S(2)}, u32[]{:S(2)}) collective-permute-start(bf16[384,128]{1,0:T(8,128)(2,1)S(1)} %get-tuple-element.19), channel_id=1, source_target_pairs={{0,14},{1,15},{2,12},{3,13},{4,10},{5,11},{6,8},{7,9},{8,6},{9,7},... | collective-permute-start | bytes 294920 | tf_op jit(solution)/shard_map/ppermute | solution.py:534
  8.0 0.2 collective-permute-start.1
  8.2 0.4 %collective-permute-start.2 = (bf16[384,128]{1,0:T(8,128)(2,1)S(1)}, bf16[384,128]{1,0:T(8,128)(2,1)S(1)}, u32[]{:S(2)}, u32[]{:S(2)}) collective-permute-start(bf16[384,128]{1,0:T(8,128)(2,1)S(1)} %get-tuple-element.22), channel_id=1, source_target_pairs={{0,2},{1,3},{2,0},{3,1},{4,6},{5,7},{6,4},{7,5},{8,10},{9,11},{10,... | collective-permute-start | bytes 294920 | tf_op jit(solution)/shard_map/ppermute | solution.py:534
  8.7 0.0 collective-permute-start.3
  8.7 3.1 %collective-permute-start.4 = (bf16[384,128]{1,0:T(8,128)(2,1)S(1)}, bf16[384,128]{1,0:T(8,128)(2,1)S(1)}, u32[]{:S(2)}, u32[]{:S(2)}) collective-permute-start(bf16[384,128]{1,0:T(8,128)(2,1)S(1)} %get-tuple-element.24), channel_id=1, source_target_pairs={{0,6},{1,7},{2,4},{3,5},{4,2},{5,3},{6,0},{7,1},{8,14},{9,15},{10,... | collective-permute-start | bytes 294920 | tf_op jit(solution)/shard_map/ppermute | solution.py:534
  11.7 0.0 collective-permute-done.refs_1_
  11.7 6.0 %collective-permute-start.5 = (bf16[384,128]{1,0:T(8,128)(2,1)S(1)}, bf16[384,128]{1,0:T(8,128)(2,1)S(1)}, u32[]{:S(2)}, u32[]{:S(2)}) collective-permute-start(bf16[384,128]{1,0:T(8,128)(2,1)S(1)} %get-tuple-element.25), channel_id=1, source_target_pairs={{0,10},{1,11},{2,8},{3,9},{4,14},{5,15},{6,12},{7,13},{8,2},{9,3},... | collective-permute-start | bytes 294920 | tf_op jit(solution)/shard_map/ppermute | solution.py:534
  17.8 0.0 collective-permute-done.1.refs_0_.refs_2_
  17.8 1.3 %collective-permute-start.6 = (bf16[384,128]{1,0:T(8,128)(2,1)S(1)}, bf16[384,128]{1,0:T(8,128)(2,1)S(1)}, u32[]{:S(2)}, u32[]{:S(2)}) collective-permute-start(bf16[384,128]{1,0:T(8,128)(2,1)S(1)} %get-tuple-element.26), channel_id=1, source_target_pairs={{0,8},{1,9},{2,10},{3,11},{4,12},{5,13},{6,14},{7,15},{8,0},{9,1},... | collective-permute-start | bytes 294920 | tf_op jit(solution)/shard_map/ppermute | solution.py:534
  21.0 0.0 collective-permute-done.2.refs_1_.refs_3_
  21.0 0.1 collective-permute-start.7
  21.1 0.0 collective-permute-done.3.refs_0_.refs_4_
  21.1 0.6 %collective-permute-start.8 = (bf16[2,384,128]{2,1,0:T(8,128)(2,1)S(1)}, bf16[2,384,128]{2,1,0:T(8,128)(2,1)S(1)}, u32[]{:S(2)}, u32[]{:S(2)}) collective-permute-start(bf16[2,384,128]{2,1,0:T(8,128)(2,1)S(1)} %shard_map.176), channel_id=1, source_target_pairs={{0,1},{1,0},{2,3},{3,2},{4,5},{5,4},{6,7},{7,6},{8,9},{9,8},{10,11... | collective-permute-start | bytes 589832 | tf_op jit(solution)/shard_map/ppermute | solution.py:534
  21.7 0.0 collective-permute-done.4.refs_1_.refs_5_
  21.7 0.1 collective-permute-start.9
  21.8 1.9 %collective-permute-done.5.refs_0_.refs_6_ = bf16[384,128]{1,0:T(8,128)(2,1)S(1)} collective-permute-done((bf16[384,128]{1,0:T(8,128)(2,1)S(1)}, bf16[384,128]{1,0:T(8,128)(2,1)S(1)}, u32[]{:S(2)}, u32[]{:S(2)}) %collective-permute-start.5) | collective-permute-done | bytes 98336 | tf_op jit(solution)/shard_map/ppermute | solution.py:534
  23.7 1.0 %collective-permute-done.6.refs_1_.refs_7_ = bf16[384,128]{1,0:T(8,128)(2,1)S(1)} collective-permute-done((bf16[384,128]{1,0:T(8,128)(2,1)S(1)}, bf16[384,128]{1,0:T(8,128)(2,1)S(1)}, u32[]{:S(2)}, u32[]{:S(2)}) %collective-permute-start.6) | collective-permute-done | bytes 98336 | tf_op jit(solution)/shard_map/ppermute | solution.py:534
  24.7 0.1 collective-permute-start.10
  24.8 0.0 collective-permute-done.7.refs_8_
  24.8 0.0 collective-permute-done.8.refs_9_
  24.8 0.0 collective-permute-done.9.refs_10_
  24.8 1.4 %collective-permute-done.10.refs_11_ = bf16[2,384,128]{2,1,0:T(8,128)(2,1)S(1)} collective-permute-done((bf16[2,384,128]{2,1,0:T(8,128)(2,1)S(1)}, bf16[2,384,128]{2,1,0:T(8,128)(2,1)S(1)}, u32[]{:S(2)}, u32[]{:S(2)}) %collective-permute-start.10) | collective-permute-done | bytes 196640 | tf_op jit(solution)/shard_map/ppermute | solution.py:534
  26.2 0.8 %shard_map.179 = (bf16[256,128]{1,0:T(8,128)(2,1)S(1)}, bf16[256,128]{1,0:T(8,128)(2,1)S(1)}, bf16[256,128]{1,0:T(8,128)(2,1)S(1)}, bf16[256,128]{1,0:T(8,128)(2,1)S(1)}) custom-call(s32[8,128]{1,0:T(8,128)S(1)} %get-tuple-element.20.bounds, bf16[384,128]{1,0:T(8,128)(2,1)S(1)} %get-tuple-element.18.refs_0_, ...), custom_call_target="tpu_custom_call" | custom-call | tf_op jit(solution)/shard_map/pallas_call | solution.py:595
  27.0 2.5 %collective-permute-start.11 = (bf16[256,128]{1,0:T(8,128)(2,1)S(1)}, bf16[256,128]{1,0:T(8,128)(2,1)S(1)}, u32[]{:S(2)}, u32[]{:S(2)}) collective-permute-start(bf16[256,128]{1,0:T(8,128)(2,1)S(1)} %get-tuple-element.28), channel_id=1, source_target_pairs={{0,14},{1,11},{2,12},{3,9},{4,10},{5,15},{6,8},{7,13},{8,6},{9,3},... | collective-permute-start | bytes 196616 | tf_op jit(solution)/shard_map/ppermute | solution.py:603
  29.5 1.5 %collective-permute-start.12 = (bf16[256,128]{1,0:T(8,128)(2,1)S(1)}, bf16[256,128]{1,0:T(8,128)(2,1)S(1)}, u32[]{:S(2)}, u32[]{:S(2)}) collective-permute-start(bf16[256,128]{1,0:T(8,128)(2,1)S(1)} %get-tuple-element.29), channel_id=1, source_target_pairs={{0,12},{1,9},{2,14},{3,11},{4,8},{5,13},{6,10},{7,15},{8,4},{9,1},... | collective-permute-start | bytes 196616 | tf_op jit(solution)/shard_map/ppermute | solution.py:603
  31.0 1.4 %collective-permute-start.13 = (bf16[256,128]{1,0:T(8,128)(2,1)S(1)}, bf16[256,128]{1,0:T(8,128)(2,1)S(1)}, u32[]{:S(2)}, u32[]{:S(2)}) collective-permute-start(bf16[256,128]{1,0:T(8,128)(2,1)S(1)} %get-tuple-element.30), channel_id=1, source_target_pairs={{0,2},{1,7},{2,0},{3,5},{4,6},{5,3},{6,4},{7,1},{8,10},{9,15},{10,... | collective-permute-start | bytes 196616 | tf_op jit(solution)/shard_map/ppermute | solution.py:603
  32.4 0.7 %collective-permute-start.14 = (bf16[256,128]{1,0:T(8,128)(2,1)S(1)}, bf16[256,128]{1,0:T(8,128)(2,1)S(1)}, u32[]{:S(2)}, u32[]{:S(2)}) collective-permute-start(bf16[256,128]{1,0:T(8,128)(2,1)S(1)} %get-tuple-element.31), channel_id=1, source_target_pairs={{0,0},{1,5},{2,2},{3,7},{4,4},{5,1},{6,6},{7,3},{8,8},{9,13},{10,1... | collective-permute-start | bytes 196616 | tf_op jit(solution)/shard_map/ppermute | solution.py:603
  33.0 1.4 %collective-permute-done.11.refs_0_ = bf16[256,128]{1,0:T(8,128)(2,1)S(1)} collective-permute-done((bf16[256,128]{1,0:T(8,128)(2,1)S(1)}, bf16[256,128]{1,0:T(8,128)(2,1)S(1)}, u32[]{:S(2)}, u32[]{:S(2)}) %collective-permute-start.11) | collective-permute-done | bytes 65568 | tf_op jit(solution)/shard_map/ppermute | solution.py:603
  34.5 1.2 %collective-permute-done.12.refs_1_ = bf16[256,128]{1,0:T(8,128)(2,1)S(1)} collective-permute-done((bf16[256,128]{1,0:T(8,128)(2,1)S(1)}, bf16[256,128]{1,0:T(8,128)(2,1)S(1)}, u32[]{:S(2)}, u32[]{:S(2)}) %collective-permute-start.12) | collective-permute-done | bytes 65568 | tf_op jit(solution)/shard_map/ppermute | solution.py:603
  35.6 0.0 collective-permute-done.13.refs_2_
  35.6 0.0 collective-permute-done.14.refs_3_
  35.6 0.5 %collective-permute-start.15 = (bf16[4,128,128]{2,1,0:T(8,128)(2,1)S(1)}, bf16[4,128,128]{2,1,0:T(8,128)(2,1)S(1)}, u32[]{:S(2)}, u32[]{:S(2)}) collective-permute-start(bf16[4,128,128]{2,1,0:T(8,128)(2,1)S(1)} %shard_map.180), channel_id=1, source_target_pairs={{0,1},{1,0},{2,3},{3,2},{4,5},{5,4},{6,7},{7,6},{8,9},{9,8},{10,11... | collective-permute-start | bytes 393224 | tf_op jit(solution)/shard_map/ppermute | solution.py:534
  36.2 1.0 %collective-permute-done.15.refs_4_ = bf16[4,128,128]{2,1,0:T(8,128)(2,1)S(1)} collective-permute-done((bf16[4,128,128]{2,1,0:T(8,128)(2,1)S(1)}, bf16[4,128,128]{2,1,0:T(8,128)(2,1)S(1)}, u32[]{:S(2)}, u32[]{:S(2)}) %collective-permute-start.15) | collective-permute-done | bytes 131104 | tf_op jit(solution)/shard_map/ppermute | solution.py:534
  37.2 0.8 %shard_map.181 = (bf16[16,4096]{1,0:T(8,128)(2,1)}, bf16[8,2048]{1,0:T(8,128)(2,1)}, bf16[16,2048]{1,0:T(8,128)(2,1)}, bf16[8,2048]{1,0:T(8,128)(2,1)}) custom-call(bf16[256,128]{1,0:T(8,128)(2,1)S(1)} %collective-permute-done.11.refs_0_, bf16[256,128]{1,0:T(8,128)(2,1)S(1)} %collective-permute-done.12.refs_1_, ...), custom_call_target="tpu_custom_call" | custom-call | tf_op jit(solution)/shard_map/pallas_call | solution.py:613
  (5 shorter events, 0.1 us)
Async XLA Ops:
  1.9 9.8 %collective-permute-start = (bf16[384,128]{1,0:T(8,128)(2,1)S(1)}, bf16[384,128]{1,0:T(8,128)(2,1)S(1)}, u32[]{:S(2)}, u32[]{:S(2)}) collective-permute-start(bf16[384,128]{1,0:T(8,128)(2,1)S(1)} %get-tuple-element.19), channel_id=1, source_target_pairs={{0,14},{1,15},{2,12},{3,13},{4,10},{5,11},{6,8},{7,9},{8,6},{9,7},... | collective-permute-start | bytes 294920 | tf_op jit(solution)/shard_map/ppermute | solution.py:534
  8.0 9.7 %collective-permute-start.1 = (bf16[384,128]{1,0:T(8,128)(2,1)S(1)}, bf16[384,128]{1,0:T(8,128)(2,1)S(1)}, u32[]{:S(2)}, u32[]{:S(2)}) collective-permute-start(bf16[384,128]{1,0:T(8,128)(2,1)S(1)} %get-tuple-element.21), channel_id=1, source_target_pairs={{0,12},{1,13},{2,14},{3,15},{4,8},{5,9},{6,10},{7,11},{8,4},{9,5},... | collective-permute-start | bytes 294920 | tf_op jit(solution)/shard_map/ppermute | solution.py:534
  8.2 12.8 %collective-permute-start.2 = (bf16[384,128]{1,0:T(8,128)(2,1)S(1)}, bf16[384,128]{1,0:T(8,128)(2,1)S(1)}, u32[]{:S(2)}, u32[]{:S(2)}) collective-permute-start(bf16[384,128]{1,0:T(8,128)(2,1)S(1)} %get-tuple-element.22), channel_id=1, source_target_pairs={{0,2},{1,3},{2,0},{3,1},{4,6},{5,7},{6,4},{7,5},{8,10},{9,11},{10,... | collective-permute-start | bytes 294920 | tf_op jit(solution)/shard_map/ppermute | solution.py:534
  8.7 12.5 %collective-permute-start.3 = (bf16[384,128]{1,0:T(8,128)(2,1)S(1)}, bf16[384,128]{1,0:T(8,128)(2,1)S(1)}, u32[]{:S(2)}, u32[]{:S(2)}) collective-permute-start(bf16[384,128]{1,0:T(8,128)(2,1)S(1)} %get-tuple-element.23), channel_id=1, source_target_pairs={{0,4},{1,5},{2,6},{3,7},{4,0},{5,1},{6,2},{7,3},{8,12},{9,13},{10,... | collective-permute-start | bytes 294920 | tf_op jit(solution)/shard_map/ppermute | solution.py:534
  8.7 13.0 %collective-permute-start.4 = (bf16[384,128]{1,0:T(8,128)(2,1)S(1)}, bf16[384,128]{1,0:T(8,128)(2,1)S(1)}, u32[]{:S(2)}, u32[]{:S(2)}) collective-permute-start(bf16[384,128]{1,0:T(8,128)(2,1)S(1)} %get-tuple-element.24), channel_id=1, source_target_pairs={{0,6},{1,7},{2,4},{3,5},{4,2},{5,3},{6,0},{7,1},{8,14},{9,15},{10,... | collective-permute-start | bytes 294920 | tf_op jit(solution)/shard_map/ppermute | solution.py:534
  11.7 12.0 %collective-permute-start.5 = (bf16[384,128]{1,0:T(8,128)(2,1)S(1)}, bf16[384,128]{1,0:T(8,128)(2,1)S(1)}, u32[]{:S(2)}, u32[]{:S(2)}) collective-permute-start(bf16[384,128]{1,0:T(8,128)(2,1)S(1)} %get-tuple-element.25), channel_id=1, source_target_pairs={{0,10},{1,11},{2,8},{3,9},{4,14},{5,15},{6,12},{7,13},{8,2},{9,3},... | collective-permute-start | bytes 294920 | tf_op jit(solution)/shard_map/ppermute | solution.py:534
  17.8 7.0 %collective-permute-start.6 = (bf16[384,128]{1,0:T(8,128)(2,1)S(1)}, bf16[384,128]{1,0:T(8,128)(2,1)S(1)}, u32[]{:S(2)}, u32[]{:S(2)}) collective-permute-start(bf16[384,128]{1,0:T(8,128)(2,1)S(1)} %get-tuple-element.26), channel_id=1, source_target_pairs={{0,8},{1,9},{2,10},{3,11},{4,12},{5,13},{6,14},{7,15},{8,0},{9,1},... | collective-permute-start | bytes 294920 | tf_op jit(solution)/shard_map/ppermute | solution.py:534
  21.0 3.8 %collective-permute-start.7 = (bf16[2,384,128]{2,1,0:T(8,128)(2,1)S(1)}, bf16[2,384,128]{2,1,0:T(8,128)(2,1)S(1)}, u32[]{:S(2)}, u32[]{:S(2)}) collective-permute-start(bf16[2,384,128]{2,1,0:T(8,128)(2,1)S(1)} %get-tuple-element.27), channel_id=1, source_target_pairs={{0,1},{1,0},{2,3},{3,2},{4,5},{5,4},{6,7},{7,6},{8,9},{9,8},{10,11... | collective-permute-start | bytes 589832 | tf_op jit(solution)/shard_map/ppermute | solution.py:534
  21.1 3.7 %collective-permute-start.8 = (bf16[2,384,128]{2,1,0:T(8,128)(2,1)S(1)}, bf16[2,384,128]{2,1,0:T(8,128)(2,1)S(1)}, u32[]{:S(2)}, u32[]{:S(2)}) collective-permute-start(bf16[2,384,128]{2,1,0:T(8,128)(2,1)S(1)} %shard_map.176), channel_id=1, source_target_pairs={{0,1},{1,0},{2,3},{3,2},{4,5},{5,4},{6,7},{7,6},{8,9},{9,8},{10,11... | collective-permute-start | bytes 589832 | tf_op jit(solution)/shard_map/ppermute | solution.py:534
  21.7 3.1 %collective-permute-start.9 = (bf16[2,384,128]{2,1,0:T(8,128)(2,1)S(1)}, bf16[2,384,128]{2,1,0:T(8,128)(2,1)S(1)}, u32[]{:S(2)}, u32[]{:S(2)}) collective-permute-start(bf16[2,384,128]{2,1,0:T(8,128)(2,1)S(1)} %shard_map.177), channel_id=1, source_target_pairs={{0,1},{1,0},{2,3},{3,2},{4,5},{5,4},{6,7},{7,6},{8,9},{9,8},{10,11... | collective-permute-start | bytes 589832 | tf_op jit(solution)/shard_map/ppermute | solution.py:534
  24.7 1.5 %collective-permute-start.10 = (bf16[2,384,128]{2,1,0:T(8,128)(2,1)S(1)}, bf16[2,384,128]{2,1,0:T(8,128)(2,1)S(1)}, u32[]{:S(2)}, u32[]{:S(2)}) collective-permute-start(bf16[2,384,128]{2,1,0:T(8,128)(2,1)S(1)} %shard_map.178), channel_id=1, source_target_pairs={{0,1},{1,0},{2,3},{3,2},{4,5},{5,4},{6,7},{7,6},{8,9},{9,8},{10,11... | collective-permute-start | bytes 589832 | tf_op jit(solution)/shard_map/ppermute | solution.py:534
  27.0 7.4 %collective-permute-start.11 = (bf16[256,128]{1,0:T(8,128)(2,1)S(1)}, bf16[256,128]{1,0:T(8,128)(2,1)S(1)}, u32[]{:S(2)}, u32[]{:S(2)}) collective-permute-start(bf16[256,128]{1,0:T(8,128)(2,1)S(1)} %get-tuple-element.28), channel_id=1, source_target_pairs={{0,14},{1,11},{2,12},{3,9},{4,10},{5,15},{6,8},{7,13},{8,6},{9,3},... | collective-permute-start | bytes 196616 | tf_op jit(solution)/shard_map/ppermute | solution.py:603
  29.5 6.1 %collective-permute-start.12 = (bf16[256,128]{1,0:T(8,128)(2,1)S(1)}, bf16[256,128]{1,0:T(8,128)(2,1)S(1)}, u32[]{:S(2)}, u32[]{:S(2)}) collective-permute-start(bf16[256,128]{1,0:T(8,128)(2,1)S(1)} %get-tuple-element.29), channel_id=1, source_target_pairs={{0,12},{1,9},{2,14},{3,11},{4,8},{5,13},{6,10},{7,15},{8,4},{9,1},... | collective-permute-start | bytes 196616 | tf_op jit(solution)/shard_map/ppermute | solution.py:603
  31.0 4.6 %collective-permute-start.13 = (bf16[256,128]{1,0:T(8,128)(2,1)S(1)}, bf16[256,128]{1,0:T(8,128)(2,1)S(1)}, u32[]{:S(2)}, u32[]{:S(2)}) collective-permute-start(bf16[256,128]{1,0:T(8,128)(2,1)S(1)} %get-tuple-element.30), channel_id=1, source_target_pairs={{0,2},{1,7},{2,0},{3,5},{4,6},{5,3},{6,4},{7,1},{8,10},{9,15},{10,... | collective-permute-start | bytes 196616 | tf_op jit(solution)/shard_map/ppermute | solution.py:603
  32.4 3.2 %collective-permute-start.14 = (bf16[256,128]{1,0:T(8,128)(2,1)S(1)}, bf16[256,128]{1,0:T(8,128)(2,1)S(1)}, u32[]{:S(2)}, u32[]{:S(2)}) collective-permute-start(bf16[256,128]{1,0:T(8,128)(2,1)S(1)} %get-tuple-element.31), channel_id=1, source_target_pairs={{0,0},{1,5},{2,2},{3,7},{4,4},{5,1},{6,6},{7,3},{8,8},{9,13},{10,1... | collective-permute-start | bytes 196616 | tf_op jit(solution)/shard_map/ppermute | solution.py:603
  35.6 1.5 %collective-permute-start.15 = (bf16[4,128,128]{2,1,0:T(8,128)(2,1)S(1)}, bf16[4,128,128]{2,1,0:T(8,128)(2,1)S(1)}, u32[]{:S(2)}, u32[]{:S(2)}) collective-permute-start(bf16[4,128,128]{2,1,0:T(8,128)(2,1)S(1)} %shard_map.180), channel_id=1, source_target_pairs={{0,1},{1,0},{2,3},{3,2},{4,5},{5,4},{6,7},{7,6},{8,9},{9,8},{10,11... | collective-permute-start | bytes 393224 | tf_op jit(solution)/shard_map/ppermute | solution.py:534

commit v19 on v18

--- a/solution.py
+++ b/solution.py
@@ -385,7 +385,7 @@
 def shares(chips):
     quarter = chips // 4
     far = list(zip(range(chips - 1, 3 * quarter - 1, -1), range(3 * quarter - 1, 2 * quarter - 1, -1)))
-    near = list(zip(range(quarter - 1, -1, -1), range(2 * quarter - 1, quarter - 1, -1)))
+    near = list(zip(range(quarter - 1, -1, -1), range(quarter, 2 * quarter)))
     return far + near
 
 

time: 38.1 us -> 38.7 us (1.016)
  starting transfers between devices: 24.4 us -> 25.1 us
    ppermute x12, starting transfers between devices: 18.4 us -> 19.1 us  [swap(): return lax.ppermute(piece, 'seq', [(i, i ^ step) for i in range(n)])]
where the time goes in v19:
time: 38.7 us; the launch traced here: 38.5 us
  starting transfers between devices  25.1 us (65%)
  waiting for transfers between devices  7.85 us (20%)
  Pallas kernels  2.91 us (8%)
  between operations  2.7 us (7%)
    ppermute x12, starting transfers between devices, swap(): return lax.ppermute(piece, 'seq', [(i, i ^ step) for i in range(n)])  19.1 us
    ppermute x4, starting transfers between devices, shards_packed(): lax.ppermute(piece, 'seq', [(i, i ^ 2 * pair[i % 2]) for i in range(n)])  6 us
    ppermute x12, waiting for transfers between devices, swap(): return lax.ppermute(piece, 'seq', [(i, i ^ step) for i in range(n)])  5.32 us
    ppermute x4, waiting for transfers between devices, shards_packed(): lax.ppermute(piece, 'seq', [(i, i ^ 2 * pair[i % 2]) for i in range(n)])  2.54 us
    pallas_call x1, Pallas kernels, shards_packed(): pl.pallas_call(functools.partial(pack_kernel, chips), out_shape=[pltpu.VM...  1.31 us
    pallas_call x1, Pallas kernels, shards_packed(): pl.pallas_call(functools.partial(attend_kernel, chips, rows, parts, pairs...  0.79 us
  transfers between devices with their start and end apart: 16, of which 6 were waited for; matrix products, arithmetic and copies ran while one was open for 0% of the time, Pallas kernels for 0%

profile of v19, /device:TPU:0, one launch (start us, length us, event | category | flops | bytes accessed | tf_op | source)
XLA Modules:
  0.0 38.5 jit_solution(5831841172528632002)
XLA Ops:
  0.6 1.3 %shard_map.174 = (bf16[384,128]{1,0:T(8,128)(2,1)S(1)}, bf16[384,128]{1,0:T(8,128)(2,1)S(1)}, bf16[384,128]{1,0:T(8,128)(2,1)S(1)}, bf16[384,128]{1,0:T(8,128)(2...) custom-call(bf16[16,4096]{1,0:T(8,128)(2,1)} %refs_0_.1, ...), custom_call_target="tpu_custom_call" | custom-call | tf_op jit(solution)/shard_map/pallas_call | solution.py:564
  1.9 6.1 %collective-permute-start = (bf16[384,128]{1,0:T(8,128)(2,1)S(1)}, bf16[384,128]{1,0:T(8,128)(2,1)S(1)}, u32[]{:S(2)}, u32[]{:S(2)}) collective-permute-start(bf16[384,128]{1,0:T(8,128)(2,1)S(1)} %get-tuple-element.19), channel_id=1, source_target_pairs={{0,14},{1,15},{2,12},{3,13},{4,10},{5,11},{6,8},{7,9},{8,6},{9,7},... | collective-permute-start | bytes 294920 | tf_op jit(solution)/shard_map/ppermute | solution.py:534
  8.0 0.2 collective-permute-start.1
  8.2 0.4 %collective-permute-start.2 = (bf16[384,128]{1,0:T(8,128)(2,1)S(1)}, bf16[384,128]{1,0:T(8,128)(2,1)S(1)}, u32[]{:S(2)}, u32[]{:S(2)}) collective-permute-start(bf16[384,128]{1,0:T(8,128)(2,1)S(1)} %get-tuple-element.22), channel_id=1, source_target_pairs={{0,2},{1,3},{2,0},{3,1},{4,6},{5,7},{6,4},{7,5},{8,10},{9,11},{10,... | collective-permute-start | bytes 294920 | tf_op jit(solution)/shard_map/ppermute | solution.py:534
  8.7 0.0 collective-permute-start.3
  8.7 3.1 %collective-permute-start.4 = (bf16[384,128]{1,0:T(8,128)(2,1)S(1)}, bf16[384,128]{1,0:T(8,128)(2,1)S(1)}, u32[]{:S(2)}, u32[]{:S(2)}) collective-permute-start(bf16[384,128]{1,0:T(8,128)(2,1)S(1)} %get-tuple-element.24), channel_id=1, source_target_pairs={{0,6},{1,7},{2,4},{3,5},{4,2},{5,3},{6,0},{7,1},{8,14},{9,15},{10,... | collective-permute-start | bytes 294920 | tf_op jit(solution)/shard_map/ppermute | solution.py:534
  11.7 0.0 collective-permute-done.refs_1_
  11.7 6.0 %collective-permute-start.5 = (bf16[384,128]{1,0:T(8,128)(2,1)S(1)}, bf16[384,128]{1,0:T(8,128)(2,1)S(1)}, u32[]{:S(2)}, u32[]{:S(2)}) collective-permute-start(bf16[384,128]{1,0:T(8,128)(2,1)S(1)} %get-tuple-element.25), channel_id=1, source_target_pairs={{0,10},{1,11},{2,8},{3,9},{4,14},{5,15},{6,12},{7,13},{8,2},{9,3},... | collective-permute-start | bytes 294920 | tf_op jit(solution)/shard_map/ppermute | solution.py:534
  17.8 0.0 collective-permute-done.1.refs_0_.refs_2_
  17.8 1.3 %collective-permute-start.6 = (bf16[384,128]{1,0:T(8,128)(2,1)S(1)}, bf16[384,128]{1,0:T(8,128)(2,1)S(1)}, u32[]{:S(2)}, u32[]{:S(2)}) collective-permute-start(bf16[384,128]{1,0:T(8,128)(2,1)S(1)} %get-tuple-element.26), channel_id=1, source_target_pairs={{0,8},{1,9},{2,10},{3,11},{4,12},{5,13},{6,14},{7,15},{8,0},{9,1},... | collective-permute-start | bytes 294920 | tf_op jit(solution)/shard_map/ppermute | solution.py:534
  21.0 0.0 collective-permute-done.2.refs_1_.refs_3_
  21.0 0.1 collective-permute-start.7
  21.1 0.0 collective-permute-done.3.refs_0_.refs_4_
  21.1 0.6 %collective-permute-start.8 = (bf16[2,384,128]{2,1,0:T(8,128)(2,1)S(1)}, bf16[2,384,128]{2,1,0:T(8,128)(2,1)S(1)}, u32[]{:S(2)}, u32[]{:S(2)}) collective-permute-start(bf16[2,384,128]{2,1,0:T(8,128)(2,1)S(1)} %shard_map.176), channel_id=1, source_target_pairs={{0,1},{1,0},{2,3},{3,2},{4,5},{5,4},{6,7},{7,6},{8,9},{9,8},{10,11... | collective-permute-start | bytes 589832 | tf_op jit(solution)/shard_map/ppermute | solution.py:534
  21.7 0.0 collective-permute-done.4.refs_1_.refs_5_
  21.7 0.1 collective-permute-start.9
  21.8 1.9 %collective-permute-done.5.refs_0_.refs_6_ = bf16[384,128]{1,0:T(8,128)(2,1)S(1)} collective-permute-done((bf16[384,128]{1,0:T(8,128)(2,1)S(1)}, bf16[384,128]{1,0:T(8,128)(2,1)S(1)}, u32[]{:S(2)}, u32[]{:S(2)}) %collective-permute-start.5) | collective-permute-done | bytes 98336 | tf_op jit(solution)/shard_map/ppermute | solution.py:534
  23.7 1.0 %collective-permute-done.6.refs_1_.refs_7_ = bf16[384,128]{1,0:T(8,128)(2,1)S(1)} collective-permute-done((bf16[384,128]{1,0:T(8,128)(2,1)S(1)}, bf16[384,128]{1,0:T(8,128)(2,1)S(1)}, u32[]{:S(2)}, u32[]{:S(2)}) %collective-permute-start.6) | collective-permute-done | bytes 98336 | tf_op jit(solution)/shard_map/ppermute | solution.py:534
  24.7 0.1 collective-permute-start.10
  24.8 0.0 collective-permute-done.7.refs_8_
  24.8 0.0 collective-permute-done.8.refs_9_
  24.8 0.0 collective-permute-done.9.refs_10_
  24.8 1.4 %collective-permute-done.10.refs_11_ = bf16[2,384,128]{2,1,0:T(8,128)(2,1)S(1)} collective-permute-done((bf16[2,384,128]{2,1,0:T(8,128)(2,1)S(1)}, bf16[2,384,128]{2,1,0:T(8,128)(2,1)S(1)}, u32[]{:S(2)}, u32[]{:S(2)}) %collective-permute-start.10) | collective-permute-done | bytes 196640 | tf_op jit(solution)/shard_map/ppermute | solution.py:534
  26.2 0.8 %shard_map.179 = (bf16[256,128]{1,0:T(8,128)(2,1)S(1)}, bf16[256,128]{1,0:T(8,128)(2,1)S(1)}, bf16[256,128]{1,0:T(8,128)(2,1)S(1)}, bf16[256,128]{1,0:T(8,128)(2,1)S(1)}) custom-call(s32[8,128]{1,0:T(8,128)S(1)} %get-tuple-element.20.bounds, bf16[384,128]{1,0:T(8,128)(2,1)S(1)} %get-tuple-element.18.refs_0_, ...), custom_call_target="tpu_custom_call" | custom-call | tf_op jit(solution)/shard_map/pallas_call | solution.py:595
  27.0 2.5 %collective-permute-start.11 = (bf16[256,128]{1,0:T(8,128)(2,1)S(1)}, bf16[256,128]{1,0:T(8,128)(2,1)S(1)}, u32[]{:S(2)}, u32[]{:S(2)}) collective-permute-start(bf16[256,128]{1,0:T(8,128)(2,1)S(1)} %get-tuple-element.28), channel_id=1, source_target_pairs={{0,14},{1,11},{2,12},{3,9},{4,10},{5,15},{6,8},{7,13},{8,6},{9,3},... | collective-permute-start | bytes 196616 | tf_op jit(solution)/shard_map/ppermute | solution.py:603
  29.5 1.5 %collective-permute-start.12 = (bf16[256,128]{1,0:T(8,128)(2,1)S(1)}, bf16[256,128]{1,0:T(8,128)(2,1)S(1)}, u32[]{:S(2)}, u32[]{:S(2)}) collective-permute-start(bf16[256,128]{1,0:T(8,128)(2,1)S(1)} %get-tuple-element.29), channel_id=1, source_target_pairs={{0,12},{1,9},{2,14},{3,11},{4,8},{5,13},{6,10},{7,15},{8,4},{9,1},... | collective-permute-start | bytes 196616 | tf_op jit(solution)/shard_map/ppermute | solution.py:603
  31.0 1.4 %collective-permute-start.13 = (bf16[256,128]{1,0:T(8,128)(2,1)S(1)}, bf16[256,128]{1,0:T(8,128)(2,1)S(1)}, u32[]{:S(2)}, u32[]{:S(2)}) collective-permute-start(bf16[256,128]{1,0:T(8,128)(2,1)S(1)} %get-tuple-element.30), channel_id=1, source_target_pairs={{0,2},{1,5},{2,0},{3,7},{4,6},{5,1},{6,4},{7,3},{8,10},{9,13},{10,... | collective-permute-start | bytes 196616 | tf_op jit(solution)/shard_map/ppermute | solution.py:603
  32.4 0.7 %collective-permute-start.14 = (bf16[256,128]{1,0:T(8,128)(2,1)S(1)}, bf16[256,128]{1,0:T(8,128)(2,1)S(1)}, u32[]{:S(2)}, u32[]{:S(2)}) collective-permute-start(bf16[256,128]{1,0:T(8,128)(2,1)S(1)} %get-tuple-element.31), channel_id=1, source_target_pairs={{0,0},{1,7},{2,2},{3,5},{4,4},{5,3},{6,6},{7,1},{8,8},{9,15},{10,1... | collective-permute-start | bytes 196616 | tf_op jit(solution)/shard_map/ppermute | solution.py:603
  33.0 1.4 %collective-permute-done.11.refs_0_ = bf16[256,128]{1,0:T(8,128)(2,1)S(1)} collective-permute-done((bf16[256,128]{1,0:T(8,128)(2,1)S(1)}, bf16[256,128]{1,0:T(8,128)(2,1)S(1)}, u32[]{:S(2)}, u32[]{:S(2)}) %collective-permute-start.11) | collective-permute-done | bytes 65568 | tf_op jit(solution)/shard_map/ppermute | solution.py:603
  34.5 1.1 %collective-permute-done.12.refs_1_ = bf16[256,128]{1,0:T(8,128)(2,1)S(1)} collective-permute-done((bf16[256,128]{1,0:T(8,128)(2,1)S(1)}, bf16[256,128]{1,0:T(8,128)(2,1)S(1)}, u32[]{:S(2)}, u32[]{:S(2)}) %collective-permute-start.12) | collective-permute-done | bytes 65568 | tf_op jit(solution)/shard_map/ppermute | solution.py:603
  35.6 0.0 collective-permute-done.13.refs_2_
  35.6 0.0 collective-permute-done.14.refs_3_
  35.6 1.2 %collective-permute-start.15 = (bf16[4,128,128]{2,1,0:T(8,128)(2,1)S(1)}, bf16[4,128,128]{2,1,0:T(8,128)(2,1)S(1)}, u32[]{:S(2)}, u32[]{:S(2)}) collective-permute-start(bf16[4,128,128]{2,1,0:T(8,128)(2,1)S(1)} %shard_map.180), channel_id=1, source_target_pairs={{0,1},{1,0},{2,3},{3,2},{4,5},{5,4},{6,7},{7,6},{8,9},{9,8},{10,11... | collective-permute-start | bytes 393224 | tf_op jit(solution)/shard_map/ppermute | solution.py:534
  36.8 1.0 %collective-permute-done.15.refs_4_ = bf16[4,128,128]{2,1,0:T(8,128)(2,1)S(1)} collective-permute-done((bf16[4,128,128]{2,1,0:T(8,128)(2,1)S(1)}, bf16[4,128,128]{2,1,0:T(8,128)(2,1)S(1)}, u32[]{:S(2)}, u32[]{:S(2)}) %collective-permute-start.15) | collective-permute-done | bytes 131104 | tf_op jit(solution)/shard_map/ppermute | solution.py:534
  37.8 0.8 %shard_map.181 = (bf16[16,4096]{1,0:T(8,128)(2,1)}, bf16[8,2048]{1,0:T(8,128)(2,1)}, bf16[16,2048]{1,0:T(8,128)(2,1)}, bf16[8,2048]{1,0:T(8,128)(2,1)}) custom-call(bf16[256,128]{1,0:T(8,128)(2,1)S(1)} %collective-permute-done.11.refs_0_, bf16[256,128]{1,0:T(8,128)(2,1)S(1)} %collective-permute-done.12.refs_1_, ...), custom_call_target="tpu_custom_call" | custom-call | tf_op jit(solution)/shard_map/pallas_call | solution.py:613
  (5 shorter events, 0.1 us)
Async XLA Ops:
  1.9 9.8 %collective-permute-start = (bf16[384,128]{1,0:T(8,128)(2,1)S(1)}, bf16[384,128]{1,0:T(8,128)(2,1)S(1)}, u32[]{:S(2)}, u32[]{:S(2)}) collective-permute-start(bf16[384,128]{1,0:T(8,128)(2,1)S(1)} %get-tuple-element.19), channel_id=1, source_target_pairs={{0,14},{1,15},{2,12},{3,13},{4,10},{5,11},{6,8},{7,9},{8,6},{9,7},... | collective-permute-start | bytes 294920 | tf_op jit(solution)/shard_map/ppermute | solution.py:534
  8.0 9.7 %collective-permute-start.1 = (bf16[384,128]{1,0:T(8,128)(2,1)S(1)}, bf16[384,128]{1,0:T(8,128)(2,1)S(1)}, u32[]{:S(2)}, u32[]{:S(2)}) collective-permute-start(bf16[384,128]{1,0:T(8,128)(2,1)S(1)} %get-tuple-element.21), channel_id=1, source_target_pairs={{0,12},{1,13},{2,14},{3,15},{4,8},{5,9},{6,10},{7,11},{8,4},{9,5},... | collective-permute-start | bytes 294920 | tf_op jit(solution)/shard_map/ppermute | solution.py:534
  8.2 12.8 %collective-permute-start.2 = (bf16[384,128]{1,0:T(8,128)(2,1)S(1)}, bf16[384,128]{1,0:T(8,128)(2,1)S(1)}, u32[]{:S(2)}, u32[]{:S(2)}) collective-permute-start(bf16[384,128]{1,0:T(8,128)(2,1)S(1)} %get-tuple-element.22), channel_id=1, source_target_pairs={{0,2},{1,3},{2,0},{3,1},{4,6},{5,7},{6,4},{7,5},{8,10},{9,11},{10,... | collective-permute-start | bytes 294920 | tf_op jit(solution)/shard_map/ppermute | solution.py:534
  8.7 12.5 %collective-permute-start.3 = (bf16[384,128]{1,0:T(8,128)(2,1)S(1)}, bf16[384,128]{1,0:T(8,128)(2,1)S(1)}, u32[]{:S(2)}, u32[]{:S(2)}) collective-permute-start(bf16[384,128]{1,0:T(8,128)(2,1)S(1)} %get-tuple-element.23), channel_id=1, source_target_pairs={{0,4},{1,5},{2,6},{3,7},{4,0},{5,1},{6,2},{7,3},{8,12},{9,13},{10,... | collective-permute-start | bytes 294920 | tf_op jit(solution)/shard_map/ppermute | solution.py:534
  8.7 13.0 %collective-permute-start.4 = (bf16[384,128]{1,0:T(8,128)(2,1)S(1)}, bf16[384,128]{1,0:T(8,128)(2,1)S(1)}, u32[]{:S(2)}, u32[]{:S(2)}) collective-permute-start(bf16[384,128]{1,0:T(8,128)(2,1)S(1)} %get-tuple-element.24), channel_id=1, source_target_pairs={{0,6},{1,7},{2,4},{3,5},{4,2},{5,3},{6,0},{7,1},{8,14},{9,15},{10,... | collective-permute-start | bytes 294920 | tf_op jit(solution)/shard_map/ppermute | solution.py:534
  11.7 12.0 %collective-permute-start.5 = (bf16[384,128]{1,0:T(8,128)(2,1)S(1)}, bf16[384,128]{1,0:T(8,128)(2,1)S(1)}, u32[]{:S(2)}, u32[]{:S(2)}) collective-permute-start(bf16[384,128]{1,0:T(8,128)(2,1)S(1)} %get-tuple-element.25), channel_id=1, source_target_pairs={{0,10},{1,11},{2,8},{3,9},{4,14},{5,15},{6,12},{7,13},{8,2},{9,3},... | collective-permute-start | bytes 294920 | tf_op jit(solution)/shard_map/ppermute | solution.py:534
  17.8 7.0 %collective-permute-start.6 = (bf16[384,128]{1,0:T(8,128)(2,1)S(1)}, bf16[384,128]{1,0:T(8,128)(2,1)S(1)}, u32[]{:S(2)}, u32[]{:S(2)}) collective-permute-start(bf16[384,128]{1,0:T(8,128)(2,1)S(1)} %get-tuple-element.26), channel_id=1, source_target_pairs={{0,8},{1,9},{2,10},{3,11},{4,12},{5,13},{6,14},{7,15},{8,0},{9,1},... | collective-permute-start | bytes 294920 | tf_op jit(solution)/shard_map/ppermute | solution.py:534
  21.0 3.8 %collective-permute-start.7 = (bf16[2,384,128]{2,1,0:T(8,128)(2,1)S(1)}, bf16[2,384,128]{2,1,0:T(8,128)(2,1)S(1)}, u32[]{:S(2)}, u32[]{:S(2)}) collective-permute-start(bf16[2,384,128]{2,1,0:T(8,128)(2,1)S(1)} %get-tuple-element.27), channel_id=1, source_target_pairs={{0,1},{1,0},{2,3},{3,2},{4,5},{5,4},{6,7},{7,6},{8,9},{9,8},{10,11... | collective-permute-start | bytes 589832 | tf_op jit(solution)/shard_map/ppermute | solution.py:534
  21.1 3.7 %collective-permute-start.8 = (bf16[2,384,128]{2,1,0:T(8,128)(2,1)S(1)}, bf16[2,384,128]{2,1,0:T(8,128)(2,1)S(1)}, u32[]{:S(2)}, u32[]{:S(2)}) collective-permute-start(bf16[2,384,128]{2,1,0:T(8,128)(2,1)S(1)} %shard_map.176), channel_id=1, source_target_pairs={{0,1},{1,0},{2,3},{3,2},{4,5},{5,4},{6,7},{7,6},{8,9},{9,8},{10,11... | collective-permute-start | bytes 589832 | tf_op jit(solution)/shard_map/ppermute | solution.py:534
  21.7 3.1 %collective-permute-start.9 = (bf16[2,384,128]{2,1,0:T(8,128)(2,1)S(1)}, bf16[2,384,128]{2,1,0:T(8,128)(2,1)S(1)}, u32[]{:S(2)}, u32[]{:S(2)}) collective-permute-start(bf16[2,384,128]{2,1,0:T(8,128)(2,1)S(1)} %shard_map.177), channel_id=1, source_target_pairs={{0,1},{1,0},{2,3},{3,2},{4,5},{5,4},{6,7},{7,6},{8,9},{9,8},{10,11... | collective-permute-start | bytes 589832 | tf_op jit(solution)/shard_map/ppermute | solution.py:534
  24.7 1.5 %collective-permute-start.10 = (bf16[2,384,128]{2,1,0:T(8,128)(2,1)S(1)}, bf16[2,384,128]{2,1,0:T(8,128)(2,1)S(1)}, u32[]{:S(2)}, u32[]{:S(2)}) collective-permute-start(bf16[2,384,128]{2,1,0:T(8,128)(2,1)S(1)} %shard_map.178), channel_id=1, source_target_pairs={{0,1},{1,0},{2,3},{3,2},{4,5},{5,4},{6,7},{7,6},{8,9},{9,8},{10,11... | collective-permute-start | bytes 589832 | tf_op jit(solution)/shard_map/ppermute | solution.py:534
  27.0 7.4 %collective-permute-start.11 = (bf16[256,128]{1,0:T(8,128)(2,1)S(1)}, bf16[256,128]{1,0:T(8,128)(2,1)S(1)}, u32[]{:S(2)}, u32[]{:S(2)}) collective-permute-start(bf16[256,128]{1,0:T(8,128)(2,1)S(1)} %get-tuple-element.28), channel_id=1, source_target_pairs={{0,14},{1,11},{2,12},{3,9},{4,10},{5,15},{6,8},{7,13},{8,6},{9,3},... | collective-permute-start | bytes 196616 | tf_op jit(solution)/shard_map/ppermute | solution.py:603
  29.5 6.1 %collective-permute-start.12 = (bf16[256,128]{1,0:T(8,128)(2,1)S(1)}, bf16[256,128]{1,0:T(8,128)(2,1)S(1)}, u32[]{:S(2)}, u32[]{:S(2)}) collective-permute-start(bf16[256,128]{1,0:T(8,128)(2,1)S(1)} %get-tuple-element.29), channel_id=1, source_target_pairs={{0,12},{1,9},{2,14},{3,11},{4,8},{5,13},{6,10},{7,15},{8,4},{9,1},... | collective-permute-start | bytes 196616 | tf_op jit(solution)/shard_map/ppermute | solution.py:603
  31.0 4.6 %collective-permute-start.13 = (bf16[256,128]{1,0:T(8,128)(2,1)S(1)}, bf16[256,128]{1,0:T(8,128)(2,1)S(1)}, u32[]{:S(2)}, u32[]{:S(2)}) collective-permute-start(bf16[256,128]{1,0:T(8,128)(2,1)S(1)} %get-tuple-element.30), channel_id=1, source_target_pairs={{0,2},{1,5},{2,0},{3,7},{4,6},{5,1},{6,4},{7,3},{8,10},{9,13},{10,... | collective-permute-start | bytes 196616 | tf_op jit(solution)/shard_map/ppermute | solution.py:603
  32.4 3.2 %collective-permute-start.14 = (bf16[256,128]{1,0:T(8,128)(2,1)S(1)}, bf16[256,128]{1,0:T(8,128)(2,1)S(1)}, u32[]{:S(2)}, u32[]{:S(2)}) collective-permute-start(bf16[256,128]{1,0:T(8,128)(2,1)S(1)} %get-tuple-element.31), channel_id=1, source_target_pairs={{0,0},{1,7},{2,2},{3,5},{4,4},{5,3},{6,6},{7,1},{8,8},{9,15},{10,1... | collective-permute-start | bytes 196616 | tf_op jit(solution)/shard_map/ppermute | solution.py:603
  35.6 2.2 %collective-permute-start.15 = (bf16[4,128,128]{2,1,0:T(8,128)(2,1)S(1)}, bf16[4,128,128]{2,1,0:T(8,128)(2,1)S(1)}, u32[]{:S(2)}, u32[]{:S(2)}) collective-permute-start(bf16[4,128,128]{2,1,0:T(8,128)(2,1)S(1)} %shard_map.180), channel_id=1, source_target_pairs={{0,1},{1,0},{2,3},{3,2},{4,5},{5,4},{6,7},{7,6},{8,9},{9,8},{10,11... | collective-permute-start | bytes 393224 | tf_op jit(solution)/shard_map/ppermute | solution.py:534
